TPU v7x, 32 devices: a whole 2x2x4 slice. The times are simulated.
32 devices in a mesh: dp: 2 (over core), mp: 16 (over z, y, x).
Axes of the slice: x: 2, y: 2, z: 4, core: 2. Of those that a mesh axis runs over, the one named last changes fastest.
Arguments:
- tokens: bfloat16 [512, 8192], P('mp', 'dp'), may hold values from -48 to 48
- lengths: int32 [2], P('dp'), may hold values from 512 to 4096, as said below
- norm_gain: float32 [512], P('mp'), may hold values from 0.5 to 1.5
- norm_bias: float32 [512], P('mp'), may hold values from -1.5 to 1.5
- log_step: float32 [512], P('mp'), may hold values from -4.6 to -2.3
- decay_log: float32 [512, 32], P('mp'), may hold values from -2.3 to 0
- frequency: float32 [512, 32], P('mp'), may hold values from 0.1 to 10
- readout: float32 [512, 64], P('mp'), may hold values from -2 to 2
- liquid_readout: float32 [512, 64], P('mp'), may hold values from -2 to 2
- skip_gain: float32 [512], P('mp'), may hold values from -1 to 1
- value_weight: bfloat16 [512, 512], P(None, 'mp'), may hold values from -0.25 to 0.25
- gate_weight: bfloat16 [512, 512], P(None, 'mp'), may hold values from -0.25 to 0.25
- value_bias: bfloat16 [512], P('mp'), may hold values from -1.5 to 1.5
- gate_bias: bfloat16 [512], P('mp'), may hold values from -1.5 to 1.5
- grad_out: bfloat16 [512, 8192], P('mp', 'dp'), may hold values from -6 to 6
Outputs:
- layer_out: bfloat16 [512, 8192], P('mp', 'dp')
- grad_tokens: float32 [512, 8192], P('mp', 'dp')
- gain_grad: float32 [512], P('mp')
- bias_grad: float32 [512], P('mp')
- step_grad: float32 [512], P('mp')
- decay_grad: float32 [512, 32], P('mp')
- frequency_grad: float32 [512, 32], P('mp')
- readout_grad: float32 [512, 64], P('mp')
- liquid_grad: float32 [512, 64], P('mp')
- skip_grad: float32 [512], P('mp')
- value_grad: float32 [512, 512], P(None, 'mp')
- gate_grad: float32 [512, 512], P(None, 'mp')
- value_bias_grad: float32 [512], P('mp')
- gate_bias_grad: float32 [512], P('mp')
Inputs may be any that keep to these rules, and one draw needn't show every extreme that they name: `lengths`: A document's valid length; some document is full and some has 512 valid positions.
All inputs are finite; a program needn't handle non-finite values.
Results may differ from a plain program's by a relative error of at most 0.002.
The roundings to bfloat16 on the way count: a program that leaves them out, or rounds other values in their place, can miss the bound.
Values may be sent and summed in bfloat16 or wider, within the bound.
No kernel may reach another device: no remote copies, remote signals or barrier semaphores. Data moves between devices by JAX's collectives and lax.ppermute only.
A program may use at most 128 MiB of HBM per device.

v0:
```python
from functools import partial

import jax
import jax.numpy as jnp
import numpy as np
from jax import lax
from jax.sharding import PartitionSpec as P

H = 512
BLK = 256


def mode_tables(log_step, decay_log, frequency, block, block_count):
    step_size = jnp.exp(log_step)[:, None]
    real_rate = -jnp.exp(decay_log)
    real_step = step_size * real_rate
    imag_step = step_size * frequency
    growth = jnp.exp(real_step)
    num_real = growth * jnp.cos(imag_step) - 1.0
    num_imag = growth * jnp.sin(imag_step)
    denominator = real_rate * real_rate + frequency * frequency
    in_real = (num_real * real_rate + num_imag * frequency) / denominator
    in_imag = (num_imag * real_rate - num_real * frequency) / denominator

    def powers(places):
        envelope = jnp.exp(real_step[:, :, None] * places)
        phases = imag_step[:, :, None] * places
        return (envelope * jnp.cos(phases), envelope * jnp.sin(phases))

    near = powers(jnp.arange(block).astype(jnp.float32))
    backward_pow = powers(-jnp.arange(block).astype(jnp.float32))
    feed = powers((block - np.arange(block)).astype(np.float32))
    lags = np.arange(block_count)[:, None] - 1 - np.arange(block_count)[None, :]
    earlier = jnp.asarray((lags >= 0).astype(np.float32)).reshape(1, 1, block_count, block_count)
    jump_places = (block * np.maximum(lags, 0)).astype(np.float32).reshape(-1)
    jump_real, jump_imag = powers(jnp.asarray(jump_places))
    shape = jump_real.shape[:2] + (block_count, block_count)
    jump = (jump_real.reshape(shape) * earlier, jump_imag.reshape(shape) * earlier)
    return (in_real, in_imag, near, backward_pow, feed, jump)


def block_conv(coeffs, tables, rows):
    in_real, in_imag, near, backward_pow, feed, jump = tables
    mode_count = in_real.shape[1]
    block = rows.shape[3]
    high = lax.Precision.HIGHEST
    coef_real = coeffs[:, :mode_count]
    coef_imag = coeffs[:, mode_count:]
    prod_real = coef_real * in_real - coef_imag * in_imag
    prod_imag = coef_real * in_imag + coef_imag * in_real
    lead_real = prod_real[:, :, None] * near[0] - prod_imag[:, :, None] * near[1]
    lead_imag = prod_real[:, :, None] * near[1] + prod_imag[:, :, None] * near[0]
    lag_matrix = 2.0 * (
        jnp.einsum("hmr,hmc->hrc", lead_real, backward_pow[0], precision=high)
        - jnp.einsum("hmr,hmc->hrc", lead_imag, backward_pow[1], precision=high)
    )
    lower = jnp.asarray(np.arange(block)[:, None] >= np.arange(block)[None, :])[None]
    toeplitz = jnp.where(lower, lag_matrix, 0.0)
    inside = jnp.einsum("hdnc,hrc->hdnr", rows, toeplitz, precision=high)
    up_real = jnp.einsum("hmc,hdnc->hmdn", feed[0], rows, precision=high)
    up_imag = jnp.einsum("hmc,hdnc->hmdn", feed[1], rows, precision=high)
    st_real = jnp.einsum("hmnk,hmdk->hmdn", jump[0], up_real, precision=high) - jnp.einsum(
        "hmnk,hmdk->hmdn", jump[1], up_imag, precision=high
    )
    st_imag = jnp.einsum("hmnk,hmdk->hmdn", jump[0], up_imag, precision=high) + jnp.einsum(
        "hmnk,hmdk->hmdn", jump[1], up_real, precision=high
    )
    pr = prod_real[:, :, None, None]
    pi = prod_imag[:, :, None, None]
    acc_real = pr * st_real - pi * st_imag
    acc_imag = pr * st_imag + pi * st_real
    cross = 2.0 * (
        jnp.einsum("hmdn,hmi->hdni", acc_real, near[0], precision=high)
        - jnp.einsum("hmdn,hmi->hdni", acc_imag, near[1], precision=high)
    )
    return inside + cross


def local_mixer(
    normed,
    norm_gain,
    norm_bias,
    log_step,
    decay_log,
    frequency,
    readout,
    liquid_readout,
    skip_gain,
    valid_mask,
    doc_count,
    block,
):
    local_width, tok_rows = normed.shape
    length = tok_rows // doc_count
    block_count = length // block
    signal = (normed * norm_gain[:, None] + norm_bias[:, None]) * valid_mask
    signal_docs = signal.reshape(local_width, doc_count, length)
    earlier = jnp.concatenate(
        [jnp.zeros((local_width, doc_count, 1), jnp.float32), signal_docs[:, :, :-1]], axis=2
    )
    liquid_docs = signal_docs * earlier
    tables = mode_tables(log_step, decay_log, frequency, block, block_count)
    block_shape = (local_width, doc_count, block_count, block)
    convolved = block_conv(readout, tables, signal_docs.reshape(block_shape)) + block_conv(
        liquid_readout, tables, liquid_docs.reshape(block_shape)
    )
    mixer_pre = convolved.reshape(local_width, tok_rows) + skip_gain[:, None] * signal
    return valid_mask * jax.nn.gelu(mixer_pre, approximate=True)


def per_device(
    tokens,
    lengths,
    norm_gain,
    norm_bias,
    log_step,
    decay_log,
    frequency,
    readout,
    liquid_readout,
    skip_gain,
    value_weight,
    gate_weight,
    value_bias,
    gate_bias,
    grad_out,
):
    local_width, tok_rows = tokens.shape
    doc_count = lengths.shape[0]
    length = tok_rows // doc_count
    token_vals = tokens.astype(jnp.float32)
    places = jnp.arange(length, dtype=jnp.int32)
    valid_mask = (places[None, :] < lengths[:, None]).astype(jnp.float32)
    row_sum, row_squares = lax.psum(
        (jnp.sum(token_vals, axis=0), jnp.sum(token_vals * token_vals, axis=0)), "mp"
    )
    row_mean = row_sum / H
    row_var = row_squares / H - row_mean * row_mean
    inv_std = lax.rsqrt(row_var + 1e-05)[None, :]
    normed = (token_vals - row_mean[None, :]) * inv_std
    mixer_fn = partial(local_mixer, valid_mask=valid_mask, doc_count=doc_count, block=BLK)
    mixed, mixer_back = jax.vjp(
        mixer_fn,
        normed,
        norm_gain,
        norm_bias,
        log_step,
        decay_log,
        frequency,
        readout,
        liquid_readout,
        skip_gain,
    )
    mixed_low = mixed.astype(jnp.bfloat16)
    grad_in = grad_out.astype(jnp.float32)
    contract_first = (((0,), (0,)), ((), ()))
    contract_last = (((1,), (1,)), ((), ()))
    weight_cat = jnp.concatenate([value_weight, gate_weight], axis=1)
    bias_cat = jnp.concatenate([value_bias, gate_bias]).astype(jnp.float32)
    weight_rows = weight_cat
    projected = (
        lax.dot_general(
            weight_rows,
            lax.all_gather(mixed_low, "mp", axis=0, tiled=True),
            contract_first,
            preferred_element_type=jnp.float32,
        )
        + bias_cat[:, None]
    )
    value_pre = projected[:local_width]
    gate_pre = projected[local_width:]
    gate_sig = jax.nn.sigmoid(gate_pre)
    glu_out = value_pre * gate_sig
    grad_pre = jnp.concatenate(
        [grad_in * gate_sig, grad_in * value_pre * gate_sig * (1.0 - gate_sig)], axis=0
    ).astype(jnp.bfloat16)
    bias_grads = jnp.sum(grad_pre.astype(jnp.float32), axis=1)
    weight_grads = lax.dot_general(
        lax.all_gather(mixed_low, "mp", axis=0, tiled=True),
        grad_pre,
        contract_last,
        preferred_element_type=jnp.float32,
    )
    weight_rows = weight_cat
    grad_mixed = lax.psum_scatter(
        jnp.dot(weight_rows, grad_pre, preferred_element_type=jnp.float32),
        "mp",
        scatter_dimension=0,
        tiled=True,
    )
    value_wgrad = weight_grads[:, :local_width]
    gate_wgrad = weight_grads[:, local_width:]
    value_bgrad = bias_grads[:local_width]
    gate_bgrad = bias_grads[local_width:]
    layer_out = (token_vals + glu_out).astype(jnp.bfloat16)
    back_grads = mixer_back(grad_mixed)
    grad_normed = back_grads[0]
    norm_first, norm_second = (
        lax.psum(jnp.sum(grad_normed, axis=0).astype(jnp.bfloat16), "mp").astype(jnp.float32),
        lax.psum(jnp.sum(grad_normed * normed, axis=0).astype(jnp.bfloat16), "mp").astype(
            jnp.float32
        ),
    )
    grad_tokens = (
        inv_std * (grad_normed - norm_first[None, :] / H - normed * norm_second[None, :] / H)
        + grad_in
    )
    summed = lax.psum(
        (
            back_grads[1],
            back_grads[2],
            back_grads[3],
            back_grads[4],
            back_grads[5],
            back_grads[6],
            back_grads[7],
            back_grads[8],
            value_wgrad,
            gate_wgrad,
            value_bgrad,
            gate_bgrad,
        ),
        "dp",
    )
    return (layer_out, grad_tokens) + tuple(summed)


def solution(mesh):
    in_specs = (
        P("mp", "dp"),
        P("dp"),
        P("mp"),
        P("mp"),
        P("mp"),
        P("mp", None),
        P("mp", None),
        P("mp", None),
        P("mp", None),
        P("mp"),
        P(None, "mp"),
        P(None, "mp"),
        P("mp"),
        P("mp"),
        P("mp", "dp"),
    )
    out_specs = (
        P("mp", "dp"),
        P("mp", "dp"),
        P("mp"),
        P("mp"),
        P("mp"),
        P("mp", None),
        P("mp", None),
        P("mp", None),
        P("mp", None),
        P("mp"),
        P(None, "mp"),
        P(None, "mp"),
        P("mp"),
        P("mp"),
    )
    return jax.shard_map(
        per_device, mesh=mesh, in_specs=in_specs, out_specs=out_specs, check_vma=False
    )
```

profile of v0, /device:TPU:0, one launch (start us, length us, event | category | flops | bytes accessed | tf_op | source)
XLA Modules:
  0.0 811.6 jit_solution(6821184270844527234)
XLA Ops:
  10.7 78.6 %all-reduce.6 = (f32[4096]{0:T(1024)S(1)}, f32[4096]{0:T(1024)S(1)}) all-reduce(f32[4096]{0:T(1024)S(1)} %get-tuple-element.60, f32[4096]{0:T(1024)S(1)} %get-tuple-element.59), channel_id=1, replica_groups=mesh['dp'=2,'mp'=16] {'mp'}, use_global_device_ids=true, to_apply=%region_3.0 | all-reduce | flops 8192 | bytes 65536 | tf_op jit(solution)/shard_map/psum | solution.py:134
  111.4 28.9 %multiply_reduce_fusion.10 = (f32[32,32,16]{1,2,0:T(8,128)S(1)}, f32[32,32,16]{1,2,0:T(8,128)S(1)}, f32[32,32,16]{1,2,0:T(8,128)S(1)}, f32[32,32,16]{1,2,0:T(8,1...) fusion(f32[32,32,16]{1,2,0:T(8,128)S(1)} %fusion.107, ...), kind=kLoop, calls=%fused_computation.44 | loop fusion | flops 5636096 | bytes 796672 | tf_op jit(solution)/shard_map/jvp(hmnk,hmdk->hmdn)/dot_general | solution.py:62
  149.4 14.4 %fusion.125 = f32[32,256,256]{2,1,0:T(8,128)S(1)} fusion(f32[256]{0:T(256)S(1)} %fusion.306, f32[32,32]{1,0:T(8,128)S(1)} %get-tuple-element.141, f32[32,32]{1,0:T(8,128)S(1)} %get-tuple-element.119, f32[256]{0:T(256)S(1)} %iota_convert_fusion, f32[32,32]{1,0:T(8,128)S(1)} %get-tuple-element.151, f32[32,32]{1,0:T(8,128)S(1)} %get-tuple-element.140), kind=kOutput, calls=%fused_computation.170 | convolution fusion | flops 807927808 | bytes 8407040 | tf_op jit(solution)/shard_map/jvp(hmr,hmc->hrc)/dot_general | solution.py:54
  164.1 14.6 %fusion.123 = f32[32,256,256]{2,1,0:T(8,128)S(1)} fusion(f32[32,32]{1,0:T(8,128)S(1)} %get-tuple-element.150, f32[32,32]{1,0:T(8,128)S(1)} %get-tuple-element.115, f32[256]{0:T(256)S(1)} %fusion.306, f32[32,32]{1,0:T(8,128)S(1)} %get-tuple-element.119, f32[256]{0:T(256)S(1)} %iota_convert_fusion, f32[32,32]{1,0:T(8,128)S(1)} %get-tuple-element.151), kind=kOutput, calls=%fused_computation.169 | convolution fusion | flops 807927808 | bytes 8407040 | tf_op jit(solution)/shard_map/jvp(hmr,hmc->hrc)/dot_general | solution.py:54
  187.6 15.5 %multiply_select_fusion.1 = f32[32,256,256]{2,1,0:T(8,128)S(1)} fusion(f32[32,256,256]{2,1,0:T(8,128)S(1)} %fusion.125, pred[256,256]{1,0:T(8,128)(4,1)S(1)} %copy.150, f32[256]{0:T(256)S(1)} %fusion.306, f32[32,32]{1,0:T(8,128)S(1)} %get-tuple-element.141, f32[32,32]{1,0:T(8,128)S(1)} %get-tuple-element.119, f32[256]{0:T(256)S(1)} %iota_convert_fusion, ...), kind=kOutput, calls=%fused_computation.3 | convolution fusion | flops 814219264 | bytes 16861184 | tf_op jit(solution)/shard_map/jvp(hmr,hmc->hrc)/dot_general | solution.py:55
  203.1 15.6 %multiply_select_fusion = f32[32,256,256]{2,1,0:T(8,128)S(1)} fusion(f32[32,256,256]{2,1,0:T(8,128)S(1)} %fusion.123, pred[256,256]{1,0:T(8,128)(4,1)S(1)} %copy.150, f32[32,32]{1,0:T(8,128)S(1)} %get-tuple-element.150, f32[32,32]{1,0:T(8,128)S(1)} %get-tuple-element.115, f32[256]{0:T(256)S(1)} %fusion.306, f32[32,32]{1,0:T(8,128)S(1)} %get-tuple-element.119, ...), kind=kOutput, calls=%fused_computation.2 | convolution fusion | flops 814219264 | bytes 16861184 | tf_op jit(solution)/shard_map/jvp(hmr,hmc->hrc)/dot_general | solution.py:55
  218.7 7.1 convolution_add_fusion.10
  225.9 7.0 fusion.79
  234.5 71.9 %all-gather.2.cloned.1.call-done = bf16[512,4096]{1,0:T(8,128)(2,1)} async-done(((bf16[32,4096]{1,0:T(8,128)(2,1)}), bf16[512,4096]{1,0:T(8,128)(2,1)}) %all-gather.2.cloned.1.call-update) | async-done | bytes 4194320 | tf_op jit(solution)/shard_map/all_gather | solution.py:164
  322.2 171.2 %reduce-scatter.2.cloned.1.call-done = f32[32,4096]{1,0:T(8,128)} async-done(((f32[512,4096]{1,0:T(8,128)}), f32[32,4096]{1,0:T(8,128)}) %reduce-scatter.2.cloned.1.call-update) | async-done | bytes 524304 | tf_op jit(solution)/shard_map/reduce_scatter | solution.py:185
  507.2 25.3 %fusion.25 = (f32[32,32]{1,0:T(8,128)}, f32[32,32]{1,0:T(8,128)}, f32[32,32,16]{1,2,0:T(8,128)S(1)}, f32[32,32,16]{1,2,0:T(8,128)S(1)}, f32[32,32,16]{1,2,0:T(8,...) fusion(f32[32,32,16]{1,2,0:T(8,128)S(1)} %get-tuple-element.130, ...), kind=kLoop, calls=%fused_computation.32 | loop fusion | flops 13498368 | bytes 1198080 | tf_op jit(solution)/shard_map/transpose(jvp())/reduce_sum | solution.py:26
  540.2 6.8 fusion.342
  547.1 11.5 %fusion.14 = f32[32,32,256]{2,1,0:T(8,128)S(1)} fusion(f32[32,256,256]{2,1,0:T(8,128)S(1)} %fusion.342, pred[256,256]{1,0:T(8,128)(4,1)S(1)} %copy.150, f32[256]{0:T(256)S(1)} %copy-done.74, f32[32,32]{1,0:T(8,128)S(1)} %get-tuple-element.119, f32[32,32]{1,0:T(8,128)S(1)} %get-tuple-element.151), kind=kOutput, calls=%fused_computation.20 | convolution fusion | flops 810287104 | bytes 9511936 | tf_op jit(solution)/shard_map/transpose(jvp(hmr,hmc->hrc))/dot_general | solution.py:54
  558.6 11.7 %fusion.4 = f32[32,32,256]{2,1,0:T(8,128)S(1)} fusion(f32[32,256,256]{2,1,0:T(8,128)S(1)} %fusion.342, pred[256,256]{1,0:T(8,128)(4,1)S(1)} %copy.150, f32[256]{0:T(256)S(1)} %copy-done.74, f32[32,32]{1,0:T(8,128)S(1)} %get-tuple-element.119, f32[32,32]{1,0:T(8,128)S(1)} %get-tuple-element.151), kind=kOutput, calls=%fused_computation.8 | convolution fusion | flops 812384256 | bytes 9511936 | tf_op jit(solution)/shard_map/transpose(jvp(hmr,hmc->hrc))/dot_general | solution.py:55
  575.0 11.0 %fusion.15 = f32[32,32,256]{2,1,0:T(8,128)} fusion(f32[32,256,256]{2,1,0:T(8,128)S(1)} %fusion.342, pred[256,256]{1,0:T(8,128)(4,1)S(1)} %copy.150, f32[32,32]{1,0:T(8,128)S(1)} %copy-done.46, f32[32,32]{1,0:T(8,128)S(1)} %get-tuple-element.115, f32[32,32]{1,0:T(8,128)S(1)} %get-tuple-element.119, f32[256]{0:T(256)S(1)} %copy-done.71, ...), kind=kOutput, calls=%fused_computation.21 | convolution fusion | flops 811335680 | bytes 9520128 | tf_op jit(solution)/shard_map/transpose(jvp(hmr,hmc->hrc))/dot_general | solution.py:54
  586.0 6.8 fusion.343
  592.8 11.5 %fusion.16 = f32[32,32,256]{2,1,0:T(8,128)S(1)} fusion(f32[32,256,256]{2,1,0:T(8,128)S(1)} %fusion.343, pred[256,256]{1,0:T(8,128)(4,1)S(1)} %copy.150, f32[256]{0:T(256)S(1)} %copy-done.74, f32[32,32]{1,0:T(8,128)S(1)} %get-tuple-element.119, f32[32,32]{1,0:T(8,128)S(1)} %get-tuple-element.151), kind=kOutput, calls=%fused_computation.22 | convolution fusion | flops 810287104 | bytes 9511936 | tf_op jit(solution)/shard_map/transpose(jvp(hmr,hmc->hrc))/dot_general | solution.py:54
  604.3 12.5 %fusion = f32[32,32,256]{2,1,0:T(8,128)} fusion(f32[32,256,256]{2,1,0:T(8,128)S(1)} %fusion.343, pred[256,256]{1,0:T(8,128)(4,1)S(1)} %copy.150, f32[256]{0:T(256)S(1)} %copy-done.74, f32[32,32]{1,0:T(8,128)S(1)} %get-tuple-element.119, f32[32,32]{1,0:T(8,128)S(1)} %get-tuple-element.151), kind=kOutput, calls=%fused_computation.4 | convolution fusion | flops 812384256 | bytes 9511936 | tf_op jit(solution)/shard_map/transpose(jvp(hmr,hmc->hrc))/dot_general | solution.py:55
  616.9 11.3 %fusion.2 = f32[32,32,256]{2,1,0:T(8,128)} fusion(f32[32,256,256]{2,1,0:T(8,128)S(1)} %fusion.343, pred[256,256]{1,0:T(8,128)(4,1)S(1)} %copy.150, f32[32,32]{1,0:T(8,128)S(1)} %copy-done.43, f32[32,32]{1,0:T(8,128)S(1)} %get-tuple-element.119, f32[256]{0:T(256)S(1)} %copy-done.71, f32[32,32]{1,0:T(8,128)S(1)} %get-tuple-element.151, f32[32,32]{1,0:T(8,128)S(1)} %copy-done.40), kind=kOutput, calls=%fused_computation.6 | convolution fusion | flops 813432832 | bytes 9520128 | tf_op jit(solution)/shard_map/transpose(jvp(hmr,hmc->hrc))/dot_general | solution.py:55
  652.8 8.3 %convolution_add_fusion.7 = f32[32,16,256]{2,1,0:T(8,128)} fusion(f32[32,16,256]{2,1,0:T(8,128)S(1)} %convolution_add_fusion.11, f32[32,16,256]{2,1,0:T(8,128)S(1)} %bitcast.124, f32[32,256,256]{2,1,0:T(8,128)} %copy-done), kind=kOutput, calls=%fused_computation.115 | convolution fusion | flops 402784256 | bytes 9961472 | tf_op jit(solution)/shard_map/transpose(jvp(hdnc,hrc->hdnr))/dot_general | solution.py:59
  669.2 77.8 %all-reduce.9 = (bf16[4096]{0:T(1024)(128)(2,1)}, bf16[4096]{0:T(1024)(128)(2,1)}) all-reduce(bf16[4096]{0:T(1024)(128)(2,1)} %get-tuple-element.31, bf16[4096]{0:T(1024)(128)(2,1)} %get-tuple-element.32), channel_id=1, replica_groups=mesh['dp'=2,'mp'=16] {'mp'}, use_global_device_ids=true, to_apply=%region_8.9 | all-reduce | flops 8192 | bytes 32768 | tf_op jit(solution)/shard_map/psum | solution.py:200
  750.9 12.3 %fusion.75 = f32[32,32,256]{2,1,0:T(8,128)S(1)} fusion(f32[32,32,256]{2,1,0:T(8,128)} %fusion.15, f32[32,256,256]{2,1,0:T(8,128)} %copy-done.2, pred[256,256]{1,0:T(8,128)(4,1)S(1)} %copy.150, f32[32,32]{1,0:T(8,128)} %copy-done.42, f32[32,32]{1,0:T(8,128)S(1)} %get-tuple-element.119, f32[256]{0:T(256)} %copy-done.70, ...), kind=kOutput, calls=%fused_computation.113 | convolution fusion | flops 811597824 | bytes 10568704 | tf_op jit(solution)/shard_map/transpose(jvp(hmr,hmc->hrc))/dot_general | solution.py:54
  763.2 12.5 %fusion.76 = f32[32,32,256]{2,1,0:T(8,128)S(1)} fusion(f32[32,32,256]{2,1,0:T(8,128)S(1)} %copy-done.110, f32[32,256,256]{2,1,0:T(8,128)} %copy-done.1, pred[256,256]{1,0:T(8,128)(4,1)S(1)} %copy.150, f32[32,32]{1,0:T(8,128)S(1)} %copy-done.47, f32[32,32]{1,0:T(8,128)S(1)} %get-tuple-element.115, f32[32,32]{1,0:T(8,128)S(1)} %get-tuple-element.119, ...), kind=kOutput, calls=%fused_computation.114 | convolution fusion | flops 813694976 | bytes 10568704 | tf_op jit(solution)/shard_map/transpose(jvp(hmr,hmc->hrc))/dot_general | solution.py:55
  779.9 17.1 %fusion.102 = (f32[32,32]{1,0:T(8,128)S(1)}, f32[32,32]{1,0:T(8,128)S(1)}, f32[32,32]{1,0:T(8,128)S(1)}, f32[32,32]{1,0:T(8,128)S(1)}, f32[32,32]{1,0:T(8,128)S(...) fusion(f32[32,32,256]{2,1,0:T(8,128)S(1)} %convolution_add_fusi, ...), kind=kOutput, calls=%fused_computation.148 | convolution fusion | flops 68421632 | bytes 11209728 | tf_op jit(solution)/shard_map/transpose(jvp(hmc,hdnc->hmdn))/dot_general | solution.py:61
  (306 shorter events, 133.9 us)
Async XLA Ops:
  7.2 89.8 %copy-start.108 = (f32[256]{0:T(256)S(1)}, f32[256]{0:T(256)}, u32[]{:S(2)}) copy-start(f32[256]{0:T(256)} %constant.42.clone) | copy-start | bytes 3076
  7.2 94.3 %copy-start.4 = (bf16[32,4096]{1,0:T(8,128)(2,1)S(1)}, bf16[32,4096]{1,0:T(8,128)(2,1)}, u32[]{:S(2)}) copy-start(bf16[32,4096]{1,0:T(8,128)(2,1)} %param.20) | copy-start | bytes 786436
  7.2 94.3 %copy-start.84 = (f32[32]{0:T(128)S(1)}, f32[32]{0:T(128)}, u32[]{:S(2)}) copy-start(f32[32]{0:T(128)} %param.22) | copy-start | bytes 388
  7.2 94.3 %copy-start.87 = (f32[32]{0:T(128)S(1)}, f32[32]{0:T(128)}, u32[]{:S(2)}) copy-start(f32[32]{0:T(128)} %param.23) | copy-start | bytes 388
  7.2 299.2 %all-gather.2.cloned.1.call-start = ((), (), s32[]{:S(2)}) async-start(), calls=%async_computation.1 | async-start | bytes 4456448 | tf_op jit(solution)/shard_map/all_gather | solution.py:164
  7.3 195.8 %copy-start.70 = (f32[256]{0:T(256)}, f32[256]{0:T(256)S(1)}, u32[]{:S(2)}) copy-start(f32[256]{0:T(256)S(1)} %iota_convert_fusion) | copy-start | bytes 3076
  7.3 195.8 %copy-start.73 = (f32[256]{0:T(256)}, f32[256]{0:T(256)S(1)}, u32[]{:S(2)}) copy-start(f32[256]{0:T(256)S(1)} %fusion.306) | copy-start | bytes 3076
  8.6 93.3 %copy-start.97 = (f32[32]{0:T(128)}, f32[32]{0:T(128)S(1)}, u32[]{:S(2)}) copy-start(f32[32]{0:T(128)S(1)} %exp.28) | copy-start | bytes 388
  8.6 93.3 %copy-start.48 = (f32[4096]{0:T(1024)}, f32[4096]{0:T(1024)S(1)}, u32[]{:S(2)}) copy-start(f32[4096]{0:T(1024)S(1)} %fusion.302) | copy-start | bytes 49156
  9.5 92.5 %copy-start.64 = (f32[32,32]{1,0:T(8,128)}, f32[32,32]{1,0:T(8,128)S(1)}, u32[]{:S(2)}) copy-start(f32[32,32]{1,0:T(8,128)S(1)} %get-tuple-element.118) | copy-start | bytes 12292
  9.6 92.4 %copy-start.66 = (f32[32,32]{1,0:T(8,128)}, f32[32,32]{1,0:T(8,128)S(1)}, u32[]{:S(2)}) copy-start(f32[32,32]{1,0:T(8,128)S(1)} %sin.23) | copy-start | bytes 12292
  90.6 495.4 %copy-start.5 = (f32[4,8,16,256]{3,2,1,0:T(8,128)}, f32[4,8,16,256]{3,2,1,0:T(8,128)S(1)}, u32[]{:S(2)}) copy-start(f32[4,8,16,256]{3,2,1,0:T(8,128)S(1)} %copy.142) | copy-start | bytes 1572868
  234.3 259.0 %reduce-scatter.2.cloned.1.call-start = ((), (), s32[]{:S(2)}) async-start(), calls=%async_computation.2 | async-start | bytes 8912896 | tf_op jit(solution)/shard_map/reduce_scatter | solution.py:185
  234.5 71.9 %copy-start.50 = (bf16[512,64]{0,1:T(8,128)(2,1)}, bf16[512,64]{0,1:T(8,128)(2,1)S(1)}, u32[]{:S(2)}) copy-start(bf16[512,64]{0,1:T(8,128)(2,1)S(1)} %constant_dynamic-update-slice_fusion) | copy-start | bytes 196612
  316.8 485.2 %all-reduce.12.cloned.1.call-start = ((), (), s32[]{:S(2)}) async-start(), calls=%async_computation.3 | async-start | bytes 262144 | tf_op jit(solution)/shard_map/psum | solution.py:208
  317.8 182.8 %copy-start.15 = (f32[32,32,16]{1,2,0:T(8,128)S(1)}, f32[32,32,16]{1,2,0:T(8,128)}, u32[]{:S(2)}) copy-start(f32[32,32,16]{1,2,0:T(8,128)} %copy-done.14) | copy-start | bytes 196612
  317.8 182.8 %copy-start.18 = (f32[32,32,16]{1,2,0:T(8,128)S(1)}, f32[32,32,16]{1,2,0:T(8,128)}, u32[]{:S(2)}) copy-start(f32[32,32,16]{1,2,0:T(8,128)} %copy-done.17) | copy-start | bytes 196612
  317.8 182.8 %copy-start.21 = (f32[32,32,16]{1,2,0:T(8,128)S(1)}, f32[32,32,16]{1,2,0:T(8,128)}, u32[]{:S(2)}) copy-start(f32[32,32,16]{1,2,0:T(8,128)} %copy-done.20) | copy-start | bytes 196612
  317.8 182.8 %copy-start.24 = (f32[32,32,16]{1,2,0:T(8,128)S(1)}, f32[32,32,16]{1,2,0:T(8,128)}, u32[]{:S(2)}) copy-start(f32[32,32,16]{1,2,0:T(8,128)} %copy-done.23) | copy-start | bytes 196612
  532.6 95.6 %copy-start.53 = (f32[32,32,16]{1,2,0:T(8,128)}, f32[32,32,16]{1,2,0:T(8,128)S(1)}, u32[]{:S(2)}) copy-start(f32[32,32,16]{1,2,0:T(8,128)S(1)} %get-tuple-element.35) | copy-start | bytes 196612
  532.6 95.6 %copy-start.55 = (f32[32,32,16]{1,2,0:T(8,128)}, f32[32,32,16]{1,2,0:T(8,128)S(1)}, u32[]{:S(2)}) copy-start(f32[32,32,16]{1,2,0:T(8,128)S(1)} %get-tuple-element.36) | copy-start | bytes 196612
  532.6 100.0 %copy-start.35 = (f32[32,32,16]{1,2,0:T(8,128)}, f32[32,32,16]{1,2,0:T(8,128)S(1)}, u32[]{:S(2)}) copy-start(f32[32,32,16]{1,2,0:T(8,128)S(1)} %get-tuple-element.34) | copy-start | bytes 196612
  532.6 100.0 %copy-start.36 = (f32[32,32,16]{1,2,0:T(8,128)}, f32[32,32,16]{1,2,0:T(8,128)S(1)}, u32[]{:S(2)}) copy-start(f32[32,32,16]{1,2,0:T(8,128)S(1)} %get-tuple-element.37) | copy-start | bytes 196612
  661.2 87.2 %copy-start.6 = (f32[4,8,16,256]{3,2,1,0:T(8,128)S(1)}, f32[4,8,16,256]{3,2,1,0:T(8,128)}, u32[]{:S(2)}) copy-start(f32[4,8,16,256]{3,2,1,0:T(8,128)} %copy-done.5) | copy-start | bytes 1572868
  (92 other events, 1642.7 us)
Sparse Core Ops, SparseCore 0:
  234.5 71.9 all-gather.1
  316.9 176.4 reduce-scatter.1
  496.3 20.3 all-reduce.11
where the time goes:
time: 827 us; the launch traced here: 812 us
  matrix products  308 us (37%)
  waiting for transfers between devices  243 us (29%)
  blocking collectives  161 us (19%)
  other arithmetic  71.3 us (9%)
  between operations  16.5 us (2%)
  local copies, waits for them, and re-layouts  11.8 us (1%)
    reduce_scatter x1, waiting for transfers between devices, per_device(): lax.psum_scatter(jnp.dot(weight_rows, grad_pre, preferred_element_type=jn...  171 us
    dot_general x6, matrix products, block_conv(): jnp.einsum('hmr,hmc->hrc', lead_imag, backward_pow[1], precision=high)  79.1 us
    psum x1, blocking collectives, per_device(): lax.psum((jnp.sum(token_vals, axis=0), jnp.sum(token_vals * token_vals, a...  78.6 us
    psum x1, blocking collectives, per_device(): lax.psum(jnp.sum(grad_normed * normed, axis=0).astype(jnp.bfloat16), 'mp')  77.8 us
    dot_general x6, matrix products, block_conv(): jnp.einsum('hmr,hmc->hrc', lead_real, backward_pow[0], precision=high)  75.3 us
    all_gather x1, waiting for transfers between devices, per_device(): lax.all_gather(mixed_low, 'mp', axis=0, tiled=True)  71.9 us
    dot_general x6, matrix products, block_conv(): inside = jnp.einsum('hdnc,hrc->hdnr', rows, toeplitz, precision=high)  41.1 us
    dot_general x6, matrix products, block_conv(): up_imag = jnp.einsum('hmc,hdnc->hmdn', feed[1], rows, precision=high)  39.2 us
  transfers between devices with their start and end apart: 3, of which 2 were waited for; matrix products, arithmetic and copies ran while one was open for 28% of the time, Pallas kernels for 0%

commit v1 on v0

v1 whole, which is shorter than its diff:
```python
from functools import partial

import jax
import jax.numpy as jnp
import numpy as np
from jax import lax
from jax.experimental import pallas as pl
from jax.experimental.pallas import tpu as pltpu
from jax.sharding import PartitionSpec as P

B = 128
G = 4
F32 = jnp.float32
BF16 = jnp.bfloat16
NN = (((1,), (0,)), ((), ()))
NT = (((1,), (1,)), ((), ()))
TN = (((0,), (0,)), ((), ()))
EPS = 1e-05
VMEM = pl.BlockSpec(memory_space=pltpu.VMEM)
SMEM = pl.BlockSpec(memory_space=pltpu.SMEM)


def params(mb=48):
    return pltpu.CompilerParams(vmem_limit_bytes=mb * 1024 * 1024)


def cost(us):
    return pl.CostEstimate(flops=int(us * 1e9), bytes_accessed=int(us * 1e6), transcendentals=0)


def dot(a, b, dims=NN):
    return lax.dot_general(a, b, dims, preferred_element_type=F32)


def split(v):
    hi = v.astype(BF16)
    return hi, (v - hi.astype(F32)).astype(BF16)


def sincos(x):
    k = jnp.floor(x * 0.6366197723675814 + 0.5)
    y = ((x - k * 1.5703125) - k * 4.837512969970703e-4) - k * 7.54978995489188e-8
    y2 = y * y
    s = y + y * y2 * (-1.6666654611e-1 + y2 * (8.3321608736e-3 - y2 * 1.9515295891e-4))
    c = 1.0 - 0.5 * y2 + y2 * y2 * (4.166664568298827e-2 + y2 * (-1.388731625493765e-3 + y2 * 2.443315711809948e-5))
    q = k.astype(jnp.int32)
    odd = (q & 1) == 1
    sin = jnp.where(odd, c, s)
    cos = jnp.where(odd, s, c)
    sin = jnp.where((q & 2) == 2, -sin, sin)
    cos = jnp.where(((q + 1) & 2) == 2, -cos, cos)
    return sin, cos


def row_iota(shape):
    return lax.broadcasted_iota(jnp.int32, shape, 0)


def lane_iota(shape):
    return lax.broadcasted_iota(jnp.int32, shape, 1)


def shift_rows(x, k):
    n = x.shape[0]
    if abs(k) % 8 == 0:
        zero = jnp.zeros((abs(k), x.shape[1]), x.dtype)
        if k > 0:
            return jnp.concatenate([zero, x[: n - k]], axis=0)
        return jnp.concatenate([x[-k:], zero], axis=0)
    rows = row_iota(x.shape)
    keep = rows >= k if k > 0 else rows < n + k
    return jnp.where(keep, pltpu.roll(x, k % n, 0), 0.0)


def shift_token(x, k):
    n = x.shape[0]
    lanes = lane_iota(x.shape)
    rows = row_iota(x.shape)
    turned = pltpu.roll(x, k % B, 1)
    wrapped = pltpu.roll(turned, k % n, 0)
    if k > 0:
        wrapped = jnp.where(rows >= 1, wrapped, 0.0)
        return jnp.where(lanes == 0, wrapped, turned)
    wrapped = jnp.where(rows < n - 1, wrapped, 0.0)
    return jnp.where(lanes == B - 1, wrapped, turned)


def swap_halves(x):
    return pltpu.roll(x, B // 2, 1)


def scan_rows(x, jump_ref, ci, direction):
    x = shift_rows(x, direction)
    step = 0
    while (1 << step) < x.shape[0]:
        moved = shift_rows(x, direction * (1 << step))
        x = x + moved * jump_ref[2 * step, pl.ds(ci, 1), :] + swap_halves(moved) * jump_ref[2 * step + 1, pl.ds(ci, 1), :]
        step += 1
    return x


def start_kernel(half_ref, x_ref, g_ref, w_ref, bias_ref, stat_ref, pay_ref):
    C, L = x_ref.shape
    mp, _, nt = pay_ref.shape
    kh = w_ref.shape[2] // nt
    for n in range(L // B):
        x = x_ref[:, n * B : (n + 1) * B].astype(F32)
        mean = jnp.sum(x, axis=0, keepdims=True) * (1.0 / C)
        dev = x - mean
        stat_ref[0, n : n + 1, :] = mean
        stat_ref[1, n : n + 1, :] = jnp.sum(dev * dev, axis=0, keepdims=True)
    wt = w_ref[half_ref[0]]
    bias = bias_ref[...]
    for j in range(mp):
        pay_ref[j, 0:C, :] = x_ref[:, j * nt : (j + 1) * nt]
        pay_ref[j, C : 2 * C, :] = g_ref[:, j * nt : (j + 1) * nt]
        for q in range(kh):
            pay_ref[j, (2 + q) * C : (3 + q) * C, :] = wt[:, q * nt : (q + 1) * nt]
        pay_ref[j, (2 + kh) * C :, :] = bias


def table_kernel(
    rates_ref, coef_ref, f_ref, w_ref, t_ref, wb_ref, near_ref, jump_ref, wout_ref, cols, *, C, M
):
    i = pl.program_id(0)

    @pl.when(i == 0)
    def _():
        log_step = rates_ref[0]
        decay = rates_ref[1]
        freq = rates_ref[2]
        step_size = jnp.exp(log_step)
        real_rate = -jnp.exp(decay)
        re = step_size * real_rate
        im = step_size * freq
        growth = jnp.exp(re)
        sin, cos = sincos(im)
        num_re = growth * cos - 1.0
        num_im = growth * sin
        den = real_rate * real_rate + freq * freq
        in_re = (num_re * real_rate + num_im * freq) / den
        in_im = (num_im * real_rate - num_re * freq) / den
        coef = coef_ref[...]
        first = lane_iota(coef.shape) < B // 2
        w = coef * in_re + swap_halves(coef) * jnp.where(first, -in_im, in_im)
        wout_ref[...] = w
        sin, cos = sincos(im * float(B))
        mag = jnp.exp(re * float(B))
        a_re, a_im = mag * cos, mag * sin
        for k in range(jump_ref.shape[0] // 2):
            jump_ref[2 * k] = a_re
            jump_ref[2 * k + 1] = jnp.where(first, -a_im, a_im)
            a_re, a_im = a_re * a_re - a_im * a_im, 2.0 * a_re * a_im
        pad = jnp.zeros((B - C, B), F32)
        cols[0] = jnp.concatenate([re, pad], axis=0).T
        cols[1] = jnp.concatenate([im, pad], axis=0).T
        cols[2] = jnp.concatenate([w, pad], axis=0).T

    back = (B - i * G) % B
    al = pltpu.roll(cols[0, 0:M, :], back, 1)
    om = pltpu.roll(cols[1, 0:M, :], back, 1)
    ww = pltpu.roll(cols[2], back, 1)
    place = lane_iota((M, B)).astype(F32)
    ahead = float(B) - place
    rows = row_iota((B, B))
    lanes = lane_iota((B, B))
    zero = jnp.zeros((M, B), BF16)
    for j in range(G):
        a = jnp.broadcast_to(al[:, j : j + 1], (M, B))
        o = jnp.broadcast_to(om[:, j : j + 1], (M, B))
        w = [jnp.broadcast_to(ww[q * M : (q + 1) * M, j : j + 1], (M, B)) for q in range(4)]
        sin, cos = sincos(o * place)
        mag = jnp.exp(a * place)
        n_re, n_im = mag * cos, mag * sin
        sin, cos = sincos(o * ahead)
        mag = jnp.exp(a * ahead)
        f_re, f_im = mag * cos, mag * sin
        for q, part in enumerate(split(n_re)):
            near_ref[j, q * B : q * B + M, :] = part
            near_ref[j, q * B + M : q * B + 2 * M, :] = part
        for q, part in enumerate(split(n_im)):
            near_ref[j, q * B + 2 * M : q * B + 3 * M, :] = part
            near_ref[j, q * B + 3 * M : q * B + 4 * M, :] = part
        for q, (re_part, im_part) in enumerate(zip(split(f_re), split(f_im))):
            f_ref[j, q * B : q * B + M, 0:B] = re_part
            f_ref[j, q * B : q * B + M, B:] = zero
            f_ref[j, q * B + M : q * B + 2 * M, 0:B] = zero
            f_ref[j, q * B + M : q * B + 2 * M, B:] = re_part
            f_ref[j, q * B + 2 * M : q * B + 3 * M, 0:B] = im_part
            f_ref[j, q * B + 2 * M : q * B + 3 * M, B:] = zero
            f_ref[j, q * B + 3 * M : q * B + 4 * M, 0:B] = zero
            f_ref[j, q * B + 3 * M : q * B + 4 * M, B:] = im_part
        for h in range(2):
            w_re, w_im = 2.0 * w[h], 2.0 * w[2 + h]
            e_re = w_re * n_re - w_im * n_im
            e_im = -(w_re * n_im + w_im * n_re)
            for q, part in enumerate(split(e_re)):
                w_ref[j, h * M : (h + 1) * M, q * B : (q + 1) * B] = part
            for q, part in enumerate(split(e_im)):
                w_ref[j, (2 + h) * M : (3 + h) * M, q * B : (q + 1) * B] = part
            kern = jnp.broadcast_to(jnp.sum(e_re, axis=0, keepdims=True), (B, B))
            toe = jnp.where(lanes >= rows, pltpu.roll(kern, 0, 1, stride=1, stride_axis=0), 0.0)
            for q, part in enumerate(split(toe)):
                t_ref[j, h * B : (h + 1) * B, q * B : (q + 1) * B] = part
            b_re = w_re * f_re - w_im * f_im
            b_im = -(w_re * f_im + w_im * f_re)
            for q, part in enumerate(split(b_re)):
                wb_ref[j, 0:M, (2 * q + h) * B : (2 * q + h + 1) * B] = part
                wb_ref[j, M : 2 * M, (2 * q + h) * B : (2 * q + h + 1) * B] = zero
            for q, part in enumerate(split(b_im)):
                wb_ref[j, 2 * M : 3 * M, (2 * q + h) * B : (2 * q + h + 1) * B] = part
                wb_ref[j, 3 * M : 4 * M, (2 * q + h) * B : (2 * q + h + 1) * B] = zero


def token_stats(stat_ref, length, count):
    mean = stat_ref[0]
    inv = lax.rsqrt(stat_ref[1] * (1.0 / count) + EPS)
    place = row_iota(mean.shape) * B + lane_iota(mean.shape)
    return mean, inv, (place < length).astype(F32)


def mixer_kernel(
    len_ref, vec_ref, x_ref, stat_ref, f_ref, w_ref, t_ref, jump_ref,
    mixed_ref, slope_ref, state_ref, lift_ref, xs, ms, tok, *, count,
):
    i = pl.program_id(0)
    C, L = x_ref.shape
    N = L // B
    nt = mixed_ref.shape[2]

    @pl.when(i == 0)
    def _():
        for n in range(N):
            xs[n * C : (n + 1) * C, :] = x_ref[:, n * B : (n + 1) * B].astype(F32)
        mean, inv, mask = token_stats(stat_ref, len_ref[0], count)
        tok[0] = mean
        tok[1] = inv
        tok[2] = mask

    ahead = float(B) - lane_iota((N, B)).astype(F32)
    for j in range(G):
        ci = i * G + j
        mask = tok[2]
        normed = (xs[pl.ds(ci, N, stride=C), :] - tok[0]) * tok[1]
        sig = mask * (normed * vec_ref[0, ci] + vec_ref[1, ci])
        liq = sig * shift_token(sig, 1)
        u = jnp.concatenate([sig, liq], axis=1)
        u2 = jnp.concatenate([sig * ahead, liq * ahead], axis=1)
        u_hi, u_lo = split(u)
        u2_hi, u2_lo = split(u2)
        up = dot(jnp.concatenate([u_hi, u_lo, u2_hi, u2_lo], axis=0), f_ref[j], NT)
        lift = up[2 * N : 3 * N, :B] + (up[2 * N : 3 * N, B:] + up[3 * N :, :B])
        state = scan_rows(up[:N, :B] + (up[:N, B:] + up[N : 2 * N, :B]), jump_ref, ci, 1)
        s_hi, s_lo = split(state)
        out = dot(jnp.concatenate([u_hi, u_lo], axis=0), t_ref[j]) + dot(
            jnp.concatenate([s_hi, s_lo], axis=0), w_ref[j]
        )
        y = out[:N, :B] + (out[:N, B:] + out[N:, :B]) + vec_ref[2, ci] * sig
        y2 = y * y
        th = jnp.tanh(0.7978845608028654 * (y + 0.044715 * (y * y2)))
        half = 0.5 * (1.0 + th)
        ms[pl.ds(pl.multiple_of(ci * N, N), N), :] = mask * (y * half)
        slope_ref[j] = mask * (half + 0.5 * y * (1.0 - th * th) * (0.7978845608028654 * (1.0 + 0.134145 * y2)))
        state_ref[j] = state
        lift_ref[j] = lift

    @pl.when(i == pl.num_programs(0) - 1)
    def _():
        per = nt // B
        for n in range(N):
            mixed_ref[n // per, :, (n % per) * B : (n % per + 1) * B] = ms[pl.ds(n, C, stride=N), :].astype(BF16)


def glu_kernel(half_ref, mixed_ref, first_ref, other_ref, lay_ref, gm_ref, keep_ref, send_ref, gp, wt, *, C):
    mp, _, nt = mixed_ref.shape
    H = mp * C
    kh = H // nt
    own = half_ref[0]
    mixed = mixed_ref[...].reshape(H, nt)
    for q in range(kh):
        at = slice(q * nt, (q + 1) * nt)
        wt[own, :, at] = first_ref[:, (2 + q) * C : (3 + q) * C, :].reshape(H, nt)
        wt[1 - own, :, at] = other_ref[:, q * C : (q + 1) * C, :].reshape(H, nt)
    step = B
    per = step // C
    at = (2 + kh) * C
    bias = first_ref[:, at : at + 16, 0:B].astype(F32)[:, 0, :]
    bias = jnp.concatenate([bias, jnp.zeros((B - mp, B), F32)], axis=0).T
    for s in range(mp // per):
        lo = s * step
        col_v = jnp.concatenate([bias[0:C, k : k + 1] for k in range(s * per, (s + 1) * per)], axis=0)
        col_g = jnp.concatenate([bias[C : 2 * C, k : k + 1] for k in range(s * per, (s + 1) * per)], axis=0)
        value = dot(wt[0, lo : lo + step, :], mixed) + col_v
        gate = dot(wt[1, lo : lo + step, :], mixed) + col_g
        sig = jax.nn.sigmoid(gate)
        x = first_ref[s * per : (s + 1) * per, 0:C, :].reshape(step, nt).astype(F32)
        g = first_ref[s * per : (s + 1) * per, C : 2 * C, :].reshape(step, nt).astype(F32)
        lay_ref[s * per : (s + 1) * per] = (x + value * sig).astype(BF16).reshape(per, C, nt)
        gv = g * sig
        gp[0, lo : lo + step, :] = gv.astype(BF16)
        gp[1, lo : lo + step, :] = (gv * value * (1.0 - sig)).astype(BF16)
    for s in range(mp // per):
        at = slice(s * step, (s + 1) * step)
        gm = dot(wt[0, :, at], gp[0], TN) + dot(wt[1, :, at], gp[1], TN)
        hi, lo = split(gm)
        gm_ref[s * per : (s + 1) * per, 0:C, :] = hi.reshape(per, C, nt)
        gm_ref[s * per : (s + 1) * per, C:, :] = lo.reshape(per, C, nt)
    keep_ref[...] = gp[own]
    send_ref[...] = gp[1 - own]


def weight_kernel(keep_ref, got_ref, mixed_ref, theirs_ref, lay_ref, pay_ref):
    mp, C, nt = mixed_ref.shape
    H = mp * C
    kh = H // nt
    step = B
    per = step // C
    pay_ref[:, 0:C, :] = lay_ref[...]
    mixed = mixed_ref[...].reshape(H, nt)
    theirs = theirs_ref[...].reshape(H, nt)
    ones = jnp.ones((16, nt), BF16)
    rows = row_iota((16, B))
    at = (1 + 2 * kh) * C
    for s in range(mp // per):
        mine, other = keep_ref[s * step : (s + 1) * step, :], got_ref[s * step : (s + 1) * step, :]
        parts = split(dot(mine, mixed, NT) + dot(other, theirs, NT))
        for q in range(kh):
            for h, part in enumerate(parts):
                lo = (1 + 2 * q + h) * C
                pay_ref[s * per : (s + 1) * per, lo : lo + C, :] = part[:, q * nt : (q + 1) * nt].reshape(per, C, nt)
        hi, lo = split(dot(ones, mine, NT) + dot(ones, other, NT))
        put = jnp.where(rows == 0, hi.astype(F32), jnp.where(rows == 1, lo.astype(F32), 0.0)).astype(BF16)
        for k in range(per):
            pay_ref[s * per + k, at : at + 16, 0:B] = put
            if nt > B:
                pay_ref[s * per + k, at : at + 16, B:] = jnp.zeros((16, nt - B), BF16)


def back_kernel(
    len_ref, vec_ref, x_ref, stat_ref, gm_ref, slope_ref, state_ref, lift_ref,
    t_ref, wb_ref, near_ref, jump_ref,
    gn_ref, sum_ref, row_ref, xs, gs, ns, tok, *, count,
):
    i = pl.program_id(0)
    C, L = x_ref.shape
    N = L // B
    nt = gm_ref.shape[2]
    per = nt // B

    @pl.when(i == 0)
    def _():
        for n in range(N):
            xs[n * C : (n + 1) * C, :] = x_ref[:, n * B : (n + 1) * B].astype(F32)
            at = slice((n % per) * B, (n % per + 1) * B)
            gs[n * C : (n + 1) * C, :] = gm_ref[n // per, 0:C, at].astype(F32) + gm_ref[n // per, C:, at].astype(F32)
        mean, inv, mask = token_stats(stat_ref, len_ref[0], count)
        tok[0] = mean
        tok[1] = inv
        tok[2] = mask
        sum_ref[...] = jnp.zeros_like(sum_ref)

    place = lane_iota((N, B)).astype(F32)
    lag = lane_iota((8, B)).astype(F32)
    rows2 = row_iota((B, B))
    lanes2 = lane_iota((B, B))
    flip = (lanes2 + rows2 == B - 1).astype(BF16)
    rows16 = row_iota((16, B))
    for j in range(G):
        ci = i * G + j
        mask = tok[2]
        normed = (xs[pl.ds(ci, N, stride=C), :] - tok[0]) * tok[1]
        sig = mask * (normed * vec_ref[0, ci] + vec_ref[1, ci])
        prev = shift_token(sig, 1)
        liq = sig * prev
        u_hi, u_lo = split(jnp.concatenate([sig, liq], axis=1))
        g = gs[pl.ds(ci, N, stride=C), :] * slope_ref[j]
        g_hi, g_lo = split(g)
        g3 = jnp.concatenate([g_hi, g_hi, g_lo], axis=0)
        sums = []
        for q in range(2):
            at = slice(q * B, (q + 1) * B)
            turned = dot(flip, jnp.concatenate([u_hi[:, at], u_lo[:, at], u_hi[:, at]], axis=0), NT).astype(BF16)
            corr = jnp.where(lanes2 + rows2 >= B - 1, dot(turned, g3), 0.0)
            sums.append(jnp.sum(pltpu.roll(corr, 1, 1, stride=1, stride_axis=0), axis=0, keepdims=True))
        main, liquid = sums
        lags = jnp.where(rows16 == 0, main, jnp.where(rows16 == 1, liquid, 0.0))
        lags = jnp.where(rows16 == 2, main * lag[0:1], jnp.where(rows16 == 3, liquid * lag[0:1], lags))
        left_hi, left_lo = split(jnp.concatenate([g, g * place, lags], axis=0))
        R = 2 * N + 16
        z = dot(jnp.concatenate([left_hi, left_lo], axis=0), near_ref[j], NT)
        z = z[:R, :B] + (z[:R, B:] + z[R:, :B])
        p, p_place, inner = z[:N], z[N : 2 * N], z[2 * N :]
        r = scan_rows(p, jump_ref, ci, -1)
        r_hi, r_lo = split(r)
        lhs_g = jnp.concatenate([g_hi, g_lo], axis=0)
        big = dot(jnp.concatenate([r_hi, r_lo], axis=0), wb_ref[j])
        one = dot(lhs_g, t_ref[j, :, :B], NT)
        two = dot(g_hi, t_ref[j, :, B:], NT)
        both = one[:N] + (one[N:] + two) + (big[:N, : 2 * B] + (big[:N, 2 * B :] + big[N:, : 2 * B]))
        gl = both[:, B:]
        grad = both[:, :B] + vec_ref[2, ci] * g + gl * prev + shift_token(gl * sig, -1)
        masked = mask * grad
        gn = masked * vec_ref[0, ci]
        sum_ref[0] += gn
        sum_ref[1] += gn * normed
        ns[pl.ds(pl.multiple_of(ci * N, N), N), :] = gn
        state, lift = state_ref[j], lift_ref[j]
        state_x, r_x = swap_halves(state), swap_halves(r)
        carry = p_place + float(B) * (r * jump_ref[0, pl.ds(ci, 1), :] + r_x * jump_ref[1, pl.ds(ci, 1), :])
        total = [
            p * state, p * state_x,
            carry * state + lift * r, carry * state_x + lift * r_x,
            masked * normed, masked, g * sig,
        ]
        put = jnp.where(rows16 >= 8, pltpu.roll(inner, 8, 0), 0.0)
        for q, v in enumerate(total):
            put = jnp.where(rows16 == q, jnp.sum(v, axis=0, keepdims=True), put)
        row_ref[j] = put

    @pl.when(i == pl.num_programs(0) - 1)
    def _():
        for n in range(N):
            gn_ref[:, n * B : (n + 1) * B] = ns[pl.ds(n, C, stride=N), :]


def last_kernel(x_ref, g_ref, gn_ref, stat_ref, sum_ref, out_ref, *, count):
    C, L = x_ref.shape
    for n in range(L // B):
        at = slice(n * B, (n + 1) * B)
        mean = stat_ref[0, n : n + 1, :]
        inv = lax.rsqrt(stat_ref[1, n : n + 1, :] * (1.0 / count) + EPS)
        first = sum_ref[0, n : n + 1, :] * (1.0 / count)
        second = sum_ref[1, n : n + 1, :] * (1.0 / count)
        normed = (x_ref[:, at].astype(F32) - mean) * inv
        out_ref[:, at] = inv * (gn_ref[:, at] - first - normed * second) + g_ref[:, at].astype(F32)


def gather_kernel(pay_ref, out_ref, sum_ref):
    mp, _, nt = pay_ref.shape
    C = out_ref.shape[0]
    kh = sum_ref.shape[1] // nt
    for s in range(mp):
        out_ref[:, s * nt : (s + 1) * nt] = pay_ref[s, 0:C, :]
    for q in range(kh):
        at = slice((1 + 2 * q) * C, (3 + 2 * q) * C)
        total = jnp.sum(pay_ref[:, at, :].astype(F32), axis=0)
        sum_ref[0:C, q * nt : (q + 1) * nt] = total[:C] + total[C:]
    tail = jnp.sum(pay_ref[:, (1 + 2 * kh) * C :, 0:B].astype(F32), axis=0)
    sum_ref[C:, 0:B] = jnp.broadcast_to(tail[0:1] + tail[1:2], (8, B))
    sum_ref[C:, B:] = jnp.zeros((8, sum_ref.shape[1] - B), F32)


def rounds_of(size):
    rounds, bit = [], 1
    while bit < size:
        if bit * 2 < size:
            rounds.append((bit, 2 * bit, 3 * bit))
            bit *= 4
        else:
            rounds.append((bit,))
            bit *= 2
    return rounds


def exchange(v, axis, size, off):
    return lax.ppermute(v, axis, [(k, k ^ off) for k in range(size)])


def all_stats(stat, size, local):
    count = float(local)
    for offs in rounds_of(size):
        parts = [stat] + [exchange(stat, "mp", size, o) for o in offs]
        mean = sum(p[0] for p in parts) * (1.0 / len(parts))
        spread = sum(p[1] for p in parts) + count * sum((p[0] - mean) * (p[0] - mean) for p in parts)
        stat = jnp.stack([mean, spread])
        count *= len(parts)
    return stat


def all_sums(v, size):
    for offs in rounds_of(size):
        v = sum([exchange(v, "mp", size, o) for o in offs], v)
    return v


def sum_docs(v, size, stride):
    total = v
    for k in range(stride, size, stride):
        total = total + lax.ppermute(v, "dp", [(q, (q + k) % size) for q in range(size)])
    return total


def partner(v, size):
    return lax.ppermute(v, "dp", [(q, q ^ 1) for q in range(size)])


def mode_terms(log_step, decay_log, frequency, readout, liquid_readout):
    M = decay_log.shape[1]
    step_size = jnp.exp(log_step)[:, None]
    real_rate = -jnp.exp(decay_log)
    real_step = step_size * real_rate
    imag_step = step_size * frequency
    growth = jnp.exp(real_step)
    num_real = growth * jnp.cos(imag_step) - 1.0
    num_imag = growth * jnp.sin(imag_step)
    denominator = real_rate * real_rate + frequency * frequency
    in_real = (num_real * real_rate + num_imag * frequency) / denominator
    in_imag = (num_imag * real_rate - num_real * frequency) / denominator

    def mix(coeffs):
        re, im = coeffs[:, :M], coeffs[:, M:]
        return re * in_real - im * in_imag, re * in_imag + im * in_real

    return mix(readout) + mix(liquid_readout) + (real_step, imag_step)


def per_device(
    mp, dp,
    tokens, lengths, norm_gain, norm_bias, log_step, decay_log, frequency, readout, liquid_readout,
    skip_gain, value_weight, gate_weight, value_bias, gate_bias, grad_out,
):
    C, L = tokens.shape
    H = value_weight.shape[0]
    M = decay_log.shape[1]
    N = L // B
    nt = L // mp
    kh = H // nt
    steps = max(1, (N - 1).bit_length())
    shape = jax.ShapeDtypeStruct

    half = lax.rem(lax.axis_index("dp"), 2).astype(jnp.int32)
    halves = half.reshape(1)
    bias = jnp.pad(jnp.concatenate([value_bias, gate_bias])[None], ((0, 15), (0, nt - 2 * C)))
    weights = jnp.stack([value_weight.T, gate_weight.T])
    stat, pay = pl.pallas_call(
        start_kernel,
        out_shape=(shape((2, N, B), F32), shape((mp, (2 + kh) * C + 16, nt), BF16)),
        in_specs=[SMEM] + [VMEM] * 4,
        out_specs=(VMEM, VMEM),
        compiler_params=params(),
        cost_estimate=cost(2),
    )(halves, tokens, grad_out, weights, bias)
    first = lax.all_to_all(pay, "mp", split_axis=0, concat_axis=0, tiled=True)
    other = partner(first[:, 2 * C : (2 + kh) * C, :], dp)

    rates = jnp.stack(
        [jnp.broadcast_to(log_step[:, None], (C, 4 * M)), jnp.tile(decay_log, (1, 4)), jnp.tile(frequency, (1, 4))]
    )
    coef = jnp.concatenate([readout[:, :M], liquid_readout[:, :M], readout[:, M:], liquid_readout[:, M:]], axis=1)

    def whole(*dims):
        return pl.BlockSpec(dims, lambda i: (0,) * len(dims))

    def chan(*dims):
        return pl.BlockSpec((G,) + dims, lambda i: (i,) + (0,) * len(dims))

    f_tab, w_tab, t_tab, wb_tab, near_tab, jump, w_all = pl.pallas_call(
        partial(table_kernel, C=C, M=M),
        grid=(C // G,),
        out_shape=(
            shape((C, 2 * B, 2 * B), BF16),
            shape((C, B, 2 * B), BF16),
            shape((C, 2 * B, 2 * B), BF16),
            shape((C, B, 4 * B), BF16),
            shape((C, 2 * B, B), BF16),
            shape((2 * steps, C, B), F32),
            shape((C, B), F32),
        ),
        in_specs=[whole(3, C, B), whole(C, B)],
        out_specs=(
            chan(2 * B, 2 * B), chan(B, 2 * B), chan(2 * B, 2 * B), chan(B, 4 * B), chan(2 * B, B),
            whole(2 * steps, C, B), whole(C, B),
        ),
        scratch_shapes=[pltpu.VMEM((3, B, B), F32)],
        compiler_params=params(),
        cost_estimate=cost(8),
    )(rates, coef)

    stat = all_stats(stat, mp, C)
    vecs = jnp.stack([norm_gain, norm_bias, skip_gain])
    mixed, slope, state, lift = pl.pallas_call(
        partial(mixer_kernel, count=H),
        grid=(C // G,),
        out_shape=(
            shape((mp, C, nt), BF16), shape((C, N, B), F32), shape((C, N, B), F32), shape((C, N, B), F32),
        ),
        in_specs=[
            SMEM, SMEM, whole(C, L), whole(2, N, B), chan(2 * B, 2 * B), chan(B, 2 * B), chan(2 * B, 2 * B),
            whole(2 * steps, C, B),
        ],
        out_specs=(whole(mp, C, nt), chan(N, B), chan(N, B), chan(N, B)),
        scratch_shapes=[pltpu.VMEM((N * C, B), F32), pltpu.VMEM((N * C, B), F32), pltpu.VMEM((3, N, B), F32)],
        compiler_params=params(),
        cost_estimate=cost(18),
    )(lengths, vecs, tokens, stat, f_tab, w_tab, t_tab, jump)

    mixed, first, other = lax.optimization_barrier((mixed, first, other))
    mixed_tok = lax.all_to_all(mixed, "mp", split_axis=0, concat_axis=0, tiled=True)
    theirs = partner(mixed_tok, dp)
    lay, gm, keep, send = pl.pallas_call(
        partial(glu_kernel, C=C),
        out_shape=(
            shape((mp, C, nt), BF16), shape((mp, 2 * C, nt), BF16), shape((H, nt), BF16), shape((H, nt), BF16),
        ),
        in_specs=[SMEM] + [VMEM] * 3,
        out_specs=(VMEM,) * 4,
        scratch_shapes=[pltpu.VMEM((2, H, nt), BF16), pltpu.VMEM((2, H, H), BF16)],
        compiler_params=params(),
        cost_estimate=cost(3),
    )(halves, mixed_tok, first, other)
    gm = lax.all_to_all(gm, "mp", split_axis=0, concat_axis=0, tiled=True)
    pay = pl.pallas_call(
        weight_kernel,
        out_shape=shape((mp, (1 + 2 * kh) * C + 16, nt), BF16),
        in_specs=[VMEM] * 5,
        out_specs=VMEM,
        compiler_params=params(),
        cost_estimate=cost(2),
    )(keep, partner(send, dp), mixed_tok, theirs, lay)
    pay, gm = lax.optimization_barrier((pay, gm))
    third = lax.all_to_all(pay, "mp", split_axis=0, concat_axis=0, tiled=True)

    gn, sums, rows = pl.pallas_call(
        partial(back_kernel, count=H),
        grid=(C // G,),
        out_shape=(shape((C, L), F32), shape((2, N, B), F32), shape((C, 16, B), F32)),
        in_specs=[
            SMEM, SMEM, whole(C, L), whole(2, N, B), whole(mp, 2 * C, nt), chan(N, B), chan(N, B), chan(N, B),
            chan(2 * B, 2 * B), chan(B, 4 * B), chan(2 * B, B), whole(2 * steps, C, B),
        ],
        out_specs=(whole(C, L), whole(2, N, B), chan(16, B)),
        scratch_shapes=[
            pltpu.VMEM((N * C, B), F32), pltpu.VMEM((N * C, B), F32), pltpu.VMEM((N * C, B), F32),
            pltpu.VMEM((3, N, B), F32),
        ],
        compiler_params=params(),
        cost_estimate=cost(32),
    )(lengths, vecs, tokens, stat, gm, slope, state, lift, t_tab, wb_tab, near_tab, jump)

    sums, third = lax.optimization_barrier((sums, third))
    sums = all_sums(sums, mp)
    grad_tokens = pl.pallas_call(
        partial(last_kernel, count=H),
        out_shape=shape((C, L), F32),
        in_specs=[VMEM] * 5,
        out_specs=VMEM,
        compiler_params=params(),
        cost_estimate=cost(1),
    )(tokens, grad_out, gn, stat, sums)

    layer_out, wsum = pl.pallas_call(
        gather_kernel,
        out_shape=(shape((C, L), BF16), shape((C + 8, H), F32)),
        in_specs=[VMEM],
        out_specs=(VMEM, VMEM),
        compiler_params=params(),
        cost_estimate=cost(1),
    )(third)
    wsum = sum_docs(wsum, dp, 2)
    rows = sum_docs(rows, dp, 1)
    across = partner(wsum, dp)
    value_all = jnp.where(half == 0, wsum, across)
    gate_all = jnp.where(half == 0, across, wsum)
    value_wgrad, gate_wgrad = value_all[:C].T, gate_all[:C].T
    at = (lax.axis_index("mp") % (B // C)) * C
    value_bgrad = lax.dynamic_slice(value_all[C], (at,), (C,))
    gate_bgrad = lax.dynamic_slice(gate_all[C], (at,), (C,))

    half = B // 2

    def complex_rows(a, b):
        return rows[:, a, :half] - rows[:, a, half:], rows[:, b, :half] + rows[:, b, half:]

    g_re, g_im = complex_rows(0, 1)
    d_re, d_im = complex_rows(2, 3)
    main, liquid = slice(0, M), slice(M, 2 * M)

    def inner(a, part):
        lo = half if part else 0
        return jnp.concatenate([rows[:, a, lo : lo + M], rows[:, a + 1, lo + M : lo + 2 * M]], axis=1)

    g_re, g_im = g_re + inner(8, 0), g_im + inner(8, 1)
    d_re, d_im = d_re + inner(10, 0), d_im + inner(10, 1)
    w_re, w_im = w_all[:, :half], w_all[:, half:]
    l_re = w_re * d_re - w_im * d_im
    l_im = w_re * d_im + w_im * d_re
    cot = (
        2.0 * g_re[:, main], -2.0 * g_im[:, main], 2.0 * g_re[:, liquid], -2.0 * g_im[:, liquid],
        2.0 * (l_re[:, main] + l_re[:, liquid]), -2.0 * (l_im[:, main] + l_im[:, liquid]),
    )
    _, back = jax.vjp(mode_terms, log_step, decay_log, frequency, readout, liquid_readout)
    step_grad, decay_grad, frequency_grad, readout_grad, liquid_grad = back(cot)
    plain = jnp.sum(rows[:, 4:7, :], axis=2)
    return (
        layer_out, grad_tokens, plain[:, 0], plain[:, 1], step_grad, decay_grad, frequency_grad, readout_grad,
        liquid_grad, plain[:, 2], value_wgrad, gate_wgrad, value_bgrad, gate_bgrad,
    )


def solution(mesh):
    row, col, act = P("mp"), P(None, "mp"), P("mp", "dp")
    wide = P("mp", None)
    in_specs = (act, P("dp"), row, row, row, wide, wide, wide, wide, row, col, col, row, row, act)
    out_specs = (act, act, row, row, row, wide, wide, wide, wide, row, col, col, row, row)
    return jax.shard_map(
        partial(per_device, mesh.shape["mp"], mesh.shape["dp"]),
        mesh=mesh, in_specs=in_specs, out_specs=out_specs, check_vma=False,
    )
```

time: 827 us -> 168 us (0.20); the launches traced: 812 us -> 167 us
  matrix products: 308 us -> 0 us
  waiting for transfers between devices: 243 us -> 32.1 us
  blocking collectives: 161 us -> 14.9 us
  other arithmetic: 71.3 us -> 5.72 us
  Pallas kernels: 0 us -> 64.3 us
  starting transfers between devices: 0.34 us -> 32.6 us
  between operations: 16.5 us -> 1.65 us
    dot_general x43 -> x0, matrix products: 308 us -> none  [the longest x6 79.1 us: block_conv(): jnp.einsum('hmr,hmc->hrc', lead_imag, backward_pow[1], precision=high)]
    reduce_scatter x1 -> x0, waiting for transfers between devices: 171 us -> none  [per_device(): lax.psum_scatter(jnp.dot(weight_rows, grad_pre, preferred_element_type=jn...]
    psum x3 -> x0, blocking collectives: 161 us -> none  [the longest x1 78.6 us: per_device(): lax.psum((jnp.sum(token_vals, axis=0), jnp.sum(token_vals * token_vals, a...]
    all_gather x1 -> x0, waiting for transfers between devices: 71.9 us -> none  [per_device(): lax.all_gather(mixed_low, 'mp', axis=0, tiled=True)]
    pallas_call x0 -> x8, Pallas kernels: none -> 64.3 us  [the longest x1 31.8 us: per_device(): pl.pallas_call(partial(back_kernel, count=H), grid=(C // G,), out_shape=(...]
    reduce_sum x5 -> x1, other arithmetic: 30.4 us -> 0.11 us  [per_device(): plain = jnp.sum(rows[:, 4:7, :], axis=2)]
    dot_general x1 -> x0, other arithmetic: 28.9 us -> none  [block_conv(): jnp.einsum('hmnk,hmdk->hmdn', jump[1], up_imag, precision=high)]
    ppermute x0 -> x17, waiting for transfers between devices: none -> 21.4 us  [the longest x12 18.5 us: exchange(): return lax.ppermute(v, axis, [(k, k ^ off) for k in range(size)])]
  transfers between devices with their start and end apart: 3 -> 20, of which waited for: 2 -> 10; matrix products, arithmetic and copies ran while one was open for 28% -> 3% of each run, Pallas kernels for 0% -> 37%
where the time goes in v1:
time: 168 us; the launch traced here: 167 us
  Pallas kernels  64.3 us (38%)
  starting transfers between devices  32.6 us (19%)
  waiting for transfers between devices  32.1 us (19%)
  local copies, waits for them, and re-layouts  15.7 us (9%)
  blocking collectives  14.9 us (9%)
  other arithmetic  5.72 us (3%)
    pallas_call x1, Pallas kernels, per_device(): pl.pallas_call(partial(back_kernel, count=H), grid=(C // G,), out_shape=(...  31.8 us
    ppermute x12, waiting for transfers between devices, exchange(): return lax.ppermute(v, axis, [(k, k ^ off) for k in range(size)])  18.5 us
    pallas_call x1, Pallas kernels, per_device(): pl.pallas_call(partial(mixer_kernel, count=H), grid=(C // G,), out_shape=...  17.6 us
    ppermute x12, starting transfers between devices, exchange(): return lax.ppermute(v, axis, [(k, k ^ off) for k in range(size)])  15.9 us
    all_to_all x1, blocking collectives, per_device(): lax.all_to_all(mixed, 'mp', split_axis=0, concat_axis=0, tiled=True)  14.9 us
    unnamed x44, local copies, waits for them, and re-layouts  11.6 us
    all_to_all x1, waiting for transfers between devices, per_device(): gm = lax.all_to_all(gm, 'mp', split_axis=0, concat_axis=0, tiled=True)  10.7 us
    all_to_all x1, starting transfers between devices, per_device(): first = lax.all_to_all(pay, 'mp', split_axis=0, concat_axis=0, tiled=True)  8.46 us
  transfers between devices with their start and end apart: 20, of which 10 were waited for; matrix products, arithmetic and copies ran while one was open for 3% of the time, Pallas kernels for 37%

profile of v1, /device:TPU:0, one launch (start us, length us, event | category | flops | bytes accessed | tf_op | source)
XLA Modules:
  0.0 166.9 jit_solution(8852093193785976175)
XLA Ops:
  5.2 8.5 %all-to-all-start = ((bf16[16,144,256]{2,1,0:T(8,128)(2,1)}), bf16[16,144,256]{2,1,0:T(8,128)(2,1)S(1)}, u32[]{:S(2)}, u32[]{:S(2)}) async-start(bf16[16,144,256]{2,1,0:T(8,128)(2,1)} %get-tuple-element.49), calls=%async_computation | async-start | bytes 2359296 | tf_op jit(solution)/shard_map/all_to_all | solution.py:543
  13.7 1.9 %collective-permute-start = (f32[2,32,128]{2,1,0:T(8,128)S(1)}, f32[2,32,128]{2,1,0:T(8,128)S(1)}, u32[]{:S(2)}, u32[]{:S(2)}) collective-permute-start(f32[2,32,128]{2,1,0:T(8,128)S(1)} %get-tuple-element.43), channel_id=1, source_target_pairs={{0,1},{1,0},{2,3},{3,2},{4,5},{5,4},{6,7},{7,6},{8,9},{9,8},{10,11... | collective-permute-start | bytes 98312 | tf_op jit(solution)/shard_map/ppermute | solution.py:466
  17.8 8.1 %shard_map.255 = (bf16[32,256,256]{2,1,0:T(8,128)(2,1)}, bf16[32,128,256]{2,1,0:T(8,128)(2,1)S(1)}, bf16[32,256,256]{2,1,0:T(8,128)(2,1)}, bf16[32,128,512]{2,1,...) custom-call(f32[3,32,128]{2,1,0:T(8,128)S(1)} %pad_maximum_fusion.1.rates_ref,, ...), custom_call_target="tpu_custom_call" | custom-call | flops 8000000000 | bytes 8000000 | tf_op jit(solution)/shard_map/pallas_call | solution.py:557
  28.6 1.9 %collective-permute-start.3 = (f32[2,32,128]{2,1,0:T(8,128)S(1)}, f32[2,32,128]{2,1,0:T(8,128)S(1)}, u32[]{:S(2)}, u32[]{:S(2)}) collective-permute-start(f32[2,32,128]{2,1,0:T(8,128)S(1)} %pad_maximum_fusion.2), channel_id=1, source_target_pairs={{0,4},{1,5},{2,6},{3,7},{4,0},{5,1},{6,2},{7,3},{8,12},{9,13},{10,... | collective-permute-start | bytes 98312 | tf_op jit(solution)/shard_map/ppermute | solution.py:466
  30.5 2.4 %collective-permute-start.4 = (f32[2,32,128]{2,1,0:T(8,128)S(1)}, f32[2,32,128]{2,1,0:T(8,128)S(1)}, u32[]{:S(2)}, u32[]{:S(2)}) collective-permute-start(f32[2,32,128]{2,1,0:T(8,128)S(1)} %pad_maximum_fusion.2), channel_id=1, source_target_pairs={{0,8},{1,9},{2,10},{3,11},{4,12},{5,13},{6,14},{7,15},{8,0},{9,1},... | collective-permute-start | bytes 98312 | tf_op jit(solution)/shard_map/ppermute | solution.py:466
  34.2 10.4 %collective-permute-done.4 = f32[2,32,128]{2,1,0:T(8,128)S(1)} collective-permute-done((f32[2,32,128]{2,1,0:T(8,128)S(1)}, f32[2,32,128]{2,1,0:T(8,128)S(1)}, u32[]{:S(2)}, u32[]{:S(2)}) %collective-permute-start.4) | collective-permute-done | bytes 32800 | tf_op jit(solution)/shard_map/ppermute | solution.py:466
  44.8 1.6 copy-done.7
  46.4 17.6 %shard_map.256 = (bf16[16,32,256]{2,1,0:T(8,128)(2,1)S(1)}, f32[32,32,128]{2,1,0:T(8,128)S(1)}, f32[32,32,128]{2,1,0:T(8,128)S(1)}, f32[32,32,128]{2,1,0:T(8,128)S(1)}) custom-call(s32[1]{0:T(128)S(6)} %copy.89.len_ref, f32[3,32]{1,0:T(4,128)S(1)} %pad_maximum_fusion.5.vec_ref, bf16[32,4096]{1,0:T(8,128)(2,1)S(1)} %copy-done.1, ...), custom_call_target="tpu_custom_call" | custom-call | flops 17999998976 | bytes 18000000 | tf_op jit(solution)/shard_map/pallas_call | solution.py:581
  64.9 14.9 %all_to_all.20.mixed_ref = bf16[16,32,256]{2,1,0:T(8,128)(2,1)S(1)} all-to-all(bf16[16,32,256]{2,1,0:T(8,128)(2,1)S(1)} %get-tuple-element.50), channel_id=1, replica_groups=mesh['dp'=2,'mp'=16] {'mp'}, dimensions={0} | all-to-all | bytes 524288 | tf_op jit(solution)/shard_map/all_to_all | solution.py:598
  79.8 1.8 %shard_map.257 = (bf16[16,32,256]{2,1,0:T(8,128)(2,1)S(1)}, bf16[16,64,256]{2,1,0:T(8,128)(2,1)}, bf16[512,256]{1,0:T(8,128)(2,1)S(1)}, bf16[512,256]{1,0:T(8,128)(2,1)S(1)}) custom-call(s32[1]{0:T(128)} %bitcast.3.half_ref, bf16[16,32,256]{2,1,0:T(8,128)(2,1)S(1)} %all_to_all.20.mixed_ref, bf16[16,144,256]{2,1,0:T(8,128)(2,1)S(1)} %all-to-all-done.first_ref, ...), custom_call_target="tpu_custom_call" | custom-call | flops 3000000000 | bytes 3000000 | tf_op jit(solution)/shard_map/pallas_call | solution.py:600
  81.6 3.6 %all-to-all-start.2 = ((bf16[16,64,256]{2,1,0:T(8,128)(2,1)}), bf16[16,64,256]{2,1,0:T(8,128)(2,1)S(1)}, u32[]{:S(2)}, u32[]{:S(2)}) async-start(bf16[16,64,256]{2,1,0:T(8,128)(2,1)} %get-tuple-element.56), calls=%async_computation.2 | async-start | bytes 1048576 | tf_op jit(solution)/shard_map/all_to_all | solution.py:611
  87.2 2.1 %shard_map.258 = bf16[16,176,256]{2,1,0:T(8,128)(2,1)} custom-call(bf16[512,256]{1,0:T(8,128)(2,1)S(1)} %get-tuple-element.53.keep_ref, bf16[512,256]{1,0:T(8,128)(2,1)S(1)} %collective-permute-done.7.got_ref, bf16[16,32,256]{2,1,0:T(8,128)(2,1)S(1)} %all_to_all.20.mixed_ref, bf16[16,32,256]{2,1,0:T(8,128)(2,1)S(1)} %collective-permute-done.8.theirs_ref, ...), custom_call_target="tpu_custom_call" | custom-call | flops 2000000000 | bytes 2000000 | tf_op jit(solution)/shard_map/pallas_call | solution.py:612
  89.2 10.7 %all-to-all-done.2.gm_ref = bf16[16,64,256]{2,1,0:T(8,128)(2,1)S(1)} async-done(((bf16[16,64,256]{2,1,0:T(8,128)(2,1)}), bf16[16,64,256]{2,1,0:T(8,128)(2,1)S(1)}, u32[]{:S(2)}, u32[]{:S(2)}) %all-to-all-start.2) | async-done | bytes 524320 | tf_op jit(solution)/shard_map/all_to_all | solution.py:611
  99.9 3.9 %all-to-all-start.3 = ((bf16[16,176,256]{2,1,0:T(8,128)(2,1)}), bf16[16,176,256]{2,1,0:T(8,128)(2,1)S(1)}, u32[]{:S(2)}, u32[]{:S(2)}) async-start(bf16[16,176,256]{2,1,0:T(8,128)(2,1)} %shard_map.258), calls=%async_computation.3 | async-start | bytes 2883584 | tf_op jit(solution)/shard_map/all_to_all | solution.py:621
  103.8 1.6 copy-done.5
  108.5 31.8 %shard_map.259 = (f32[32,4096]{1,0:T(8,128)S(1)}, f32[2,32,128]{2,1,0:T(8,128)S(1)}, f32[32,16,128]{2,1,0:T(8,128)S(1)}) custom-call(s32[1]{0:T(128)S(6)} %copy.89.len_ref, f32[3,32]{1,0:T(4,128)S(1)} %pad_maximum_fusion.5.vec_ref, bf16[32,4096]{1,0:T(8,128)(2,1)S(1)} %copy-done.1, f32[2,32,128]{2,1,0:T(8,128)S(1)} %pad_maximum_fusion.3.stat_ref, ...), custom_call_target="tpu_custom_call" | custom-call | flops 32000000000 | bytes 32000000 | tf_op jit(solution)/shard_map/pallas_call | solution.py:623
  140.5 1.5 collective-permute-done.15
  146.5 1.9 %collective-permute-start.10 = (f32[2,32,128]{2,1,0:T(8,128)S(1)}, f32[2,32,128]{2,1,0:T(8,128)S(1)}, u32[]{:S(2)}, u32[]{:S(2)}) collective-permute-start(f32[2,32,128]{2,1,0:T(8,128)S(1)} %get-tuple-element.68), channel_id=1, source_target_pairs={{0,2},{1,3},{2,0},{3,1},{4,6},{5,7},{6,4},{7,5},{8,10},{9,11},{10,... | collective-permute-start | bytes 98312 | tf_op jit(solution)/shard_map/ppermute | solution.py:466
  148.4 1.5 collective-permute-start.11
  150.7 2.8 %collective-permute-done.11 = f32[2,32,128]{2,1,0:T(8,128)S(1)} collective-permute-done((f32[2,32,128]{2,1,0:T(8,128)S(1)}, f32[2,32,128]{2,1,0:T(8,128)S(1)}, u32[]{:S(2)}, u32[]{:S(2)}) %collective-permute-start.11) | collective-permute-done | bytes 32800 | tf_op jit(solution)/shard_map/ppermute | solution.py:466
  153.8 1.5 collective-permute-start.12
  155.3 2.4 %collective-permute-start.13 = (f32[2,32,128]{2,1,0:T(8,128)S(1)}, f32[2,32,128]{2,1,0:T(8,128)S(1)}, u32[]{:S(2)}, u32[]{:S(2)}) collective-permute-start(f32[2,32,128]{2,1,0:T(8,128)S(1)} %add_add_fusion.1), channel_id=1, source_target_pairs={{0,8},{1,9},{2,10},{3,11},{4,12},{5,13},{6,14},{7,15},{8,0},{9,1},... | collective-permute-start | bytes 98312 | tf_op jit(solution)/shard_map/ppermute | solution.py:466
  159.0 1.8 %collective-permute-done.13 = f32[2,32,128]{2,1,0:T(8,128)S(1)} collective-permute-done((f32[2,32,128]{2,1,0:T(8,128)S(1)}, f32[2,32,128]{2,1,0:T(8,128)S(1)}, u32[]{:S(2)}, u32[]{:S(2)}) %collective-permute-start.13) | collective-permute-done | bytes 32800 | tf_op jit(solution)/shard_map/ppermute | solution.py:466
  160.9 2.6 %collective-permute-done.14 = f32[2,32,128]{2,1,0:T(8,128)S(1)} collective-permute-done((f32[2,32,128]{2,1,0:T(8,128)S(1)}, f32[2,32,128]{2,1,0:T(8,128)S(1)}, u32[]{:S(2)}, u32[]{:S(2)}) %collective-permute-start.14) | collective-permute-done | bytes 32800 | tf_op jit(solution)/shard_map/ppermute | solution.py:466
  (110 shorter events, 26.5 us)
Async XLA Ops:
  5.2 39.4 %all-to-all-start = ((bf16[16,144,256]{2,1,0:T(8,128)(2,1)}), bf16[16,144,256]{2,1,0:T(8,128)(2,1)S(1)}, u32[]{:S(2)}, u32[]{:S(2)}) async-start(bf16[16,144,256]{2,1,0:T(8,128)(2,1)} %get-tuple-element.49), calls=%async_computation | async-start | bytes 2359296 | tf_op jit(solution)/shard_map/all_to_all | solution.py:543
  13.7 14.8 %collective-permute-start = (f32[2,32,128]{2,1,0:T(8,128)S(1)}, f32[2,32,128]{2,1,0:T(8,128)S(1)}, u32[]{:S(2)}, u32[]{:S(2)}) collective-permute-start(f32[2,32,128]{2,1,0:T(8,128)S(1)} %get-tuple-element.43), channel_id=1, source_target_pairs={{0,1},{1,0},{2,3},{3,2},{4,5},{5,4},{6,7},{7,6},{8,9},{9,8},{10,11... | collective-permute-start | bytes 98312 | tf_op jit(solution)/shard_map/ppermute | solution.py:466
  15.6 12.9 %collective-permute-start.1 = (f32[2,32,128]{2,1,0:T(8,128)S(1)}, f32[2,32,128]{2,1,0:T(8,128)S(1)}, u32[]{:S(2)}, u32[]{:S(2)}) collective-permute-start(f32[2,32,128]{2,1,0:T(8,128)S(1)} %get-tuple-element.43), channel_id=1, source_target_pairs={{0,2},{1,3},{2,0},{3,1},{4,6},{5,7},{6,4},{7,5},{8,10},{9,11},{10,... | collective-permute-start | bytes 98312 | tf_op jit(solution)/shard_map/ppermute | solution.py:466
  17.1 11.4 %collective-permute-start.2 = (f32[2,32,128]{2,1,0:T(8,128)S(1)}, f32[2,32,128]{2,1,0:T(8,128)S(1)}, u32[]{:S(2)}, u32[]{:S(2)}) collective-permute-start(f32[2,32,128]{2,1,0:T(8,128)S(1)} %get-tuple-element.43), channel_id=1, source_target_pairs={{0,3},{1,2},{2,1},{3,0},{4,7},{5,6},{6,5},{7,4},{8,11},{9,10},{10,... | collective-permute-start | bytes 98312 | tf_op jit(solution)/shard_map/ppermute | solution.py:466
  17.8 27.1 %copy-start.1 = (bf16[32,4096]{1,0:T(8,128)(2,1)S(1)}, bf16[32,4096]{1,0:T(8,128)(2,1)}, u32[]{:S(2)}) copy-start(bf16[32,4096]{1,0:T(8,128)(2,1)} %x_ref.7) | copy-start | bytes 786436
  28.6 5.6 %collective-permute-start.3 = (f32[2,32,128]{2,1,0:T(8,128)S(1)}, f32[2,32,128]{2,1,0:T(8,128)S(1)}, u32[]{:S(2)}, u32[]{:S(2)}) collective-permute-start(f32[2,32,128]{2,1,0:T(8,128)S(1)} %pad_maximum_fusion.2), channel_id=1, source_target_pairs={{0,4},{1,5},{2,6},{3,7},{4,0},{5,1},{6,2},{7,3},{8,12},{9,13},{10,... | collective-permute-start | bytes 98312 | tf_op jit(solution)/shard_map/ppermute | solution.py:466
  30.5 14.1 %collective-permute-start.4 = (f32[2,32,128]{2,1,0:T(8,128)S(1)}, f32[2,32,128]{2,1,0:T(8,128)S(1)}, u32[]{:S(2)}, u32[]{:S(2)}) collective-permute-start(f32[2,32,128]{2,1,0:T(8,128)S(1)} %pad_maximum_fusion.2), channel_id=1, source_target_pairs={{0,8},{1,9},{2,10},{3,11},{4,12},{5,13},{6,14},{7,15},{8,0},{9,1},... | collective-permute-start | bytes 98312 | tf_op jit(solution)/shard_map/ppermute | solution.py:466
  32.9 11.8 %collective-permute-start.5 = (f32[2,32,128]{2,1,0:T(8,128)S(1)}, f32[2,32,128]{2,1,0:T(8,128)S(1)}, u32[]{:S(2)}, u32[]{:S(2)}) collective-permute-start(f32[2,32,128]{2,1,0:T(8,128)S(1)} %pad_maximum_fusion.2), channel_id=1, source_target_pairs={{0,12},{1,13},{2,14},{3,15},{4,8},{5,9},{6,10},{7,11},{8,4},{9,5},... | collective-permute-start | bytes 98312 | tf_op jit(solution)/shard_map/ppermute | solution.py:466
  44.7 20.1 %collective-permute-start.6 = (bf16[16,64,256]{2,1,0:T(8,128)(2,1)S(1)}, bf16[16,64,256]{2,1,0:T(8,128)(2,1)S(1)}, u32[]{:S(2)}, u32[]{:S(2)}) collective-permute-start(bf16[16,64,256]{2,1,0:T(8,128)(2,1)S(1)} %slice.242), channel_id=1, source_target_pairs={{0,16},{16,0},{1,17},{17,1},{2,18},{18,2},{3,19},{19,3},{4,20},{20... | collective-permute-start | bytes 1572872 | tf_op jit(solution)/shard_map/ppermute | solution.py:494
  64.9 16.7 %copy-start.8 = (f32[32,32,128]{2,1,0:T(8,128)}, f32[32,32,128]{2,1,0:T(8,128)S(1)}, u32[]{:S(2)}) copy-start(f32[32,32,128]{2,1,0:T(8,128)S(1)} %get-tuple-element.58.slope_ref) | copy-start | bytes 1572868
  64.9 16.7 %copy-start.10 = (f32[32,32,128]{2,1,0:T(8,128)}, f32[32,32,128]{2,1,0:T(8,128)S(1)}, u32[]{:S(2)}) copy-start(f32[32,32,128]{2,1,0:T(8,128)S(1)} %get-tuple-element.59.state_ref) | copy-start | bytes 1572868
  81.6 18.3 %all-to-all-start.2 = ((bf16[16,64,256]{2,1,0:T(8,128)(2,1)}), bf16[16,64,256]{2,1,0:T(8,128)(2,1)S(1)}, u32[]{:S(2)}, u32[]{:S(2)}) async-start(bf16[16,64,256]{2,1,0:T(8,128)(2,1)} %get-tuple-element.56), calls=%async_computation.2 | async-start | bytes 1048576 | tf_op jit(solution)/shard_map/all_to_all | solution.py:611
  85.2 1.6 collective-permute-start.7
  85.3 1.9 %collective-permute-start.8 = (bf16[16,32,256]{2,1,0:T(8,128)(2,1)S(1)}, bf16[16,32,256]{2,1,0:T(8,128)(2,1)S(1)}, u32[]{:S(2)}, u32[]{:S(2)}) collective-permute-start(bf16[16,32,256]{2,1,0:T(8,128)(2,1)S(1)} %all_to_all.20.mixed_ref), channel_id=1, source_target_pairs={{0,16},{16,0},{1,17},{17,1},{2,18},{18,2},{3,19},{19,3},{4,20},{20... | collective-permute-start | bytes 786440 | tf_op jit(solution)/shard_map/ppermute | solution.py:494
  99.9 46.6 %all-to-all-start.3 = ((bf16[16,176,256]{2,1,0:T(8,128)(2,1)}), bf16[16,176,256]{2,1,0:T(8,128)(2,1)S(1)}, u32[]{:S(2)}, u32[]{:S(2)}) async-start(bf16[16,176,256]{2,1,0:T(8,128)(2,1)} %shard_map.258), calls=%async_computation.3 | async-start | bytes 2883584 | tf_op jit(solution)/shard_map/all_to_all | solution.py:621
  140.3 1.6 collective-permute-start.15
  145.1 18.3 %copy-start.3 = (bf16[32,4096]{1,0:T(8,128)(2,1)S(1)}, bf16[32,4096]{1,0:T(8,128)(2,1)}, u32[]{:S(2)}) copy-start(bf16[32,4096]{1,0:T(8,128)(2,1)} %g_ref.3) | copy-start | bytes 786436
  146.5 4.2 %collective-permute-start.10 = (f32[2,32,128]{2,1,0:T(8,128)S(1)}, f32[2,32,128]{2,1,0:T(8,128)S(1)}, u32[]{:S(2)}, u32[]{:S(2)}) collective-permute-start(f32[2,32,128]{2,1,0:T(8,128)S(1)} %get-tuple-element.68), channel_id=1, source_target_pairs={{0,2},{1,3},{2,0},{3,1},{4,6},{5,7},{6,4},{7,5},{8,10},{9,11},{10,... | collective-permute-start | bytes 98312 | tf_op jit(solution)/shard_map/ppermute | solution.py:466
  148.4 5.1 %collective-permute-start.11 = (f32[2,32,128]{2,1,0:T(8,128)S(1)}, f32[2,32,128]{2,1,0:T(8,128)S(1)}, u32[]{:S(2)}, u32[]{:S(2)}) collective-permute-start(f32[2,32,128]{2,1,0:T(8,128)S(1)} %get-tuple-element.68), channel_id=1, source_target_pairs={{0,3},{1,2},{2,1},{3,0},{4,7},{5,6},{6,5},{7,4},{8,11},{9,10},{10,... | collective-permute-start | bytes 98312 | tf_op jit(solution)/shard_map/ppermute | solution.py:466
  149.9 3.9 %collective-permute-start.9 = (f32[2,32,128]{2,1,0:T(8,128)S(1)}, f32[2,32,128]{2,1,0:T(8,128)S(1)}, u32[]{:S(2)}, u32[]{:S(2)}) collective-permute-start(f32[2,32,128]{2,1,0:T(8,128)S(1)} %get-tuple-element.68), channel_id=1, source_target_pairs={{0,1},{1,0},{2,3},{3,2},{4,5},{5,4},{6,7},{7,6},{8,9},{9,8},{10,11... | collective-permute-start | bytes 98312 | tf_op jit(solution)/shard_map/ppermute | solution.py:466
  153.8 5.2 %collective-permute-start.12 = (f32[2,32,128]{2,1,0:T(8,128)S(1)}, f32[2,32,128]{2,1,0:T(8,128)S(1)}, u32[]{:S(2)}, u32[]{:S(2)}) collective-permute-start(f32[2,32,128]{2,1,0:T(8,128)S(1)} %add_add_fusion.1), channel_id=1, source_target_pairs={{0,4},{1,5},{2,6},{3,7},{4,0},{5,1},{6,2},{7,3},{8,12},{9,13},{10,... | collective-permute-start | bytes 98312 | tf_op jit(solution)/shard_map/ppermute | solution.py:466
  155.3 5.5 %collective-permute-start.13 = (f32[2,32,128]{2,1,0:T(8,128)S(1)}, f32[2,32,128]{2,1,0:T(8,128)S(1)}, u32[]{:S(2)}, u32[]{:S(2)}) collective-permute-start(f32[2,32,128]{2,1,0:T(8,128)S(1)} %add_add_fusion.1), channel_id=1, source_target_pairs={{0,8},{1,9},{2,10},{3,11},{4,12},{5,13},{6,14},{7,15},{8,0},{9,1},... | collective-permute-start | bytes 98312 | tf_op jit(solution)/shard_map/ppermute | solution.py:466
  157.7 5.7 %collective-permute-start.14 = (f32[2,32,128]{2,1,0:T(8,128)S(1)}, f32[2,32,128]{2,1,0:T(8,128)S(1)}, u32[]{:S(2)}, u32[]{:S(2)}) collective-permute-start(f32[2,32,128]{2,1,0:T(8,128)S(1)} %add_add_fusion.1), channel_id=1, source_target_pairs={{0,12},{1,13},{2,14},{3,15},{4,8},{5,9},{6,10},{7,11},{8,4},{9,5},... | collective-permute-start | bytes 98312 | tf_op jit(solution)/shard_map/ppermute | solution.py:466
  159.0 5.4 %collective-permute-start.16 = (f32[40,512]{1,0:T(8,128)S(1)}, f32[40,512]{1,0:T(8,128)S(1)}, u32[]{:S(2)}, u32[]{:S(2)}) collective-permute-start(f32[40,512]{1,0:T(8,128)S(1)} %get-tuple-element.71), channel_id=1, source_target_pairs={{0,16},{16,0},{1,17},{17,1},{2,18},{18,2},{3,19},{19,3},{4,20},{20... | collective-permute-start | bytes 245768 | tf_op jit(solution)/shard_map/ppermute | solution.py:494
  (18 other events, 118.6 us)

commit v2 on v1

v2 whole, which is shorter than its diff:
```python
from functools import partial

import jax
import jax.numpy as jnp
import numpy as np
from jax import lax
from jax.experimental import pallas as pl
from jax.experimental.pallas import tpu as pltpu
from jax.sharding import PartitionSpec as P

B = 128
G = 8
F32 = jnp.float32
BF16 = jnp.bfloat16
NN = (((1,), (0,)), ((), ()))
NT = (((1,), (1,)), ((), ()))
TN = (((0,), (0,)), ((), ()))
EPS = 1e-05
VMEM = pl.BlockSpec(memory_space=pltpu.VMEM)
SMEM = pl.BlockSpec(memory_space=pltpu.SMEM)


def params(mb):
    return pltpu.CompilerParams(vmem_limit_bytes=mb * 1024 * 1024)


def cost(us):
    return pl.CostEstimate(flops=int(us * 1e9), bytes_accessed=int(us * 1e6), transcendentals=0)


def dot(a, b, dims=NN):
    return lax.dot_general(a, b, dims, preferred_element_type=F32)


def split(v):
    hi = v.astype(BF16)
    return hi, (v - hi.astype(F32)).astype(BF16)


def sincos(x):
    k = jnp.floor(x * 0.6366197723675814 + 0.5)
    y = ((x - k * 1.5703125) - k * 4.837512969970703e-4) - k * 7.54978995489188e-8
    y2 = y * y
    s = y + y * y2 * (-1.6666654611e-1 + y2 * (8.3321608736e-3 - y2 * 1.9515295891e-4))
    c = 1.0 - 0.5 * y2 + y2 * y2 * (4.166664568298827e-2 + y2 * (-1.388731625493765e-3 + y2 * 2.443315711809948e-5))
    q = k.astype(jnp.int32)
    odd = (q & 1) == 1
    sin = jnp.where(odd, c, s)
    cos = jnp.where(odd, s, c)
    sin = jnp.where((q & 2) == 2, -sin, sin)
    cos = jnp.where(((q + 1) & 2) == 2, -cos, cos)
    return sin, cos


def row_iota(shape):
    return lax.broadcasted_iota(jnp.int32, shape, 0)


def lane_iota(shape):
    return lax.broadcasted_iota(jnp.int32, shape, 1)


def shift_token(x, k):
    n = x.shape[0]
    lanes = lane_iota(x.shape)
    rows = row_iota(x.shape)
    turned = pltpu.roll(x, k % B, 1)
    wrapped = pltpu.roll(turned, k % n, 0)
    if k > 0:
        wrapped = jnp.where(rows >= 1, wrapped, 0.0)
        return jnp.where(lanes == 0, wrapped, turned)
    wrapped = jnp.where(rows < n - 1, wrapped, 0.0)
    return jnp.where(lanes == B - 1, wrapped, turned)


def swap_halves(x):
    return pltpu.roll(x, B // 2, 1)


def scan_blocks(v_ref, out_ref, turned_ref, jump, N, backward):
    a_re, a_im = jump
    s = jnp.zeros((G, B), F32)
    t = s
    for k in range(N):
        n = N - 1 - k if backward else k
        out_ref[pl.ds(n, G, stride=N), :] = s
        turned_ref[pl.ds(n, G, stride=N), :] = t
        v = v_ref[pl.ds(n, G, stride=N), :]
        s, t = a_re * s + (a_im * t + v), a_re * t + (swap_halves(v) - a_im * s)


def start_kernel(place_ref, bias_ref, x_hbm, g_hbm, v_hbm, w_hbm, stat_ref, pay_ref, x_ref, g_ref, wt_ref, sems):
    C, L = x_ref.shape
    N = L // B
    mp, rows, nt = pay_ref.shape
    kh = rows // C - 2
    moves = [pltpu.make_async_copy(x_hbm, x_ref, sems.at[0]), pltpu.make_async_copy(g_hbm, g_ref, sems.at[1])]
    for move in moves:
        move.start()
    for half, ref in enumerate((v_hbm, w_hbm)):

        @pl.when(place_ref[0] == half)
        def _():
            pltpu.make_async_copy(ref, wt_ref, sems.at[2]).start()

    moves[0].wait()
    for n in range(N):
        x = x_ref[:, n * B : (n + 1) * B].astype(F32)
        mean = jnp.sum(x, axis=0, keepdims=True) * (1.0 / C)
        dev = x - mean
        stat_ref[n : n + 1, :] = mean
        stat_ref[N + n : N + n + 1, :] = jnp.sum(dev * dev, axis=0, keepdims=True)
    own = row_iota((mp, B))
    stat_ref[2 * N :, :] = jnp.where(own == place_ref[1], bias_ref[...], 0.0)
    for j in range(mp):
        pay_ref[j, kh * C : (kh + 1) * C, :] = x_ref[:, j * nt : (j + 1) * nt]
    moves[1].wait()
    for j in range(mp):
        pay_ref[j, (kh + 1) * C :, :] = g_ref[:, j * nt : (j + 1) * nt]
    pltpu.make_async_copy(v_hbm, wt_ref, sems.at[2]).wait()
    for j in range(mp):
        for q in range(kh):
            pay_ref[j, q * C : (q + 1) * C, :] = wt_ref[:, q * nt : (q + 1) * nt]


def join_stats(parts, N, count):
    mean = sum(p[:N] for p in parts) * (1.0 / len(parts))
    spread = sum(p[N : 2 * N] for p in parts) + count * sum((p[:N] - mean) * (p[:N] - mean) for p in parts)
    return mean, spread, sum(p[2 * N :] for p in parts)


def columns(arrays, cols, C):
    pad = jnp.zeros((B - C, B), F32)
    for q, v in enumerate(arrays):
        cols[q] = jnp.concatenate([v, pad], axis=0).T


def channel_waves(cols, i, M):
    back = (B - i * G) % B
    al = pltpu.roll(cols[0, 0:M, :], back, 1)
    om = pltpu.roll(cols[1, 0:M, :], back, 1)
    ww = 2.0 * pltpu.roll(cols[2], back, 1)
    place = lane_iota((M, B)).astype(F32)
    ahead = float(B) - place
    out = []
    for j in range(G):
        a = jnp.broadcast_to(al[:, j : j + 1], (M, B))
        o = jnp.broadcast_to(om[:, j : j + 1], (M, B))
        w = [jnp.broadcast_to(ww[q * M : (q + 1) * M, j : j + 1], (M, B)) for q in range(4)]
        sin, cos = sincos(o * place)
        mag = jnp.exp(a * place)
        near = mag * cos, mag * sin
        sin, cos = sincos(o * ahead)
        mag = jnp.exp(a * ahead)
        out.append((near, (mag * cos, mag * sin), w))
    return out


def toeplitz_rows(kern, start):
    return pltpu.roll(jnp.broadcast_to(kern, (B, B)), start, 1, stride=1, stride_axis=0)


def table_kernel(rates_ref, coef_ref, f_ref, again_ref, t_ref, jump_ref, wout_ref, cols, *, C, M):
    i = pl.program_id(0)

    @pl.when(i == 0)
    def _():
        step_size = jnp.exp(rates_ref[0])
        real_rate = -jnp.exp(rates_ref[1])
        freq = rates_ref[2]
        re = step_size * real_rate
        im = step_size * freq
        growth = jnp.exp(re)
        sin, cos = sincos(im)
        num_re = growth * cos - 1.0
        num_im = growth * sin
        den = real_rate * real_rate + freq * freq
        in_re = (num_re * real_rate + num_im * freq) / den
        in_im = (num_im * real_rate - num_re * freq) / den
        coef = coef_ref[...]
        first = lane_iota(coef.shape) < B // 2
        w = coef * in_re + swap_halves(coef) * jnp.where(first, -in_im, in_im)
        wout_ref[...] = w
        sin, cos = sincos(im * float(B))
        mag = jnp.exp(re * float(B))
        jump_ref[0] = mag * cos
        jump_ref[1] = mag * jnp.where(first, -sin, sin)
        columns((re, im, w), cols, C)

    rows = row_iota((B, B))
    lanes = lane_iota((B, B))
    odd = (lanes & M) == M
    every = range(G)
    waves = channel_waves(cols, i, M)
    feeds = [jnp.concatenate([f_re, f_re, f_im, f_im], axis=0).T for _, (f_re, f_im), _ in waves]
    kerns = []
    for j in every:
        (n_re, n_im), _, w = waves[j]
        for h in range(2):
            w_re, w_im = w[h], w[2 + h]
            e_re = w_re * n_re - w_im * n_im
            e_im = -(w_re * n_im + w_im * n_re)
            kerns.append(jnp.sum(e_re, axis=0, keepdims=True))
            for q, v in enumerate(split(e_re)):
                t_ref[j, 2 * B + h * M : 2 * B + (h + 1) * M, q * B : (q + 1) * B] = v
            for q, v in enumerate(split(e_im)):
                t_ref[j, 2 * B + (2 + h) * M : 2 * B + (3 + h) * M, q * B : (q + 1) * B] = v
    rolled = [toeplitz_rows(kern, 0) for kern in kerns]
    for j in every:
        for h in range(2):
            part = jnp.where(odd if h == 1 else ~odd, feeds[j], 0.0)
            for q, v in enumerate(split(part)):
                f_ref[j, h * B : (h + 1) * B, q * B : (q + 1) * B] = v
                again_ref[j, h * B : (h + 1) * B, q * B : (q + 1) * B] = v
            toe = jnp.where(lanes >= rows, rolled[2 * j + h], 0.0)
            for q, v in enumerate(split(toe)):
                t_ref[j, h * B : (h + 1) * B, q * B : (q + 1) * B] = v


def back_table_kernel(rates_ref, w_ref, t_ref, near_ref, cols, *, C, M):
    i = pl.program_id(0)

    @pl.when(i == 0)
    def _():
        step_size = jnp.exp(rates_ref[0])
        columns((step_size * -jnp.exp(rates_ref[1]), step_size * rates_ref[2], w_ref[...]), cols, C)

    rows = row_iota((B, B))
    lanes = lane_iota((B, B))
    zero = jnp.zeros((M, B), BF16)
    every = range(G)
    waves = channel_waves(cols, i, M)
    turned = [jnp.concatenate([n_re, n_re, n_im, n_im], axis=0).T for (n_re, n_im), _, _ in waves]
    kerns, starts = [], []
    for j in every:
        (n_re, n_im), (f_re, f_im), w = waves[j]
        for h in range(2):
            w_re, w_im = w[h], w[2 + h]
            b_re = w_re * f_re - w_im * f_im
            b_im = -(w_re * f_im + w_im * f_re)
            kerns.append(jnp.sum(b_re, axis=0, keepdims=True))
            starts.append(jnp.sum(w_re * n_re - w_im * n_im, axis=0, keepdims=True)[:, 0:1])
            for part, v2 in ((0, b_re), (2, b_im)):
                for q, v in enumerate(split(v2)):
                    at = slice((2 * q + h) * B, (2 * q + h + 1) * B)
                    t_ref[j, B + part * M : B + (part + 1) * M, at] = v
                    t_ref[j, B + (part + 1) * M : B + (part + 2) * M, at] = zero
    rolled = [toeplitz_rows(kern, 0) for kern in kerns]
    for j in every:
        for q, v in enumerate(split(turned[j])):
            near_ref[j, :, q * B : (q + 1) * B] = v
        for h in range(2):
            start = jnp.broadcast_to(starts[2 * j + h], (B, B))
            toe = jnp.where(lanes < rows, rolled[2 * j + h], jnp.where(lanes == rows, start, 0.0))
            for q, v in enumerate(split(toe)):
                t_ref[j, 0:B, (2 * q + h) * B : (2 * q + h + 1) * B] = v


def token_stats(stat_ref, length, count):
    mean = stat_ref[0]
    inv = lax.rsqrt(stat_ref[1] * (1.0 / count) + EPS)
    place = row_iota(mean.shape) * B + lane_iota(mean.shape)
    return mean, inv, (place < length).astype(F32)


def mixer_kernel(len_ref, vec_ref, x_ref, *refs, count, parts):
    part_refs, refs = refs[:parts], refs[parts:]
    f_ref, t_ref, jump_ref = refs[:3]
    mixed_ref, slope_ref, state_ref, other_ref, stat_ref, bias_ref = refs[3:9]
    xs, ms, tok, us, ups, sts, ots = refs[9:]
    i = pl.program_id(0)
    C, L = x_ref.shape
    N = L // B
    nt = mixed_ref.shape[2]

    @pl.when(i == 0)
    def _():
        for n in range(N):
            xs[n * C : (n + 1) * C, :] = x_ref[:, n * B : (n + 1) * B].astype(F32)
        stat_ref[0], stat_ref[1], bias_ref[...] = join_stats([r[...] for r in part_refs], N, count / parts)
        mean, inv, mask = token_stats(stat_ref, len_ref[0], count)
        tok[0] = mean
        tok[1] = inv
        tok[2] = mask

    for j in range(G):
        ci = i * G + j
        normed = (xs[pl.ds(ci, N, stride=C), :] - tok[0]) * tok[1]
        sig = tok[2] * (normed * vec_ref[0, ci] + vec_ref[1, ci])
        liq = sig * shift_token(sig, 1)
        for q, v in enumerate((sig, liq)):
            hi, lo = split(v)
            us[j, 0:N, q * B : (q + 1) * B] = hi
            us[j, N:, q * B : (q + 1) * B] = lo
        slope_ref[j] = sig
    ups_all = [dot(us[j], f_ref[j]) for j in range(G)]
    for j, up in enumerate(ups_all):
        ups[j * N : (j + 1) * N, :] = up[:N, :B] + (up[:N, B:] + up[N:, :B])
    at = pl.ds(pl.multiple_of(i * G, G), G)
    scan_blocks(ups, sts, ots, (jump_ref[0, at, :], jump_ref[1, at, :]), N, False)
    left = []
    for j in range(G):
        state = sts[j * N : (j + 1) * N, :]
        state_ref[j] = state
        other_ref[j] = ots[j * N : (j + 1) * N, :]
        left.append(jnp.concatenate([us[j], jnp.concatenate(split(state), axis=0)], axis=1))
    outs = [dot(left[j], t_ref[j]) for j in range(G)]
    for j, out in enumerate(outs):
        ci = i * G + j
        mask = tok[2]
        y = out[:N, :B] + (out[:N, B:] + out[N:, :B]) + vec_ref[2, ci] * slope_ref[j]
        y2 = y * y
        th = jnp.tanh(0.7978845608028654 * (y + 0.044715 * (y * y2)))
        half = 0.5 * (1.0 + th)
        ms[pl.ds(pl.multiple_of(ci * N, N), N), :] = mask * (y * half)
        slope_ref[j] = mask * (half + 0.5 * y * (1.0 - th * th) * (0.7978845608028654 * (1.0 + 0.134145 * y2)))

    @pl.when(i == pl.num_programs(0) - 1)
    def _():
        per = nt // B
        for n in range(N):
            mixed_ref[n // per, :, (n % per) * B : (n % per + 1) * B] = ms[pl.ds(n, C, stride=N), :].astype(BF16)


def glu_kernel(half_ref, in_ref, first_ref, other_ref, bias_ref, gm_ref, keep_ref, send_ref, gp, wt):
    mp, C, nt = in_ref.shape
    H = mp * C
    kh = H // nt
    own = half_ref[0]
    mixed = in_ref[...].reshape(H, nt)
    for q in range(kh):
        at = slice(q * nt, (q + 1) * nt)
        wt[own, :, at] = first_ref[:, q * C : (q + 1) * C, :].reshape(H, nt)
        wt[1 - own, :, at] = other_ref[:, q * C : (q + 1) * C, :].reshape(H, nt)
    step = B
    per = step // C
    bias = jnp.concatenate([bias_ref[...], jnp.zeros((B - mp, B), F32)], axis=0).T
    for s in range(mp // per):
        lo = s * step
        col_v = jnp.concatenate([bias[0:C, k : k + 1] for k in range(s * per, (s + 1) * per)], axis=0)
        col_g = jnp.concatenate([bias[C : 2 * C, k : k + 1] for k in range(s * per, (s + 1) * per)], axis=0)
        value = dot(wt[0, lo : lo + step, :], mixed) + col_v
        gate = dot(wt[1, lo : lo + step, :], mixed) + col_g
        sig = jax.nn.sigmoid(gate)
        x = first_ref[s * per : (s + 1) * per, kh * C : (kh + 1) * C, :].reshape(step, nt).astype(F32)
        g = first_ref[s * per : (s + 1) * per, (kh + 1) * C :, :].reshape(step, nt).astype(F32)
        gm_ref[s * per : (s + 1) * per, 2 * C :, :] = (x + value * sig).astype(BF16).reshape(per, C, nt)
        gv = g * sig
        gp[0, lo : lo + step, :] = gv.astype(BF16)
        gp[1, lo : lo + step, :] = (gv * value * (1.0 - sig)).astype(BF16)
    for s in range(mp // per):
        at = slice(s * step, (s + 1) * step)
        gm = dot(wt[0, :, at], gp[0], TN) + dot(wt[1, :, at], gp[1], TN)
        hi, lo = split(gm)
        gm_ref[s * per : (s + 1) * per, 0:C, :] = hi.reshape(per, C, nt)
        gm_ref[s * per : (s + 1) * per, C : 2 * C, :] = lo.reshape(per, C, nt)
    keep_ref[...] = gp[own]
    send_ref[...] = gp[1 - own]


def weight_kernel(place_ref, keep_ref, got_ref, mixed_ref, theirs_ref, *refs, C, mp):
    outs, wg = refs[:-1], refs[-1]
    nt = mixed_ref.shape[1]
    ways = len(outs)
    per = mp // ways
    total = dot(keep_ref[...], mixed_ref[...], NT) + dot(got_ref[...], theirs_ref[...], NT)
    for m in range(mp):
        at = (m // ways) * C
        wg[m % ways, at : at + C, :] = total[m * C : (m + 1) * C]
    ones = jnp.ones((8, nt), BF16)
    tail = dot(ones, keep_ref[...], NT) + dot(ones, got_ref[...], NT)
    for q in range(ways):
        wg[q, per * C :, :] = tail
    for k in range(ways):
        outs[k][...] = wg[lax.rem(place_ref[1], ways) ^ k]


def fold_kernel(place_ref, *refs, ways, got, C, seen):
    parts, outs, acc = refs[:got], refs[got:-1], refs[-1]
    total = parts[0][...]
    for p in parts[1:]:
        total = total + p[...]
    blocks = (total.shape[0] - 8) // C
    for z in range(blocks):
        at = (z // ways) * C
        acc[z % ways, at : at + C, :] = total[z * C : (z + 1) * C]
    for q in range(ways):
        acc[q, (blocks // ways) * C :, :] = total[blocks * C :]
    for k in range(ways):
        outs[k][...] = acc[lax.rem(lax.div(place_ref[1], seen), ways) ^ k]


def back_kernel(
    len_ref, vec_ref, x_ref, stat_ref, gm_ref, slope_ref, t_ref, near_ref, jump_ref,
    gn_ref, sum_ref, row_ref, g_ref, p_ref, r_ref, turned_ref, xs, gs, ns, tok, hs, ps, rs, rts, tab, sem, *, count,
):
    i = pl.program_id(0)
    C, L = x_ref.shape
    N = L // B
    nt = gm_ref.shape[2]
    per = nt // B

    def fetch(k):
        at = pl.ds(k * G, G)
        return pltpu.make_async_copy(t_ref.at[at], tab.at[at], sem.at[k])

    @pl.when(i == 0)
    def _():
        for k in range(C // G):
            fetch(k).start()
        for n in range(N):
            xs[n * C : (n + 1) * C, :] = x_ref[:, n * B : (n + 1) * B].astype(F32)
            at = slice((n % per) * B, (n % per + 1) * B)
            gs[n * C : (n + 1) * C, :] = gm_ref[n // per, 0:C, at].astype(F32) + gm_ref[n // per, C : 2 * C, at].astype(F32)
        mean, inv, mask = token_stats(stat_ref, len_ref[0], count)
        tok[0] = mean
        tok[1] = inv
        tok[2] = mask
        sum_ref[...] = jnp.zeros_like(sum_ref)

    for j in range(G):
        ci = i * G + j
        g = gs[pl.ds(ci, N, stride=C), :] * slope_ref[j]
        g_ref[j] = g
        hi, lo = split(g)
        hs[j, 0:N, :] = hi
        hs[j, N:, :] = lo
    z_all = [dot(hs[j], near_ref[j]) for j in range(G)]
    for j, z in enumerate(z_all):
        p = z[:N, :B] + (z[:N, B:] + z[N:, :B])
        p_ref[j] = p
        ps[j * N : (j + 1) * N, :] = p
    at = pl.ds(pl.multiple_of(i * G, G), G)
    scan_blocks(ps, rs, rts, (jump_ref[0, at, :], jump_ref[1, at, :]), N, True)
    left = []
    for j in range(G):
        r = rs[j * N : (j + 1) * N, :]
        r_ref[j] = r
        turned_ref[j] = rts[j * N : (j + 1) * N, :]
        left.append(jnp.concatenate([hs[j], jnp.concatenate(split(r), axis=0)], axis=1))
    fetch(i).wait()
    both_all = [dot(left[j], tab[i * G + j]) for j in range(G)]
    for j, both in enumerate(both_all):
        ci = i * G + j
        mask = tok[2]
        normed = (xs[pl.ds(ci, N, stride=C), :] - tok[0]) * tok[1]
        sig = mask * (normed * vec_ref[0, ci] + vec_ref[1, ci])
        both = both[:N, : 2 * B] + (both[:N, 2 * B :] + both[N:, : 2 * B])
        gl = both[:, B:]
        grad = both[:, :B] + vec_ref[2, ci] * g_ref[j] + gl * shift_token(sig, 1) + shift_token(gl * sig, -1)
        masked = mask * grad
        gn = masked * vec_ref[0, ci]
        sum_ref[0] += gn
        sum_ref[1] += gn * normed
        ns[pl.ds(pl.multiple_of(ci * N, N), N), :] = gn
        for q, v in enumerate((g_ref[j] * sig, masked * normed, masked)):
            row_ref[j, q * 8 : (q + 1) * 8, :] = sum(v[8 * k : 8 * k + 8] for k in range(N // 8))

    @pl.when(i == pl.num_programs(0) - 1)
    def _():
        for n in range(N):
            gn_ref[:, n * B : (n + 1) * B] = ns[pl.ds(n, C, stride=N), :]


def lift_kernel(len_ref, vec_ref, x_ref, stat_ref, f_ref, u_ref, lift_ref, xs, tok, *, count):
    i = pl.program_id(0)
    C, L = x_ref.shape
    N = L // B

    @pl.when(i == 0)
    def _():
        for n in range(N):
            xs[n * C : (n + 1) * C, :] = x_ref[:, n * B : (n + 1) * B].astype(F32)
        tok[0], tok[1], tok[2] = token_stats(stat_ref, len_ref[0], count)

    ahead = float(B) - lane_iota((N, B)).astype(F32)
    flip = (lane_iota((B, B)) + row_iota((B, B)) == B - 1).astype(BF16)
    flat, left = [], []
    for j in range(G):
        ci = i * G + j
        normed = (xs[pl.ds(ci, N, stride=C), :] - tok[0]) * tok[1]
        sig = tok[2] * (normed * vec_ref[0, ci] + vec_ref[1, ci])
        liq = sig * shift_token(sig, 1)
        flat.append(jnp.concatenate(split(sig) + split(liq), axis=0))
        left.append(jnp.concatenate(split(jnp.concatenate([sig * ahead, liq * ahead], axis=1)), axis=0))
    turned_all = [dot(v, flip).astype(BF16) for v in flat]
    lifts = [dot(left[j], f_ref[j]) for j in range(G)]
    for j in range(G):
        turned, lift = turned_all[j], lifts[j]
        for q in range(2):
            at = slice(q * B, (q + 1) * B)
            u_ref[j, 0 : 2 * N, at] = turned[2 * q * N : (2 * q + 2) * N]
            u_ref[j, 2 * N :, at] = turned[2 * q * N : (2 * q + 1) * N]
        lift_ref[j] = lift[:N, :B] + (lift[:N, B:] + lift[N:, :B])


def sums_kernel(u_ref, lift_ref, g_ref, p_ref, r_ref, rx_ref, state_ref, sx_ref, near_ref, jump_ref, row_ref):
    i = pl.program_id(0)
    _, N, _ = g_ref.shape
    place = lane_iota((N, B)).astype(F32)
    rows2, lanes2 = row_iota((B, B)), lane_iota((B, B))
    inside = lanes2 + rows2 >= B - 1
    rows16 = row_iota((16, B))
    lag = lane_iota((16, B)).astype(F32)
    R = N + 16
    every = range(G)
    turned = []
    for j in every:
        g_hi, g_lo = split(g_ref[j])
        turned.append(jnp.concatenate([g_hi, g_hi, g_lo], axis=0).T)
    corr = [dot(turned[j], u_ref[j]) for j in every]
    left = []
    for j in every:
        lags = []
        for q in range(2):
            part = jnp.where(inside, corr[j][:, q * B : (q + 1) * B], 0.0)
            lags.append(jnp.sum(pltpu.roll(part, 1, 1, stride=1, stride_axis=0), axis=0, keepdims=True))
        pair = jnp.where((rows16 & 1) == 0, lags[0], lags[1])
        pair = jnp.where(rows16 < 2, pair, jnp.where(rows16 < 4, pair * lag, 0.0))
        left.append(jnp.concatenate(split(jnp.concatenate([g_ref[j] * place, pair], axis=0)), axis=0))
    both = [dot(left[j], near_ref[j]) for j in every]
    for j in every:
        ci = i * G + j
        z = both[j][:R, :B] + (both[j][:R, B:] + both[j][R:, :B])
        row_ref[j, 0:8, :] = z[N : N + 8]
        p, r, state, lift = p_ref[j], r_ref[j], state_ref[j], lift_ref[j]
        state_x, r_x = sx_ref[j], rx_ref[j]
        carry = z[:N] + float(B) * (r * jump_ref[0, pl.ds(ci, 1), :] + r_x * jump_ref[1, pl.ds(ci, 1), :])
        total = [p * state, p * state_x, carry * state + lift * r, carry * state_x + lift * r_x]
        for q, v in enumerate(total):
            row_ref[j, 8 + 8 * q : 16 + 8 * q, :] = sum(v[8 * k : 8 * k + 8] for k in range(N // 8))


def join_kernel(plain_ref, ref, out_ref):
    odd = (lane_iota((out_ref.shape[1], B)) & (B // 4)) != 0
    for q in range(2):
        out_ref[q] = jnp.where(odd, ref[:, 2 * q + 1, :], ref[:, 2 * q, :])
    for q in range(4):
        out_ref[2 + q] = jnp.sum(ref[:, 8 + 8 * q : 16 + 8 * q, :], axis=1)
    for q in range(3):
        out_ref[6 + q] = jnp.sum(plain_ref[:, 8 * q : 8 * q + 8, :], axis=1)


def finish_kernel(
    place_ref, mine_ref, theirs_ref, w_ref, step_ref, decay_ref, freq_ref, read_ref, liquid_ref, wsum_ref, across_ref,
    value_ref, gate_ref, vbias_ref, gbias_ref, step_out, decay_out, freq_out, read_out, liquid_out,
    skip_out, gain_out, bias_out, *, M,
):
    C = decay_ref.shape[0]
    half = B // 2

    def emit(first, second):
        value_ref[...] = first[0:C, :]
        gate_ref[...] = second[0:C, :]
        per = B // C
        group = place_ref[1] // per
        back = (B - (place_ref[1] % per) * C) % B
        for out, v in ((vbias_ref, first), (gbias_ref, second)):
            lanes = v[C : C + 8, pl.ds(pl.multiple_of(group * B, B), B)]
            out[...] = pltpu.roll(lanes, back, 1)[0:1, 0:C]

    @pl.when(place_ref[0] == 0)
    def _():
        emit(wsum_ref, across_ref)

    @pl.when(place_ref[0] == 1)
    def _():
        emit(across_ref, wsum_ref)

    rows = [mine_ref[q] + theirs_ref[q] for q in range(9)]

    def parts(a, b, c):
        return a[:, :half] - a[:, half:] + c[:, :half], b[:, :half] + b[:, half:] + c[:, half:]

    g_re, g_im = parts(rows[2], rows[3], rows[0])
    d_re, d_im = parts(rows[4], rows[5], rows[1])
    w = w_ref[...]
    w_re, w_im = w[:, :half], w[:, half:]
    l_re = w_re * d_re - w_im * d_im
    l_im = w_re * d_im + w_im * d_re
    cot = (
        2.0 * g_re[:, :M], -2.0 * g_im[:, :M], 2.0 * g_re[:, M:], -2.0 * g_im[:, M:],
        2.0 * (l_re[:, :M] + l_re[:, M:]), -2.0 * (l_im[:, :M] + l_im[:, M:]),
    )
    step = jnp.sum(jnp.where(row_iota((C, C)) == lane_iota((C, C)), step_ref[...], 0.0), axis=1, keepdims=True)
    _, back = jax.vjp(mode_terms, step, decay_ref[...], freq_ref[...], read_ref[...], liquid_ref[...])
    step_grad, decay_out[...], freq_out[...], read_out[...], liquid_out[...] = back(cot)
    lanes = lane_iota((B, B))
    pad = jnp.zeros((B - C, 1), F32)
    plain = jnp.zeros((B, B), F32)
    for q, v in enumerate([step_grad] + [jnp.sum(rows[6 + q], axis=1, keepdims=True) for q in range(3)]):
        plain = jnp.where(lanes == q, jnp.concatenate([v, pad], axis=0), plain)
    plain = plain.T
    for q, out in enumerate((step_out, skip_out, gain_out, bias_out)):
        out[...] = plain[q : q + 1, 0:C]


def last_kernel(x_ref, g_ref, gn_ref, stat_ref, sum_ref, out_ref, *, count):
    C, L = x_ref.shape
    for n in range(L // B):
        at = slice(n * B, (n + 1) * B)
        mean = stat_ref[0, n : n + 1, :]
        inv = lax.rsqrt(stat_ref[1, n : n + 1, :] * (1.0 / count) + EPS)
        first = sum_ref[0, n : n + 1, :] * (1.0 / count)
        second = sum_ref[1, n : n + 1, :] * (1.0 / count)
        normed = (x_ref[:, at].astype(F32) - mean) * inv
        out_ref[:, at] = inv * (gn_ref[:, at] - first - normed * second) + g_ref[:, at].astype(F32)


def gather_kernel(pay_ref, out_ref):
    mp, _, nt = pay_ref.shape
    C = out_ref.shape[0]
    for s in range(mp):
        out_ref[:, s * nt : (s + 1) * nt] = pay_ref[s, 2 * C :, :]


def total_kernel(*refs):
    total = refs[0][...]
    for p in refs[1:-1]:
        total = total + p[...]
    refs[-1][...] = total


def rounds_of(size):
    rounds, bit = [], 1
    while bit < size:
        if bit * 2 < size:
            rounds.append((bit, 2 * bit, 3 * bit))
            bit *= 4
        else:
            rounds.append((bit,))
            bit *= 2
    return rounds


def exchange(v, axis, size, off):
    return lax.ppermute(v, axis, [(k, k ^ off) for k in range(size)])


def all_sums(v, size):
    for offs in rounds_of(size):
        v = sum([exchange(v, "mp", size, o) for o in offs], v)
    return v


def sum_docs(v, size, stride):
    total = v
    for k in range(stride, size, stride):
        total = total + lax.ppermute(v, "dp", [(q, (q + k) % size) for q in range(size)])
    return total


def partner(v, size):
    return lax.ppermute(v, "dp", [(q, q ^ 1) for q in range(size)])


def mode_terms(log_step, decay_log, frequency, readout, liquid_readout):
    M = decay_log.shape[1]
    step_size = jnp.exp(log_step)
    real_rate = -jnp.exp(decay_log)
    real_step = step_size * real_rate
    imag_step = step_size * frequency
    growth = jnp.exp(real_step)
    num_real = growth * jnp.cos(imag_step) - 1.0
    num_imag = growth * jnp.sin(imag_step)
    denominator = real_rate * real_rate + frequency * frequency
    in_real = (num_real * real_rate + num_imag * frequency) / denominator
    in_imag = (num_imag * real_rate - num_real * frequency) / denominator

    def mix(coeffs):
        re, im = coeffs[:, :M], coeffs[:, M:]
        return re * in_real - im * in_imag, re * in_imag + im * in_real

    return mix(readout) + mix(liquid_readout) + (real_step, imag_step)


def per_device(
    mp, dp,
    tokens, lengths, norm_gain, norm_bias, log_step, decay_log, frequency, readout, liquid_readout,
    skip_gain, value_weight, gate_weight, value_bias, gate_bias, grad_out,
):
    C, L = tokens.shape
    H = value_weight.shape[0]
    M = decay_log.shape[1]
    N = L // B
    nt = L // mp
    kh = H // nt
    shape = jax.ShapeDtypeStruct

    place = jnp.stack([lax.axis_index("dp") & 1, lax.axis_index("mp")]).astype(jnp.int32)
    rounds = rounds_of(mp)
    small, large = 16, 28

    def pin(v):
        return pltpu.with_memory_space_constraint(v, pltpu.HBM)

    def call(kernel, out, n_in, smem=0, us=1, scratch=(), mb=small):
        return pl.pallas_call(
            kernel,
            out_shape=out,
            in_specs=[SMEM] * smem + [VMEM] * (n_in - smem),
            out_specs=jax.tree.map(lambda _: VMEM, out),
            scratch_shapes=list(scratch),
            compiler_params=params(mb),
            cost_estimate=cost(us),
        )

    def whole(*dims):
        return pl.BlockSpec(dims, lambda i: (0,) * len(dims))

    def chan(*dims, at=0):
        return pl.BlockSpec((G,) + dims, lambda i: (i + at,) + (0,) * len(dims))

    def by_channel(kernel, out, in_specs, out_specs, us, scratch, mb=small, channels=C):
        return pl.pallas_call(
            kernel,
            grid=(channels // G,),
            out_shape=out,
            in_specs=in_specs,
            out_specs=out_specs,
            scratch_shapes=scratch,
            compiler_params=params(mb),
            cost_estimate=cost(us),
        )

    vm = pltpu.VMEM
    blocks = shape((C, N, B), F32)
    far = pltpu.HBM
    far_blocks = far((C, N, B), F32)
    def pin(v):
        return pltpu.with_memory_space_constraint(v, far)

    bias = jnp.pad(jnp.concatenate([value_bias, gate_bias]).astype(F32)[None], ((0, 0), (0, B - 2 * C)))
    hbm = pl.BlockSpec(memory_space=pltpu.HBM)
    stat, pay = pl.pallas_call(
        start_kernel,
        out_shape=(shape((2 * N + mp, B), F32), shape((mp, (2 + kh) * C, nt), BF16)),
        in_specs=[SMEM, VMEM, hbm, hbm, hbm, hbm],
        out_specs=(VMEM, VMEM),
        scratch_shapes=[
            pltpu.VMEM((C, L), BF16), pltpu.VMEM((C, L), BF16), pltpu.VMEM((C, H), BF16), pltpu.SemaphoreType.DMA((3,)),
        ],
        compiler_params=params(small),
        cost_estimate=cost(3),
    )(place, bias, pin(tokens), pin(grad_out), pin(value_weight.T), pin(gate_weight.T))
    first = lax.all_to_all(pay, "mp", split_axis=0, concat_axis=0, tiled=True)

    rates = jnp.stack(
        [jnp.broadcast_to(log_step[:, None], (C, 4 * M)), jnp.tile(decay_log, (1, 4)), jnp.tile(frequency, (1, 4))]
    )
    coef = jnp.concatenate([readout[:, :M], liquid_readout[:, :M], readout[:, M:], liquid_readout[:, M:]], axis=1)
    f_near, f_tab, t_tab, jump, w_all = by_channel(
        partial(table_kernel, C=C, M=M),
        (
            shape((C, 2 * B, 2 * B), BF16), far((C, 2 * B, 2 * B), BF16), shape((C, 3 * B, 2 * B), BF16),
            shape((2, C, B), F32), shape((C, B), F32),
        ),
        [whole(3, C, B), whole(C, B)],
        (chan(2 * B, 2 * B), chan(2 * B, 2 * B), chan(3 * B, 2 * B), whole(2, C, B), whole(C, B)),
        6,
        [vm((3, B, B), F32)],
    )(rates, coef)

    count = C
    for k, offs in enumerate(rounds[::-1]):
        parts = [stat] + [exchange(stat, "mp", mp, o) for o in offs]
        if k == 0:
            parts[1], parts[-1], t_tab = lax.optimization_barrier((parts[1], parts[-1], t_tab))
        if k < len(rounds) - 1:
            stat = jnp.concatenate(join_stats(parts, N, float(count)), axis=0)
            count *= len(parts)

    vecs = jnp.stack([norm_gain, norm_bias, skip_gain])
    mixed, slope, state, state_x, stat, bias = by_channel(
        partial(mixer_kernel, count=H, parts=len(parts)),
        (shape((mp, C, nt), BF16), far_blocks, far_blocks, far_blocks, shape((2, N, B), F32), shape((mp, B), F32)),
        [SMEM, SMEM, whole(C, L)] + [whole(2 * N + mp, B)] * len(parts)
        + [chan(2 * B, 2 * B), chan(3 * B, 2 * B), whole(2, C, B)],
        (whole(mp, C, nt), chan(N, B), chan(N, B), chan(N, B), whole(2, N, B), whole(mp, B)),
        6,
        [
            vm((N * C, B), F32), vm((N * C, B), F32), vm((3, N, B), F32), vm((G, 2 * N, 2 * B), BF16),
            vm((G * N, B), F32), vm((G * N, B), F32), vm((G * N, B), F32),
        ],
    )(lengths, vecs, tokens, *parts, f_near, t_tab, jump)

    mixed, first, rates = lax.optimization_barrier((mixed, first, rates))
    other_w = partner(first[:, : kh * C, :], dp)
    mixed_tok = lax.all_to_all(mixed, "mp", split_axis=0, concat_axis=0, tiled=True)
    back_tab, near_tab = by_channel(
        partial(back_table_kernel, C=C, M=M),
        (far((C, 2 * B, 4 * B), BF16), far((C, B, 2 * B), BF16)),
        [whole(3, C, B), whole(C, B)],
        (chan(2 * B, 4 * B), chan(B, 2 * B)),
        7,
        [vm((3, B, B), F32)],
    )(rates, w_all)
    mixed_tok, back_tab = lax.optimization_barrier((mixed_tok, back_tab))
    gm, keep, send = call(
        glu_kernel,
        (shape((mp, 3 * C, nt), BF16),) + (shape((H, nt), BF16),) * 2,
        5, 1, 2, [vm((2, H, nt), BF16), vm((2, H, H), BF16)],
    )(place, mixed_tok, first, other_w, bias)
    mixed_tok = mixed_tok.reshape(H, nt)
    gm, f_tab = lax.optimization_barrier((gm, f_tab))
    gm = lax.all_to_all(gm, "mp", split_axis=0, concat_axis=0, tiled=True)
    u_rev, lift = by_channel(
        partial(lift_kernel, count=H),
        (far((C, 3 * N, 2 * B), BF16), far_blocks),
        [SMEM, SMEM, whole(C, L), whole(2, N, B), chan(2 * B, 2 * B)],
        (chan(3 * N, 2 * B), chan(N, B)),
        3,
        [vm((N * C, B), F32), vm((3, N, B), F32)],
        56,
    )(lengths, vecs, tokens, stat, pin(f_tab))
    gm, lift = lax.optimization_barrier((gm, lift))

    ways = len(rounds[0]) + 1
    rows_left = mp // ways
    outs = call(
        partial(weight_kernel, C=C, mp=mp), (shape((rows_left * C + 8, H), F32),) * ways, 5, 1, 2,
        [vm((ways, rows_left * C + 8, H), F32)],
    )(place, keep, partner(send, dp), mixed_tok, partner(mixed_tok, dp))
    terms = [outs[0]] + [exchange(v, "mp", mp, o) for v, o in zip(outs[1:], rounds[0])]

    gn, sums, plain, g_pre, p_blk, r_blk, rx_blk = by_channel(
        partial(back_kernel, count=H),
        (shape((C, L), F32), shape((2, N, B), F32), shape((C, 24, B), F32)) + (blocks,) * 4,
        [
            SMEM, SMEM, whole(C, L), whole(2, N, B), whole(mp, 3 * C, nt), chan(N, B),
            pl.BlockSpec(memory_space=pltpu.HBM), chan(B, 2 * B), whole(2, C, B),
        ],
        (whole(C, L), whole(2, N, B), chan(24, B)) + (chan(N, B),) * 4,
        7,
        [
            vm((N * C, B), F32), vm((N * C, B), F32), vm((N * C, B), F32), vm((3, N, B), F32),
            vm((G, 2 * N, B), BF16), vm((G * N, B), F32), vm((G * N, B), F32), vm((G * N, B), F32),
            vm((C, 2 * B, 4 * B), BF16), pltpu.SemaphoreType.DMA((C // G,)),
        ],
        large,
    )(lengths, vecs, tokens, stat, gm, pin(slope), pin(back_tab), pin(near_tab), jump)

    for k, offs in enumerate(rounds[::-1]):
        got = [exchange(sums, "mp", mp, o) for o in offs]
        if k == len(rounds) - 1:
            g_pre, sums = lax.optimization_barrier((g_pre, sums))
            rows = by_channel(
                sums_kernel,
                shape((C, 40, B), F32),
                [chan(3 * N, 2 * B)] + [chan(N, B)] * 7 + [chan(B, 2 * B), whole(2, C, B)],
                chan(40, B),
                20,
                [],
            )(pin(u_rev), pin(lift), g_pre, p_blk, r_blk, rx_blk, pin(state), pin(state_x), pin(near_tab), jump)
            *got, rows = lax.optimization_barrier((*got, rows))
        sums = sum(got, sums)
    grad_tokens = call(partial(last_kernel, count=H), shape((C, L), F32), 5)(tokens, grad_out, gn, stat, sums)
    layer_out = call(gather_kernel, shape((C, L), BF16), 1)(gm)
    rows = call(join_kernel, shape((9, C, B), F32), 2)(plain, rows)
    others = sum_docs(rows, dp, 1) - rows if dp > 2 else partner(rows, dp)

    seen = ways
    terms[0], plain = lax.optimization_barrier((terms[0], plain))
    for offs in rounds[1:]:
        ways = len(offs) + 1
        rows_left //= ways
        outs = call(
            partial(fold_kernel, ways=ways, got=len(terms), C=C, seen=seen),
            (shape((rows_left * C + 8, H), F32),) * ways,
            1 + len(terms), 1, 1, [vm((ways, rows_left * C + 8, H), F32)],
        )(place, *terms)
        terms = [outs[0]] + [exchange(v, "mp", mp, o) for v, o in zip(outs[1:], offs)]
        seen *= ways
    wsum = call(total_kernel, shape((C + 8, H), F32), len(terms))(*terms)
    wsum = sum_docs(wsum, dp, 2)
    across = partner(wsum, dp)
    thin, wide = shape((C, M), F32), shape((C, 2 * M), F32)
    line = shape((1, C), F32)
    (
        value_wgrad, gate_wgrad, vb, gb, step_grad, decay_grad, frequency_grad, readout_grad, liquid_grad,
        skip_grad, gain_grad, bias_grad,
    ) = call(
        partial(finish_kernel, M=M),
        (shape((C, H), F32), shape((C, H), F32), line, line, line, thin, thin, wide, wide, line, line, line),
        11, 1,
    )(
        place, rows, others, w_all, log_step[None], decay_log, frequency, readout, liquid_readout, wsum, across,
    )
    return (
        layer_out, grad_tokens, gain_grad[0], bias_grad[0], step_grad[0], decay_grad, frequency_grad, readout_grad,
        liquid_grad, skip_grad[0], value_wgrad.T, gate_wgrad.T, vb[0], gb[0],
    )


def solution(mesh):
    row, col, act = P("mp"), P(None, "mp"), P("mp", "dp")
    wide = P("mp", None)
    in_specs = (act, P("dp"), row, row, row, wide, wide, wide, wide, row, col, col, row, row, act)
    out_specs = (act, act, row, row, row, wide, wide, wide, wide, row, col, col, row, row)
    return jax.shard_map(
        partial(per_device, mesh.shape["mp"], mesh.shape["dp"]),
        mesh=mesh, in_specs=in_specs, out_specs=out_specs, check_vma=False,
    )
```

time: 168 us -> 119 us (0.71)
  Pallas kernels: 64.3 us -> 47.9 us
  blocking collectives: 14.9 us -> 0 us
  local copies, waits for them, and re-layouts: 15.7 us -> 1.09 us
  starting transfers between devices: 32.6 us -> 44.7 us
  waiting for transfers between devices: 32.1 us -> 21.6 us
  other arithmetic: 5.72 us -> 0.98 us
    pallas_call x8 -> x15, Pallas kernels: 64.3 us -> 47.9 us  [the longest x1 7.68 us: per_device(): by_channel(partial(back_kernel, count=H), (shape((C, L), F32), shape((2,...]
    all_to_all x1 -> x0, blocking collectives: 14.9 us -> none  [per_device(): lax.all_to_all(mixed, 'mp', split_axis=0, concat_axis=0, tiled=True)]
    unnamed x44 -> x34, local copies, waits for them, and re-layouts: 11.6 us -> 0.69 us
    ppermute x12 -> x18, starting transfers between devices: 15.9 us -> 25.3 us  [exchange(): return lax.ppermute(v, axis, [(k, k ^ off) for k in range(size)])]
    ppermute x12 -> x18, waiting for transfers between devices: 18.5 us -> 9.15 us  [exchange(): return lax.ppermute(v, axis, [(k, k ^ off) for k in range(size)])]
    add_any x4 -> x0, other arithmetic: 3.03 us -> none  [the longest x2 1.37 us: mix(): re, im = (coeffs[:, :M], coeffs[:, M:])]
    all_to_all x1, starting transfers between devices: 3.57 us -> 5.69 us  [per_device(): gm = lax.all_to_all(gm, 'mp', split_axis=0, concat_axis=0, tiled=True)]
    all_to_all x1, starting transfers between devices: 3.89 us -> 5.8 us  [per_device(): lax.all_to_all(mixed, 'mp', split_axis=0, concat_axis=0, tiled=True)]
  transfers between devices with their start and end apart: 20 -> 26, of which waited for: 10 -> 7; matrix products, arithmetic and copies ran while one was open for 3% -> 0% of each run, Pallas kernels for 37% -> 35%
where the time goes in v2:
time: 119 us; the launch traced here: 118 us
  Pallas kernels  47.9 us (40%)
  starting transfers between devices  44.7 us (38%)
  waiting for transfers between devices  21.6 us (18%)
  between operations  1.65 us (1%)
    ppermute x18, starting transfers between devices, exchange(): return lax.ppermute(v, axis, [(k, k ^ off) for k in range(size)])  25.3 us
    all_to_all x1, waiting for transfers between devices, per_device(): gm = lax.all_to_all(gm, 'mp', split_axis=0, concat_axis=0, tiled=True)  9.76 us
    ppermute x18, waiting for transfers between devices, exchange(): return lax.ppermute(v, axis, [(k, k ^ off) for k in range(size)])  9.15 us
    pallas_call x1, Pallas kernels, per_device(): by_channel(partial(back_kernel, count=H), (shape((C, L), F32), shape((2,...  7.68 us
    pallas_call x1, Pallas kernels, per_device(): by_channel(partial(back_table_kernel, C=C, M=M), (far((C, 2 * B, 4 * B),...  7.15 us
    all_to_all x1, starting transfers between devices, per_device(): first = lax.all_to_all(pay, 'mp', split_axis=0, concat_axis=0, tiled=True)  7.08 us
    pallas_call x1, Pallas kernels, per_device(): by_channel(partial(table_kernel, C=C, M=M), (shape((C, 2 * B, 2 * B), BF1...  6.28 us
    pallas_call x1, Pallas kernels, per_device(): by_channel(partial(mixer_kernel, count=H, parts=len(parts)), (shape((mp,...  6.07 us
  transfers between devices with their start and end apart: 26, of which 7 were waited for; matrix products, arithmetic and copies ran while one was open for 0% of the time, Pallas kernels for 35%

profile of v2, /device:TPU:0, one launch (start us, length us, event | category | flops | bytes accessed | tf_op | source)
XLA Modules:
  0.0 117.9 jit_solution(11871896381613723419)
XLA Ops:
  1.5 2.7 %shard_map.254 = (f32[80,128]{1,0:T(8,128)S(1)}, bf16[16,128,256]{2,1,0:T(8,128)(2,1)}) custom-call(s32[2]{0:T(128)S(1)} %pad_add_fusion.place_ref.half_ref, f32[1,128]{1,0:T(1,128)S(1)} %fusion.4.bias_ref, bf16[32,4096]{1,0:T(8,128)(2,1)} %x_ref.7, bf16[32,4096]{1,0:T(8,128)(2,1)} %g_ref.1, bf16[32,512]{1,0:T(8,128)(2,1)} %bitcast.25, bf16[32,512]{1,0:T(8,128)(2,1)} %bitcast.26), custom_call_target="tpu_custom_call" | custom-call | flops 3000000000 | bytes 3000000 | tf_op jit(solution)/shard_map/pallas_call | solution.py:735
  4.2 4.1 %collective-permute-start.2 = (f32[80,128]{1,0:T(8,128)S(1)}, f32[80,128]{1,0:T(8,128)S(1)}, u32[]{:S(2)}, u32[]{:S(2)}) collective-permute-start(f32[80,128]{1,0:T(8,128)S(1)} %get-tuple-element.80), channel_id=1, source_target_pairs={{0,8},{1,9},{2,10},{3,11},{4,12},{5,13},{6,14},{7,15},{8,0},{9,1},... | collective-permute-start | bytes 122888 | tf_op jit(solution)/shard_map/ppermute | solution.py:637
  8.3 1.6 %collective-permute-start = (f32[80,128]{1,0:T(8,128)S(1)}, f32[80,128]{1,0:T(8,128)S(1)}, u32[]{:S(2)}, u32[]{:S(2)}) collective-permute-start(f32[80,128]{1,0:T(8,128)S(1)} %get-tuple-element.80), channel_id=1, source_target_pairs={{0,4},{1,5},{2,6},{3,7},{4,0},{5,1},{6,2},{7,3},{8,12},{9,13},{10,... | collective-permute-start | bytes 122888 | tf_op jit(solution)/shard_map/ppermute | solution.py:637
  9.9 7.1 %all-to-all-start = ((bf16[16,128,256]{2,1,0:T(8,128)(2,1)}), bf16[16,128,256]{2,1,0:T(8,128)(2,1)S(1)}, u32[]{:S(2)}, u32[]{:S(2)}) async-start(bf16[16,128,256]{2,1,0:T(8,128)(2,1)} %get-tuple-element.88), calls=%async_computation | async-start | bytes 2097152 | tf_op jit(solution)/shard_map/all_to_all | solution.py:746
  17.6 6.3 %shard_map.255 = (bf16[32,256,256]{2,1,0:T(8,128)(2,1)S(1)}, bf16[32,256,256]{2,1,0:T(8,128)(2,1)}, bf16[32,384,256]{2,1,0:T(8,128)(2,1)S(1)}, f32[2,32,128]{2,1,0:T(8,128)S(1)}, f32[32,128]{1,0:T(8,128)S(1)}) custom-call(f32[3,32,128]{2,1,0:T(8,128)S(1)} %pad_maximum_fusion.rates_ref, f32[32,128]{1,0:T(8,128)S(1)} %pad_maximum_fusion.2.coef_ref), custom_call_target="tpu_custom_call" | custom-call | flops 6000000000 | bytes 6000000 | tf_op jit(solution)/shard_map/pallas_call | solution.py:752
  23.9 2.0 %collective-permute-start.3 = (f32[80,128]{1,0:T(8,128)S(1)}, f32[80,128]{1,0:T(8,128)S(1)}, u32[]{:S(2)}, u32[]{:S(2)}) collective-permute-start(f32[80,128]{1,0:T(8,128)S(1)} %pad_maximum_fusion.1.refs_0_), channel_id=1, source_target_pairs={{0,1},{1,0},{2,3},{3,2},{4,5},{5,4},{6,7},{7,6},{8,9},{9,8},{10,11... | collective-permute-start | bytes 122888 | tf_op jit(solution)/shard_map/ppermute | solution.py:637
  28.1 2.9 %collective-permute-done.3.refs_1_ = f32[80,128]{1,0:T(8,128)S(1)} collective-permute-done((f32[80,128]{1,0:T(8,128)S(1)}, f32[80,128]{1,0:T(8,128)S(1)}, u32[]{:S(2)}, u32[]{:S(2)}) %collective-permute-start.3) | collective-permute-done | bytes 40992 | tf_op jit(solution)/shard_map/ppermute | solution.py:637
  31.0 1.7 %collective-permute-done.5.refs_3_ = f32[80,128]{1,0:T(8,128)S(1)} collective-permute-done((f32[80,128]{1,0:T(8,128)S(1)}, f32[80,128]{1,0:T(8,128)S(1)}, u32[]{:S(2)}, u32[]{:S(2)}) %collective-permute-start.5) | collective-permute-done | bytes 40992 | tf_op jit(solution)/shard_map/ppermute | solution.py:637
  32.7 6.1 %shard_map.256 = (bf16[16,32,256]{2,1,0:T(8,128)(2,1)}, f32[32,32,128]{2,1,0:T(8,128)}, f32[32,32,128]{2,1,0:T(8,128)}, f32[32,32,128]{2,1,0:T(8,128)}, f32[2,32...) custom-call(s32[1]{0:T(128)S(6)} %copy.29.len_ref, f32[3,32]{1,0:T(4,128)S(1)} %pad_maximum_fusion.3.vec_ref, ...), custom_call_target="tpu_custom_call" | custom-call | flops 6000000000 | bytes 6000000 | tf_op jit(solution)/shard_map/pallas_call | solution.py:774
  40.6 5.8 %all-to-all-start.1 = ((bf16[16,32,256]{2,1,0:T(8,128)(2,1)}), bf16[16,32,256]{2,1,0:T(8,128)(2,1)S(1)}, u32[]{:S(2)}, u32[]{:S(2)}) async-start(bf16[16,32,256]{2,1,0:T(8,128)(2,1)} %get-tuple-element.89), calls=%async_computation.1 | async-start | bytes 524288 | tf_op jit(solution)/shard_map/all_to_all | solution.py:789
  46.6 7.2 %shard_map.257 = (bf16[32,256,512]{2,1,0:T(8,128)(2,1)}, bf16[32,128,256]{2,1,0:T(8,128)(2,1)}) custom-call(f32[3,32,128]{2,1,0:T(8,128)S(1)} %pad_maximum_fusion.rates_ref, f32[32,128]{1,0:T(8,128)S(1)} %get-tuple-element.91.w_ref), custom_call_target="tpu_custom_call" | custom-call | flops 7000000000 | bytes 7000000 | tf_op jit(solution)/shard_map/pallas_call | solution.py:790
  54.9 2.4 %shard_map.258 = (bf16[16,96,256]{2,1,0:T(8,128)(2,1)}, bf16[512,256]{1,0:T(8,128)(2,1)S(1)}, bf16[512,256]{1,0:T(8,128)(2,1)S(1)}) custom-call(s32[2]{0:T(128)S(1)} %pad_add_fusion.place_ref.half_ref, bf16[16,32,256]{2,1,0:T(8,128)(2,1)S(1)} %all-to-all-done.1.in_ref, bf16[16,128,256]{2,1,0:T(8,128)(2,1)S(1)} %all-to-all-done.first_ref, ...), custom_call_target="tpu_custom_call" | custom-call | flops 2000000000 | bytes 2000000 | tf_op jit(solution)/shard_map/pallas_call | solution.py:799
  57.3 5.7 %all-to-all-start.2 = ((bf16[16,96,256]{2,1,0:T(8,128)(2,1)}), bf16[16,96,256]{2,1,0:T(8,128)(2,1)S(1)}, u32[]{:S(2)}, u32[]{:S(2)}) async-start(bf16[16,96,256]{2,1,0:T(8,128)(2,1)} %get-tuple-element.98), calls=%async_computation.2 | async-start | bytes 1572864 | tf_op jit(solution)/shard_map/all_to_all | solution.py:806
  63.6 5.0 %shard_map.259 = (bf16[32,96,256]{2,1,0:T(8,128)(2,1)}, f32[32,32,128]{2,1,0:T(8,128)}) custom-call(s32[1]{0:T(128)S(6)} %copy.29.len_ref, f32[3,32]{1,0:T(4,128)} %copy-done.4, bf16[32,4096]{1,0:T(8,128)(2,1)} %x_ref.7, f32[2,32,128]{2,1,0:T(8,128)} %copy-done.12, bf16[32,256,256]{2,1,0:T(8,128)(2,1)} %get-tuple-element.100.f_ref), custom_call_target="tpu_custom_call" | custom-call | flops 3000000000 | bytes 3000000 | tf_op jit(solution)/shard_map/pallas_call | solution.py:807
  69.8 1.9 %collective-permute-start.16 = (f32[136,512]{1,0:T(8,128)S(1)}, f32[136,512]{1,0:T(8,128)S(1)}, u32[]{:S(2)}, u32[]{:S(2)}) collective-permute-start(f32[136,512]{1,0:T(8,128)S(1)} %get-tuple-element.127), channel_id=1, source_target_pairs={{0,1},{1,0},{2,3},{3,2},{4,5},{5,4},{6,7},{7,6},{8,9},{9,8},{10,11... | collective-permute-start | bytes 835592 | tf_op jit(solution)/shard_map/ppermute | solution.py:637
  73.4 9.8 %all-to-all-done.2.pay_ref.gm_ref = bf16[16,96,256]{2,1,0:T(8,128)(2,1)S(1)} async-done(((bf16[16,96,256]{2,1,0:T(8,128)(2,1)}), bf16[16,96,256]{2,1,0:T(8,128)(2,1)S(1)}, u32[]{:S(2)}, u32[]{:S(2)}) %all-to-all-start.2) | async-done | bytes 786464 | tf_op jit(solution)/shard_map/all_to_all | solution.py:806
  83.1 7.7 %shard_map.261 = (f32[32,4096]{1,0:T(8,128)S(1)}, f32[2,32,128]{2,1,0:T(8,128)S(1)}, f32[32,24,128]{2,1,0:T(8,128)S(1)}, f32[32,32,128]{2,1,0:T(8,128)S(1)}, f32...) custom-call(s32[1]{0:T(128)S(6)} %copy.29.len_ref, f32[3,32]{1,0:T(4,128)S(1)} %copy-done.5, ...), custom_call_target="tpu_custom_call" | custom-call | flops 7000000000 | bytes 7000000 | tf_op jit(solution)/shard_map/pallas_call | solution.py:826
  90.8 2.6 %collective-permute-start.9 = (f32[2,32,128]{2,1,0:T(8,128)S(1)}, f32[2,32,128]{2,1,0:T(8,128)S(1)}, u32[]{:S(2)}, u32[]{:S(2)}) collective-permute-start(f32[2,32,128]{2,1,0:T(8,128)S(1)} %get-tuple-element.108), channel_id=1, source_target_pairs={{0,12},{1,13},{2,14},{3,15},{4,8},{5,9},{6,10},{7,11},{8,4},{9,5},... | collective-permute-start | bytes 98312 | tf_op jit(solution)/shard_map/ppermute | solution.py:637
  93.4 1.5 %collective-permute-start.8 = (f32[2,32,128]{2,1,0:T(8,128)S(1)}, f32[2,32,128]{2,1,0:T(8,128)S(1)}, u32[]{:S(2)}, u32[]{:S(2)}) collective-permute-start(f32[2,32,128]{2,1,0:T(8,128)S(1)} %get-tuple-element.108), channel_id=1, source_target_pairs={{0,8},{1,9},{2,10},{3,11},{4,12},{5,13},{6,14},{7,15},{8,0},{9,1},... | collective-permute-start | bytes 98312 | tf_op jit(solution)/shard_map/ppermute | solution.py:637
  96.7 1.7 %collective-permute-start.19 = (f32[40,512]{1,0:T(8,128)S(1)}, f32[40,512]{1,0:T(8,128)S(1)}, u32[]{:S(2)}, u32[]{:S(2)}) collective-permute-start(f32[40,512]{1,0:T(8,128)S(1)} %get-tuple-element.131), channel_id=1, source_target_pairs={{0,4},{1,5},{2,6},{3,7},{4,0},{5,1},{6,2},{7,3},{8,12},{9,13},{10,... | collective-permute-start | bytes 245768 | tf_op jit(solution)/shard_map/ppermute | solution.py:637
  101.1 1.5 %collective-permute-start.11 = (f32[2,32,128]{2,1,0:T(8,128)S(1)}, f32[2,32,128]{2,1,0:T(8,128)S(1)}, u32[]{:S(2)}, u32[]{:S(2)}) collective-permute-start(f32[2,32,128]{2,1,0:T(8,128)S(1)} %add_add_fusion.1), channel_id=1, source_target_pairs={{0,2},{1,3},{2,0},{3,1},{4,6},{5,7},{6,4},{7,5},{8,10},{9,11},{10,... | collective-permute-start | bytes 98312 | tf_op jit(solution)/shard_map/ppermute | solution.py:637
  103.4 5.0 %shard_map.262.ref = f32[32,40,128]{2,1,0:T(8,128)S(1)} custom-call(bf16[32,96,256]{2,1,0:T(8,128)(2,1)} %get-tuple-element.110.u_ref, f32[32,32,128]{2,1,0:T(8,128)} %get-tuple-element.111.lift_ref, f32[32,32,128]{2,1,0:T(8,128)S(1)} %get-tuple-element.112.g_ref, f32[32,32,128]{2,1,0:T(8,128)S(1)} %get-tuple-element.113.p_ref, ...), custom_call_target="tpu_custom_call" | custom-call | flops 20000000000 | bytes 20000000 | tf_op jit(solution)/shard_map/pallas_call | solution.py:847
  110.2 4.6 %collective-permute-done.21.refs_3_ = f32[40,512]{1,0:T(8,128)S(1)} collective-permute-done((f32[40,512]{1,0:T(8,128)S(1)}, f32[40,512]{1,0:T(8,128)S(1)}, u32[]{:S(2)}, u32[]{:S(2)}) %collective-permute-start.21) | collective-permute-done | bytes 81952 | tf_op jit(solution)/shard_map/ppermute | solution.py:637
  116.1 1.8 %shard_map.268 = (f32[32,512]{1,0:T(8,128)}, f32[32,512]{1,0:T(8,128)}, f32[1,32]{1,0:T(1,128)}, f32[1,32]{1,0:T(1,128)}, f32[1,32]{1,0:T(1,128)}, /*index=5*/f3...) custom-call(s32[2]{0:T(128)S(1)} %pad_add_fusion.place_ref.half_ref,, ...), custom_call_target="tpu_custom_call" | custom-call | flops 1000000000 | bytes 1000000 | tf_op jit(solution)/shard_map/pallas_call | solution.py:882
  (94 shorter events, 17.8 us)
Async XLA Ops:
  4.2 19.6 %collective-permute-start.2 = (f32[80,128]{1,0:T(8,128)S(1)}, f32[80,128]{1,0:T(8,128)S(1)}, u32[]{:S(2)}, u32[]{:S(2)}) collective-permute-start(f32[80,128]{1,0:T(8,128)S(1)} %get-tuple-element.80), channel_id=1, source_target_pairs={{0,8},{1,9},{2,10},{3,11},{4,12},{5,13},{6,14},{7,15},{8,0},{9,1},... | collective-permute-start | bytes 122888 | tf_op jit(solution)/shard_map/ppermute | solution.py:637
  8.3 15.5 %collective-permute-start = (f32[80,128]{1,0:T(8,128)S(1)}, f32[80,128]{1,0:T(8,128)S(1)}, u32[]{:S(2)}, u32[]{:S(2)}) collective-permute-start(f32[80,128]{1,0:T(8,128)S(1)} %get-tuple-element.80), channel_id=1, source_target_pairs={{0,4},{1,5},{2,6},{3,7},{4,0},{5,1},{6,2},{7,3},{8,12},{9,13},{10,... | collective-permute-start | bytes 122888 | tf_op jit(solution)/shard_map/ppermute | solution.py:637
  9.9 13.9 %collective-permute-start.1 = (f32[80,128]{1,0:T(8,128)S(1)}, f32[80,128]{1,0:T(8,128)S(1)}, u32[]{:S(2)}, u32[]{:S(2)}) collective-permute-start(f32[80,128]{1,0:T(8,128)S(1)} %get-tuple-element.80), channel_id=1, source_target_pairs={{0,12},{1,13},{2,14},{3,15},{4,8},{5,9},{6,10},{7,11},{8,4},{9,5},... | collective-permute-start | bytes 122888 | tf_op jit(solution)/shard_map/ppermute | solution.py:637
  9.9 30.7 %all-to-all-start = ((bf16[16,128,256]{2,1,0:T(8,128)(2,1)}), bf16[16,128,256]{2,1,0:T(8,128)(2,1)S(1)}, u32[]{:S(2)}, u32[]{:S(2)}) async-start(bf16[16,128,256]{2,1,0:T(8,128)(2,1)} %get-tuple-element.88), calls=%async_computation | async-start | bytes 2097152 | tf_op jit(solution)/shard_map/all_to_all | solution.py:746
  23.9 7.1 %collective-permute-start.3 = (f32[80,128]{1,0:T(8,128)S(1)}, f32[80,128]{1,0:T(8,128)S(1)}, u32[]{:S(2)}, u32[]{:S(2)}) collective-permute-start(f32[80,128]{1,0:T(8,128)S(1)} %pad_maximum_fusion.1.refs_0_), channel_id=1, source_target_pairs={{0,1},{1,0},{2,3},{3,2},{4,5},{5,4},{6,7},{7,6},{8,9},{9,8},{10,11... | collective-permute-start | bytes 122888 | tf_op jit(solution)/shard_map/ppermute | solution.py:637
  25.9 5.1 %collective-permute-start.4 = (f32[80,128]{1,0:T(8,128)S(1)}, f32[80,128]{1,0:T(8,128)S(1)}, u32[]{:S(2)}, u32[]{:S(2)}) collective-permute-start(f32[80,128]{1,0:T(8,128)S(1)} %pad_maximum_fusion.1.refs_0_), channel_id=1, source_target_pairs={{0,2},{1,3},{2,0},{3,1},{4,6},{5,7},{6,4},{7,5},{8,10},{9,11},{10,... | collective-permute-start | bytes 122888 | tf_op jit(solution)/shard_map/ppermute | solution.py:637
  27.3 5.3 %collective-permute-start.5 = (f32[80,128]{1,0:T(8,128)S(1)}, f32[80,128]{1,0:T(8,128)S(1)}, u32[]{:S(2)}, u32[]{:S(2)}) collective-permute-start(f32[80,128]{1,0:T(8,128)S(1)} %pad_maximum_fusion.1.refs_0_), channel_id=1, source_target_pairs={{0,3},{1,2},{2,1},{3,0},{4,7},{5,6},{6,5},{7,4},{8,11},{9,10},{10,... | collective-permute-start | bytes 122888 | tf_op jit(solution)/shard_map/ppermute | solution.py:637
  40.6 14.3 %all-to-all-start.1 = ((bf16[16,32,256]{2,1,0:T(8,128)(2,1)}), bf16[16,32,256]{2,1,0:T(8,128)(2,1)S(1)}, u32[]{:S(2)}, u32[]{:S(2)}) async-start(bf16[16,32,256]{2,1,0:T(8,128)(2,1)} %get-tuple-element.89), calls=%async_computation.1 | async-start | bytes 524288 | tf_op jit(solution)/shard_map/all_to_all | solution.py:789
  46.5 8.5 %collective-permute-start.6 = (bf16[16,64,256]{2,1,0:T(8,128)(2,1)S(1)}, bf16[16,64,256]{2,1,0:T(8,128)(2,1)S(1)}, u32[]{:S(2)}, u32[]{:S(2)}) collective-permute-start(bf16[16,64,256]{2,1,0:T(8,128)(2,1)S(1)} %slice.75), channel_id=1, source_target_pairs={{0,16},{16,0},{1,17},{17,1},{2,18},{18,2},{3,19},{19,3},{4,20},{20... | collective-permute-start | bytes 1572872 | tf_op jit(solution)/shard_map/ppermute | solution.py:654
  57.3 25.8 %all-to-all-start.2 = ((bf16[16,96,256]{2,1,0:T(8,128)(2,1)}), bf16[16,96,256]{2,1,0:T(8,128)(2,1)S(1)}, u32[]{:S(2)}, u32[]{:S(2)}) async-start(bf16[16,96,256]{2,1,0:T(8,128)(2,1)} %get-tuple-element.98), calls=%async_computation.2 | async-start | bytes 1572864 | tf_op jit(solution)/shard_map/all_to_all | solution.py:806
  63.0 5.6 %collective-permute-start.15 = (bf16[512,256]{1,0:T(8,128)(2,1)S(1)}, bf16[512,256]{1,0:T(8,128)(2,1)S(1)}, u32[]{:S(2)}, u32[]{:S(2)}) collective-permute-start(bf16[512,256]{1,0:T(8,128)(2,1)S(1)} %bitcast.19), channel_id=1, source_target_pairs={{0,16},{16,0},{1,17},{17,1},{2,18},{18,2},{3,19},{19,3},{4,20},{20... | collective-permute-start | bytes 786440 | tf_op jit(solution)/shard_map/ppermute | solution.py:654
  63.3 5.3 %collective-permute-start.14 = (bf16[512,256]{1,0:T(8,128)(2,1)S(1)}, bf16[512,256]{1,0:T(8,128)(2,1)S(1)}, u32[]{:S(2)}, u32[]{:S(2)}) collective-permute-start(bf16[512,256]{1,0:T(8,128)(2,1)S(1)} %get-tuple-element.124), channel_id=1, source_target_pairs={{0,16},{16,0},{1,17},{17,1},{2,18},{18,2},{3,19},{19,3},{4,20},{20... | collective-permute-start | bytes 786440 | tf_op jit(solution)/shard_map/ppermute | solution.py:654
  69.8 25.8 %collective-permute-start.16 = (f32[136,512]{1,0:T(8,128)S(1)}, f32[136,512]{1,0:T(8,128)S(1)}, u32[]{:S(2)}, u32[]{:S(2)}) collective-permute-start(f32[136,512]{1,0:T(8,128)S(1)} %get-tuple-element.127), channel_id=1, source_target_pairs={{0,1},{1,0},{2,3},{3,2},{4,5},{5,4},{6,7},{7,6},{8,9},{9,8},{10,11... | collective-permute-start | bytes 835592 | tf_op jit(solution)/shard_map/ppermute | solution.py:637
  71.7 24.3 %collective-permute-start.17 = (f32[136,512]{1,0:T(8,128)S(1)}, f32[136,512]{1,0:T(8,128)S(1)}, u32[]{:S(2)}, u32[]{:S(2)}) collective-permute-start(f32[136,512]{1,0:T(8,128)S(1)} %get-tuple-element.128), channel_id=1, source_target_pairs={{0,2},{1,3},{2,0},{3,1},{4,6},{5,7},{6,4},{7,5},{8,10},{9,11},{10,... | collective-permute-start | bytes 835592 | tf_op jit(solution)/shard_map/ppermute | solution.py:637
  73.2 22.8 %collective-permute-start.18 = (f32[136,512]{1,0:T(8,128)S(1)}, f32[136,512]{1,0:T(8,128)S(1)}, u32[]{:S(2)}, u32[]{:S(2)}) collective-permute-start(f32[136,512]{1,0:T(8,128)S(1)} %get-tuple-element.129), channel_id=1, source_target_pairs={{0,3},{1,2},{2,1},{3,0},{4,7},{5,6},{6,5},{7,4},{8,11},{9,10},{10,... | collective-permute-start | bytes 835592 | tf_op jit(solution)/shard_map/ppermute | solution.py:637
  90.8 9.0 %collective-permute-start.9 = (f32[2,32,128]{2,1,0:T(8,128)S(1)}, f32[2,32,128]{2,1,0:T(8,128)S(1)}, u32[]{:S(2)}, u32[]{:S(2)}) collective-permute-start(f32[2,32,128]{2,1,0:T(8,128)S(1)} %get-tuple-element.108), channel_id=1, source_target_pairs={{0,12},{1,13},{2,14},{3,15},{4,8},{5,9},{6,10},{7,11},{8,4},{9,5},... | collective-permute-start | bytes 98312 | tf_op jit(solution)/shard_map/ppermute | solution.py:637
  93.4 6.4 %collective-permute-start.8 = (f32[2,32,128]{2,1,0:T(8,128)S(1)}, f32[2,32,128]{2,1,0:T(8,128)S(1)}, u32[]{:S(2)}, u32[]{:S(2)}) collective-permute-start(f32[2,32,128]{2,1,0:T(8,128)S(1)} %get-tuple-element.108), channel_id=1, source_target_pairs={{0,8},{1,9},{2,10},{3,11},{4,12},{5,13},{6,14},{7,15},{8,0},{9,1},... | collective-permute-start | bytes 98312 | tf_op jit(solution)/shard_map/ppermute | solution.py:637
  96.7 13.5 %collective-permute-start.19 = (f32[40,512]{1,0:T(8,128)S(1)}, f32[40,512]{1,0:T(8,128)S(1)}, u32[]{:S(2)}, u32[]{:S(2)}) collective-permute-start(f32[40,512]{1,0:T(8,128)S(1)} %get-tuple-element.131), channel_id=1, source_target_pairs={{0,4},{1,5},{2,6},{3,7},{4,0},{5,1},{6,2},{7,3},{8,12},{9,13},{10,... | collective-permute-start | bytes 245768 | tf_op jit(solution)/shard_map/ppermute | solution.py:637
  98.4 11.8 %collective-permute-start.20 = (f32[40,512]{1,0:T(8,128)S(1)}, f32[40,512]{1,0:T(8,128)S(1)}, u32[]{:S(2)}, u32[]{:S(2)}) collective-permute-start(f32[40,512]{1,0:T(8,128)S(1)} %get-tuple-element.132), channel_id=1, source_target_pairs={{0,8},{1,9},{2,10},{3,11},{4,12},{5,13},{6,14},{7,15},{8,0},{9,1},... | collective-permute-start | bytes 245768 | tf_op jit(solution)/shard_map/ppermute | solution.py:637
  99.8 8.6 %collective-permute-start.10 = (f32[2,32,128]{2,1,0:T(8,128)S(1)}, f32[2,32,128]{2,1,0:T(8,128)S(1)}, u32[]{:S(2)}, u32[]{:S(2)}) collective-permute-start(f32[2,32,128]{2,1,0:T(8,128)S(1)} %add_add_fusion.1), channel_id=1, source_target_pairs={{0,1},{1,0},{2,3},{3,2},{4,5},{5,4},{6,7},{7,6},{8,9},{9,8},{10,11... | collective-permute-start | bytes 98312 | tf_op jit(solution)/shard_map/ppermute | solution.py:637
  101.1 8.7 %collective-permute-start.11 = (f32[2,32,128]{2,1,0:T(8,128)S(1)}, f32[2,32,128]{2,1,0:T(8,128)S(1)}, u32[]{:S(2)}, u32[]{:S(2)}) collective-permute-start(f32[2,32,128]{2,1,0:T(8,128)S(1)} %add_add_fusion.1), channel_id=1, source_target_pairs={{0,2},{1,3},{2,0},{3,1},{4,6},{5,7},{6,4},{7,5},{8,10},{9,11},{10,... | collective-permute-start | bytes 98312 | tf_op jit(solution)/shard_map/ppermute | solution.py:637
  102.6 7.2 %collective-permute-start.12 = (f32[2,32,128]{2,1,0:T(8,128)S(1)}, f32[2,32,128]{2,1,0:T(8,128)S(1)}, u32[]{:S(2)}, u32[]{:S(2)}) collective-permute-start(f32[2,32,128]{2,1,0:T(8,128)S(1)} %add_add_fusion.1), channel_id=1, source_target_pairs={{0,3},{1,2},{2,1},{3,0},{4,7},{5,6},{6,5},{7,4},{8,11},{9,10},{10,... | collective-permute-start | bytes 98312 | tf_op jit(solution)/shard_map/ppermute | solution.py:637
  108.4 6.3 %collective-permute-start.21 = (f32[40,512]{1,0:T(8,128)S(1)}, f32[40,512]{1,0:T(8,128)S(1)}, u32[]{:S(2)}, u32[]{:S(2)}) collective-permute-start(f32[40,512]{1,0:T(8,128)S(1)} %get-tuple-element.133), channel_id=1, source_target_pairs={{0,12},{1,13},{2,14},{3,15},{4,8},{5,9},{6,10},{7,11},{8,4},{9,5},... | collective-permute-start | bytes 245768 | tf_op jit(solution)/shard_map/ppermute | solution.py:637
  110.1 6.1 %collective-permute-start.13 = (f32[9,32,128]{2,1,0:T(8,128)S(1)}, f32[9,32,128]{2,1,0:T(8,128)S(1)}, u32[]{:S(2)}, u32[]{:S(2)}) collective-permute-start(f32[9,32,128]{2,1,0:T(8,128)S(1)} %shard_map.264.mine_ref), channel_id=1, source_target_pairs={{0,16},{16,0},{1,17},{17,1},{2,18},{18,2},{3,19},{19,3},{4,20},{20... | collective-permute-start | bytes 442376 | tf_op jit(solution)/shard_map/ppermute | solution.py:654
  (19 other events, 201.9 us)

commit v3 on v2

--- a/solution.py
+++ b/solution.py
@@ -9,7 +9,8 @@
 from jax.sharding import PartitionSpec as P
 
 B = 128
-G = 8
+TABLE_GROUP = 8
+MIXER_GROUP = 16
 F32 = jnp.float32
 BF16 = jnp.bfloat16
 NN = (((1,), (0,)), ((), ()))
@@ -79,6 +80,7 @@
 
 def scan_blocks(v_ref, out_ref, turned_ref, jump, N, backward):
     a_re, a_im = jump
+    G = v_ref.shape[0] // N
     s = jnp.zeros((G, B), F32)
     t = s
     for k in range(N):
@@ -89,19 +91,22 @@
         s, t = a_re * s + (a_im * t + v), a_re * t + (swap_halves(v) - a_im * s)
 
 
-def start_kernel(place_ref, bias_ref, x_hbm, g_hbm, v_hbm, w_hbm, stat_ref, pay_ref, x_ref, g_ref, wt_ref, sems):
+def start_kernel(
+    place_ref, x_hbm, g_hbm, v_hbm, w_hbm, vb_hbm, gb_hbm, stat_ref, pay_ref, x_ref, g_ref, wt_ref, vb_ref, gb_ref, sems,
+):
     C, L = x_ref.shape
     N = L // B
     mp, rows, nt = pay_ref.shape
     kh = rows // C - 2
-    moves = [pltpu.make_async_copy(x_hbm, x_ref, sems.at[0]), pltpu.make_async_copy(g_hbm, g_ref, sems.at[1])]
+    pairs = ((x_hbm, x_ref), (g_hbm, g_ref), (vb_hbm, vb_ref), (gb_hbm, gb_ref))
+    moves = [pltpu.make_async_copy(src, dst, sems.at[1 + k]) for k, (src, dst) in enumerate(pairs)]
     for move in moves:
         move.start()
     for half, ref in enumerate((v_hbm, w_hbm)):
 
         @pl.when(place_ref[0] == half)
         def _():
-            pltpu.make_async_copy(ref, wt_ref, sems.at[2]).start()
+            pltpu.make_async_copy(ref, wt_ref, sems.at[0]).start()
 
     moves[0].wait()
     for n in range(N):
@@ -111,13 +116,16 @@
         stat_ref[n : n + 1, :] = mean
         stat_ref[N + n : N + n + 1, :] = jnp.sum(dev * dev, axis=0, keepdims=True)
     own = row_iota((mp, B))
-    stat_ref[2 * N :, :] = jnp.where(own == place_ref[1], bias_ref[...], 0.0)
+    moves[2].wait()
+    moves[3].wait()
+    bias = jnp.concatenate([vb_ref[...].astype(F32), gb_ref[...].astype(F32), jnp.zeros((1, B - 2 * C), F32)], axis=1)
+    stat_ref[2 * N :, :] = jnp.where(own == place_ref[1], bias, 0.0)
     for j in range(mp):
         pay_ref[j, kh * C : (kh + 1) * C, :] = x_ref[:, j * nt : (j + 1) * nt]
     moves[1].wait()
     for j in range(mp):
         pay_ref[j, (kh + 1) * C :, :] = g_ref[:, j * nt : (j + 1) * nt]
-    pltpu.make_async_copy(v_hbm, wt_ref, sems.at[2]).wait()
+    pltpu.make_async_copy(v_hbm, wt_ref, sems.at[0]).wait()
     for j in range(mp):
         for q in range(kh):
             pay_ref[j, q * C : (q + 1) * C, :] = wt_ref[:, q * nt : (q + 1) * nt]
@@ -135,7 +143,7 @@
         cols[q] = jnp.concatenate([v, pad], axis=0).T
 
 
-def channel_waves(cols, i, M):
+def channel_waves(cols, i, M, G):
     back = (B - i * G) % B
     al = pltpu.roll(cols[0, 0:M, :], back, 1)
     om = pltpu.roll(cols[1, 0:M, :], back, 1)
@@ -162,6 +170,7 @@
 
 def table_kernel(rates_ref, coef_ref, f_ref, again_ref, t_ref, jump_ref, wout_ref, cols, *, C, M):
     i = pl.program_id(0)
+    G = f_ref.shape[0]
 
     @pl.when(i == 0)
     def _():
@@ -191,7 +200,7 @@
     lanes = lane_iota((B, B))
     odd = (lanes & M) == M
     every = range(G)
-    waves = channel_waves(cols, i, M)
+    waves = channel_waves(cols, i, M, G)
     feeds = [jnp.concatenate([f_re, f_re, f_im, f_im], axis=0).T for _, (f_re, f_im), _ in waves]
     kerns = []
     for j in every:
@@ -219,6 +228,7 @@
 
 def back_table_kernel(rates_ref, w_ref, t_ref, near_ref, cols, *, C, M):
     i = pl.program_id(0)
+    G = t_ref.shape[0]
 
     @pl.when(i == 0)
     def _():
@@ -229,7 +239,7 @@
     lanes = lane_iota((B, B))
     zero = jnp.zeros((M, B), BF16)
     every = range(G)
-    waves = channel_waves(cols, i, M)
+    waves = channel_waves(cols, i, M, G)
     turned = [jnp.concatenate([n_re, n_re, n_im, n_im], axis=0).T for (n_re, n_im), _, _ in waves]
     kerns, starts = [], []
     for j in every:
@@ -269,6 +279,7 @@
     mixed_ref, slope_ref, state_ref, other_ref, stat_ref, bias_ref = refs[3:9]
     xs, ms, tok, us, ups, sts, ots = refs[9:]
     i = pl.program_id(0)
+    G = f_ref.shape[0]
     C, L = x_ref.shape
     N = L // B
     nt = mixed_ref.shape[2]
@@ -391,23 +402,26 @@
 
 
 def back_kernel(
-    len_ref, vec_ref, x_ref, stat_ref, gm_ref, slope_ref, t_ref, near_ref, jump_ref,
-    gn_ref, sum_ref, row_ref, g_ref, p_ref, r_ref, turned_ref, xs, gs, ns, tok, hs, ps, rs, rts, tab, sem, *, count,
+    len_ref, vec_ref, x_ref, stat_ref, gm_ref, slope_hbm, t_ref, near_hbm, jump_ref,
+    layer_ref, gn_ref, sum_ref, row_ref, g_ref, p_ref, r_ref, turned_ref, xs, gs, ns, tok, hs, ps, rs, rts, tab, near_ref, slope_ref, sem, *, count,
 ):
     i = pl.program_id(0)
+    G = g_ref.shape[0]
     C, L = x_ref.shape
     N = L // B
     nt = gm_ref.shape[2]
     per = nt // B
 
-    def fetch(k):
+    def fetch(q, k):
+        src, dst = ((slope_hbm, slope_ref), (near_hbm, near_ref), (t_ref, tab))[q]
         at = pl.ds(k * G, G)
-        return pltpu.make_async_copy(t_ref.at[at], tab.at[at], sem.at[k])
+        return pltpu.make_async_copy(src.at[at], dst.at[at], sem.at[q, k])
 
     @pl.when(i == 0)
     def _():
         for k in range(C // G):
-            fetch(k).start()
+            for q in range(3):
+                fetch(q, k).start()
         for n in range(N):
             xs[n * C : (n + 1) * C, :] = x_ref[:, n * B : (n + 1) * B].astype(F32)
             at = slice((n % per) * B, (n % per + 1) * B)
@@ -417,15 +431,19 @@
         tok[1] = inv
         tok[2] = mask
         sum_ref[...] = jnp.zeros_like(sum_ref)
-
+        for m in range(gm_ref.shape[0]):
+            layer_ref[:, m * nt : (m + 1) * nt] = gm_ref[m, 2 * C :, :]
+
+    fetch(0, i).wait()
     for j in range(G):
         ci = i * G + j
-        g = gs[pl.ds(ci, N, stride=C), :] * slope_ref[j]
+        g = gs[pl.ds(ci, N, stride=C), :] * slope_ref[ci]
         g_ref[j] = g
         hi, lo = split(g)
         hs[j, 0:N, :] = hi
         hs[j, N:, :] = lo
-    z_all = [dot(hs[j], near_ref[j]) for j in range(G)]
+    fetch(1, i).wait()
+    z_all = [dot(hs[j], near_ref[i * G + j]) for j in range(G)]
     for j, z in enumerate(z_all):
         p = z[:N, :B] + (z[:N, B:] + z[N:, :B])
         p_ref[j] = p
@@ -438,7 +456,7 @@
         r_ref[j] = r
         turned_ref[j] = rts[j * N : (j + 1) * N, :]
         left.append(jnp.concatenate([hs[j], jnp.concatenate(split(r), axis=0)], axis=1))
-    fetch(i).wait()
+    fetch(2, i).wait()
     both_all = [dot(left[j], tab[i * G + j]) for j in range(G)]
     for j, both in enumerate(both_all):
         ci = i * G + j
@@ -464,6 +482,7 @@
 
 def lift_kernel(len_ref, vec_ref, x_ref, stat_ref, f_ref, u_ref, lift_ref, xs, tok, *, count):
     i = pl.program_id(0)
+    G = f_ref.shape[0]
     C, L = x_ref.shape
     N = L // B
 
@@ -496,6 +515,7 @@
 
 def sums_kernel(u_ref, lift_ref, g_ref, p_ref, r_ref, rx_ref, state_ref, sx_ref, near_ref, jump_ref, row_ref):
     i = pl.program_id(0)
+    G = g_ref.shape[0]
     _, N, _ = g_ref.shape
     place = lane_iota((N, B)).astype(F32)
     rows2, lanes2 = row_iota((B, B)), lane_iota((B, B))
@@ -607,13 +627,6 @@
         out_ref[:, at] = inv * (gn_ref[:, at] - first - normed * second) + g_ref[:, at].astype(F32)
 
 
-def gather_kernel(pay_ref, out_ref):
-    mp, _, nt = pay_ref.shape
-    C = out_ref.shape[0]
-    for s in range(mp):
-        out_ref[:, s * nt : (s + 1) * nt] = pay_ref[s, 2 * C :, :]
-
-
 def total_kernel(*refs):
     total = refs[0][...]
     for p in refs[1:-1]:
@@ -689,7 +702,7 @@
 
     place = jnp.stack([lax.axis_index("dp") & 1, lax.axis_index("mp")]).astype(jnp.int32)
     rounds = rounds_of(mp)
-    small, large = 16, 28
+    small, large = 16, 32
 
     def pin(v):
         return pltpu.with_memory_space_constraint(v, pltpu.HBM)
@@ -708,13 +721,13 @@
     def whole(*dims):
         return pl.BlockSpec(dims, lambda i: (0,) * len(dims))
 
-    def chan(*dims, at=0):
-        return pl.BlockSpec((G,) + dims, lambda i: (i + at,) + (0,) * len(dims))
-
-    def by_channel(kernel, out, in_specs, out_specs, us, scratch, mb=small, channels=C):
+    def chan_by(group):
+        return lambda *dims: pl.BlockSpec((group,) + dims, lambda i: (i,) + (0,) * len(dims))
+
+    def by_channel(kernel, out, in_specs, out_specs, us, scratch, mb=small, group=TABLE_GROUP):
         return pl.pallas_call(
             kernel,
-            grid=(channels // G,),
+            grid=(C // group,),
             out_shape=out,
             in_specs=in_specs,
             out_specs=out_specs,
@@ -724,25 +737,29 @@
         )
 
     vm = pltpu.VMEM
+    G = min(MIXER_GROUP, C)
+    chan, few = chan_by(G), chan_by(TABLE_GROUP)
     blocks = shape((C, N, B), F32)
     far = pltpu.HBM
     far_blocks = far((C, N, B), F32)
     def pin(v):
         return pltpu.with_memory_space_constraint(v, far)
 
-    bias = jnp.pad(jnp.concatenate([value_bias, gate_bias]).astype(F32)[None], ((0, 0), (0, B - 2 * C)))
     hbm = pl.BlockSpec(memory_space=pltpu.HBM)
     stat, pay = pl.pallas_call(
         start_kernel,
         out_shape=(shape((2 * N + mp, B), F32), shape((mp, (2 + kh) * C, nt), BF16)),
-        in_specs=[SMEM, VMEM, hbm, hbm, hbm, hbm],
+        in_specs=[SMEM] + [hbm] * 6,
         out_specs=(VMEM, VMEM),
         scratch_shapes=[
-            pltpu.VMEM((C, L), BF16), pltpu.VMEM((C, L), BF16), pltpu.VMEM((C, H), BF16), pltpu.SemaphoreType.DMA((3,)),
+            pltpu.VMEM((C, L), BF16), pltpu.VMEM((C, L), BF16), pltpu.VMEM((C, H), BF16),
+            pltpu.VMEM((1, C), BF16), pltpu.VMEM((1, C), BF16), pltpu.SemaphoreType.DMA((5,)),
         ],
         compiler_params=params(small),
         cost_estimate=cost(3),
-    )(place, bias, pin(tokens), pin(grad_out), pin(value_weight.T), pin(gate_weight.T))
+    )(
+        place, pin(tokens), pin(grad_out), pin(value_weight.T), pin(gate_weight.T), pin(value_bias[None]), pin(gate_bias[None])
+    )
     first = lax.all_to_all(pay, "mp", split_axis=0, concat_axis=0, tiled=True)
 
     rates = jnp.stack(
@@ -756,7 +773,7 @@
             shape((2, C, B), F32), shape((C, B), F32),
         ),
         [whole(3, C, B), whole(C, B)],
-        (chan(2 * B, 2 * B), chan(2 * B, 2 * B), chan(3 * B, 2 * B), whole(2, C, B), whole(C, B)),
+        (few(2 * B, 2 * B), few(2 * B, 2 * B), few(3 * B, 2 * B), whole(2, C, B), whole(C, B)),
         6,
         [vm((3, B, B), F32)],
     )(rates, coef)
@@ -782,6 +799,8 @@
             vm((N * C, B), F32), vm((N * C, B), F32), vm((3, N, B), F32), vm((G, 2 * N, 2 * B), BF16),
             vm((G * N, B), F32), vm((G * N, B), F32), vm((G * N, B), F32),
         ],
+        large,
+        G,
     )(lengths, vecs, tokens, *parts, f_near, t_tab, jump)
 
     mixed, first, rates = lax.optimization_barrier((mixed, first, rates))
@@ -791,7 +810,7 @@
         partial(back_table_kernel, C=C, M=M),
         (far((C, 2 * B, 4 * B), BF16), far((C, B, 2 * B), BF16)),
         [whole(3, C, B), whole(C, B)],
-        (chan(2 * B, 4 * B), chan(B, 2 * B)),
+        (few(2 * B, 4 * B), few(B, 2 * B)),
         7,
         [vm((3, B, B), F32)],
     )(rates, w_all)
@@ -807,8 +826,8 @@
     u_rev, lift = by_channel(
         partial(lift_kernel, count=H),
         (far((C, 3 * N, 2 * B), BF16), far_blocks),
-        [SMEM, SMEM, whole(C, L), whole(2, N, B), chan(2 * B, 2 * B)],
-        (chan(3 * N, 2 * B), chan(N, B)),
+        [SMEM, SMEM, whole(C, L), whole(2, N, B), few(2 * B, 2 * B)],
+        (few(3 * N, 2 * B), few(N, B)),
         3,
         [vm((N * C, B), F32), vm((3, N, B), F32)],
         56,
@@ -823,46 +842,28 @@
     )(place, keep, partner(send, dp), mixed_tok, partner(mixed_tok, dp))
     terms = [outs[0]] + [exchange(v, "mp", mp, o) for v, o in zip(outs[1:], rounds[0])]
 
-    gn, sums, plain, g_pre, p_blk, r_blk, rx_blk = by_channel(
+    layer_out, gn, sums, plain, g_pre, p_blk, r_blk, rx_blk = by_channel(
         partial(back_kernel, count=H),
-        (shape((C, L), F32), shape((2, N, B), F32), shape((C, 24, B), F32)) + (blocks,) * 4,
+        (shape((C, L), BF16), shape((C, L), F32), shape((2, N, B), F32), shape((C, 24, B), F32)) + (blocks,) * 4,
         [
-            SMEM, SMEM, whole(C, L), whole(2, N, B), whole(mp, 3 * C, nt), chan(N, B),
-            pl.BlockSpec(memory_space=pltpu.HBM), chan(B, 2 * B), whole(2, C, B),
+            SMEM, SMEM, VMEM, VMEM, VMEM, hbm, hbm, hbm, VMEM,
         ],
-        (whole(C, L), whole(2, N, B), chan(24, B)) + (chan(N, B),) * 4,
+        (whole(C, L), whole(C, L), whole(2, N, B), chan(24, B)) + (chan(N, B),) * 4,
         7,
         [
             vm((N * C, B), F32), vm((N * C, B), F32), vm((N * C, B), F32), vm((3, N, B), F32),
             vm((G, 2 * N, B), BF16), vm((G * N, B), F32), vm((G * N, B), F32), vm((G * N, B), F32),
-            vm((C, 2 * B, 4 * B), BF16), pltpu.SemaphoreType.DMA((C // G,)),
+            vm((C, 2 * B, 4 * B), BF16), vm((C, B, 2 * B), BF16), vm((C, N, B), F32),
+            pltpu.SemaphoreType.DMA((3, C // G)),
         ],
         large,
+        G,
     )(lengths, vecs, tokens, stat, gm, pin(slope), pin(back_tab), pin(near_tab), jump)
-
-    for k, offs in enumerate(rounds[::-1]):
-        got = [exchange(sums, "mp", mp, o) for o in offs]
-        if k == len(rounds) - 1:
-            g_pre, sums = lax.optimization_barrier((g_pre, sums))
-            rows = by_channel(
-                sums_kernel,
-                shape((C, 40, B), F32),
-                [chan(3 * N, 2 * B)] + [chan(N, B)] * 7 + [chan(B, 2 * B), whole(2, C, B)],
-                chan(40, B),
-                20,
-                [],
-            )(pin(u_rev), pin(lift), g_pre, p_blk, r_blk, rx_blk, pin(state), pin(state_x), pin(near_tab), jump)
-            *got, rows = lax.optimization_barrier((*got, rows))
-        sums = sum(got, sums)
-    grad_tokens = call(partial(last_kernel, count=H), shape((C, L), F32), 5)(tokens, grad_out, gn, stat, sums)
-    layer_out = call(gather_kernel, shape((C, L), BF16), 1)(gm)
-    rows = call(join_kernel, shape((9, C, B), F32), 2)(plain, rows)
-    others = sum_docs(rows, dp, 1) - rows if dp > 2 else partner(rows, dp)
 
     seen = ways
     terms[0], plain = lax.optimization_barrier((terms[0], plain))
-    for offs in rounds[1:]:
-        ways = len(offs) + 1
+    while seen < mp:
+        ways, offs = 2, (seen,)
         rows_left //= ways
         outs = call(
             partial(fold_kernel, ways=ways, got=len(terms), C=C, seen=seen),
@@ -871,6 +872,26 @@
         )(place, *terms)
         terms = [outs[0]] + [exchange(v, "mp", mp, o) for v, o in zip(outs[1:], offs)]
         seen *= ways
+    for k, offs in enumerate(rounds[::-1]):
+        got = [exchange(sums, "mp", mp, o) for o in offs]
+        if k == len(rounds) - 1:
+            g_pre, sums, terms[0] = lax.optimization_barrier((g_pre, sums, terms[0]))
+            rows = by_channel(
+                sums_kernel,
+                shape((C, 40, B), F32),
+                [chan(3 * N, 2 * B)] + [chan(N, B)] * 7 + [chan(B, 2 * B), whole(2, C, B)],
+                chan(40, B),
+                20,
+                [],
+                large,
+                G,
+            )(pin(u_rev), pin(lift), g_pre, p_blk, r_blk, rx_blk, pin(state), pin(state_x), pin(near_tab), jump)
+            got, rows, terms = lax.optimization_barrier((got, rows, terms))
+        sums = sum(got, sums)
+    grad_tokens = call(partial(last_kernel, count=H), shape((C, L), F32), 5)(tokens, grad_out, gn, stat, sums)
+    rows = call(join_kernel, shape((9, C, B), F32), 2)(plain, rows)
+    others = sum_docs(rows, dp, 1) - rows if dp > 2 else partner(rows, dp)
+
     wsum = call(total_kernel, shape((C + 8, H), F32), len(terms))(*terms)
     wsum = sum_docs(wsum, dp, 2)
     across = partner(wsum, dp)

time: 119 us -> 113 us (0.950)
  Pallas kernels: 47.9 us -> 45.6 us
  waiting for transfers between devices: 21.6 us -> 19.7 us
    ppermute x18 -> x17, waiting for transfers between devices: 9.15 us -> 6.62 us  [exchange(): return lax.ppermute(v, axis, [(k, k ^ off) for k in range(size)])]
    pallas_call x1, Pallas kernels: 5.01 us -> 3.78 us  [per_device(): by_channel(sums_kernel, shape((C, 40, B), F32), [chan(3 * N, 2 * B)] + [c...]
    ppermute x18 -> x17, starting transfers between devices: 25.3 us -> 24.1 us  [exchange(): return lax.ppermute(v, axis, [(k, k ^ off) for k in range(size)])]
    pallas_call x2 -> x1, Pallas kernels: 8.4 us -> 7.5 us  [per_device(): by_channel(partial(back_kernel, count=H), (shape((C, L), BF16), shape((C,...]
  transfers between devices with their start and end apart: 26 -> 25, of which waited for: 7 -> 8; matrix products, arithmetic and copies ran while one was open for 0% -> 0% of each run, Pallas kernels for 35% -> 34%
where the time goes in v3:
time: 113 us; the launch traced here: 112 us
  Pallas kernels  45.6 us (40%)
  starting transfers between devices  43.9 us (39%)
  waiting for transfers between devices  19.7 us (17%)
  between operations  1.75 us (2%)
    ppermute x17, starting transfers between devices, exchange(): return lax.ppermute(v, axis, [(k, k ^ off) for k in range(size)])  24.1 us
    all_to_all x1, waiting for transfers between devices, per_device(): gm = lax.all_to_all(gm, 'mp', split_axis=0, concat_axis=0, tiled=True)  9.74 us
    pallas_call x1, Pallas kernels, per_device(): by_channel(partial(back_kernel, count=H), (shape((C, L), BF16), shape((C,...  7.5 us
    pallas_call x1, Pallas kernels, per_device(): by_channel(partial(back_table_kernel, C=C, M=M), (far((C, 2 * B, 4 * B),...  7.15 us
    all_to_all x1, starting transfers between devices, per_device(): first = lax.all_to_all(pay, 'mp', split_axis=0, concat_axis=0, tiled=True)  7.08 us
    ppermute x17, waiting for transfers between devices, exchange(): return lax.ppermute(v, axis, [(k, k ^ off) for k in range(size)])  6.62 us
    pallas_call x1, Pallas kernels, per_device(): by_channel(partial(table_kernel, C=C, M=M), (shape((C, 2 * B, 2 * B), BF1...  6.28 us
    all_to_all x1, starting transfers between devices, per_device(): lax.all_to_all(mixed, 'mp', split_axis=0, concat_axis=0, tiled=True)  5.8 us
  transfers between devices with their start and end apart: 25, of which 8 were waited for; matrix products, arithmetic and copies ran while one was open for 0% of the time, Pallas kernels for 34%

profile of v3, /device:TPU:0, one launch (start us, length us, event | category | flops | bytes accessed | tf_op | source)
XLA Modules:
  0.0 112.3 jit_solution(3103346942543179551)
XLA Ops:
  0.7 2.8 %shard_map.254 = (f32[80,128]{1,0:T(8,128)S(1)}, bf16[16,128,256]{2,1,0:T(8,128)(2,1)}) custom-call(s32[2]{0:T(128)S(1)} %pad_add_fusion.place_ref.half_ref, bf16[32,4096]{1,0:T(8,128)(2,1)} %x_ref.7, bf16[32,4096]{1,0:T(8,128)(2,1)} %g_ref.1, bf16[32,512]{1,0:T(8,128)(2,1)} %bitcast.25, bf16[32,512]{1,0:T(8,128)(2,1)} %bitcast.26, bf16[1,32]{1,0:T(2,128)(2,1)} %bitcast.27, ...), custom_call_target="tpu_custom_call" | custom-call | flops 3000000000 | bytes 3000000 | tf_op jit(solution)/shard_map/pallas_call | solution.py:749
  3.6 4.1 %collective-permute-start.2 = (f32[80,128]{1,0:T(8,128)S(1)}, f32[80,128]{1,0:T(8,128)S(1)}, u32[]{:S(2)}, u32[]{:S(2)}) collective-permute-start(f32[80,128]{1,0:T(8,128)S(1)} %get-tuple-element.85), channel_id=1, source_target_pairs={{0,8},{1,9},{2,10},{3,11},{4,12},{5,13},{6,14},{7,15},{8,0},{9,1},... | collective-permute-start | bytes 122888 | tf_op jit(solution)/shard_map/ppermute | solution.py:650
  7.7 1.6 %collective-permute-start = (f32[80,128]{1,0:T(8,128)S(1)}, f32[80,128]{1,0:T(8,128)S(1)}, u32[]{:S(2)}, u32[]{:S(2)}) collective-permute-start(f32[80,128]{1,0:T(8,128)S(1)} %get-tuple-element.85), channel_id=1, source_target_pairs={{0,4},{1,5},{2,6},{3,7},{4,0},{5,1},{6,2},{7,3},{8,12},{9,13},{10,... | collective-permute-start | bytes 122888 | tf_op jit(solution)/shard_map/ppermute | solution.py:650
  9.3 7.1 %all-to-all-start = ((bf16[16,128,256]{2,1,0:T(8,128)(2,1)}), bf16[16,128,256]{2,1,0:T(8,128)(2,1)S(1)}, u32[]{:S(2)}, u32[]{:S(2)}) async-start(bf16[16,128,256]{2,1,0:T(8,128)(2,1)} %get-tuple-element.94), calls=%async_computation | async-start | bytes 2097152 | tf_op jit(solution)/shard_map/all_to_all | solution.py:763
  16.9 6.3 %shard_map.255 = (bf16[32,256,256]{2,1,0:T(8,128)(2,1)S(1)}, bf16[32,256,256]{2,1,0:T(8,128)(2,1)}, bf16[32,384,256]{2,1,0:T(8,128)(2,1)S(1)}, f32[2,32,128]{2,1,0:T(8,128)S(1)}, f32[32,128]{1,0:T(8,128)S(1)}) custom-call(f32[3,32,128]{2,1,0:T(8,128)S(1)} %pad_maximum_fusion.rates_ref, f32[32,128]{1,0:T(8,128)S(1)} %pad_maximum_fusion.2.coef_ref), custom_call_target="tpu_custom_call" | custom-call | flops 6000000000 | bytes 6000000 | tf_op jit(solution)/shard_map/pallas_call | solution.py:769
  23.3 2.0 %collective-permute-start.3 = (f32[80,128]{1,0:T(8,128)S(1)}, f32[80,128]{1,0:T(8,128)S(1)}, u32[]{:S(2)}, u32[]{:S(2)}) collective-permute-start(f32[80,128]{1,0:T(8,128)S(1)} %pad_maximum_fusion.1.refs_0_), channel_id=1, source_target_pairs={{0,1},{1,0},{2,3},{3,2},{4,5},{5,4},{6,7},{7,6},{8,9},{9,8},{10,11... | collective-permute-start | bytes 122888 | tf_op jit(solution)/shard_map/ppermute | solution.py:650
  27.5 2.9 %collective-permute-done.3.refs_1_ = f32[80,128]{1,0:T(8,128)S(1)} collective-permute-done((f32[80,128]{1,0:T(8,128)S(1)}, f32[80,128]{1,0:T(8,128)S(1)}, u32[]{:S(2)}, u32[]{:S(2)}) %collective-permute-start.3) | collective-permute-done | bytes 40992 | tf_op jit(solution)/shard_map/ppermute | solution.py:650
  30.4 1.7 %collective-permute-done.5.refs_3_ = f32[80,128]{1,0:T(8,128)S(1)} collective-permute-done((f32[80,128]{1,0:T(8,128)S(1)}, f32[80,128]{1,0:T(8,128)S(1)}, u32[]{:S(2)}, u32[]{:S(2)}) %collective-permute-start.5) | collective-permute-done | bytes 40992 | tf_op jit(solution)/shard_map/ppermute | solution.py:650
  32.1 5.2 %shard_map.256 = (bf16[16,32,256]{2,1,0:T(8,128)(2,1)}, f32[32,32,128]{2,1,0:T(8,128)}, f32[32,32,128]{2,1,0:T(8,128)}, f32[32,32,128]{2,1,0:T(8,128)}, f32[2,32...) custom-call(s32[1]{0:T(128)S(6)} %copy.29.len_ref, f32[3,32]{1,0:T(4,128)S(1)} %pad_maximum_fusion.3.vec_ref, ...), custom_call_target="tpu_custom_call" | custom-call | flops 6000000000 | bytes 6000000 | tf_op jit(solution)/shard_map/pallas_call | solution.py:791
  37.9 2.1 %all-to-all-done.first_ref = bf16[16,128,256]{2,1,0:T(8,128)(2,1)S(1)} async-done(((bf16[16,128,256]{2,1,0:T(8,128)(2,1)}), bf16[16,128,256]{2,1,0:T(8,128)(2,1)S(1)}, u32[]{:S(2)}, u32[]{:S(2)}) %all-to-all-start) | async-done | bytes 1048608 | tf_op jit(solution)/shard_map/all_to_all | solution.py:763
  40.0 5.8 %all-to-all-start.1 = ((bf16[16,32,256]{2,1,0:T(8,128)(2,1)}), bf16[16,32,256]{2,1,0:T(8,128)(2,1)S(1)}, u32[]{:S(2)}, u32[]{:S(2)}) async-start(bf16[16,32,256]{2,1,0:T(8,128)(2,1)} %get-tuple-element.95), calls=%async_computation.1 | async-start | bytes 524288 | tf_op jit(solution)/shard_map/all_to_all | solution.py:808
  45.9 7.2 %shard_map.257 = (bf16[32,256,512]{2,1,0:T(8,128)(2,1)}, bf16[32,128,256]{2,1,0:T(8,128)(2,1)}) custom-call(f32[3,32,128]{2,1,0:T(8,128)S(1)} %pad_maximum_fusion.rates_ref, f32[32,128]{1,0:T(8,128)S(1)} %get-tuple-element.97.w_ref), custom_call_target="tpu_custom_call" | custom-call | flops 7000000000 | bytes 7000000 | tf_op jit(solution)/shard_map/pallas_call | solution.py:809
  54.3 2.4 %shard_map.258 = (bf16[16,96,256]{2,1,0:T(8,128)(2,1)}, bf16[512,256]{1,0:T(8,128)(2,1)S(1)}, bf16[512,256]{1,0:T(8,128)(2,1)S(1)}) custom-call(s32[2]{0:T(128)S(1)} %pad_add_fusion.place_ref.half_ref, bf16[16,32,256]{2,1,0:T(8,128)(2,1)S(1)} %all-to-all-done.1.in_ref, bf16[16,128,256]{2,1,0:T(8,128)(2,1)S(1)} %all-to-all-done.first_ref, ...), custom_call_target="tpu_custom_call" | custom-call | flops 2000000000 | bytes 2000000 | tf_op jit(solution)/shard_map/pallas_call | solution.py:818
  56.7 5.7 %all-to-all-start.2 = ((bf16[16,96,256]{2,1,0:T(8,128)(2,1)}), bf16[16,96,256]{2,1,0:T(8,128)(2,1)S(1)}, u32[]{:S(2)}, u32[]{:S(2)}) async-start(bf16[16,96,256]{2,1,0:T(8,128)(2,1)} %get-tuple-element.104), calls=%async_computation.2 | async-start | bytes 1572864 | tf_op jit(solution)/shard_map/all_to_all | solution.py:825
  63.0 5.0 %shard_map.259 = (bf16[32,96,256]{2,1,0:T(8,128)(2,1)}, f32[32,32,128]{2,1,0:T(8,128)}) custom-call(s32[1]{0:T(128)S(6)} %copy.29.len_ref, f32[3,32]{1,0:T(4,128)} %copy-done.4, bf16[32,4096]{1,0:T(8,128)(2,1)} %x_ref.7, f32[2,32,128]{2,1,0:T(8,128)} %copy-done.12, bf16[32,256,256]{2,1,0:T(8,128)(2,1)} %get-tuple-element.105.f_ref), custom_call_target="tpu_custom_call" | custom-call | flops 3000000000 | bytes 3000000 | tf_op jit(solution)/shard_map/pallas_call | solution.py:826
  69.2 2.0 %collective-permute-start.12 = (f32[136,512]{1,0:T(8,128)S(1)}, f32[136,512]{1,0:T(8,128)S(1)}, u32[]{:S(2)}, u32[]{:S(2)}) collective-permute-start(f32[136,512]{1,0:T(8,128)S(1)} %get-tuple-element.120), channel_id=1, source_target_pairs={{0,1},{1,0},{2,3},{3,2},{4,5},{5,4},{6,7},{7,6},{8,9},{9,8},{10,11... | collective-permute-start | bytes 835592 | tf_op jit(solution)/shard_map/ppermute | solution.py:650
  72.7 9.7 %all-to-all-done.2.gm_ref = bf16[16,96,256]{2,1,0:T(8,128)(2,1)S(1)} async-done(((bf16[16,96,256]{2,1,0:T(8,128)(2,1)}), bf16[16,96,256]{2,1,0:T(8,128)(2,1)S(1)}, u32[]{:S(2)}, u32[]{:S(2)}) %all-to-all-start.2) | async-done | bytes 786464 | tf_op jit(solution)/shard_map/all_to_all | solution.py:825
  82.5 7.5 %shard_map.260 = (bf16[32,4096]{1,0:T(8,128)(2,1)}, f32[32,4096]{1,0:T(8,128)S(1)}, f32[2,32,128]{2,1,0:T(8,128)S(1)}, f32[32,24,128]{2,1,0:T(8,128)S(1)}, f32[3...) custom-call(s32[1]{0:T(128)S(6)} %copy.29.len_ref, ...), custom_call_target="tpu_custom_call" | custom-call | flops 7000000000 | bytes 7000000 | tf_op jit(solution)/shard_map/pallas_call | solution.py:845
  90.0 2.6 %collective-permute-start.9 = (f32[2,32,128]{2,1,0:T(8,128)S(1)}, f32[2,32,128]{2,1,0:T(8,128)S(1)}, u32[]{:S(2)}, u32[]{:S(2)}) collective-permute-start(f32[2,32,128]{2,1,0:T(8,128)S(1)} %get-tuple-element.114), channel_id=1, source_target_pairs={{0,12},{1,13},{2,14},{3,15},{4,8},{5,9},{6,10},{7,11},{8,4},{9,5},... | collective-permute-start | bytes 98312 | tf_op jit(solution)/shard_map/ppermute | solution.py:650
  95.1 1.7 %collective-permute-start.15 = (f32[72,512]{1,0:T(8,128)S(1)}, f32[72,512]{1,0:T(8,128)S(1)}, u32[]{:S(2)}, u32[]{:S(2)}) collective-permute-start(f32[72,512]{1,0:T(8,128)S(1)} %get-tuple-element.124), channel_id=1, source_target_pairs={{0,4},{1,5},{2,6},{3,7},{4,0},{5,1},{6,2},{7,3},{8,12},{9,13},{10,... | collective-permute-start | bytes 442376 | tf_op jit(solution)/shard_map/ppermute | solution.py:650
  98.8 1.7 %collective-permute-start.17 = (f32[2,32,128]{2,1,0:T(8,128)S(1)}, f32[2,32,128]{2,1,0:T(8,128)S(1)}, u32[]{:S(2)}, u32[]{:S(2)}) collective-permute-start(f32[2,32,128]{2,1,0:T(8,128)S(1)} %add_add_fusion.1), channel_id=1, source_target_pairs={{0,2},{1,3},{2,0},{3,1},{4,6},{5,7},{6,4},{7,5},{8,10},{9,11},{10,... | collective-permute-start | bytes 98312 | tf_op jit(solution)/shard_map/ppermute | solution.py:650
  102.2 1.6 %collective-permute-start.19 = (f32[40,512]{1,0:T(8,128)S(1)}, f32[40,512]{1,0:T(8,128)S(1)}, u32[]{:S(2)}, u32[]{:S(2)}) collective-permute-start(f32[40,512]{1,0:T(8,128)S(1)} %get-tuple-element.136), channel_id=1, source_target_pairs={{0,8},{1,9},{2,10},{3,11},{4,12},{5,13},{6,14},{7,15},{8,0},{9,1},... | collective-permute-start | bytes 245768 | tf_op jit(solution)/shard_map/ppermute | solution.py:650
  103.7 3.8 %shard_map.264.ref = f32[32,40,128]{2,1,0:T(8,128)S(1)} custom-call(bf16[32,96,256]{2,1,0:T(8,128)(2,1)} %get-tuple-element.127.u_ref, f32[32,32,128]{2,1,0:T(8,128)} %get-tuple-element.128.lift_ref, f32[32,32,128]{2,1,0:T(8,128)S(1)} %get-tuple-element.129.g_ref, f32[32,32,128]{2,1,0:T(8,128)S(1)} %get-tuple-element.130.p_ref, ...), custom_call_target="tpu_custom_call" | custom-call | flops 20000000000 | bytes 20000000 | tf_op jit(solution)/shard_map/pallas_call | solution.py:879
  110.4 1.8 %shard_map.268 = (f32[32,512]{1,0:T(8,128)}, f32[32,512]{1,0:T(8,128)}, f32[1,32]{1,0:T(1,128)}, f32[1,32]{1,0:T(1,128)}, f32[1,32]{1,0:T(1,128)}, /*index=5*/f3...) custom-call(s32[2]{0:T(128)S(1)} %pad_add_fusion.place_ref.half_ref,, ...), custom_call_target="tpu_custom_call" | custom-call | flops 1000000000 | bytes 1000000 | tf_op jit(solution)/shard_map/pallas_call | solution.py:903
  (91 shorter events, 16.3 us)
Async XLA Ops:
  3.6 19.6 %collective-permute-start.2 = (f32[80,128]{1,0:T(8,128)S(1)}, f32[80,128]{1,0:T(8,128)S(1)}, u32[]{:S(2)}, u32[]{:S(2)}) collective-permute-start(f32[80,128]{1,0:T(8,128)S(1)} %get-tuple-element.85), channel_id=1, source_target_pairs={{0,8},{1,9},{2,10},{3,11},{4,12},{5,13},{6,14},{7,15},{8,0},{9,1},... | collective-permute-start | bytes 122888 | tf_op jit(solution)/shard_map/ppermute | solution.py:650
  7.7 15.5 %collective-permute-start = (f32[80,128]{1,0:T(8,128)S(1)}, f32[80,128]{1,0:T(8,128)S(1)}, u32[]{:S(2)}, u32[]{:S(2)}) collective-permute-start(f32[80,128]{1,0:T(8,128)S(1)} %get-tuple-element.85), channel_id=1, source_target_pairs={{0,4},{1,5},{2,6},{3,7},{4,0},{5,1},{6,2},{7,3},{8,12},{9,13},{10,... | collective-permute-start | bytes 122888 | tf_op jit(solution)/shard_map/ppermute | solution.py:650
  9.3 13.9 %collective-permute-start.1 = (f32[80,128]{1,0:T(8,128)S(1)}, f32[80,128]{1,0:T(8,128)S(1)}, u32[]{:S(2)}, u32[]{:S(2)}) collective-permute-start(f32[80,128]{1,0:T(8,128)S(1)} %get-tuple-element.85), channel_id=1, source_target_pairs={{0,12},{1,13},{2,14},{3,15},{4,8},{5,9},{6,10},{7,11},{8,4},{9,5},... | collective-permute-start | bytes 122888 | tf_op jit(solution)/shard_map/ppermute | solution.py:650
  9.3 30.7 %all-to-all-start = ((bf16[16,128,256]{2,1,0:T(8,128)(2,1)}), bf16[16,128,256]{2,1,0:T(8,128)(2,1)S(1)}, u32[]{:S(2)}, u32[]{:S(2)}) async-start(bf16[16,128,256]{2,1,0:T(8,128)(2,1)} %get-tuple-element.94), calls=%async_computation | async-start | bytes 2097152 | tf_op jit(solution)/shard_map/all_to_all | solution.py:763
  23.3 7.1 %collective-permute-start.3 = (f32[80,128]{1,0:T(8,128)S(1)}, f32[80,128]{1,0:T(8,128)S(1)}, u32[]{:S(2)}, u32[]{:S(2)}) collective-permute-start(f32[80,128]{1,0:T(8,128)S(1)} %pad_maximum_fusion.1.refs_0_), channel_id=1, source_target_pairs={{0,1},{1,0},{2,3},{3,2},{4,5},{5,4},{6,7},{7,6},{8,9},{9,8},{10,11... | collective-permute-start | bytes 122888 | tf_op jit(solution)/shard_map/ppermute | solution.py:650
  25.2 5.1 %collective-permute-start.4 = (f32[80,128]{1,0:T(8,128)S(1)}, f32[80,128]{1,0:T(8,128)S(1)}, u32[]{:S(2)}, u32[]{:S(2)}) collective-permute-start(f32[80,128]{1,0:T(8,128)S(1)} %pad_maximum_fusion.1.refs_0_), channel_id=1, source_target_pairs={{0,2},{1,3},{2,0},{3,1},{4,6},{5,7},{6,4},{7,5},{8,10},{9,11},{10,... | collective-permute-start | bytes 122888 | tf_op jit(solution)/shard_map/ppermute | solution.py:650
  26.7 5.3 %collective-permute-start.5 = (f32[80,128]{1,0:T(8,128)S(1)}, f32[80,128]{1,0:T(8,128)S(1)}, u32[]{:S(2)}, u32[]{:S(2)}) collective-permute-start(f32[80,128]{1,0:T(8,128)S(1)} %pad_maximum_fusion.1.refs_0_), channel_id=1, source_target_pairs={{0,3},{1,2},{2,1},{3,0},{4,7},{5,6},{6,5},{7,4},{8,11},{9,10},{10,... | collective-permute-start | bytes 122888 | tf_op jit(solution)/shard_map/ppermute | solution.py:650
  40.0 14.3 %all-to-all-start.1 = ((bf16[16,32,256]{2,1,0:T(8,128)(2,1)}), bf16[16,32,256]{2,1,0:T(8,128)(2,1)S(1)}, u32[]{:S(2)}, u32[]{:S(2)}) async-start(bf16[16,32,256]{2,1,0:T(8,128)(2,1)} %get-tuple-element.95), calls=%async_computation.1 | async-start | bytes 524288 | tf_op jit(solution)/shard_map/all_to_all | solution.py:808
  45.8 8.5 %collective-permute-start.6 = (bf16[16,64,256]{2,1,0:T(8,128)(2,1)S(1)}, bf16[16,64,256]{2,1,0:T(8,128)(2,1)S(1)}, u32[]{:S(2)}, u32[]{:S(2)}) collective-permute-start(bf16[16,64,256]{2,1,0:T(8,128)(2,1)S(1)} %slice.75), channel_id=1, source_target_pairs={{0,16},{16,0},{1,17},{17,1},{2,18},{18,2},{3,19},{19,3},{4,20},{20... | collective-permute-start | bytes 1572872 | tf_op jit(solution)/shard_map/ppermute | solution.py:667
  56.7 25.8 %all-to-all-start.2 = ((bf16[16,96,256]{2,1,0:T(8,128)(2,1)}), bf16[16,96,256]{2,1,0:T(8,128)(2,1)S(1)}, u32[]{:S(2)}, u32[]{:S(2)}) async-start(bf16[16,96,256]{2,1,0:T(8,128)(2,1)} %get-tuple-element.104), calls=%async_computation.2 | async-start | bytes 1572864 | tf_op jit(solution)/shard_map/all_to_all | solution.py:825
  62.4 5.6 %collective-permute-start.11 = (bf16[512,256]{1,0:T(8,128)(2,1)S(1)}, bf16[512,256]{1,0:T(8,128)(2,1)S(1)}, u32[]{:S(2)}, u32[]{:S(2)}) collective-permute-start(bf16[512,256]{1,0:T(8,128)(2,1)S(1)} %bitcast.19), channel_id=1, source_target_pairs={{0,16},{16,0},{1,17},{17,1},{2,18},{18,2},{3,19},{19,3},{4,20},{20... | collective-permute-start | bytes 786440 | tf_op jit(solution)/shard_map/ppermute | solution.py:667
  62.7 5.3 %collective-permute-start.10 = (bf16[512,256]{1,0:T(8,128)(2,1)S(1)}, bf16[512,256]{1,0:T(8,128)(2,1)S(1)}, u32[]{:S(2)}, u32[]{:S(2)}) collective-permute-start(bf16[512,256]{1,0:T(8,128)(2,1)S(1)} %get-tuple-element.116), channel_id=1, source_target_pairs={{0,16},{16,0},{1,17},{17,1},{2,18},{18,2},{3,19},{19,3},{4,20},{20... | collective-permute-start | bytes 786440 | tf_op jit(solution)/shard_map/ppermute | solution.py:667
  69.2 24.9 %collective-permute-start.12 = (f32[136,512]{1,0:T(8,128)S(1)}, f32[136,512]{1,0:T(8,128)S(1)}, u32[]{:S(2)}, u32[]{:S(2)}) collective-permute-start(f32[136,512]{1,0:T(8,128)S(1)} %get-tuple-element.120), channel_id=1, source_target_pairs={{0,1},{1,0},{2,3},{3,2},{4,5},{5,4},{6,7},{7,6},{8,9},{9,8},{10,11... | collective-permute-start | bytes 835592 | tf_op jit(solution)/shard_map/ppermute | solution.py:650
  71.2 23.3 %collective-permute-start.13 = (f32[136,512]{1,0:T(8,128)S(1)}, f32[136,512]{1,0:T(8,128)S(1)}, u32[]{:S(2)}, u32[]{:S(2)}) collective-permute-start(f32[136,512]{1,0:T(8,128)S(1)} %get-tuple-element.121), channel_id=1, source_target_pairs={{0,2},{1,3},{2,0},{3,1},{4,6},{5,7},{6,4},{7,5},{8,10},{9,11},{10,... | collective-permute-start | bytes 835592 | tf_op jit(solution)/shard_map/ppermute | solution.py:650
  72.6 21.8 %collective-permute-start.14 = (f32[136,512]{1,0:T(8,128)S(1)}, f32[136,512]{1,0:T(8,128)S(1)}, u32[]{:S(2)}, u32[]{:S(2)}) collective-permute-start(f32[136,512]{1,0:T(8,128)S(1)} %get-tuple-element.122), channel_id=1, source_target_pairs={{0,3},{1,2},{2,1},{3,0},{4,7},{5,6},{6,5},{7,4},{8,11},{9,10},{10,... | collective-permute-start | bytes 835592 | tf_op jit(solution)/shard_map/ppermute | solution.py:650
  90.0 6.8 %collective-permute-start.9 = (f32[2,32,128]{2,1,0:T(8,128)S(1)}, f32[2,32,128]{2,1,0:T(8,128)S(1)}, u32[]{:S(2)}, u32[]{:S(2)}) collective-permute-start(f32[2,32,128]{2,1,0:T(8,128)S(1)} %get-tuple-element.114), channel_id=1, source_target_pairs={{0,12},{1,13},{2,14},{3,15},{4,8},{5,9},{6,10},{7,11},{8,4},{9,5},... | collective-permute-start | bytes 98312 | tf_op jit(solution)/shard_map/ppermute | solution.py:650
  92.6 5.0 %collective-permute-start.8 = (f32[2,32,128]{2,1,0:T(8,128)S(1)}, f32[2,32,128]{2,1,0:T(8,128)S(1)}, u32[]{:S(2)}, u32[]{:S(2)}) collective-permute-start(f32[2,32,128]{2,1,0:T(8,128)S(1)} %get-tuple-element.114), channel_id=1, source_target_pairs={{0,8},{1,9},{2,10},{3,11},{4,12},{5,13},{6,14},{7,15},{8,0},{9,1},... | collective-permute-start | bytes 98312 | tf_op jit(solution)/shard_map/ppermute | solution.py:650
  94.1 3.9 %collective-permute-start.7 = (f32[2,32,128]{2,1,0:T(8,128)S(1)}, f32[2,32,128]{2,1,0:T(8,128)S(1)}, u32[]{:S(2)}, u32[]{:S(2)}) collective-permute-start(f32[2,32,128]{2,1,0:T(8,128)S(1)} %get-tuple-element.114), channel_id=1, source_target_pairs={{0,4},{1,5},{2,6},{3,7},{4,0},{5,1},{6,2},{7,3},{8,12},{9,13},{10,... | collective-permute-start | bytes 98312 | tf_op jit(solution)/shard_map/ppermute | solution.py:650
  95.1 6.5 %collective-permute-start.15 = (f32[72,512]{1,0:T(8,128)S(1)}, f32[72,512]{1,0:T(8,128)S(1)}, u32[]{:S(2)}, u32[]{:S(2)}) collective-permute-start(f32[72,512]{1,0:T(8,128)S(1)} %get-tuple-element.124), channel_id=1, source_target_pairs={{0,4},{1,5},{2,6},{3,7},{4,0},{5,1},{6,2},{7,3},{8,12},{9,13},{10,... | collective-permute-start | bytes 442376 | tf_op jit(solution)/shard_map/ppermute | solution.py:650
  98.0 9.5 %collective-permute-start.16 = (f32[2,32,128]{2,1,0:T(8,128)S(1)}, f32[2,32,128]{2,1,0:T(8,128)S(1)}, u32[]{:S(2)}, u32[]{:S(2)}) collective-permute-start(f32[2,32,128]{2,1,0:T(8,128)S(1)} %add_add_fusion.1), channel_id=1, source_target_pairs={{0,1},{1,0},{2,3},{3,2},{4,5},{5,4},{6,7},{7,6},{8,9},{9,8},{10,11... | collective-permute-start | bytes 98312 | tf_op jit(solution)/shard_map/ppermute | solution.py:650
  98.8 8.8 %collective-permute-start.17 = (f32[2,32,128]{2,1,0:T(8,128)S(1)}, f32[2,32,128]{2,1,0:T(8,128)S(1)}, u32[]{:S(2)}, u32[]{:S(2)}) collective-permute-start(f32[2,32,128]{2,1,0:T(8,128)S(1)} %add_add_fusion.1), channel_id=1, source_target_pairs={{0,2},{1,3},{2,0},{3,1},{4,6},{5,7},{6,4},{7,5},{8,10},{9,11},{10,... | collective-permute-start | bytes 98312 | tf_op jit(solution)/shard_map/ppermute | solution.py:650
  100.5 7.0 %collective-permute-start.18 = (f32[2,32,128]{2,1,0:T(8,128)S(1)}, f32[2,32,128]{2,1,0:T(8,128)S(1)}, u32[]{:S(2)}, u32[]{:S(2)}) collective-permute-start(f32[2,32,128]{2,1,0:T(8,128)S(1)} %add_add_fusion.1), channel_id=1, source_target_pairs={{0,3},{1,2},{2,1},{3,0},{4,7},{5,6},{6,5},{7,4},{8,11},{9,10},{10,... | collective-permute-start | bytes 98312 | tf_op jit(solution)/shard_map/ppermute | solution.py:650
  102.2 6.3 %collective-permute-start.19 = (f32[40,512]{1,0:T(8,128)S(1)}, f32[40,512]{1,0:T(8,128)S(1)}, u32[]{:S(2)}, u32[]{:S(2)}) collective-permute-start(f32[40,512]{1,0:T(8,128)S(1)} %get-tuple-element.136), channel_id=1, source_target_pairs={{0,8},{1,9},{2,10},{3,11},{4,12},{5,13},{6,14},{7,15},{8,0},{9,1},... | collective-permute-start | bytes 245768 | tf_op jit(solution)/shard_map/ppermute | solution.py:650
  108.7 1.7 %collective-permute-start.20 = (f32[9,32,128]{2,1,0:T(8,128)S(1)}, f32[9,32,128]{2,1,0:T(8,128)S(1)}, u32[]{:S(2)}, u32[]{:S(2)}) collective-permute-start(f32[9,32,128]{2,1,0:T(8,128)S(1)} %shard_map.266.mine_ref), channel_id=1, source_target_pairs={{0,16},{16,0},{1,17},{17,1},{2,18},{18,2},{3,19},{19,3},{4,20},{20... | collective-permute-start | bytes 442376 | tf_op jit(solution)/shard_map/ppermute | solution.py:667
  (18 other events, 193.0 us)

commit v4 on v3

--- a/solution.py
+++ b/solution.py
@@ -17,6 +17,7 @@
 NT = (((1,), (1,)), ((), ()))
 TN = (((0,), (0,)), ((), ()))
 EPS = 1e-05
+SQUARE_SCALE = 65536.0
 VMEM = pl.BlockSpec(memory_space=pltpu.VMEM)
 SMEM = pl.BlockSpec(memory_space=pltpu.SMEM)
 
@@ -355,16 +356,15 @@
         sig = jax.nn.sigmoid(gate)
         x = first_ref[s * per : (s + 1) * per, kh * C : (kh + 1) * C, :].reshape(step, nt).astype(F32)
         g = first_ref[s * per : (s + 1) * per, (kh + 1) * C :, :].reshape(step, nt).astype(F32)
-        gm_ref[s * per : (s + 1) * per, 2 * C :, :] = (x + value * sig).astype(BF16).reshape(per, C, nt)
+        gm_ref[s * per : (s + 1) * per, C:, :] = (x + value * sig).astype(BF16).reshape(per, C, nt)
         gv = g * sig
         gp[0, lo : lo + step, :] = gv.astype(BF16)
         gp[1, lo : lo + step, :] = (gv * value * (1.0 - sig)).astype(BF16)
     for s in range(mp // per):
         at = slice(s * step, (s + 1) * step)
         gm = dot(wt[0, :, at], gp[0], TN) + dot(wt[1, :, at], gp[1], TN)
-        hi, lo = split(gm)
-        gm_ref[s * per : (s + 1) * per, 0:C, :] = hi.reshape(per, C, nt)
-        gm_ref[s * per : (s + 1) * per, C : 2 * C, :] = lo.reshape(per, C, nt)
+        wide = gm * SQUARE_SCALE
+        gm_ref[s * per : (s + 1) * per, 0:C, :] = (wide * jnp.abs(wide)).astype(BF16).reshape(per, C, nt)
     keep_ref[...] = gp[own]
     send_ref[...] = gp[1 - own]
 
@@ -425,14 +425,15 @@
         for n in range(N):
             xs[n * C : (n + 1) * C, :] = x_ref[:, n * B : (n + 1) * B].astype(F32)
             at = slice((n % per) * B, (n % per + 1) * B)
-            gs[n * C : (n + 1) * C, :] = gm_ref[n // per, 0:C, at].astype(F32) + gm_ref[n // per, C : 2 * C, at].astype(F32)
+            square = gm_ref[n // per, 0:C, at].astype(F32)
+            gs[n * C : (n + 1) * C, :] = square * (lax.rsqrt(jnp.maximum(jnp.abs(square), 1e-37)) * (1.0 / SQUARE_SCALE))
         mean, inv, mask = token_stats(stat_ref, len_ref[0], count)
         tok[0] = mean
         tok[1] = inv
         tok[2] = mask
         sum_ref[...] = jnp.zeros_like(sum_ref)
         for m in range(gm_ref.shape[0]):
-            layer_ref[:, m * nt : (m + 1) * nt] = gm_ref[m, 2 * C :, :]
+            layer_ref[:, m * nt : (m + 1) * nt] = gm_ref[m, C:, :]
 
     fetch(0, i).wait()
     for j in range(G):
@@ -817,7 +818,7 @@
     mixed_tok, back_tab = lax.optimization_barrier((mixed_tok, back_tab))
     gm, keep, send = call(
         glu_kernel,
-        (shape((mp, 3 * C, nt), BF16),) + (shape((H, nt), BF16),) * 2,
+        (shape((mp, 2 * C, nt), BF16),) + (shape((H, nt), BF16),) * 2,
         5, 1, 2, [vm((2, H, nt), BF16), vm((2, H, H), BF16)],
     )(place, mixed_tok, first, other_w, bias)
     mixed_tok = mixed_tok.reshape(H, nt)

time: 113 us -> 107 us (0.947)
  waiting for transfers between devices: 19.7 us -> 14.5 us
    all_to_all x1, waiting for transfers between devices: 9.74 us -> 5.22 us  [per_device(): gm = lax.all_to_all(gm, 'mp', split_axis=0, concat_axis=0, tiled=True)]
  transfers between devices with their start and end apart: 25 -> 25, of which waited for: 8 -> 8; matrix products, arithmetic and copies ran while one was open for 0% -> 1% of each run, Pallas kernels for 34% -> 36%
where the time goes in v4:
time: 107 us; the launch traced here: 106 us
  Pallas kernels  45.4 us (42%)
  starting transfers between devices  43.5 us (41%)
  waiting for transfers between devices  14.5 us (14%)
  between operations  1.75 us (2%)
  local copies, waits for them, and re-layouts  1.08 us (1%)
    ppermute x17, starting transfers between devices, exchange(): return lax.ppermute(v, axis, [(k, k ^ off) for k in range(size)])  23.6 us
    pallas_call x1, Pallas kernels, per_device(): by_channel(partial(back_kernel, count=H), (shape((C, L), BF16), shape((C,...  7.5 us
    pallas_call x1, Pallas kernels, per_device(): by_channel(partial(back_table_kernel, C=C, M=M), (far((C, 2 * B, 4 * B),...  7.16 us
    all_to_all x1, starting transfers between devices, per_device(): first = lax.all_to_all(pay, 'mp', split_axis=0, concat_axis=0, tiled=True)  7.08 us
    pallas_call x1, Pallas kernels, per_device(): by_channel(partial(table_kernel, C=C, M=M), (shape((C, 2 * B, 2 * B), BF1...  6.28 us
    ppermute x17, waiting for transfers between devices, exchange(): return lax.ppermute(v, axis, [(k, k ^ off) for k in range(size)])  5.94 us
    all_to_all x1, starting transfers between devices, per_device(): lax.all_to_all(mixed, 'mp', split_axis=0, concat_axis=0, tiled=True)  5.8 us
    all_to_all x1, starting transfers between devices, per_device(): gm = lax.all_to_all(gm, 'mp', split_axis=0, concat_axis=0, tiled=True)  5.71 us
  transfers between devices with their start and end apart: 25, of which 8 were waited for; matrix products, arithmetic and copies ran while one was open for 1% of the time, Pallas kernels for 36%

profile of v4, /device:TPU:0, one launch (start us, length us, event | category | flops | bytes accessed | tf_op | source)
XLA Modules:
  0.0 106.4 jit_solution(10911421555929556367)
XLA Ops:
  0.7 2.8 %shard_map.254 = (f32[80,128]{1,0:T(8,128)S(1)}, bf16[16,128,256]{2,1,0:T(8,128)(2,1)}) custom-call(s32[2]{0:T(128)S(1)} %pad_add_fusion.place_ref.half_ref, bf16[32,4096]{1,0:T(8,128)(2,1)} %x_ref.7, bf16[32,4096]{1,0:T(8,128)(2,1)} %g_ref.1, bf16[32,512]{1,0:T(8,128)(2,1)} %bitcast.25, bf16[32,512]{1,0:T(8,128)(2,1)} %bitcast.26, bf16[1,32]{1,0:T(2,128)(2,1)} %bitcast.27, ...), custom_call_target="tpu_custom_call" | custom-call | flops 3000000000 | bytes 3000000 | tf_op jit(solution)/shard_map/pallas_call | solution.py:750
  3.6 4.1 %collective-permute-start.2 = (f32[80,128]{1,0:T(8,128)S(1)}, f32[80,128]{1,0:T(8,128)S(1)}, u32[]{:S(2)}, u32[]{:S(2)}) collective-permute-start(f32[80,128]{1,0:T(8,128)S(1)} %get-tuple-element.85), channel_id=1, source_target_pairs={{0,8},{1,9},{2,10},{3,11},{4,12},{5,13},{6,14},{7,15},{8,0},{9,1},... | collective-permute-start | bytes 122888 | tf_op jit(solution)/shard_map/ppermute | solution.py:651
  7.7 1.6 %collective-permute-start = (f32[80,128]{1,0:T(8,128)S(1)}, f32[80,128]{1,0:T(8,128)S(1)}, u32[]{:S(2)}, u32[]{:S(2)}) collective-permute-start(f32[80,128]{1,0:T(8,128)S(1)} %get-tuple-element.85), channel_id=1, source_target_pairs={{0,4},{1,5},{2,6},{3,7},{4,0},{5,1},{6,2},{7,3},{8,12},{9,13},{10,... | collective-permute-start | bytes 122888 | tf_op jit(solution)/shard_map/ppermute | solution.py:651
  9.3 7.1 %all-to-all-start = ((bf16[16,128,256]{2,1,0:T(8,128)(2,1)}), bf16[16,128,256]{2,1,0:T(8,128)(2,1)S(1)}, u32[]{:S(2)}, u32[]{:S(2)}) async-start(bf16[16,128,256]{2,1,0:T(8,128)(2,1)} %get-tuple-element.94), calls=%async_computation | async-start | bytes 2097152 | tf_op jit(solution)/shard_map/all_to_all | solution.py:764
  16.9 6.3 %shard_map.255 = (bf16[32,256,256]{2,1,0:T(8,128)(2,1)S(1)}, bf16[32,256,256]{2,1,0:T(8,128)(2,1)}, bf16[32,384,256]{2,1,0:T(8,128)(2,1)S(1)}, f32[2,32,128]{2,1,0:T(8,128)S(1)}, f32[32,128]{1,0:T(8,128)S(1)}) custom-call(f32[3,32,128]{2,1,0:T(8,128)S(1)} %pad_maximum_fusion.rates_ref, f32[32,128]{1,0:T(8,128)S(1)} %pad_maximum_fusion.2.coef_ref), custom_call_target="tpu_custom_call" | custom-call | flops 6000000000 | bytes 6000000 | tf_op jit(solution)/shard_map/pallas_call | solution.py:770
  23.3 2.0 %collective-permute-start.3 = (f32[80,128]{1,0:T(8,128)S(1)}, f32[80,128]{1,0:T(8,128)S(1)}, u32[]{:S(2)}, u32[]{:S(2)}) collective-permute-start(f32[80,128]{1,0:T(8,128)S(1)} %pad_maximum_fusion.1.refs_0_), channel_id=1, source_target_pairs={{0,1},{1,0},{2,3},{3,2},{4,5},{5,4},{6,7},{7,6},{8,9},{9,8},{10,11... | collective-permute-start | bytes 122888 | tf_op jit(solution)/shard_map/ppermute | solution.py:651
  27.5 2.9 %collective-permute-done.3.refs_1_ = f32[80,128]{1,0:T(8,128)S(1)} collective-permute-done((f32[80,128]{1,0:T(8,128)S(1)}, f32[80,128]{1,0:T(8,128)S(1)}, u32[]{:S(2)}, u32[]{:S(2)}) %collective-permute-start.3) | collective-permute-done | bytes 40992 | tf_op jit(solution)/shard_map/ppermute | solution.py:651
  30.4 1.7 %collective-permute-done.5.refs_3_ = f32[80,128]{1,0:T(8,128)S(1)} collective-permute-done((f32[80,128]{1,0:T(8,128)S(1)}, f32[80,128]{1,0:T(8,128)S(1)}, u32[]{:S(2)}, u32[]{:S(2)}) %collective-permute-start.5) | collective-permute-done | bytes 40992 | tf_op jit(solution)/shard_map/ppermute | solution.py:651
  32.1 5.2 %shard_map.256 = (bf16[16,32,256]{2,1,0:T(8,128)(2,1)}, f32[32,32,128]{2,1,0:T(8,128)}, f32[32,32,128]{2,1,0:T(8,128)}, f32[32,32,128]{2,1,0:T(8,128)}, f32[2,32...) custom-call(s32[1]{0:T(128)S(6)} %copy.29.len_ref, f32[3,32]{1,0:T(4,128)S(1)} %pad_maximum_fusion.3.vec_ref, ...), custom_call_target="tpu_custom_call" | custom-call | flops 6000000000 | bytes 6000000 | tf_op jit(solution)/shard_map/pallas_call | solution.py:792
  37.9 2.1 %all-to-all-done.first_ref = bf16[16,128,256]{2,1,0:T(8,128)(2,1)S(1)} async-done(((bf16[16,128,256]{2,1,0:T(8,128)(2,1)}), bf16[16,128,256]{2,1,0:T(8,128)(2,1)S(1)}, u32[]{:S(2)}, u32[]{:S(2)}) %all-to-all-start) | async-done | bytes 1048608 | tf_op jit(solution)/shard_map/all_to_all | solution.py:764
  40.0 5.8 %all-to-all-start.1 = ((bf16[16,32,256]{2,1,0:T(8,128)(2,1)}), bf16[16,32,256]{2,1,0:T(8,128)(2,1)S(1)}, u32[]{:S(2)}, u32[]{:S(2)}) async-start(bf16[16,32,256]{2,1,0:T(8,128)(2,1)} %get-tuple-element.95), calls=%async_computation.1 | async-start | bytes 524288 | tf_op jit(solution)/shard_map/all_to_all | solution.py:809
  45.9 7.2 %shard_map.257 = (bf16[32,256,512]{2,1,0:T(8,128)(2,1)}, bf16[32,128,256]{2,1,0:T(8,128)(2,1)}) custom-call(f32[3,32,128]{2,1,0:T(8,128)S(1)} %pad_maximum_fusion.rates_ref, f32[32,128]{1,0:T(8,128)S(1)} %get-tuple-element.97.w_ref), custom_call_target="tpu_custom_call" | custom-call | flops 7000000000 | bytes 7000000 | tf_op jit(solution)/shard_map/pallas_call | solution.py:810
  54.3 2.3 %shard_map.258 = (bf16[16,64,256]{2,1,0:T(8,128)(2,1)}, bf16[512,256]{1,0:T(8,128)(2,1)S(1)}, bf16[512,256]{1,0:T(8,128)(2,1)S(1)}) custom-call(s32[2]{0:T(128)S(1)} %pad_add_fusion.place_ref.half_ref, bf16[16,32,256]{2,1,0:T(8,128)(2,1)S(1)} %all-to-all-done.1.in_ref, bf16[16,128,256]{2,1,0:T(8,128)(2,1)S(1)} %all-to-all-done.first_ref, ...), custom_call_target="tpu_custom_call" | custom-call | flops 2000000000 | bytes 2000000 | tf_op jit(solution)/shard_map/pallas_call | solution.py:819
  56.6 5.7 %all-to-all-start.2 = ((bf16[16,64,256]{2,1,0:T(8,128)(2,1)}), bf16[16,64,256]{2,1,0:T(8,128)(2,1)S(1)}, u32[]{:S(2)}, u32[]{:S(2)}) async-start(bf16[16,64,256]{2,1,0:T(8,128)(2,1)} %get-tuple-element.104), calls=%async_computation.2 | async-start | bytes 1048576 | tf_op jit(solution)/shard_map/all_to_all | solution.py:826
  62.9 4.9 %shard_map.259 = (bf16[32,96,256]{2,1,0:T(8,128)(2,1)}, f32[32,32,128]{2,1,0:T(8,128)}) custom-call(s32[1]{0:T(128)S(6)} %copy.29.len_ref, f32[3,32]{1,0:T(4,128)} %copy-done.4, bf16[32,4096]{1,0:T(8,128)(2,1)} %x_ref.7, f32[2,32,128]{2,1,0:T(8,128)} %copy-done.10, bf16[32,256,256]{2,1,0:T(8,128)(2,1)} %get-tuple-element.105.f_ref), custom_call_target="tpu_custom_call" | custom-call | flops 3000000000 | bytes 3000000 | tf_op jit(solution)/shard_map/pallas_call | solution.py:827
  69.0 2.0 %collective-permute-start.12 = (f32[136,512]{1,0:T(8,128)S(1)}, f32[136,512]{1,0:T(8,128)S(1)}, u32[]{:S(2)}, u32[]{:S(2)}) collective-permute-start(f32[136,512]{1,0:T(8,128)S(1)} %get-tuple-element.120), channel_id=1, source_target_pairs={{0,1},{1,0},{2,3},{3,2},{4,5},{5,4},{6,7},{7,6},{8,9},{9,8},{10,11... | collective-permute-start | bytes 835592 | tf_op jit(solution)/shard_map/ppermute | solution.py:651
  71.0 1.5 %collective-permute-start.13 = (f32[136,512]{1,0:T(8,128)S(1)}, f32[136,512]{1,0:T(8,128)S(1)}, u32[]{:S(2)}, u32[]{:S(2)}) collective-permute-start(f32[136,512]{1,0:T(8,128)S(1)} %get-tuple-element.121), channel_id=1, source_target_pairs={{0,2},{1,3},{2,0},{3,1},{4,6},{5,7},{6,4},{7,5},{8,10},{9,11},{10,... | collective-permute-start | bytes 835592 | tf_op jit(solution)/shard_map/ppermute | solution.py:651
  72.6 5.2 %all-to-all-done.2.gm_ref = bf16[16,64,256]{2,1,0:T(8,128)(2,1)S(1)} async-done(((bf16[16,64,256]{2,1,0:T(8,128)(2,1)}), bf16[16,64,256]{2,1,0:T(8,128)(2,1)S(1)}, u32[]{:S(2)}, u32[]{:S(2)}) %all-to-all-start.2) | async-done | bytes 524320 | tf_op jit(solution)/shard_map/all_to_all | solution.py:826
  77.8 7.5 %shard_map.260 = (bf16[32,4096]{1,0:T(8,128)(2,1)}, f32[32,4096]{1,0:T(8,128)S(1)}, f32[2,32,128]{2,1,0:T(8,128)S(1)}, f32[32,24,128]{2,1,0:T(8,128)S(1)}, f32[3...) custom-call(s32[1]{0:T(128)S(6)} %copy.29.len_ref, ...), custom_call_target="tpu_custom_call" | custom-call | flops 7000000000 | bytes 7000000 | tf_op jit(solution)/shard_map/pallas_call | solution.py:846
  85.3 2.0 %collective-permute-start.9 = (f32[2,32,128]{2,1,0:T(8,128)S(1)}, f32[2,32,128]{2,1,0:T(8,128)S(1)}, u32[]{:S(2)}, u32[]{:S(2)}) collective-permute-start(f32[2,32,128]{2,1,0:T(8,128)S(1)} %get-tuple-element.114), channel_id=1, source_target_pairs={{0,12},{1,13},{2,14},{3,15},{4,8},{5,9},{6,10},{7,11},{8,4},{9,5},... | collective-permute-start | bytes 98312 | tf_op jit(solution)/shard_map/ppermute | solution.py:651
  94.8 1.5 %collective-permute-start.18 = (f32[2,32,128]{2,1,0:T(8,128)S(1)}, f32[2,32,128]{2,1,0:T(8,128)S(1)}, u32[]{:S(2)}, u32[]{:S(2)}) collective-permute-start(f32[2,32,128]{2,1,0:T(8,128)S(1)} %add_add_fusion.1), channel_id=1, source_target_pairs={{0,3},{1,2},{2,1},{3,0},{4,7},{5,6},{6,5},{7,4},{8,11},{9,10},{10,... | collective-permute-start | bytes 98312 | tf_op jit(solution)/shard_map/ppermute | solution.py:651
  96.8 1.9 %collective-permute-start.19 = (f32[40,512]{1,0:T(8,128)S(1)}, f32[40,512]{1,0:T(8,128)S(1)}, u32[]{:S(2)}, u32[]{:S(2)}) collective-permute-start(f32[40,512]{1,0:T(8,128)S(1)} %get-tuple-element.136), channel_id=1, source_target_pairs={{0,8},{1,9},{2,10},{3,11},{4,12},{5,13},{6,14},{7,15},{8,0},{9,1},... | collective-permute-start | bytes 245768 | tf_op jit(solution)/shard_map/ppermute | solution.py:651
  98.7 3.8 %shard_map.264.ref = f32[32,40,128]{2,1,0:T(8,128)S(1)} custom-call(bf16[32,96,256]{2,1,0:T(8,128)(2,1)} %get-tuple-element.127.u_ref, f32[32,32,128]{2,1,0:T(8,128)} %get-tuple-element.128.lift_ref, f32[32,32,128]{2,1,0:T(8,128)S(1)} %get-tuple-element.129.g_ref, f32[32,32,128]{2,1,0:T(8,128)S(1)} %get-tuple-element.130.p_ref, ...), custom_call_target="tpu_custom_call" | custom-call | flops 20000000000 | bytes 20000000 | tf_op jit(solution)/shard_map/pallas_call | solution.py:880
  104.5 1.8 %shard_map.268 = (f32[32,512]{1,0:T(8,128)}, f32[32,512]{1,0:T(8,128)}, f32[1,32]{1,0:T(1,128)}, f32[1,32]{1,0:T(1,128)}, f32[1,32]{1,0:T(1,128)}, /*index=5*/f3...) custom-call(s32[2]{0:T(128)S(1)} %pad_add_fusion.place_ref.half_ref,, ...), custom_call_target="tpu_custom_call" | custom-call | flops 1000000000 | bytes 1000000 | tf_op jit(solution)/shard_map/pallas_call | solution.py:904
  (87 shorter events, 15.9 us)
Async XLA Ops:
  3.6 19.6 %collective-permute-start.2 = (f32[80,128]{1,0:T(8,128)S(1)}, f32[80,128]{1,0:T(8,128)S(1)}, u32[]{:S(2)}, u32[]{:S(2)}) collective-permute-start(f32[80,128]{1,0:T(8,128)S(1)} %get-tuple-element.85), channel_id=1, source_target_pairs={{0,8},{1,9},{2,10},{3,11},{4,12},{5,13},{6,14},{7,15},{8,0},{9,1},... | collective-permute-start | bytes 122888 | tf_op jit(solution)/shard_map/ppermute | solution.py:651
  7.7 15.5 %collective-permute-start = (f32[80,128]{1,0:T(8,128)S(1)}, f32[80,128]{1,0:T(8,128)S(1)}, u32[]{:S(2)}, u32[]{:S(2)}) collective-permute-start(f32[80,128]{1,0:T(8,128)S(1)} %get-tuple-element.85), channel_id=1, source_target_pairs={{0,4},{1,5},{2,6},{3,7},{4,0},{5,1},{6,2},{7,3},{8,12},{9,13},{10,... | collective-permute-start | bytes 122888 | tf_op jit(solution)/shard_map/ppermute | solution.py:651
  9.3 13.9 %collective-permute-start.1 = (f32[80,128]{1,0:T(8,128)S(1)}, f32[80,128]{1,0:T(8,128)S(1)}, u32[]{:S(2)}, u32[]{:S(2)}) collective-permute-start(f32[80,128]{1,0:T(8,128)S(1)} %get-tuple-element.85), channel_id=1, source_target_pairs={{0,12},{1,13},{2,14},{3,15},{4,8},{5,9},{6,10},{7,11},{8,4},{9,5},... | collective-permute-start | bytes 122888 | tf_op jit(solution)/shard_map/ppermute | solution.py:651
  9.3 30.7 %all-to-all-start = ((bf16[16,128,256]{2,1,0:T(8,128)(2,1)}), bf16[16,128,256]{2,1,0:T(8,128)(2,1)S(1)}, u32[]{:S(2)}, u32[]{:S(2)}) async-start(bf16[16,128,256]{2,1,0:T(8,128)(2,1)} %get-tuple-element.94), calls=%async_computation | async-start | bytes 2097152 | tf_op jit(solution)/shard_map/all_to_all | solution.py:764
  23.3 7.1 %collective-permute-start.3 = (f32[80,128]{1,0:T(8,128)S(1)}, f32[80,128]{1,0:T(8,128)S(1)}, u32[]{:S(2)}, u32[]{:S(2)}) collective-permute-start(f32[80,128]{1,0:T(8,128)S(1)} %pad_maximum_fusion.1.refs_0_), channel_id=1, source_target_pairs={{0,1},{1,0},{2,3},{3,2},{4,5},{5,4},{6,7},{7,6},{8,9},{9,8},{10,11... | collective-permute-start | bytes 122888 | tf_op jit(solution)/shard_map/ppermute | solution.py:651
  25.2 5.1 %collective-permute-start.4 = (f32[80,128]{1,0:T(8,128)S(1)}, f32[80,128]{1,0:T(8,128)S(1)}, u32[]{:S(2)}, u32[]{:S(2)}) collective-permute-start(f32[80,128]{1,0:T(8,128)S(1)} %pad_maximum_fusion.1.refs_0_), channel_id=1, source_target_pairs={{0,2},{1,3},{2,0},{3,1},{4,6},{5,7},{6,4},{7,5},{8,10},{9,11},{10,... | collective-permute-start | bytes 122888 | tf_op jit(solution)/shard_map/ppermute | solution.py:651
  26.7 5.3 %collective-permute-start.5 = (f32[80,128]{1,0:T(8,128)S(1)}, f32[80,128]{1,0:T(8,128)S(1)}, u32[]{:S(2)}, u32[]{:S(2)}) collective-permute-start(f32[80,128]{1,0:T(8,128)S(1)} %pad_maximum_fusion.1.refs_0_), channel_id=1, source_target_pairs={{0,3},{1,2},{2,1},{3,0},{4,7},{5,6},{6,5},{7,4},{8,11},{9,10},{10,... | collective-permute-start | bytes 122888 | tf_op jit(solution)/shard_map/ppermute | solution.py:651
  40.0 14.3 %all-to-all-start.1 = ((bf16[16,32,256]{2,1,0:T(8,128)(2,1)}), bf16[16,32,256]{2,1,0:T(8,128)(2,1)S(1)}, u32[]{:S(2)}, u32[]{:S(2)}) async-start(bf16[16,32,256]{2,1,0:T(8,128)(2,1)} %get-tuple-element.95), calls=%async_computation.1 | async-start | bytes 524288 | tf_op jit(solution)/shard_map/all_to_all | solution.py:809
  45.8 8.5 %collective-permute-start.6 = (bf16[16,64,256]{2,1,0:T(8,128)(2,1)S(1)}, bf16[16,64,256]{2,1,0:T(8,128)(2,1)S(1)}, u32[]{:S(2)}, u32[]{:S(2)}) collective-permute-start(bf16[16,64,256]{2,1,0:T(8,128)(2,1)S(1)} %slice.75), channel_id=1, source_target_pairs={{0,16},{16,0},{1,17},{17,1},{2,18},{18,2},{3,19},{19,3},{4,20},{20... | collective-permute-start | bytes 1572872 | tf_op jit(solution)/shard_map/ppermute | solution.py:668
  56.6 21.2 %all-to-all-start.2 = ((bf16[16,64,256]{2,1,0:T(8,128)(2,1)}), bf16[16,64,256]{2,1,0:T(8,128)(2,1)S(1)}, u32[]{:S(2)}, u32[]{:S(2)}) async-start(bf16[16,64,256]{2,1,0:T(8,128)(2,1)} %get-tuple-element.104), calls=%async_computation.2 | async-start | bytes 1048576 | tf_op jit(solution)/shard_map/all_to_all | solution.py:826
  62.3 5.5 %collective-permute-start.11 = (bf16[512,256]{1,0:T(8,128)(2,1)S(1)}, bf16[512,256]{1,0:T(8,128)(2,1)S(1)}, u32[]{:S(2)}, u32[]{:S(2)}) collective-permute-start(bf16[512,256]{1,0:T(8,128)(2,1)S(1)} %bitcast.19), channel_id=1, source_target_pairs={{0,16},{16,0},{1,17},{17,1},{2,18},{18,2},{3,19},{19,3},{4,20},{20... | collective-permute-start | bytes 786440 | tf_op jit(solution)/shard_map/ppermute | solution.py:668
  62.6 5.3 %collective-permute-start.10 = (bf16[512,256]{1,0:T(8,128)(2,1)S(1)}, bf16[512,256]{1,0:T(8,128)(2,1)S(1)}, u32[]{:S(2)}, u32[]{:S(2)}) collective-permute-start(bf16[512,256]{1,0:T(8,128)(2,1)S(1)} %get-tuple-element.116), channel_id=1, source_target_pairs={{0,16},{16,0},{1,17},{17,1},{2,18},{18,2},{3,19},{19,3},{4,20},{20... | collective-permute-start | bytes 786440 | tf_op jit(solution)/shard_map/ppermute | solution.py:668
  69.0 19.5 %collective-permute-start.12 = (f32[136,512]{1,0:T(8,128)S(1)}, f32[136,512]{1,0:T(8,128)S(1)}, u32[]{:S(2)}, u32[]{:S(2)}) collective-permute-start(f32[136,512]{1,0:T(8,128)S(1)} %get-tuple-element.120), channel_id=1, source_target_pairs={{0,1},{1,0},{2,3},{3,2},{4,5},{5,4},{6,7},{7,6},{8,9},{9,8},{10,11... | collective-permute-start | bytes 835592 | tf_op jit(solution)/shard_map/ppermute | solution.py:651
  71.0 18.8 %collective-permute-start.13 = (f32[136,512]{1,0:T(8,128)S(1)}, f32[136,512]{1,0:T(8,128)S(1)}, u32[]{:S(2)}, u32[]{:S(2)}) collective-permute-start(f32[136,512]{1,0:T(8,128)S(1)} %get-tuple-element.121), channel_id=1, source_target_pairs={{0,2},{1,3},{2,0},{3,1},{4,6},{5,7},{6,4},{7,5},{8,10},{9,11},{10,... | collective-permute-start | bytes 835592 | tf_op jit(solution)/shard_map/ppermute | solution.py:651
  72.5 17.3 %collective-permute-start.14 = (f32[136,512]{1,0:T(8,128)S(1)}, f32[136,512]{1,0:T(8,128)S(1)}, u32[]{:S(2)}, u32[]{:S(2)}) collective-permute-start(f32[136,512]{1,0:T(8,128)S(1)} %get-tuple-element.122), channel_id=1, source_target_pairs={{0,3},{1,2},{2,1},{3,0},{4,7},{5,6},{6,5},{7,4},{8,11},{9,10},{10,... | collective-permute-start | bytes 835592 | tf_op jit(solution)/shard_map/ppermute | solution.py:651
  85.3 6.1 %collective-permute-start.9 = (f32[2,32,128]{2,1,0:T(8,128)S(1)}, f32[2,32,128]{2,1,0:T(8,128)S(1)}, u32[]{:S(2)}, u32[]{:S(2)}) collective-permute-start(f32[2,32,128]{2,1,0:T(8,128)S(1)} %get-tuple-element.114), channel_id=1, source_target_pairs={{0,12},{1,13},{2,14},{3,15},{4,8},{5,9},{6,10},{7,11},{8,4},{9,5},... | collective-permute-start | bytes 98312 | tf_op jit(solution)/shard_map/ppermute | solution.py:651
  87.4 4.9 %collective-permute-start.8 = (f32[2,32,128]{2,1,0:T(8,128)S(1)}, f32[2,32,128]{2,1,0:T(8,128)S(1)}, u32[]{:S(2)}, u32[]{:S(2)}) collective-permute-start(f32[2,32,128]{2,1,0:T(8,128)S(1)} %get-tuple-element.114), channel_id=1, source_target_pairs={{0,8},{1,9},{2,10},{3,11},{4,12},{5,13},{6,14},{7,15},{8,0},{9,1},... | collective-permute-start | bytes 98312 | tf_op jit(solution)/shard_map/ppermute | solution.py:651
  88.6 4.1 %collective-permute-start.7 = (f32[2,32,128]{2,1,0:T(8,128)S(1)}, f32[2,32,128]{2,1,0:T(8,128)S(1)}, u32[]{:S(2)}, u32[]{:S(2)}) collective-permute-start(f32[2,32,128]{2,1,0:T(8,128)S(1)} %get-tuple-element.114), channel_id=1, source_target_pairs={{0,4},{1,5},{2,6},{3,7},{4,0},{5,1},{6,2},{7,3},{8,12},{9,13},{10,... | collective-permute-start | bytes 98312 | tf_op jit(solution)/shard_map/ppermute | solution.py:651
  90.4 5.8 %collective-permute-start.15 = (f32[72,512]{1,0:T(8,128)S(1)}, f32[72,512]{1,0:T(8,128)S(1)}, u32[]{:S(2)}, u32[]{:S(2)}) collective-permute-start(f32[72,512]{1,0:T(8,128)S(1)} %get-tuple-element.124), channel_id=1, source_target_pairs={{0,4},{1,5},{2,6},{3,7},{4,0},{5,1},{6,2},{7,3},{8,12},{9,13},{10,... | collective-permute-start | bytes 442376 | tf_op jit(solution)/shard_map/ppermute | solution.py:651
  92.7 9.9 %collective-permute-start.16 = (f32[2,32,128]{2,1,0:T(8,128)S(1)}, f32[2,32,128]{2,1,0:T(8,128)S(1)}, u32[]{:S(2)}, u32[]{:S(2)}) collective-permute-start(f32[2,32,128]{2,1,0:T(8,128)S(1)} %add_add_fusion.1), channel_id=1, source_target_pairs={{0,1},{1,0},{2,3},{3,2},{4,5},{5,4},{6,7},{7,6},{8,9},{9,8},{10,11... | collective-permute-start | bytes 98312 | tf_op jit(solution)/shard_map/ppermute | solution.py:651
  93.7 8.9 %collective-permute-start.17 = (f32[2,32,128]{2,1,0:T(8,128)S(1)}, f32[2,32,128]{2,1,0:T(8,128)S(1)}, u32[]{:S(2)}, u32[]{:S(2)}) collective-permute-start(f32[2,32,128]{2,1,0:T(8,128)S(1)} %add_add_fusion.1), channel_id=1, source_target_pairs={{0,2},{1,3},{2,0},{3,1},{4,6},{5,7},{6,4},{7,5},{8,10},{9,11},{10,... | collective-permute-start | bytes 98312 | tf_op jit(solution)/shard_map/ppermute | solution.py:651
  94.8 7.8 %collective-permute-start.18 = (f32[2,32,128]{2,1,0:T(8,128)S(1)}, f32[2,32,128]{2,1,0:T(8,128)S(1)}, u32[]{:S(2)}, u32[]{:S(2)}) collective-permute-start(f32[2,32,128]{2,1,0:T(8,128)S(1)} %add_add_fusion.1), channel_id=1, source_target_pairs={{0,3},{1,2},{2,1},{3,0},{4,7},{5,6},{6,5},{7,4},{8,11},{9,10},{10,... | collective-permute-start | bytes 98312 | tf_op jit(solution)/shard_map/ppermute | solution.py:651
  96.8 5.8 %collective-permute-start.19 = (f32[40,512]{1,0:T(8,128)S(1)}, f32[40,512]{1,0:T(8,128)S(1)}, u32[]{:S(2)}, u32[]{:S(2)}) collective-permute-start(f32[40,512]{1,0:T(8,128)S(1)} %get-tuple-element.136), channel_id=1, source_target_pairs={{0,8},{1,9},{2,10},{3,11},{4,12},{5,13},{6,14},{7,15},{8,0},{9,1},... | collective-permute-start | bytes 245768 | tf_op jit(solution)/shard_map/ppermute | solution.py:651
  102.8 1.7 %collective-permute-start.20 = (f32[9,32,128]{2,1,0:T(8,128)S(1)}, f32[9,32,128]{2,1,0:T(8,128)S(1)}, u32[]{:S(2)}, u32[]{:S(2)}) collective-permute-start(f32[9,32,128]{2,1,0:T(8,128)S(1)} %shard_map.266.mine_ref), channel_id=1, source_target_pairs={{0,16},{16,0},{1,17},{17,1},{2,18},{18,2},{3,19},{19,3},{4,20},{20... | collective-permute-start | bytes 442376 | tf_op jit(solution)/shard_map/ppermute | solution.py:668
  (16 other events, 167.6 us)

commit v5 on v4

--- a/solution.py
+++ b/solution.py
@@ -98,7 +98,7 @@
     C, L = x_ref.shape
     N = L // B
     mp, rows, nt = pay_ref.shape
-    kh = rows // C - 2
+    few = rows - 2 * C
     pairs = ((x_hbm, x_ref), (g_hbm, g_ref), (vb_hbm, vb_ref), (gb_hbm, gb_ref))
     moves = [pltpu.make_async_copy(src, dst, sems.at[1 + k]) for k, (src, dst) in enumerate(pairs)]
     for move in moves:
@@ -122,14 +122,16 @@
     bias = jnp.concatenate([vb_ref[...].astype(F32), gb_ref[...].astype(F32), jnp.zeros((1, B - 2 * C), F32)], axis=1)
     stat_ref[2 * N :, :] = jnp.where(own == place_ref[1], bias, 0.0)
     for j in range(mp):
-        pay_ref[j, kh * C : (kh + 1) * C, :] = x_ref[:, j * nt : (j + 1) * nt]
+        pay_ref[j, few : few + C, :] = x_ref[:, j * nt : (j + 1) * nt]
     moves[1].wait()
     for j in range(mp):
-        pay_ref[j, (kh + 1) * C :, :] = g_ref[:, j * nt : (j + 1) * nt]
+        pay_ref[j, few + C :, :] = g_ref[:, j * nt : (j + 1) * nt]
     pltpu.make_async_copy(v_hbm, wt_ref, sems.at[0]).wait()
+    parts = wt_ref.shape[1] // B
     for j in range(mp):
-        for q in range(kh):
-            pay_ref[j, q * C : (q + 1) * C, :] = wt_ref[:, q * nt : (q + 1) * nt]
+        lanes = slice(j % parts * B, (j % parts + 1) * B)
+        for q in range(nt // B):
+            pay_ref[j, 0:few, q * B : (q + 1) * B] = wt_ref[q * few : (q + 1) * few, lanes]
 
 
 def join_stats(parts, N, count):
@@ -227,11 +229,12 @@
                 t_ref[j, h * B : (h + 1) * B, q * B : (q + 1) * B] = v
 
 
-def back_table_kernel(rates_ref, w_ref, t_ref, near_ref, cols, *, C, M):
-    i = pl.program_id(0)
+def back_table_kernel(rates_ref, w_ref, *refs, C, M, start):
+    t_ref, near_ref, cols = refs[-3:]
+    i = pl.program_id(0) + start
     G = t_ref.shape[0]
 
-    @pl.when(i == 0)
+    @pl.when(i == start)
     def _():
         step_size = jnp.exp(rates_ref[0])
         columns((step_size * -jnp.exp(rates_ref[1]), step_size * rates_ref[2], w_ref[...]), cols, C)
@@ -334,16 +337,20 @@
             mixed_ref[n // per, :, (n % per) * B : (n % per + 1) * B] = ms[pl.ds(n, C, stride=N), :].astype(BF16)
 
 
-def glu_kernel(half_ref, in_ref, first_ref, other_ref, bias_ref, gm_ref, keep_ref, send_ref, gp, wt):
+def glu_kernel(place_ref, in_ref, first_ref, bias_ref, *refs, parts):
+    own_refs, other_refs, refs = refs[:parts], refs[parts : 2 * parts], refs[2 * parts :]
+    gm_ref, keep_ref, send_ref, gp, wt = refs
     mp, C, nt = in_ref.shape
     H = mp * C
-    kh = H // nt
-    own = half_ref[0]
+    few = own_refs[0].shape[1]
+    own = place_ref[0]
     mixed = in_ref[...].reshape(H, nt)
-    for q in range(kh):
-        at = slice(q * nt, (q + 1) * nt)
-        wt[own, :, at] = first_ref[:, q * C : (q + 1) * C, :].reshape(H, nt)
-        wt[1 - own, :, at] = other_ref[:, q * C : (q + 1) * C, :].reshape(H, nt)
+    for k in range(parts):
+        lanes = pl.ds(pl.multiple_of((lax.rem(place_ref[1], parts) ^ k) * B, B), B)
+        for q in range(nt // B):
+            at = slice(q * few, (q + 1) * few)
+            wt[own, :, at, lanes] = own_refs[k][:, :, q * B : (q + 1) * B]
+            wt[1 - own, :, at, lanes] = other_refs[k][:, :, q * B : (q + 1) * B]
     step = B
     per = step // C
     bias = jnp.concatenate([bias_ref[...], jnp.zeros((B - mp, B), F32)], axis=0).T
@@ -351,18 +358,19 @@
         lo = s * step
         col_v = jnp.concatenate([bias[0:C, k : k + 1] for k in range(s * per, (s + 1) * per)], axis=0)
         col_g = jnp.concatenate([bias[C : 2 * C, k : k + 1] for k in range(s * per, (s + 1) * per)], axis=0)
-        value = dot(wt[0, lo : lo + step, :], mixed) + col_v
-        gate = dot(wt[1, lo : lo + step, :], mixed) + col_g
+        at = slice(s * per, (s + 1) * per)
+        value = dot(wt[0, at].reshape(step, H), mixed) + col_v
+        gate = dot(wt[1, at].reshape(step, H), mixed) + col_g
         sig = jax.nn.sigmoid(gate)
-        x = first_ref[s * per : (s + 1) * per, kh * C : (kh + 1) * C, :].reshape(step, nt).astype(F32)
-        g = first_ref[s * per : (s + 1) * per, (kh + 1) * C :, :].reshape(step, nt).astype(F32)
+        x = first_ref[at, few : few + C, :].reshape(step, nt).astype(F32)
+        g = first_ref[at, few + C :, :].reshape(step, nt).astype(F32)
         gm_ref[s * per : (s + 1) * per, C:, :] = (x + value * sig).astype(BF16).reshape(per, C, nt)
         gv = g * sig
         gp[0, lo : lo + step, :] = gv.astype(BF16)
         gp[1, lo : lo + step, :] = (gv * value * (1.0 - sig)).astype(BF16)
     for s in range(mp // per):
         at = slice(s * step, (s + 1) * step)
-        gm = dot(wt[0, :, at], gp[0], TN) + dot(wt[1, :, at], gp[1], TN)
+        gm = sum(dot(wt[h, :, :, at].reshape(H, step), gp[h], TN) for h in range(2))
         wide = gm * SQUARE_SCALE
         gm_ref[s * per : (s + 1) * per, 0:C, :] = (wide * jnp.abs(wide)).astype(BF16).reshape(per, C, nt)
     keep_ref[...] = gp[own]
@@ -698,7 +706,7 @@
     M = decay_log.shape[1]
     N = L // B
     nt = L // mp
-    kh = H // nt
+    few_rows = C * B // nt
     shape = jax.ShapeDtypeStruct
 
     place = jnp.stack([lax.axis_index("dp") & 1, lax.axis_index("mp")]).astype(jnp.int32)
@@ -749,7 +757,7 @@
     hbm = pl.BlockSpec(memory_space=pltpu.HBM)
     stat, pay = pl.pallas_call(
         start_kernel,
-        out_shape=(shape((2 * N + mp, B), F32), shape((mp, (2 + kh) * C, nt), BF16)),
+        out_shape=(shape((2 * N + mp, B), F32), shape((mp, few_rows + 2 * C, nt), BF16)),
         in_specs=[SMEM] + [hbm] * 6,
         out_specs=(VMEM, VMEM),
         scratch_shapes=[
@@ -767,6 +775,13 @@
         [jnp.broadcast_to(log_step[:, None], (C, 4 * M)), jnp.tile(decay_log, (1, 4)), jnp.tile(frequency, (1, 4))]
     )
     coef = jnp.concatenate([readout[:, :M], liquid_readout[:, :M], readout[:, M:], liquid_readout[:, M:]], axis=1)
+    count = C
+    for k, offs in enumerate(rounds[::-1]):
+        parts = [stat] + [exchange(stat, "mp", mp, o) for o in offs]
+        if k < len(rounds) - 1:
+            stat = jnp.concatenate(join_stats(parts, N, float(count)), axis=0)
+            count *= len(parts)
+            stat, rates = lax.optimization_barrier((stat, rates))
     f_near, f_tab, t_tab, jump, w_all = by_channel(
         partial(table_kernel, C=C, M=M),
         (
@@ -778,20 +793,12 @@
         6,
         [vm((3, B, B), F32)],
     )(rates, coef)
-
-    count = C
-    for k, offs in enumerate(rounds[::-1]):
-        parts = [stat] + [exchange(stat, "mp", mp, o) for o in offs]
-        if k == 0:
-            parts[1], parts[-1], t_tab = lax.optimization_barrier((parts[1], parts[-1], t_tab))
-        if k < len(rounds) - 1:
-            stat = jnp.concatenate(join_stats(parts, N, float(count)), axis=0)
-            count *= len(parts)
+    parts, t_tab = lax.optimization_barrier((parts, t_tab))
 
     vecs = jnp.stack([norm_gain, norm_bias, skip_gain])
     mixed, slope, state, state_x, stat, bias = by_channel(
         partial(mixer_kernel, count=H, parts=len(parts)),
-        (shape((mp, C, nt), BF16), far_blocks, far_blocks, far_blocks, shape((2, N, B), F32), shape((mp, B), F32)),
+        (shape((mp, C, nt), BF16), far_blocks, far_blocks, far_blocks, far((2, N, B), F32), shape((mp, B), F32)),
         [SMEM, SMEM, whole(C, L)] + [whole(2 * N + mp, B)] * len(parts)
         + [chan(2 * B, 2 * B), chan(3 * B, 2 * B), whole(2, C, B)],
         (whole(mp, C, nt), chan(N, B), chan(N, B), chan(N, B), whole(2, N, B), whole(mp, B)),
@@ -805,24 +812,37 @@
     )(lengths, vecs, tokens, *parts, f_near, t_tab, jump)
 
     mixed, first, rates = lax.optimization_barrier((mixed, first, rates))
-    other_w = partner(first[:, : kh * C, :], dp)
+    own_w = [first[:, :few_rows, :]]
+    own_w += [exchange(own_w[0], "mp", mp, o) for o in rounds[0]]
+    other_w = [partner(v, dp) for v in own_w]
     mixed_tok = lax.all_to_all(mixed, "mp", split_axis=0, concat_axis=0, tiled=True)
-    back_tab, near_tab = by_channel(
-        partial(back_table_kernel, C=C, M=M),
-        (far((C, 2 * B, 4 * B), BF16), far((C, B, 2 * B), BF16)),
-        [whole(3, C, B), whole(C, B)],
-        (few(2 * B, 4 * B), few(B, 2 * B)),
-        7,
-        [vm((3, B, B), F32)],
-    )(rates, w_all)
-    mixed_tok, back_tab = lax.optimization_barrier((mixed_tok, back_tab))
+    half_steps = C // TABLE_GROUP // 2
+
+    def back_tables(held, start, steps):
+        def block(*dims):
+            return pl.BlockSpec((TABLE_GROUP,) + dims, lambda i: (i + start,) + (0,) * len(dims))
+
+        return pl.pallas_call(
+            partial(back_table_kernel, C=C, M=M, start=start),
+            grid=(steps,),
+            out_shape=(far((C, 2 * B, 4 * B), BF16), far((C, B, 2 * B), BF16)),
+            in_specs=[whole(3, C, B), whole(C, B)] + [hbm] * len(held),
+            out_specs=(block(2 * B, 4 * B), block(B, 2 * B)),
+            scratch_shapes=[vm((3, B, B), F32)],
+            input_output_aliases={2 + k: k for k in range(len(held))},
+            compiler_params=params(small),
+            cost_estimate=cost(4),
+        )(rates, w_all, *[pin(v) for v in held])
+
+    tables = back_tables([], 0, half_steps)
+    mixed_tok, tables = lax.optimization_barrier((mixed_tok, tables))
     gm, keep, send = call(
-        glu_kernel,
+        partial(glu_kernel, parts=len(own_w)),
         (shape((mp, 2 * C, nt), BF16),) + (shape((H, nt), BF16),) * 2,
-        5, 1, 2, [vm((2, H, nt), BF16), vm((2, H, H), BF16)],
-    )(place, mixed_tok, first, other_w, bias)
+        4 + 2 * len(own_w), 1, 2, [vm((2, H, nt), BF16), vm((2, mp, C, H), BF16)],
+    )(place, mixed_tok, first, bias, *own_w, *other_w)
     mixed_tok = mixed_tok.reshape(H, nt)
-    gm, f_tab = lax.optimization_barrier((gm, f_tab))
+    gm, f_tab, rates = lax.optimization_barrier((gm, f_tab, rates))
     gm = lax.all_to_all(gm, "mp", split_axis=0, concat_axis=0, tiled=True)
     u_rev, lift = by_channel(
         partial(lift_kernel, count=H),
@@ -833,7 +853,8 @@
         [vm((N * C, B), F32), vm((3, N, B), F32)],
         56,
     )(lengths, vecs, tokens, stat, pin(f_tab))
-    gm, lift = lax.optimization_barrier((gm, lift))
+    back_tab, near_tab = back_tables(tables, half_steps, half_steps)
+    gm, lift, back_tab = lax.optimization_barrier((gm, lift, back_tab))
 
     ways = len(rounds[0]) + 1
     rows_left = mp // ways

time: 107 us -> 103 us (0.963)
  waiting for transfers between devices: 14.5 us -> 5.44 us
  starting transfers between devices: 43.5 us -> 48.1 us
  Pallas kernels: 45.4 us -> 46.8 us
    ppermute x17 -> x20, starting transfers between devices: 23.6 us -> 28.3 us  [exchange(): return lax.ppermute(v, axis, [(k, k ^ off) for k in range(size)])]
    ppermute x17 -> x20, waiting for transfers between devices: 5.94 us -> 1.38 us  [exchange(): return lax.ppermute(v, axis, [(k, k ^ off) for k in range(size)])]
    all_to_all x1, waiting for transfers between devices: 5.22 us -> 0.76 us  [per_device(): gm = lax.all_to_all(gm, 'mp', split_axis=0, concat_axis=0, tiled=True)]
    all_to_all x1, waiting for transfers between devices: 2.12 us -> 0.18 us  [per_device(): first = lax.all_to_all(pay, 'mp', split_axis=0, concat_axis=0, tiled=True)]
    all_to_all x1, starting transfers between devices: 5.71 us -> 3.79 us  [per_device(): gm = lax.all_to_all(gm, 'mp', split_axis=0, concat_axis=0, tiled=True)]
    all_to_all x1, waiting for transfers between devices: 1.21 us -> 3.1 us  [per_device(): lax.all_to_all(mixed, 'mp', split_axis=0, concat_axis=0, tiled=True)]
    pallas_call x2 -> x3, Pallas kernels: 9.49 us -> 11.1 us  [the longest x2 8.63 us: back_tables(): pl.pallas_call(partial(back_table_kernel, C=C, M=M, start=start), grid=(s...]
    ppermute x5 -> x8, starting transfers between devices: 1.27 us -> 2.27 us  [partner(): return lax.ppermute(v, 'dp', [(q, q ^ 1) for q in range(size)])]
  transfers between devices with their start and end apart: 25 -> 31, of which waited for: 8 -> 6; matrix products, arithmetic and copies ran while one was open for 1% -> 1% of each run, Pallas kernels for 36% -> 39%
where the time goes in v5:
time: 103 us
  starting transfers between devices  48.1 us (47%)
  Pallas kernels  46.8 us (45%)
  waiting for transfers between devices  5.44 us (5%)
  between operations  1.84 us (2%)
    ppermute x20, starting transfers between devices, exchange(): return lax.ppermute(v, axis, [(k, k ^ off) for k in range(size)])  28.3 us
    pallas_call x2, Pallas kernels, back_tables(): pl.pallas_call(partial(back_table_kernel, C=C, M=M, start=start), grid=(s...  8.63 us
    pallas_call x1, Pallas kernels, per_device(): by_channel(partial(back_kernel, count=H), (shape((C, L), BF16), shape((C,...  7.5 us
    all_to_all x1, starting transfers between devices, per_device(): first = lax.all_to_all(pay, 'mp', split_axis=0, concat_axis=0, tiled=True)  7.01 us
    all_to_all x1, starting transfers between devices, per_device(): lax.all_to_all(mixed, 'mp', split_axis=0, concat_axis=0, tiled=True)  6.74 us
    pallas_call x1, Pallas kernels, per_device(): by_channel(partial(table_kernel, C=C, M=M), (shape((C, 2 * B, 2 * B), BF1...  6.24 us
    pallas_call x1, Pallas kernels, per_device(): by_channel(partial(mixer_kernel, count=H, parts=len(parts)), (shape((mp,...  5.27 us
    pallas_call x1, Pallas kernels, per_device(): by_channel(partial(lift_kernel, count=H), (far((C, 3 * N, 2 * B), BF16),...  4.91 us
  transfers between devices with their start and end apart: 31, of which 6 were waited for; matrix products, arithmetic and copies ran while one was open for 1% of the time, Pallas kernels for 39%

profile of v5, /device:TPU:0, one launch (start us, length us, event | category | flops | bytes accessed | tf_op | source)
XLA Modules:
  0.0 102.8 jit_solution(10317158664185575012)
XLA Ops:
  0.8 2.7 %shard_map.254 = (f32[80,128]{1,0:T(8,128)S(1)}, bf16[16,80,256]{2,1,0:T(8,128)(2,1)}) custom-call(s32[2]{0:T(128)S(1)} %pad_add_fusion.place_ref, bf16[32,4096]{1,0:T(8,128)(2,1)} %x_ref.7, bf16[32,4096]{1,0:T(8,128)(2,1)} %g_ref.1, bf16[32,512]{1,0:T(8,128)(2,1)} %bitcast.25, bf16[32,512]{1,0:T(8,128)(2,1)} %bitcast.26, bf16[1,32]{1,0:T(2,128)(2,1)} %bitcast.27, ...), custom_call_target="tpu_custom_call" | custom-call | flops 3000000000 | bytes 3000000 | tf_op jit(solution)/shard_map/pallas_call | solution.py:758
  3.5 5.1 %collective-permute-start.2 = (f32[80,128]{1,0:T(8,128)S(1)}, f32[80,128]{1,0:T(8,128)S(1)}, u32[]{:S(2)}, u32[]{:S(2)}) collective-permute-start(f32[80,128]{1,0:T(8,128)S(1)} %get-tuple-element.94), channel_id=1, source_target_pairs={{0,12},{1,13},{2,14},{3,15},{4,8},{5,9},{6,10},{7,11},{8,4},{9,5},... | collective-permute-start | bytes 122888 | tf_op jit(solution)/shard_map/ppermute | solution.py:659
  9.2 7.0 %all-to-all-start = ((bf16[16,80,256]{2,1,0:T(8,128)(2,1)}), bf16[16,80,256]{2,1,0:T(8,128)(2,1)S(1)}, u32[]{:S(2)}, u32[]{:S(2)}) async-start(bf16[16,80,256]{2,1,0:T(8,128)(2,1)} %get-tuple-element.107), calls=%async_computation | async-start | bytes 1310720 | tf_op jit(solution)/shard_map/all_to_all | solution.py:772
  17.5 2.0 %collective-permute-start.3 = (f32[80,128]{1,0:T(8,128)S(1)}, f32[80,128]{1,0:T(8,128)S(1)}, u32[]{:S(2)}, u32[]{:S(2)}) collective-permute-start(f32[80,128]{1,0:T(8,128)S(1)} %pad_maximum_fusion.1.refs_0_), channel_id=1, source_target_pairs={{0,1},{1,0},{2,3},{3,2},{4,5},{5,4},{6,7},{7,6},{8,9},{9,8},{10,11... | collective-permute-start | bytes 122888 | tf_op jit(solution)/shard_map/ppermute | solution.py:659
  21.1 6.2 %shard_map.255 = (bf16[32,256,256]{2,1,0:T(8,128)(2,1)S(1)}, bf16[32,256,256]{2,1,0:T(8,128)(2,1)}, bf16[32,384,256]{2,1,0:T(8,128)(2,1)S(1)}, f32[2,32,128]{2,1,0:T(8,128)S(1)}, f32[32,128]{1,0:T(8,128)S(1)}) custom-call(f32[3,32,128]{2,1,0:T(8,128)S(1)} %pad_maximum_fusion.rates_ref, f32[32,128]{1,0:T(8,128)S(1)} %pad_maximum_fusion.2.coef_ref), custom_call_target="tpu_custom_call" | custom-call | flops 6000000000 | bytes 6000000 | tf_op jit(solution)/shard_map/pallas_call | solution.py:785
  27.4 5.3 %shard_map.256 = (bf16[16,32,256]{2,1,0:T(8,128)(2,1)}, f32[32,32,128]{2,1,0:T(8,128)}, f32[32,32,128]{2,1,0:T(8,128)}, f32[32,32,128]{2,1,0:T(8,128)}, f32[2,32,128]{2,1,0:T(8,128)}, /*index=5*/f32[16,128]{1,0:T(8,128)S(1)}) custom-call(s32[1]{0:T(128)S(6)} %copy.33.len_ref, f32[3,32]{1,0:T(4,128)S(1)} %pad_maximum_fusion.3.vec_ref, ...), custom_call_target="tpu_custom_call" | custom-call | flops 6000000000 | bytes 6000000 | tf_op jit(solution)/shard_map/pallas_call | solution.py:799
  32.8 1.8 %collective-permute-start.6 = (bf16[16,16,256]{2,1,0:T(8,128)(2,1)S(1)}, bf16[16,16,256]{2,1,0:T(8,128)(2,1)S(1)}, u32[]{:S(2)}, u32[]{:S(2)}) collective-permute-start(bf16[16,16,256]{2,1,0:T(8,128)(2,1)S(1)} %slice.75.refs_0_), channel_id=1, source_target_pairs={{0,1},{1,0},{2,3},{3,2},{4,5},{5,4},{6,7},{7,6},{8,9},{9,8},{10,11... | collective-permute-start | bytes 393224 | tf_op jit(solution)/shard_map/ppermute | solution.py:659
  36.4 6.7 %all-to-all-start.1 = ((bf16[16,32,256]{2,1,0:T(8,128)(2,1)}), bf16[16,32,256]{2,1,0:T(8,128)(2,1)S(1)}, u32[]{:S(2)}, u32[]{:S(2)}) async-start(bf16[16,32,256]{2,1,0:T(8,128)(2,1)} %get-tuple-element.108), calls=%async_computation.1 | async-start | bytes 524288 | tf_op jit(solution)/shard_map/all_to_all | solution.py:818
  44.2 4.3 %shard_map.257 = (bf16[32,256,512]{2,1,0:T(8,128)(2,1)}, bf16[32,128,256]{2,1,0:T(8,128)(2,1)}) custom-call(f32[3,32,128]{2,1,0:T(8,128)S(1)} %pad_maximum_fusion.rates_ref, f32[32,128]{1,0:T(8,128)S(1)} %get-tuple-element.110.w_ref), custom_call_target="tpu_custom_call" | custom-call | flops 4000000000 | bytes 4000000 | tf_op jit(solution)/shard_map/pallas_call | solution.py:825
  48.5 3.1 %all-to-all-done.1.in_ref = bf16[16,32,256]{2,1,0:T(8,128)(2,1)S(1)} async-done(((bf16[16,32,256]{2,1,0:T(8,128)(2,1)}), bf16[16,32,256]{2,1,0:T(8,128)(2,1)S(1)}, u32[]{:S(2)}, u32[]{:S(2)}) %all-to-all-start.1) | async-done | bytes 262176 | tf_op jit(solution)/shard_map/all_to_all | solution.py:818
  51.7 2.4 %shard_map.258 = (bf16[16,64,256]{2,1,0:T(8,128)(2,1)}, bf16[512,256]{1,0:T(8,128)(2,1)S(1)}, bf16[512,256]{1,0:T(8,128)(2,1)S(1)}) custom-call(s32[2]{0:T(128)S(1)} %pad_add_fusion.place_ref, bf16[16,32,256]{2,1,0:T(8,128)(2,1)S(1)} %all-to-all-done.1.in_ref, bf16[16,80,256]{2,1,0:T(8,128)(2,1)S(1)} %all-to-all-done.first_ref, ...), custom_call_target="tpu_custom_call" | custom-call | flops 2000000000 | bytes 2000000 | tf_op jit(solution)/shard_map/pallas_call | solution.py:839
  54.1 3.8 %all-to-all-start.2 = ((bf16[16,64,256]{2,1,0:T(8,128)(2,1)}), bf16[16,64,256]{2,1,0:T(8,128)(2,1)S(1)}, u32[]{:S(2)}, u32[]{:S(2)}) async-start(bf16[16,64,256]{2,1,0:T(8,128)(2,1)} %get-tuple-element.118), calls=%async_computation.2 | async-start | bytes 1048576 | tf_op jit(solution)/shard_map/all_to_all | solution.py:846
  58.5 4.3 %shard_map.260 = (bf16[32,256,512]{2,1,0:T(8,128)(2,1)}, bf16[32,128,256]{2,1,0:T(8,128)(2,1)}) custom-call(f32[3,32,128]{2,1,0:T(8,128)S(1)} %pad_maximum_fusion.rates_ref, f32[32,128]{1,0:T(8,128)S(1)} %get-tuple-element.110.w_ref, bf16[32,256,512]{2,1,0:T(8,128)(2,1)} %get-tuple-element.122.refs_0_, ...), custom_call_target="tpu_custom_call", output_to_operand_aliasing={{0}: (2, {}), {1}: (3, {})} | custom-call | flops 4000000000 | bytes 4000000 | tf_op jit(solution)/shard_map/pallas_call | solution.py:825
  62.8 4.9 %shard_map.259 = (bf16[32,96,256]{2,1,0:T(8,128)(2,1)}, f32[32,32,128]{2,1,0:T(8,128)}) custom-call(s32[1]{0:T(128)S(6)} %copy.33.len_ref, f32[3,32]{1,0:T(4,128)} %copy-done.4, bf16[32,4096]{1,0:T(8,128)(2,1)} %x_ref.7, f32[2,32,128]{2,1,0:T(8,128)} %get-tuple-element.105.stat_ref, bf16[32,256,256]{2,1,0:T(8,128)(2,1)} %get-tuple-element.119.f_ref), custom_call_target="tpu_custom_call" | custom-call | flops 3000000000 | bytes 3000000 | tf_op jit(solution)/shard_map/pallas_call | solution.py:847
  68.9 2.0 %collective-permute-start.18 = (f32[136,512]{1,0:T(8,128)S(1)}, f32[136,512]{1,0:T(8,128)S(1)}, u32[]{:S(2)}, u32[]{:S(2)}) collective-permute-start(f32[136,512]{1,0:T(8,128)S(1)} %get-tuple-element.138), channel_id=1, source_target_pairs={{0,1},{1,0},{2,3},{3,2},{4,5},{5,4},{6,7},{7,6},{8,9},{9,8},{10,11... | collective-permute-start | bytes 835592 | tf_op jit(solution)/shard_map/ppermute | solution.py:659
  70.8 1.5 %collective-permute-start.19 = (f32[136,512]{1,0:T(8,128)S(1)}, f32[136,512]{1,0:T(8,128)S(1)}, u32[]{:S(2)}, u32[]{:S(2)}) collective-permute-start(f32[136,512]{1,0:T(8,128)S(1)} %get-tuple-element.139), channel_id=1, source_target_pairs={{0,2},{1,3},{2,0},{3,1},{4,6},{5,7},{6,4},{7,5},{8,10},{9,11},{10,... | collective-permute-start | bytes 835592 | tf_op jit(solution)/shard_map/ppermute | solution.py:659
  73.2 7.5 %shard_map.261 = (bf16[32,4096]{1,0:T(8,128)(2,1)}, f32[32,4096]{1,0:T(8,128)S(1)}, f32[2,32,128]{2,1,0:T(8,128)S(1)}, f32[32,24,128]{2,1,0:T(8,128)S(1)}, f32[3...) custom-call(s32[1]{0:T(128)S(6)} %copy.33.len_ref, ...), custom_call_target="tpu_custom_call" | custom-call | flops 7000000000 | bytes 7000000 | tf_op jit(solution)/shard_map/pallas_call | solution.py:867
  80.7 3.0 %collective-permute-start.15 = (f32[2,32,128]{2,1,0:T(8,128)S(1)}, f32[2,32,128]{2,1,0:T(8,128)S(1)}, u32[]{:S(2)}, u32[]{:S(2)}) collective-permute-start(f32[2,32,128]{2,1,0:T(8,128)S(1)} %get-tuple-element.132), channel_id=1, source_target_pairs={{0,12},{1,13},{2,14},{3,15},{4,8},{5,9},{6,10},{7,11},{8,4},{9,5},... | collective-permute-start | bytes 98312 | tf_op jit(solution)/shard_map/ppermute | solution.py:659
  86.0 1.5 %collective-permute-start.21 = (f32[72,512]{1,0:T(8,128)S(1)}, f32[72,512]{1,0:T(8,128)S(1)}, u32[]{:S(2)}, u32[]{:S(2)}) collective-permute-start(f32[72,512]{1,0:T(8,128)S(1)} %get-tuple-element.142), channel_id=1, source_target_pairs={{0,4},{1,5},{2,6},{3,7},{4,0},{5,1},{6,2},{7,3},{8,12},{9,13},{10,... | collective-permute-start | bytes 442376 | tf_op jit(solution)/shard_map/ppermute | solution.py:659
  88.6 1.6 %collective-permute-start.22 = (f32[2,32,128]{2,1,0:T(8,128)S(1)}, f32[2,32,128]{2,1,0:T(8,128)S(1)}, u32[]{:S(2)}, u32[]{:S(2)}) collective-permute-start(f32[2,32,128]{2,1,0:T(8,128)S(1)} %add_add_fusion.1), channel_id=1, source_target_pairs={{0,1},{1,0},{2,3},{3,2},{4,5},{5,4},{6,7},{7,6},{8,9},{9,8},{10,11... | collective-permute-start | bytes 98312 | tf_op jit(solution)/shard_map/ppermute | solution.py:659
  90.2 1.5 %collective-permute-start.23 = (f32[2,32,128]{2,1,0:T(8,128)S(1)}, f32[2,32,128]{2,1,0:T(8,128)S(1)}, u32[]{:S(2)}, u32[]{:S(2)}) collective-permute-start(f32[2,32,128]{2,1,0:T(8,128)S(1)} %add_add_fusion.1), channel_id=1, source_target_pairs={{0,2},{1,3},{2,0},{3,1},{4,6},{5,7},{6,4},{7,5},{8,10},{9,11},{10,... | collective-permute-start | bytes 98312 | tf_op jit(solution)/shard_map/ppermute | solution.py:659
  92.7 2.3 %collective-permute-start.25 = (f32[40,512]{1,0:T(8,128)S(1)}, f32[40,512]{1,0:T(8,128)S(1)}, u32[]{:S(2)}, u32[]{:S(2)}) collective-permute-start(f32[40,512]{1,0:T(8,128)S(1)} %get-tuple-element.154), channel_id=1, source_target_pairs={{0,8},{1,9},{2,10},{3,11},{4,12},{5,13},{6,14},{7,15},{8,0},{9,1},... | collective-permute-start | bytes 245768 | tf_op jit(solution)/shard_map/ppermute | solution.py:659
  95.1 3.8 %shard_map.265.ref = f32[32,40,128]{2,1,0:T(8,128)S(1)} custom-call(bf16[32,96,256]{2,1,0:T(8,128)(2,1)} %get-tuple-element.145.u_ref, f32[32,32,128]{2,1,0:T(8,128)} %get-tuple-element.146.lift_ref, f32[32,32,128]{2,1,0:T(8,128)S(1)} %get-tuple-element.147.g_ref, f32[32,32,128]{2,1,0:T(8,128)S(1)} %get-tuple-element.148.p_ref, ...), custom_call_target="tpu_custom_call" | custom-call | flops 20000000000 | bytes 20000000 | tf_op jit(solution)/shard_map/pallas_call | solution.py:901
  100.9 1.8 %shard_map.269 = (f32[32,512]{1,0:T(8,128)}, f32[32,512]{1,0:T(8,128)}, f32[1,32]{1,0:T(1,128)}, f32[1,32]{1,0:T(1,128)}, f32[1,32]{1,0:T(1,128)}, /*index=5*/f3...) custom-call(s32[2]{0:T(128)S(1)} %pad_add_fusion.place_ref, ...), custom_call_target="tpu_custom_call" | custom-call | flops 1000000000 | bytes 1000000 | tf_op jit(solution)/shard_map/pallas_call | solution.py:925
  (98 shorter events, 14.9 us)
Async XLA Ops:
  3.5 14.0 %collective-permute-start.2 = (f32[80,128]{1,0:T(8,128)S(1)}, f32[80,128]{1,0:T(8,128)S(1)}, u32[]{:S(2)}, u32[]{:S(2)}) collective-permute-start(f32[80,128]{1,0:T(8,128)S(1)} %get-tuple-element.94), channel_id=1, source_target_pairs={{0,12},{1,13},{2,14},{3,15},{4,8},{5,9},{6,10},{7,11},{8,4},{9,5},... | collective-permute-start | bytes 122888 | tf_op jit(solution)/shard_map/ppermute | solution.py:659
  8.6 8.9 %collective-permute-start.1 = (f32[80,128]{1,0:T(8,128)S(1)}, f32[80,128]{1,0:T(8,128)S(1)}, u32[]{:S(2)}, u32[]{:S(2)}) collective-permute-start(f32[80,128]{1,0:T(8,128)S(1)} %get-tuple-element.94), channel_id=1, source_target_pairs={{0,8},{1,9},{2,10},{3,11},{4,12},{5,13},{6,14},{7,15},{8,0},{9,1},... | collective-permute-start | bytes 122888 | tf_op jit(solution)/shard_map/ppermute | solution.py:659
  8.6 8.9 %collective-permute-start = (f32[80,128]{1,0:T(8,128)S(1)}, f32[80,128]{1,0:T(8,128)S(1)}, u32[]{:S(2)}, u32[]{:S(2)}) collective-permute-start(f32[80,128]{1,0:T(8,128)S(1)} %get-tuple-element.94), channel_id=1, source_target_pairs={{0,4},{1,5},{2,6},{3,7},{4,0},{5,1},{6,2},{7,3},{8,12},{9,13},{10,... | collective-permute-start | bytes 122888 | tf_op jit(solution)/shard_map/ppermute | solution.py:659
  9.2 23.6 %all-to-all-start = ((bf16[16,80,256]{2,1,0:T(8,128)(2,1)}), bf16[16,80,256]{2,1,0:T(8,128)(2,1)S(1)}, u32[]{:S(2)}, u32[]{:S(2)}) async-start(bf16[16,80,256]{2,1,0:T(8,128)(2,1)} %get-tuple-element.107), calls=%async_computation | async-start | bytes 1310720 | tf_op jit(solution)/shard_map/all_to_all | solution.py:772
  17.5 9.8 %collective-permute-start.3 = (f32[80,128]{1,0:T(8,128)S(1)}, f32[80,128]{1,0:T(8,128)S(1)}, u32[]{:S(2)}, u32[]{:S(2)}) collective-permute-start(f32[80,128]{1,0:T(8,128)S(1)} %pad_maximum_fusion.1.refs_0_), channel_id=1, source_target_pairs={{0,1},{1,0},{2,3},{3,2},{4,5},{5,4},{6,7},{7,6},{8,9},{9,8},{10,11... | collective-permute-start | bytes 122888 | tf_op jit(solution)/shard_map/ppermute | solution.py:659
  19.5 7.8 %collective-permute-start.4 = (f32[80,128]{1,0:T(8,128)S(1)}, f32[80,128]{1,0:T(8,128)S(1)}, u32[]{:S(2)}, u32[]{:S(2)}) collective-permute-start(f32[80,128]{1,0:T(8,128)S(1)} %pad_maximum_fusion.1.refs_0_), channel_id=1, source_target_pairs={{0,2},{1,3},{2,0},{3,1},{4,6},{5,7},{6,4},{7,5},{8,10},{9,11},{10,... | collective-permute-start | bytes 122888 | tf_op jit(solution)/shard_map/ppermute | solution.py:659
  32.8 10.4 %collective-permute-start.6 = (bf16[16,16,256]{2,1,0:T(8,128)(2,1)S(1)}, bf16[16,16,256]{2,1,0:T(8,128)(2,1)S(1)}, u32[]{:S(2)}, u32[]{:S(2)}) collective-permute-start(bf16[16,16,256]{2,1,0:T(8,128)(2,1)S(1)} %slice.75.refs_0_), channel_id=1, source_target_pairs={{0,1},{1,0},{2,3},{3,2},{4,5},{5,4},{6,7},{7,6},{8,9},{9,8},{10,11... | collective-permute-start | bytes 393224 | tf_op jit(solution)/shard_map/ppermute | solution.py:659
  34.6 9.1 %collective-permute-start.7 = (bf16[16,16,256]{2,1,0:T(8,128)(2,1)S(1)}, bf16[16,16,256]{2,1,0:T(8,128)(2,1)S(1)}, u32[]{:S(2)}, u32[]{:S(2)}) collective-permute-start(bf16[16,16,256]{2,1,0:T(8,128)(2,1)S(1)} %slice.75.refs_0_), channel_id=1, source_target_pairs={{0,2},{1,3},{2,0},{3,1},{4,6},{5,7},{6,4},{7,5},{8,10},{9,11},{10,... | collective-permute-start | bytes 393224 | tf_op jit(solution)/shard_map/ppermute | solution.py:659
  36.1 7.7 %collective-permute-start.8 = (bf16[16,16,256]{2,1,0:T(8,128)(2,1)S(1)}, bf16[16,16,256]{2,1,0:T(8,128)(2,1)S(1)}, u32[]{:S(2)}, u32[]{:S(2)}) collective-permute-start(bf16[16,16,256]{2,1,0:T(8,128)(2,1)S(1)} %slice.75.refs_0_), channel_id=1, source_target_pairs={{0,3},{1,2},{2,1},{3,0},{4,7},{5,6},{6,5},{7,4},{8,11},{9,10},{10,... | collective-permute-start | bytes 393224 | tf_op jit(solution)/shard_map/ppermute | solution.py:659
  36.4 15.2 %all-to-all-start.1 = ((bf16[16,32,256]{2,1,0:T(8,128)(2,1)}), bf16[16,32,256]{2,1,0:T(8,128)(2,1)S(1)}, u32[]{:S(2)}, u32[]{:S(2)}) async-start(bf16[16,32,256]{2,1,0:T(8,128)(2,1)} %get-tuple-element.108), calls=%async_computation.1 | async-start | bytes 524288 | tf_op jit(solution)/shard_map/all_to_all | solution.py:818
  43.1 8.5 %collective-permute-start.9 = (bf16[16,16,256]{2,1,0:T(8,128)(2,1)S(1)}, bf16[16,16,256]{2,1,0:T(8,128)(2,1)S(1)}, u32[]{:S(2)}, u32[]{:S(2)}) collective-permute-start(bf16[16,16,256]{2,1,0:T(8,128)(2,1)S(1)} %slice.75.refs_0_), channel_id=1, source_target_pairs={{0,16},{16,0},{1,17},{17,1},{2,18},{18,2},{3,19},{19,3},{4,20},{20... | collective-permute-start | bytes 393224 | tf_op jit(solution)/shard_map/ppermute | solution.py:676
  43.2 8.4 %collective-permute-start.10 = (bf16[16,16,256]{2,1,0:T(8,128)(2,1)S(1)}, bf16[16,16,256]{2,1,0:T(8,128)(2,1)S(1)}, u32[]{:S(2)}, u32[]{:S(2)}) collective-permute-start(bf16[16,16,256]{2,1,0:T(8,128)(2,1)S(1)} %collective-permute-done.6.refs_1_), channel_id=1, source_target_pairs={{0,16},{16,0},{1,17},{17,1},{2,18},{18,2},{3,19},{19,3},{4,20},{20... | collective-permute-start | bytes 393224 | tf_op jit(solution)/shard_map/ppermute | solution.py:676
  43.7 7.9 %collective-permute-start.11 = (bf16[16,16,256]{2,1,0:T(8,128)(2,1)S(1)}, bf16[16,16,256]{2,1,0:T(8,128)(2,1)S(1)}, u32[]{:S(2)}, u32[]{:S(2)}) collective-permute-start(bf16[16,16,256]{2,1,0:T(8,128)(2,1)S(1)} %collective-permute-done.7.refs_2_), channel_id=1, source_target_pairs={{0,16},{16,0},{1,17},{17,1},{2,18},{18,2},{3,19},{19,3},{4,20},{20... | collective-permute-start | bytes 393224 | tf_op jit(solution)/shard_map/ppermute | solution.py:676
  43.8 7.8 %collective-permute-start.12 = (bf16[16,16,256]{2,1,0:T(8,128)(2,1)S(1)}, bf16[16,16,256]{2,1,0:T(8,128)(2,1)S(1)}, u32[]{:S(2)}, u32[]{:S(2)}) collective-permute-start(bf16[16,16,256]{2,1,0:T(8,128)(2,1)S(1)} %collective-permute-done.8.refs_3_), channel_id=1, source_target_pairs={{0,16},{16,0},{1,17},{17,1},{2,18},{18,2},{3,19},{19,3},{4,20},{20... | collective-permute-start | bytes 393224 | tf_op jit(solution)/shard_map/ppermute | solution.py:676
  54.1 19.1 %all-to-all-start.2 = ((bf16[16,64,256]{2,1,0:T(8,128)(2,1)}), bf16[16,64,256]{2,1,0:T(8,128)(2,1)S(1)}, u32[]{:S(2)}, u32[]{:S(2)}) async-start(bf16[16,64,256]{2,1,0:T(8,128)(2,1)} %get-tuple-element.118), calls=%async_computation.2 | async-start | bytes 1048576 | tf_op jit(solution)/shard_map/all_to_all | solution.py:846
  57.9 9.8 %collective-permute-start.16 = (bf16[512,256]{1,0:T(8,128)(2,1)S(1)}, bf16[512,256]{1,0:T(8,128)(2,1)S(1)}, u32[]{:S(2)}, u32[]{:S(2)}) collective-permute-start(bf16[512,256]{1,0:T(8,128)(2,1)S(1)} %get-tuple-element.134), channel_id=1, source_target_pairs={{0,16},{16,0},{1,17},{17,1},{2,18},{18,2},{3,19},{19,3},{4,20},{20... | collective-permute-start | bytes 786440 | tf_op jit(solution)/shard_map/ppermute | solution.py:676
  58.0 9.8 %collective-permute-start.17 = (bf16[512,256]{1,0:T(8,128)(2,1)S(1)}, bf16[512,256]{1,0:T(8,128)(2,1)S(1)}, u32[]{:S(2)}, u32[]{:S(2)}) collective-permute-start(bf16[512,256]{1,0:T(8,128)(2,1)S(1)} %bitcast.19), channel_id=1, source_target_pairs={{0,16},{16,0},{1,17},{17,1},{2,18},{18,2},{3,19},{19,3},{4,20},{20... | collective-permute-start | bytes 786440 | tf_op jit(solution)/shard_map/ppermute | solution.py:676
  68.9 14.9 %collective-permute-start.18 = (f32[136,512]{1,0:T(8,128)S(1)}, f32[136,512]{1,0:T(8,128)S(1)}, u32[]{:S(2)}, u32[]{:S(2)}) collective-permute-start(f32[136,512]{1,0:T(8,128)S(1)} %get-tuple-element.138), channel_id=1, source_target_pairs={{0,1},{1,0},{2,3},{3,2},{4,5},{5,4},{6,7},{7,6},{8,9},{9,8},{10,11... | collective-permute-start | bytes 835592 | tf_op jit(solution)/shard_map/ppermute | solution.py:659
  70.8 14.3 %collective-permute-start.19 = (f32[136,512]{1,0:T(8,128)S(1)}, f32[136,512]{1,0:T(8,128)S(1)}, u32[]{:S(2)}, u32[]{:S(2)}) collective-permute-start(f32[136,512]{1,0:T(8,128)S(1)} %get-tuple-element.139), channel_id=1, source_target_pairs={{0,2},{1,3},{2,0},{3,1},{4,6},{5,7},{6,4},{7,5},{8,10},{9,11},{10,... | collective-permute-start | bytes 835592 | tf_op jit(solution)/shard_map/ppermute | solution.py:659
  72.3 13.1 %collective-permute-start.20 = (f32[136,512]{1,0:T(8,128)S(1)}, f32[136,512]{1,0:T(8,128)S(1)}, u32[]{:S(2)}, u32[]{:S(2)}) collective-permute-start(f32[136,512]{1,0:T(8,128)S(1)} %get-tuple-element.140), channel_id=1, source_target_pairs={{0,3},{1,2},{2,1},{3,0},{4,7},{5,6},{6,5},{7,4},{8,11},{9,10},{10,... | collective-permute-start | bytes 835592 | tf_op jit(solution)/shard_map/ppermute | solution.py:659
  80.7 6.8 %collective-permute-start.15 = (f32[2,32,128]{2,1,0:T(8,128)S(1)}, f32[2,32,128]{2,1,0:T(8,128)S(1)}, u32[]{:S(2)}, u32[]{:S(2)}) collective-permute-start(f32[2,32,128]{2,1,0:T(8,128)S(1)} %get-tuple-element.132), channel_id=1, source_target_pairs={{0,12},{1,13},{2,14},{3,15},{4,8},{5,9},{6,10},{7,11},{8,4},{9,5},... | collective-permute-start | bytes 98312 | tf_op jit(solution)/shard_map/ppermute | solution.py:659
  88.6 10.3 %collective-permute-start.22 = (f32[2,32,128]{2,1,0:T(8,128)S(1)}, f32[2,32,128]{2,1,0:T(8,128)S(1)}, u32[]{:S(2)}, u32[]{:S(2)}) collective-permute-start(f32[2,32,128]{2,1,0:T(8,128)S(1)} %add_add_fusion.1), channel_id=1, source_target_pairs={{0,1},{1,0},{2,3},{3,2},{4,5},{5,4},{6,7},{7,6},{8,9},{9,8},{10,11... | collective-permute-start | bytes 98312 | tf_op jit(solution)/shard_map/ppermute | solution.py:659
  90.2 8.7 %collective-permute-start.23 = (f32[2,32,128]{2,1,0:T(8,128)S(1)}, f32[2,32,128]{2,1,0:T(8,128)S(1)}, u32[]{:S(2)}, u32[]{:S(2)}) collective-permute-start(f32[2,32,128]{2,1,0:T(8,128)S(1)} %add_add_fusion.1), channel_id=1, source_target_pairs={{0,2},{1,3},{2,0},{3,1},{4,6},{5,7},{6,4},{7,5},{8,10},{9,11},{10,... | collective-permute-start | bytes 98312 | tf_op jit(solution)/shard_map/ppermute | solution.py:659
  91.7 7.2 %collective-permute-start.24 = (f32[2,32,128]{2,1,0:T(8,128)S(1)}, f32[2,32,128]{2,1,0:T(8,128)S(1)}, u32[]{:S(2)}, u32[]{:S(2)}) collective-permute-start(f32[2,32,128]{2,1,0:T(8,128)S(1)} %add_add_fusion.1), channel_id=1, source_target_pairs={{0,3},{1,2},{2,1},{3,0},{4,7},{5,6},{6,5},{7,4},{8,11},{9,10},{10,... | collective-permute-start | bytes 98312 | tf_op jit(solution)/shard_map/ppermute | solution.py:659
  (21 other events, 196.1 us)

commit v6 on v5

--- a/solution.py
+++ b/solution.py
@@ -140,30 +140,29 @@
     return mean, spread, sum(p[2 * N :] for p in parts)
 
 
-def columns(arrays, cols, C):
+def columns(re, im, turn, w, cols, C):
+    sin, cos = turn
+    group = lane_iota(re.shape) // (B // 4)
+    packed = jnp.where(group == 0, re, jnp.where(group == 1, im, jnp.where(group == 2, cos, sin)))
     pad = jnp.zeros((B - C, B), F32)
-    for q, v in enumerate(arrays):
+    for q, v in enumerate((packed, w)):
         cols[q] = jnp.concatenate([v, pad], axis=0).T
 
 
 def channel_waves(cols, i, M, G):
     back = (B - i * G) % B
-    al = pltpu.roll(cols[0, 0:M, :], back, 1)
-    om = pltpu.roll(cols[1, 0:M, :], back, 1)
-    ww = 2.0 * pltpu.roll(cols[2], back, 1)
+    pp = pltpu.roll(cols[0], back, 1)
+    ww = 2.0 * pltpu.roll(cols[1], back, 1)
     place = lane_iota((M, B)).astype(F32)
     ahead = float(B) - place
     out = []
     for j in range(G):
-        a = jnp.broadcast_to(al[:, j : j + 1], (M, B))
-        o = jnp.broadcast_to(om[:, j : j + 1], (M, B))
+        a, o, c, s = [jnp.broadcast_to(pp[q * M : (q + 1) * M, j : j + 1], (M, B)) for q in range(4)]
         w = [jnp.broadcast_to(ww[q * M : (q + 1) * M, j : j + 1], (M, B)) for q in range(4)]
         sin, cos = sincos(o * place)
         mag = jnp.exp(a * place)
-        near = mag * cos, mag * sin
-        sin, cos = sincos(o * ahead)
-        mag = jnp.exp(a * ahead)
-        out.append((near, (mag * cos, mag * sin), w))
+        rest = jnp.exp(a * ahead)
+        out.append(((mag * cos, mag * sin), (rest * (c * cos + s * sin), rest * (s * cos - c * sin)), w))
     return out
 
 
@@ -193,15 +192,16 @@
         first = lane_iota(coef.shape) < B // 2
         w = coef * in_re + swap_halves(coef) * jnp.where(first, -in_im, in_im)
         wout_ref[...] = w
-        sin, cos = sincos(im * float(B))
+        turn = sincos(im * float(B))
         mag = jnp.exp(re * float(B))
-        jump_ref[0] = mag * cos
-        jump_ref[1] = mag * jnp.where(first, -sin, sin)
-        columns((re, im, w), cols, C)
+        jump_ref[0] = mag * turn[1]
+        jump_ref[1] = mag * jnp.where(first, -turn[0], turn[0])
+        columns(re, im, turn, w, cols, C)
 
     rows = row_iota((B, B))
     lanes = lane_iota((B, B))
     odd = (lanes & M) == M
+    zero = jnp.zeros((B, B), BF16)
     every = range(G)
     waves = channel_waves(cols, i, M, G)
     feeds = [jnp.concatenate([f_re, f_re, f_im, f_im], axis=0).T for _, (f_re, f_im), _ in waves]
@@ -219,9 +219,10 @@
                 t_ref[j, 2 * B + (2 + h) * M : 2 * B + (3 + h) * M, q * B : (q + 1) * B] = v
     rolled = [toeplitz_rows(kern, 0) for kern in kerns]
     for j in every:
+        parts = split(feeds[j])
         for h in range(2):
-            part = jnp.where(odd if h == 1 else ~odd, feeds[j], 0.0)
-            for q, v in enumerate(split(part)):
+            for q, part in enumerate(parts):
+                v = jnp.where(odd if h == 1 else ~odd, part, zero)
                 f_ref[j, h * B : (h + 1) * B, q * B : (q + 1) * B] = v
                 again_ref[j, h * B : (h + 1) * B, q * B : (q + 1) * B] = v
             toe = jnp.where(lanes >= rows, rolled[2 * j + h], 0.0)
@@ -237,7 +238,8 @@
     @pl.when(i == start)
     def _():
         step_size = jnp.exp(rates_ref[0])
-        columns((step_size * -jnp.exp(rates_ref[1]), step_size * rates_ref[2], w_ref[...]), cols, C)
+        im = step_size * rates_ref[2]
+        columns(step_size * -jnp.exp(rates_ref[1]), im, sincos(im * float(B)), w_ref[...], cols, C)
 
     rows = row_iota((B, B))
     lanes = lane_iota((B, B))
@@ -791,7 +793,7 @@
         [whole(3, C, B), whole(C, B)],
         (few(2 * B, 2 * B), few(2 * B, 2 * B), few(3 * B, 2 * B), whole(2, C, B), whole(C, B)),
         6,
-        [vm((3, B, B), F32)],
+        [vm((2, B, B), F32)],
     )(rates, coef)
     parts, t_tab = lax.optimization_barrier((parts, t_tab))
 
@@ -828,7 +830,7 @@
             out_shape=(far((C, 2 * B, 4 * B), BF16), far((C, B, 2 * B), BF16)),
             in_specs=[whole(3, C, B), whole(C, B)] + [hbm] * len(held),
             out_specs=(block(2 * B, 4 * B), block(B, 2 * B)),
-            scratch_shapes=[vm((3, B, B), F32)],
+            scratch_shapes=[vm((2, B, B), F32)],
             input_output_aliases={2 + k: k for k in range(len(held))},
             compiler_params=params(small),
             cost_estimate=cost(4),

time: 103 us -> 102 us (level)
  transfers between devices with their start and end apart: 31 -> 31, of which waited for: 6 -> 6; matrix products, arithmetic and copies ran while one was open for 1% -> 1% of each run, Pallas kernels for 39% -> 38%
where the time goes in v6:
time: 102 us
  starting transfers between devices  47.6 us (47%)
  Pallas kernels  45.8 us (45%)
  waiting for transfers between devices  5.9 us (6%)
  between operations  1.84 us (2%)
    ppermute x20, starting transfers between devices, exchange(): return lax.ppermute(v, axis, [(k, k ^ off) for k in range(size)])  28.4 us
    pallas_call x2, Pallas kernels, back_tables(): pl.pallas_call(partial(back_table_kernel, C=C, M=M, start=start), grid=(s...  8.17 us
    pallas_call x1, Pallas kernels, per_device(): by_channel(partial(back_kernel, count=H), (shape((C, L), BF16), shape((C,...  7.5 us
    all_to_all x1, starting transfers between devices, per_device(): first = lax.all_to_all(pay, 'mp', split_axis=0, concat_axis=0, tiled=True)  7.01 us
    all_to_all x1, starting transfers between devices, per_device(): lax.all_to_all(mixed, 'mp', split_axis=0, concat_axis=0, tiled=True)  6.2 us
    pallas_call x1, Pallas kernels, per_device(): by_channel(partial(table_kernel, C=C, M=M), (shape((C, 2 * B, 2 * B), BF1...  5.7 us
    pallas_call x1, Pallas kernels, per_device(): by_channel(partial(mixer_kernel, count=H, parts=len(parts)), (shape((mp,...  5.27 us
    pallas_call x1, Pallas kernels, per_device(): by_channel(partial(lift_kernel, count=H), (far((C, 3 * N, 2 * B), BF16),...  4.91 us
  transfers between devices with their start and end apart: 31, of which 6 were waited for; matrix products, arithmetic and copies ran while one was open for 1% of the time, Pallas kernels for 38%

profile of v6, /device:TPU:0, one launch (start us, length us, event | category | flops | bytes accessed | tf_op | source)
XLA Modules:
  0.0 101.8 jit_solution(7981720409571751808)
XLA Ops:
  0.8 2.7 %shard_map.254 = (f32[80,128]{1,0:T(8,128)S(1)}, bf16[16,80,256]{2,1,0:T(8,128)(2,1)}) custom-call(s32[2]{0:T(128)S(1)} %pad_add_fusion.place_ref, bf16[32,4096]{1,0:T(8,128)(2,1)} %x_ref.7, bf16[32,4096]{1,0:T(8,128)(2,1)} %g_ref.1, bf16[32,512]{1,0:T(8,128)(2,1)} %bitcast.25, bf16[32,512]{1,0:T(8,128)(2,1)} %bitcast.26, bf16[1,32]{1,0:T(2,128)(2,1)} %bitcast.27, ...), custom_call_target="tpu_custom_call" | custom-call | flops 3000000000 | bytes 3000000 | tf_op jit(solution)/shard_map/pallas_call | solution.py:760
  3.5 5.1 %collective-permute-start.2 = (f32[80,128]{1,0:T(8,128)S(1)}, f32[80,128]{1,0:T(8,128)S(1)}, u32[]{:S(2)}, u32[]{:S(2)}) collective-permute-start(f32[80,128]{1,0:T(8,128)S(1)} %get-tuple-element.94), channel_id=1, source_target_pairs={{0,12},{1,13},{2,14},{3,15},{4,8},{5,9},{6,10},{7,11},{8,4},{9,5},... | collective-permute-start | bytes 122888 | tf_op jit(solution)/shard_map/ppermute | solution.py:661
  9.2 7.0 %all-to-all-start = ((bf16[16,80,256]{2,1,0:T(8,128)(2,1)}), bf16[16,80,256]{2,1,0:T(8,128)(2,1)S(1)}, u32[]{:S(2)}, u32[]{:S(2)}) async-start(bf16[16,80,256]{2,1,0:T(8,128)(2,1)} %get-tuple-element.107), calls=%async_computation | async-start | bytes 1310720 | tf_op jit(solution)/shard_map/all_to_all | solution.py:774
  17.5 2.0 %collective-permute-start.3 = (f32[80,128]{1,0:T(8,128)S(1)}, f32[80,128]{1,0:T(8,128)S(1)}, u32[]{:S(2)}, u32[]{:S(2)}) collective-permute-start(f32[80,128]{1,0:T(8,128)S(1)} %pad_maximum_fusion.1.refs_0_), channel_id=1, source_target_pairs={{0,1},{1,0},{2,3},{3,2},{4,5},{5,4},{6,7},{7,6},{8,9},{9,8},{10,11... | collective-permute-start | bytes 122888 | tf_op jit(solution)/shard_map/ppermute | solution.py:661
  21.1 5.7 %shard_map.255 = (bf16[32,256,256]{2,1,0:T(8,128)(2,1)S(1)}, bf16[32,256,256]{2,1,0:T(8,128)(2,1)}, bf16[32,384,256]{2,1,0:T(8,128)(2,1)S(1)}, f32[2,32,128]{2,1,0:T(8,128)S(1)}, f32[32,128]{1,0:T(8,128)S(1)}) custom-call(f32[3,32,128]{2,1,0:T(8,128)S(1)} %pad_maximum_fusion.rates_ref, f32[32,128]{1,0:T(8,128)S(1)} %pad_maximum_fusion.2.coef_ref), custom_call_target="tpu_custom_call" | custom-call | flops 6000000000 | bytes 6000000 | tf_op jit(solution)/shard_map/pallas_call | solution.py:787
  26.8 5.3 %shard_map.256 = (bf16[16,32,256]{2,1,0:T(8,128)(2,1)}, f32[32,32,128]{2,1,0:T(8,128)}, f32[32,32,128]{2,1,0:T(8,128)}, f32[32,32,128]{2,1,0:T(8,128)}, f32[2,32,128]{2,1,0:T(8,128)}, /*index=5*/f32[16,128]{1,0:T(8,128)S(1)}) custom-call(s32[1]{0:T(128)S(6)} %copy.33.len_ref, f32[3,32]{1,0:T(4,128)S(1)} %pad_maximum_fusion.3.vec_ref, ...), custom_call_target="tpu_custom_call" | custom-call | flops 6000000000 | bytes 6000000 | tf_op jit(solution)/shard_map/pallas_call | solution.py:801
  34.1 1.5 %collective-permute-start.7 = (bf16[16,16,256]{2,1,0:T(8,128)(2,1)S(1)}, bf16[16,16,256]{2,1,0:T(8,128)(2,1)S(1)}, u32[]{:S(2)}, u32[]{:S(2)}) collective-permute-start(bf16[16,16,256]{2,1,0:T(8,128)(2,1)S(1)} %slice.75.refs_0_), channel_id=1, source_target_pairs={{0,2},{1,3},{2,0},{3,1},{4,6},{5,7},{6,4},{7,5},{8,10},{9,11},{10,... | collective-permute-start | bytes 393224 | tf_op jit(solution)/shard_map/ppermute | solution.py:661
  36.4 6.2 %all-to-all-start.1 = ((bf16[16,32,256]{2,1,0:T(8,128)(2,1)}), bf16[16,32,256]{2,1,0:T(8,128)(2,1)S(1)}, u32[]{:S(2)}, u32[]{:S(2)}) async-start(bf16[16,32,256]{2,1,0:T(8,128)(2,1)} %get-tuple-element.108), calls=%async_computation.1 | async-start | bytes 524288 | tf_op jit(solution)/shard_map/all_to_all | solution.py:820
  43.7 4.1 %shard_map.257 = (bf16[32,256,512]{2,1,0:T(8,128)(2,1)}, bf16[32,128,256]{2,1,0:T(8,128)(2,1)}) custom-call(f32[3,32,128]{2,1,0:T(8,128)S(1)} %pad_maximum_fusion.rates_ref, f32[32,128]{1,0:T(8,128)S(1)} %get-tuple-element.110.w_ref), custom_call_target="tpu_custom_call" | custom-call | flops 4000000000 | bytes 4000000 | tf_op jit(solution)/shard_map/pallas_call | solution.py:827
  47.8 3.3 %all-to-all-done.1.in_ref = bf16[16,32,256]{2,1,0:T(8,128)(2,1)S(1)} async-done(((bf16[16,32,256]{2,1,0:T(8,128)(2,1)}), bf16[16,32,256]{2,1,0:T(8,128)(2,1)S(1)}, u32[]{:S(2)}, u32[]{:S(2)}) %all-to-all-start.1) | async-done | bytes 262176 | tf_op jit(solution)/shard_map/all_to_all | solution.py:820
  51.1 2.4 %shard_map.258 = (bf16[16,64,256]{2,1,0:T(8,128)(2,1)}, bf16[512,256]{1,0:T(8,128)(2,1)S(1)}, bf16[512,256]{1,0:T(8,128)(2,1)S(1)}) custom-call(s32[2]{0:T(128)S(1)} %pad_add_fusion.place_ref, bf16[16,32,256]{2,1,0:T(8,128)(2,1)S(1)} %all-to-all-done.1.in_ref, bf16[16,80,256]{2,1,0:T(8,128)(2,1)S(1)} %all-to-all-done.first_ref, ...), custom_call_target="tpu_custom_call" | custom-call | flops 2000000000 | bytes 2000000 | tf_op jit(solution)/shard_map/pallas_call | solution.py:841
  53.5 3.8 %all-to-all-start.2 = ((bf16[16,64,256]{2,1,0:T(8,128)(2,1)}), bf16[16,64,256]{2,1,0:T(8,128)(2,1)S(1)}, u32[]{:S(2)}, u32[]{:S(2)}) async-start(bf16[16,64,256]{2,1,0:T(8,128)(2,1)} %get-tuple-element.118), calls=%async_computation.2 | async-start | bytes 1048576 | tf_op jit(solution)/shard_map/all_to_all | solution.py:848
  57.9 4.1 %shard_map.260 = (bf16[32,256,512]{2,1,0:T(8,128)(2,1)}, bf16[32,128,256]{2,1,0:T(8,128)(2,1)}) custom-call(f32[3,32,128]{2,1,0:T(8,128)S(1)} %pad_maximum_fusion.rates_ref, f32[32,128]{1,0:T(8,128)S(1)} %get-tuple-element.110.w_ref, bf16[32,256,512]{2,1,0:T(8,128)(2,1)} %get-tuple-element.122.refs_0_, ...), custom_call_target="tpu_custom_call", output_to_operand_aliasing={{0}: (2, {}), {1}: (3, {})} | custom-call | flops 4000000000 | bytes 4000000 | tf_op jit(solution)/shard_map/pallas_call | solution.py:827
  62.0 4.9 %shard_map.259 = (bf16[32,96,256]{2,1,0:T(8,128)(2,1)}, f32[32,32,128]{2,1,0:T(8,128)}) custom-call(s32[1]{0:T(128)S(6)} %copy.33.len_ref, f32[3,32]{1,0:T(4,128)} %copy-done.4, bf16[32,4096]{1,0:T(8,128)(2,1)} %x_ref.7, f32[2,32,128]{2,1,0:T(8,128)} %get-tuple-element.105.stat_ref, bf16[32,256,256]{2,1,0:T(8,128)(2,1)} %get-tuple-element.119.f_ref), custom_call_target="tpu_custom_call" | custom-call | flops 3000000000 | bytes 3000000 | tf_op jit(solution)/shard_map/pallas_call | solution.py:849
  68.1 1.8 %collective-permute-start.18 = (f32[136,512]{1,0:T(8,128)S(1)}, f32[136,512]{1,0:T(8,128)S(1)}, u32[]{:S(2)}, u32[]{:S(2)}) collective-permute-start(f32[136,512]{1,0:T(8,128)S(1)} %get-tuple-element.138), channel_id=1, source_target_pairs={{0,1},{1,0},{2,3},{3,2},{4,5},{5,4},{6,7},{7,6},{8,9},{9,8},{10,11... | collective-permute-start | bytes 835592 | tf_op jit(solution)/shard_map/ppermute | solution.py:661
  72.4 7.5 %shard_map.261 = (bf16[32,4096]{1,0:T(8,128)(2,1)}, f32[32,4096]{1,0:T(8,128)S(1)}, f32[2,32,128]{2,1,0:T(8,128)S(1)}, f32[32,24,128]{2,1,0:T(8,128)S(1)}, f32[3...) custom-call(s32[1]{0:T(128)S(6)} %copy.33.len_ref, ...), custom_call_target="tpu_custom_call" | custom-call | flops 7000000000 | bytes 7000000 | tf_op jit(solution)/shard_map/pallas_call | solution.py:869
  80.0 2.8 %collective-permute-start.15 = (f32[2,32,128]{2,1,0:T(8,128)S(1)}, f32[2,32,128]{2,1,0:T(8,128)S(1)}, u32[]{:S(2)}, u32[]{:S(2)}) collective-permute-start(f32[2,32,128]{2,1,0:T(8,128)S(1)} %get-tuple-element.132), channel_id=1, source_target_pairs={{0,12},{1,13},{2,14},{3,15},{4,8},{5,9},{6,10},{7,11},{8,4},{9,5},... | collective-permute-start | bytes 98312 | tf_op jit(solution)/shard_map/ppermute | solution.py:661
  82.9 1.5 %collective-permute-start.13 = (f32[2,32,128]{2,1,0:T(8,128)S(1)}, f32[2,32,128]{2,1,0:T(8,128)S(1)}, u32[]{:S(2)}, u32[]{:S(2)}) collective-permute-start(f32[2,32,128]{2,1,0:T(8,128)S(1)} %get-tuple-element.132), channel_id=1, source_target_pairs={{0,4},{1,5},{2,6},{3,7},{4,0},{5,1},{6,2},{7,3},{8,12},{9,13},{10,... | collective-permute-start | bytes 98312 | tf_op jit(solution)/shard_map/ppermute | solution.py:661
  85.1 1.6 %collective-permute-start.21 = (f32[72,512]{1,0:T(8,128)S(1)}, f32[72,512]{1,0:T(8,128)S(1)}, u32[]{:S(2)}, u32[]{:S(2)}) collective-permute-start(f32[72,512]{1,0:T(8,128)S(1)} %get-tuple-element.142), channel_id=1, source_target_pairs={{0,4},{1,5},{2,6},{3,7},{4,0},{5,1},{6,2},{7,3},{8,12},{9,13},{10,... | collective-permute-start | bytes 442376 | tf_op jit(solution)/shard_map/ppermute | solution.py:661
  87.6 1.6 %collective-permute-start.22 = (f32[2,32,128]{2,1,0:T(8,128)S(1)}, f32[2,32,128]{2,1,0:T(8,128)S(1)}, u32[]{:S(2)}, u32[]{:S(2)}) collective-permute-start(f32[2,32,128]{2,1,0:T(8,128)S(1)} %add_add_fusion.1), channel_id=1, source_target_pairs={{0,1},{1,0},{2,3},{3,2},{4,5},{5,4},{6,7},{7,6},{8,9},{9,8},{10,11... | collective-permute-start | bytes 98312 | tf_op jit(solution)/shard_map/ppermute | solution.py:661
  89.2 1.5 %collective-permute-start.23 = (f32[2,32,128]{2,1,0:T(8,128)S(1)}, f32[2,32,128]{2,1,0:T(8,128)S(1)}, u32[]{:S(2)}, u32[]{:S(2)}) collective-permute-start(f32[2,32,128]{2,1,0:T(8,128)S(1)} %add_add_fusion.1), channel_id=1, source_target_pairs={{0,2},{1,3},{2,0},{3,1},{4,6},{5,7},{6,4},{7,5},{8,10},{9,11},{10,... | collective-permute-start | bytes 98312 | tf_op jit(solution)/shard_map/ppermute | solution.py:661
  91.7 2.4 %collective-permute-start.25 = (f32[40,512]{1,0:T(8,128)S(1)}, f32[40,512]{1,0:T(8,128)S(1)}, u32[]{:S(2)}, u32[]{:S(2)}) collective-permute-start(f32[40,512]{1,0:T(8,128)S(1)} %get-tuple-element.154), channel_id=1, source_target_pairs={{0,8},{1,9},{2,10},{3,11},{4,12},{5,13},{6,14},{7,15},{8,0},{9,1},... | collective-permute-start | bytes 245768 | tf_op jit(solution)/shard_map/ppermute | solution.py:661
  94.1 3.8 %shard_map.265.ref = f32[32,40,128]{2,1,0:T(8,128)S(1)} custom-call(bf16[32,96,256]{2,1,0:T(8,128)(2,1)} %get-tuple-element.145.u_ref, f32[32,32,128]{2,1,0:T(8,128)} %get-tuple-element.146.lift_ref, f32[32,32,128]{2,1,0:T(8,128)S(1)} %get-tuple-element.147.g_ref, f32[32,32,128]{2,1,0:T(8,128)S(1)} %get-tuple-element.148.p_ref, ...), custom_call_target="tpu_custom_call" | custom-call | flops 20000000000 | bytes 20000000 | tf_op jit(solution)/shard_map/pallas_call | solution.py:903
  99.9 1.8 %shard_map.269 = (f32[32,512]{1,0:T(8,128)}, f32[32,512]{1,0:T(8,128)}, f32[1,32]{1,0:T(1,128)}, f32[1,32]{1,0:T(1,128)}, f32[1,32]{1,0:T(1,128)}, /*index=5*/f3...) custom-call(s32[2]{0:T(128)S(1)} %pad_add_fusion.place_ref, ...), custom_call_target="tpu_custom_call" | custom-call | flops 1000000000 | bytes 1000000 | tf_op jit(solution)/shard_map/pallas_call | solution.py:927
  (98 shorter events, 15.8 us)
Async XLA Ops:
  3.5 14.0 %collective-permute-start.2 = (f32[80,128]{1,0:T(8,128)S(1)}, f32[80,128]{1,0:T(8,128)S(1)}, u32[]{:S(2)}, u32[]{:S(2)}) collective-permute-start(f32[80,128]{1,0:T(8,128)S(1)} %get-tuple-element.94), channel_id=1, source_target_pairs={{0,12},{1,13},{2,14},{3,15},{4,8},{5,9},{6,10},{7,11},{8,4},{9,5},... | collective-permute-start | bytes 122888 | tf_op jit(solution)/shard_map/ppermute | solution.py:661
  8.6 8.9 %collective-permute-start.1 = (f32[80,128]{1,0:T(8,128)S(1)}, f32[80,128]{1,0:T(8,128)S(1)}, u32[]{:S(2)}, u32[]{:S(2)}) collective-permute-start(f32[80,128]{1,0:T(8,128)S(1)} %get-tuple-element.94), channel_id=1, source_target_pairs={{0,8},{1,9},{2,10},{3,11},{4,12},{5,13},{6,14},{7,15},{8,0},{9,1},... | collective-permute-start | bytes 122888 | tf_op jit(solution)/shard_map/ppermute | solution.py:661
  8.6 8.9 %collective-permute-start = (f32[80,128]{1,0:T(8,128)S(1)}, f32[80,128]{1,0:T(8,128)S(1)}, u32[]{:S(2)}, u32[]{:S(2)}) collective-permute-start(f32[80,128]{1,0:T(8,128)S(1)} %get-tuple-element.94), channel_id=1, source_target_pairs={{0,4},{1,5},{2,6},{3,7},{4,0},{5,1},{6,2},{7,3},{8,12},{9,13},{10,... | collective-permute-start | bytes 122888 | tf_op jit(solution)/shard_map/ppermute | solution.py:661
  9.2 23.6 %all-to-all-start = ((bf16[16,80,256]{2,1,0:T(8,128)(2,1)}), bf16[16,80,256]{2,1,0:T(8,128)(2,1)S(1)}, u32[]{:S(2)}, u32[]{:S(2)}) async-start(bf16[16,80,256]{2,1,0:T(8,128)(2,1)} %get-tuple-element.107), calls=%async_computation | async-start | bytes 1310720 | tf_op jit(solution)/shard_map/all_to_all | solution.py:774
  17.5 9.3 %collective-permute-start.3 = (f32[80,128]{1,0:T(8,128)S(1)}, f32[80,128]{1,0:T(8,128)S(1)}, u32[]{:S(2)}, u32[]{:S(2)}) collective-permute-start(f32[80,128]{1,0:T(8,128)S(1)} %pad_maximum_fusion.1.refs_0_), channel_id=1, source_target_pairs={{0,1},{1,0},{2,3},{3,2},{4,5},{5,4},{6,7},{7,6},{8,9},{9,8},{10,11... | collective-permute-start | bytes 122888 | tf_op jit(solution)/shard_map/ppermute | solution.py:661
  19.5 7.3 %collective-permute-start.4 = (f32[80,128]{1,0:T(8,128)S(1)}, f32[80,128]{1,0:T(8,128)S(1)}, u32[]{:S(2)}, u32[]{:S(2)}) collective-permute-start(f32[80,128]{1,0:T(8,128)S(1)} %pad_maximum_fusion.1.refs_0_), channel_id=1, source_target_pairs={{0,2},{1,3},{2,0},{3,1},{4,6},{5,7},{6,4},{7,5},{8,10},{9,11},{10,... | collective-permute-start | bytes 122888 | tf_op jit(solution)/shard_map/ppermute | solution.py:661
  32.8 9.8 %collective-permute-start.6 = (bf16[16,16,256]{2,1,0:T(8,128)(2,1)S(1)}, bf16[16,16,256]{2,1,0:T(8,128)(2,1)S(1)}, u32[]{:S(2)}, u32[]{:S(2)}) collective-permute-start(bf16[16,16,256]{2,1,0:T(8,128)(2,1)S(1)} %slice.75.refs_0_), channel_id=1, source_target_pairs={{0,1},{1,0},{2,3},{3,2},{4,5},{5,4},{6,7},{7,6},{8,9},{9,8},{10,11... | collective-permute-start | bytes 393224 | tf_op jit(solution)/shard_map/ppermute | solution.py:661
  34.1 9.1 %collective-permute-start.7 = (bf16[16,16,256]{2,1,0:T(8,128)(2,1)S(1)}, bf16[16,16,256]{2,1,0:T(8,128)(2,1)S(1)}, u32[]{:S(2)}, u32[]{:S(2)}) collective-permute-start(bf16[16,16,256]{2,1,0:T(8,128)(2,1)S(1)} %slice.75.refs_0_), channel_id=1, source_target_pairs={{0,2},{1,3},{2,0},{3,1},{4,6},{5,7},{6,4},{7,5},{8,10},{9,11},{10,... | collective-permute-start | bytes 393224 | tf_op jit(solution)/shard_map/ppermute | solution.py:661
  35.6 7.7 %collective-permute-start.8 = (bf16[16,16,256]{2,1,0:T(8,128)(2,1)S(1)}, bf16[16,16,256]{2,1,0:T(8,128)(2,1)S(1)}, u32[]{:S(2)}, u32[]{:S(2)}) collective-permute-start(bf16[16,16,256]{2,1,0:T(8,128)(2,1)S(1)} %slice.75.refs_0_), channel_id=1, source_target_pairs={{0,3},{1,2},{2,1},{3,0},{4,7},{5,6},{6,5},{7,4},{8,11},{9,10},{10,... | collective-permute-start | bytes 393224 | tf_op jit(solution)/shard_map/ppermute | solution.py:661
  36.4 14.7 %all-to-all-start.1 = ((bf16[16,32,256]{2,1,0:T(8,128)(2,1)}), bf16[16,32,256]{2,1,0:T(8,128)(2,1)S(1)}, u32[]{:S(2)}, u32[]{:S(2)}) async-start(bf16[16,32,256]{2,1,0:T(8,128)(2,1)} %get-tuple-element.108), calls=%async_computation.1 | async-start | bytes 524288 | tf_op jit(solution)/shard_map/all_to_all | solution.py:820
  42.6 8.5 %collective-permute-start.9 = (bf16[16,16,256]{2,1,0:T(8,128)(2,1)S(1)}, bf16[16,16,256]{2,1,0:T(8,128)(2,1)S(1)}, u32[]{:S(2)}, u32[]{:S(2)}) collective-permute-start(bf16[16,16,256]{2,1,0:T(8,128)(2,1)S(1)} %slice.75.refs_0_), channel_id=1, source_target_pairs={{0,16},{16,0},{1,17},{17,1},{2,18},{18,2},{3,19},{19,3},{4,20},{20... | collective-permute-start | bytes 393224 | tf_op jit(solution)/shard_map/ppermute | solution.py:678
  42.7 8.4 %collective-permute-start.10 = (bf16[16,16,256]{2,1,0:T(8,128)(2,1)S(1)}, bf16[16,16,256]{2,1,0:T(8,128)(2,1)S(1)}, u32[]{:S(2)}, u32[]{:S(2)}) collective-permute-start(bf16[16,16,256]{2,1,0:T(8,128)(2,1)S(1)} %collective-permute-done.6.refs_1_), channel_id=1, source_target_pairs={{0,16},{16,0},{1,17},{17,1},{2,18},{18,2},{3,19},{19,3},{4,20},{20... | collective-permute-start | bytes 393224 | tf_op jit(solution)/shard_map/ppermute | solution.py:678
  43.2 7.9 %collective-permute-start.11 = (bf16[16,16,256]{2,1,0:T(8,128)(2,1)S(1)}, bf16[16,16,256]{2,1,0:T(8,128)(2,1)S(1)}, u32[]{:S(2)}, u32[]{:S(2)}) collective-permute-start(bf16[16,16,256]{2,1,0:T(8,128)(2,1)S(1)} %collective-permute-done.7.refs_2_), channel_id=1, source_target_pairs={{0,16},{16,0},{1,17},{17,1},{2,18},{18,2},{3,19},{19,3},{4,20},{20... | collective-permute-start | bytes 393224 | tf_op jit(solution)/shard_map/ppermute | solution.py:678
  43.3 7.8 %collective-permute-start.12 = (bf16[16,16,256]{2,1,0:T(8,128)(2,1)S(1)}, bf16[16,16,256]{2,1,0:T(8,128)(2,1)S(1)}, u32[]{:S(2)}, u32[]{:S(2)}) collective-permute-start(bf16[16,16,256]{2,1,0:T(8,128)(2,1)S(1)} %collective-permute-done.8.refs_3_), channel_id=1, source_target_pairs={{0,16},{16,0},{1,17},{17,1},{2,18},{18,2},{3,19},{19,3},{4,20},{20... | collective-permute-start | bytes 393224 | tf_op jit(solution)/shard_map/ppermute | solution.py:678
  53.5 18.9 %all-to-all-start.2 = ((bf16[16,64,256]{2,1,0:T(8,128)(2,1)}), bf16[16,64,256]{2,1,0:T(8,128)(2,1)S(1)}, u32[]{:S(2)}, u32[]{:S(2)}) async-start(bf16[16,64,256]{2,1,0:T(8,128)(2,1)} %get-tuple-element.118), calls=%async_computation.2 | async-start | bytes 1048576 | tf_op jit(solution)/shard_map/all_to_all | solution.py:848
  57.3 9.6 %collective-permute-start.16 = (bf16[512,256]{1,0:T(8,128)(2,1)S(1)}, bf16[512,256]{1,0:T(8,128)(2,1)S(1)}, u32[]{:S(2)}, u32[]{:S(2)}) collective-permute-start(bf16[512,256]{1,0:T(8,128)(2,1)S(1)} %get-tuple-element.134), channel_id=1, source_target_pairs={{0,16},{16,0},{1,17},{17,1},{2,18},{18,2},{3,19},{19,3},{4,20},{20... | collective-permute-start | bytes 786440 | tf_op jit(solution)/shard_map/ppermute | solution.py:678
  57.4 9.5 %collective-permute-start.17 = (bf16[512,256]{1,0:T(8,128)(2,1)S(1)}, bf16[512,256]{1,0:T(8,128)(2,1)S(1)}, u32[]{:S(2)}, u32[]{:S(2)}) collective-permute-start(bf16[512,256]{1,0:T(8,128)(2,1)S(1)} %bitcast.19), channel_id=1, source_target_pairs={{0,16},{16,0},{1,17},{17,1},{2,18},{18,2},{3,19},{19,3},{4,20},{20... | collective-permute-start | bytes 786440 | tf_op jit(solution)/shard_map/ppermute | solution.py:678
  68.1 14.8 %collective-permute-start.18 = (f32[136,512]{1,0:T(8,128)S(1)}, f32[136,512]{1,0:T(8,128)S(1)}, u32[]{:S(2)}, u32[]{:S(2)}) collective-permute-start(f32[136,512]{1,0:T(8,128)S(1)} %get-tuple-element.138), channel_id=1, source_target_pairs={{0,1},{1,0},{2,3},{3,2},{4,5},{5,4},{6,7},{7,6},{8,9},{9,8},{10,11... | collective-permute-start | bytes 835592 | tf_op jit(solution)/shard_map/ppermute | solution.py:661
  69.8 14.6 %collective-permute-start.19 = (f32[136,512]{1,0:T(8,128)S(1)}, f32[136,512]{1,0:T(8,128)S(1)}, u32[]{:S(2)}, u32[]{:S(2)}) collective-permute-start(f32[136,512]{1,0:T(8,128)S(1)} %get-tuple-element.139), channel_id=1, source_target_pairs={{0,2},{1,3},{2,0},{3,1},{4,6},{5,7},{6,4},{7,5},{8,10},{9,11},{10,... | collective-permute-start | bytes 835592 | tf_op jit(solution)/shard_map/ppermute | solution.py:661
  71.3 13.2 %collective-permute-start.20 = (f32[136,512]{1,0:T(8,128)S(1)}, f32[136,512]{1,0:T(8,128)S(1)}, u32[]{:S(2)}, u32[]{:S(2)}) collective-permute-start(f32[136,512]{1,0:T(8,128)S(1)} %get-tuple-element.140), channel_id=1, source_target_pairs={{0,3},{1,2},{2,1},{3,0},{4,7},{5,6},{6,5},{7,4},{8,11},{9,10},{10,... | collective-permute-start | bytes 835592 | tf_op jit(solution)/shard_map/ppermute | solution.py:661
  80.0 6.8 %collective-permute-start.15 = (f32[2,32,128]{2,1,0:T(8,128)S(1)}, f32[2,32,128]{2,1,0:T(8,128)S(1)}, u32[]{:S(2)}, u32[]{:S(2)}) collective-permute-start(f32[2,32,128]{2,1,0:T(8,128)S(1)} %get-tuple-element.132), channel_id=1, source_target_pairs={{0,12},{1,13},{2,14},{3,15},{4,8},{5,9},{6,10},{7,11},{8,4},{9,5},... | collective-permute-start | bytes 98312 | tf_op jit(solution)/shard_map/ppermute | solution.py:661
  87.6 10.3 %collective-permute-start.22 = (f32[2,32,128]{2,1,0:T(8,128)S(1)}, f32[2,32,128]{2,1,0:T(8,128)S(1)}, u32[]{:S(2)}, u32[]{:S(2)}) collective-permute-start(f32[2,32,128]{2,1,0:T(8,128)S(1)} %add_add_fusion.1), channel_id=1, source_target_pairs={{0,1},{1,0},{2,3},{3,2},{4,5},{5,4},{6,7},{7,6},{8,9},{9,8},{10,11... | collective-permute-start | bytes 98312 | tf_op jit(solution)/shard_map/ppermute | solution.py:661
  89.2 8.7 %collective-permute-start.23 = (f32[2,32,128]{2,1,0:T(8,128)S(1)}, f32[2,32,128]{2,1,0:T(8,128)S(1)}, u32[]{:S(2)}, u32[]{:S(2)}) collective-permute-start(f32[2,32,128]{2,1,0:T(8,128)S(1)} %add_add_fusion.1), channel_id=1, source_target_pairs={{0,2},{1,3},{2,0},{3,1},{4,6},{5,7},{6,4},{7,5},{8,10},{9,11},{10,... | collective-permute-start | bytes 98312 | tf_op jit(solution)/shard_map/ppermute | solution.py:661
  90.7 7.2 %collective-permute-start.24 = (f32[2,32,128]{2,1,0:T(8,128)S(1)}, f32[2,32,128]{2,1,0:T(8,128)S(1)}, u32[]{:S(2)}, u32[]{:S(2)}) collective-permute-start(f32[2,32,128]{2,1,0:T(8,128)S(1)} %add_add_fusion.1), channel_id=1, source_target_pairs={{0,3},{1,2},{2,1},{3,0},{4,7},{5,6},{6,5},{7,4},{8,11},{9,10},{10,... | collective-permute-start | bytes 98312 | tf_op jit(solution)/shard_map/ppermute | solution.py:661
  (21 other events, 194.3 us)

commit v7 on v6

--- a/solution.py
+++ b/solution.py
@@ -92,14 +92,16 @@
         s, t = a_re * s + (a_im * t + v), a_re * t + (swap_halves(v) - a_im * s)
 
 
-def start_kernel(
-    place_ref, x_hbm, g_hbm, v_hbm, w_hbm, vb_hbm, gb_hbm, stat_ref, pay_ref, x_ref, g_ref, wt_ref, vb_ref, gb_ref, sems,
-):
+def start_kernel(place_ref, x_hbm, g_hbm, v_hbm, w_hbm, *refs):
+    more, refs = refs[:2], refs[2:]
+    stat_ref, pay_ref, x_ref, g_ref, wt_ref = refs[:5]
+    held, sems = refs[5:7], refs[7]
+    vb_ref, gb_ref = held
     C, L = x_ref.shape
     N = L // B
     mp, rows, nt = pay_ref.shape
     few = rows - 2 * C
-    pairs = ((x_hbm, x_ref), (g_hbm, g_ref), (vb_hbm, vb_ref), (gb_hbm, gb_ref))
+    pairs = ((x_hbm, x_ref), (g_hbm, g_ref)) + tuple(zip(more, held))
     moves = [pltpu.make_async_copy(src, dst, sems.at[1 + k]) for k, (src, dst) in enumerate(pairs)]
     for move in moves:
         move.start()
@@ -117,8 +119,8 @@
         stat_ref[n : n + 1, :] = mean
         stat_ref[N + n : N + n + 1, :] = jnp.sum(dev * dev, axis=0, keepdims=True)
     own = row_iota((mp, B))
-    moves[2].wait()
-    moves[3].wait()
+    for move in moves[2:]:
+        move.wait()
     bias = jnp.concatenate([vb_ref[...].astype(F32), gb_ref[...].astype(F32), jnp.zeros((1, B - 2 * C), F32)], axis=1)
     stat_ref[2 * N :, :] = jnp.where(own == place_ref[1], bias, 0.0)
     for j in range(mp):
@@ -140,13 +142,38 @@
     return mean, spread, sum(p[2 * N :] for p in parts)
 
 
-def columns(re, im, turn, w, cols, C):
-    sin, cos = turn
+def mode_columns(log_step, decay, freq, coef):
+    C = decay.shape[0]
+    step_size = jnp.exp(log_step)
+    real_rate = -jnp.exp(decay)
+    re = step_size * real_rate
+    im = step_size * freq
+    growth = jnp.exp(re)
+    sin, cos = sincos(im)
+    num_re = growth * cos - 1.0
+    num_im = growth * sin
+    den = real_rate * real_rate + freq * freq
+    in_re = (num_re * real_rate + num_im * freq) / den
+    in_im = (num_im * real_rate - num_re * freq) / den
+    first = lane_iota(coef.shape) < B // 2
+    w = coef * in_re + swap_halves(coef) * jnp.where(first, -in_im, in_im)
+    sin, cos = sincos(im * float(B))
+    mag = jnp.exp(re * float(B))
+    jump = mag * cos, mag * jnp.where(first, -sin, sin)
     group = lane_iota(re.shape) // (B // 4)
     packed = jnp.where(group == 0, re, jnp.where(group == 1, im, jnp.where(group == 2, cos, sin)))
     pad = jnp.zeros((B - C, B), F32)
-    for q, v in enumerate((packed, w)):
-        cols[q] = jnp.concatenate([v, pad], axis=0).T
+    return w, jump, [jnp.concatenate([v, pad], axis=0).T for v in (packed, w)]
+
+
+def mode_kernel(step_ref, decay_ref, freq_ref, read_ref, liquid_ref, cols_ref, jump_ref, w_all_ref):
+    C, M = decay_ref.shape
+    decay, freq, read, liquid = decay_ref[...], freq_ref[...], read_ref[...], liquid_ref[...]
+    step = jnp.sum(jnp.where(row_iota((C, C)) == lane_iota((C, C)), step_ref[...], 0.0), axis=1, keepdims=True)
+    coef = jnp.concatenate([read[:, :M], liquid[:, :M], read[:, M:], liquid[:, M:]], axis=1)
+    w_all_ref[...], (jump_ref[0], jump_ref[1]), (cols_ref[0], cols_ref[1]) = mode_columns(
+        step, jnp.concatenate([decay] * 4, axis=1), jnp.concatenate([freq] * 4, axis=1), coef
+    )
 
 
 def channel_waves(cols, i, M, G):
@@ -170,34 +197,9 @@
     return pltpu.roll(jnp.broadcast_to(kern, (B, B)), start, 1, stride=1, stride_axis=0)
 
 
-def table_kernel(rates_ref, coef_ref, f_ref, again_ref, t_ref, jump_ref, wout_ref, cols, *, C, M):
+def table_kernel(cols, f_ref, again_ref, t_ref, *, M):
     i = pl.program_id(0)
     G = f_ref.shape[0]
-
-    @pl.when(i == 0)
-    def _():
-        step_size = jnp.exp(rates_ref[0])
-        real_rate = -jnp.exp(rates_ref[1])
-        freq = rates_ref[2]
-        re = step_size * real_rate
-        im = step_size * freq
-        growth = jnp.exp(re)
-        sin, cos = sincos(im)
-        num_re = growth * cos - 1.0
-        num_im = growth * sin
-        den = real_rate * real_rate + freq * freq
-        in_re = (num_re * real_rate + num_im * freq) / den
-        in_im = (num_im * real_rate - num_re * freq) / den
-        coef = coef_ref[...]
-        first = lane_iota(coef.shape) < B // 2
-        w = coef * in_re + swap_halves(coef) * jnp.where(first, -in_im, in_im)
-        wout_ref[...] = w
-        turn = sincos(im * float(B))
-        mag = jnp.exp(re * float(B))
-        jump_ref[0] = mag * turn[1]
-        jump_ref[1] = mag * jnp.where(first, -turn[0], turn[0])
-        columns(re, im, turn, w, cols, C)
-
     rows = row_iota((B, B))
     lanes = lane_iota((B, B))
     odd = (lanes & M) == M
@@ -230,20 +232,12 @@
                 t_ref[j, h * B : (h + 1) * B, q * B : (q + 1) * B] = v
 
 
-def back_table_kernel(rates_ref, w_ref, *refs, C, M, start):
-    t_ref, near_ref, cols = refs[-3:]
+def back_table_kernel(cols, *refs, M, start):
+    t_ref, near_ref = refs[-2:]
     i = pl.program_id(0) + start
     G = t_ref.shape[0]
-
-    @pl.when(i == start)
-    def _():
-        step_size = jnp.exp(rates_ref[0])
-        im = step_size * rates_ref[2]
-        columns(step_size * -jnp.exp(rates_ref[1]), im, sincos(im * float(B)), w_ref[...], cols, C)
-
     rows = row_iota((B, B))
     lanes = lane_iota((B, B))
-    zero = jnp.zeros((M, B), BF16)
     every = range(G)
     waves = channel_waves(cols, i, M, G)
     turned = [jnp.concatenate([n_re, n_re, n_im, n_im], axis=0).T for (n_re, n_im), _, _ in waves]
@@ -256,11 +250,10 @@
             b_im = -(w_re * f_im + w_im * f_re)
             kerns.append(jnp.sum(b_re, axis=0, keepdims=True))
             starts.append(jnp.sum(w_re * n_re - w_im * n_im, axis=0, keepdims=True)[:, 0:1])
-            for part, v2 in ((0, b_re), (2, b_im)):
+            for part, v2 in enumerate((b_re, b_im)):
                 for q, v in enumerate(split(v2)):
                     at = slice((2 * q + h) * B, (2 * q + h + 1) * B)
                     t_ref[j, B + part * M : B + (part + 1) * M, at] = v
-                    t_ref[j, B + (part + 1) * M : B + (part + 2) * M, at] = zero
     rolled = [toeplitz_rows(kern, 0) for kern in kerns]
     for j in every:
         for q, v in enumerate(split(turned[j])):
@@ -421,17 +414,25 @@
     N = L // B
     nt = gm_ref.shape[2]
     per = nt // B
+    quarter = B // 4
 
     def fetch(q, k):
-        src, dst = ((slope_hbm, slope_ref), (near_hbm, near_ref), (t_ref, tab))[q]
         at = pl.ds(k * G, G)
-        return pltpu.make_async_copy(src.at[at], dst.at[at], sem.at[q, k])
+        src, dst = (
+            (slope_hbm.at[at], slope_ref.at[at]),
+            (near_hbm.at[at], near_ref.at[at]),
+            (t_ref.at[at, 0:B, :], tab.at[at, 0:B, :]),
+            (t_ref.at[at, B:, :], tab.at[at, B + quarter : B + 3 * quarter, :]),
+        )[q]
+        return pltpu.make_async_copy(src, dst, sem.at[q, k])
 
     @pl.when(i == 0)
     def _():
         for k in range(C // G):
-            for q in range(3):
+            for q in range(4):
                 fetch(q, k).start()
+        tab[:, B : B + quarter, :] = jnp.zeros((C, quarter, 4 * B), BF16)
+        tab[:, B + 3 * quarter :, :] = jnp.zeros((C, quarter, 4 * B), BF16)
         for n in range(N):
             xs[n * C : (n + 1) * C, :] = x_ref[:, n * B : (n + 1) * B].astype(F32)
             at = slice((n % per) * B, (n % per + 1) * B)
@@ -468,6 +469,7 @@
         turned_ref[j] = rts[j * N : (j + 1) * N, :]
         left.append(jnp.concatenate([hs[j], jnp.concatenate(split(r), axis=0)], axis=1))
     fetch(2, i).wait()
+    fetch(3, i).wait()
     both_all = [dot(left[j], tab[i * G + j]) for j in range(G)]
     for j, both in enumerate(both_all):
         ci = i * G + j
@@ -773,28 +775,24 @@
     )
     first = lax.all_to_all(pay, "mp", split_axis=0, concat_axis=0, tiled=True)
 
-    rates = jnp.stack(
-        [jnp.broadcast_to(log_step[:, None], (C, 4 * M)), jnp.tile(decay_log, (1, 4)), jnp.tile(frequency, (1, 4))]
-    )
-    coef = jnp.concatenate([readout[:, :M], liquid_readout[:, :M], readout[:, M:], liquid_readout[:, M:]], axis=1)
     count = C
     for k, offs in enumerate(rounds[::-1]):
         parts = [stat] + [exchange(stat, "mp", mp, o) for o in offs]
         if k < len(rounds) - 1:
             stat = jnp.concatenate(join_stats(parts, N, float(count)), axis=0)
             count *= len(parts)
-            stat, rates = lax.optimization_barrier((stat, rates))
-    f_near, f_tab, t_tab, jump, w_all = by_channel(
-        partial(table_kernel, C=C, M=M),
-        (
-            shape((C, 2 * B, 2 * B), BF16), far((C, 2 * B, 2 * B), BF16), shape((C, 3 * B, 2 * B), BF16),
-            shape((2, C, B), F32), shape((C, B), F32),
-        ),
-        [whole(3, C, B), whole(C, B)],
-        (few(2 * B, 2 * B), few(2 * B, 2 * B), few(3 * B, 2 * B), whole(2, C, B), whole(C, B)),
+            stat, rates = lax.optimization_barrier((stat, decay_log))
+    cols, jump, w_all = call(
+        mode_kernel, (shape((2, B, B), F32), shape((2, C, B), F32), shape((C, B), F32)), 5
+    )(log_step[None], rates, frequency, readout, liquid_readout)
+    f_near, f_tab, t_tab = by_channel(
+        partial(table_kernel, M=M),
+        (shape((C, 2 * B, 2 * B), BF16), far((C, 2 * B, 2 * B), BF16), shape((C, 3 * B, 2 * B), BF16)),
+        [whole(2, B, B)],
+        (few(2 * B, 2 * B), few(2 * B, 2 * B), few(3 * B, 2 * B)),
         6,
-        [vm((2, B, B), F32)],
-    )(rates, coef)
+        [],
+    )(cols)
     parts, t_tab = lax.optimization_barrier((parts, t_tab))
 
     vecs = jnp.stack([norm_gain, norm_bias, skip_gain])
@@ -813,7 +811,7 @@
         G,
     )(lengths, vecs, tokens, *parts, f_near, t_tab, jump)
 
-    mixed, first, rates = lax.optimization_barrier((mixed, first, rates))
+    mixed, first, cols = lax.optimization_barrier((mixed, first, cols))
     own_w = [first[:, :few_rows, :]]
     own_w += [exchange(own_w[0], "mp", mp, o) for o in rounds[0]]
     other_w = [partner(v, dp) for v in own_w]
@@ -825,16 +823,15 @@
             return pl.BlockSpec((TABLE_GROUP,) + dims, lambda i: (i + start,) + (0,) * len(dims))
 
         return pl.pallas_call(
-            partial(back_table_kernel, C=C, M=M, start=start),
+            partial(back_table_kernel, M=M, start=start),
             grid=(steps,),
-            out_shape=(far((C, 2 * B, 4 * B), BF16), far((C, B, 2 * B), BF16)),
-            in_specs=[whole(3, C, B), whole(C, B)] + [hbm] * len(held),
-            out_specs=(block(2 * B, 4 * B), block(B, 2 * B)),
-            scratch_shapes=[vm((2, B, B), F32)],
-            input_output_aliases={2 + k: k for k in range(len(held))},
+            out_shape=(far((C, B + 2 * M, 4 * B), BF16), far((C, B, 2 * B), BF16)),
+            in_specs=[whole(2, B, B)] + [hbm] * len(held),
+            out_specs=(block(B + 2 * M, 4 * B), block(B, 2 * B)),
+            input_output_aliases={1 + k: k for k in range(len(held))},
             compiler_params=params(small),
             cost_estimate=cost(4),
-        )(rates, w_all, *[pin(v) for v in held])
+        )(cols, *[pin(v) for v in held])
 
     tables = back_tables([], 0, half_steps)
     mixed_tok, tables = lax.optimization_barrier((mixed_tok, tables))
@@ -844,7 +841,7 @@
         4 + 2 * len(own_w), 1, 2, [vm((2, H, nt), BF16), vm((2, mp, C, H), BF16)],
     )(place, mixed_tok, first, bias, *own_w, *other_w)
     mixed_tok = mixed_tok.reshape(H, nt)
-    gm, f_tab, rates = lax.optimization_barrier((gm, f_tab, rates))
+    gm, f_tab, cols = lax.optimization_barrier((gm, f_tab, cols))
     gm = lax.all_to_all(gm, "mp", split_axis=0, concat_axis=0, tiled=True)
     u_rev, lift = by_channel(
         partial(lift_kernel, count=H),
@@ -878,7 +875,7 @@
             vm((N * C, B), F32), vm((N * C, B), F32), vm((N * C, B), F32), vm((3, N, B), F32),
             vm((G, 2 * N, B), BF16), vm((G * N, B), F32), vm((G * N, B), F32), vm((G * N, B), F32),
             vm((C, 2 * B, 4 * B), BF16), vm((C, B, 2 * B), BF16), vm((C, N, B), F32),
-            pltpu.SemaphoreType.DMA((3, C // G)),
+            pltpu.SemaphoreType.DMA((4, C // G)),
         ],
         large,
         G,

time: 102 us -> 101 us (level)
    pallas_call x3 -> x4, Pallas kernels: 13.9 us -> 13.2 us  [the longest x2 7.46 us: back_tables(): pl.pallas_call(partial(back_table_kernel, M=M, start=start), grid=(steps,...]
  transfers between devices with their start and end apart: 31 -> 31, of which waited for: 6 -> 5; matrix products, arithmetic and copies ran while one was open for 1% -> 0% of each run, Pallas kernels for 38% -> 37%
where the time goes in v7:
time: 101 us
  starting transfers between devices  47.2 us (47%)
  Pallas kernels  44.8 us (44%)
  waiting for transfers between devices  6.64 us (7%)
  between operations  1.8 us (2%)
    ppermute x20, starting transfers between devices, exchange(): return lax.ppermute(v, axis, [(k, k ^ off) for k in range(size)])  28.4 us
    pallas_call x2, Pallas kernels, back_tables(): pl.pallas_call(partial(back_table_kernel, M=M, start=start), grid=(steps,...  7.46 us
    pallas_call x1, Pallas kernels, per_device(): by_channel(partial(back_kernel, count=H), (shape((C, L), BF16), shape((C,...  7.16 us
    all_to_all x1, starting transfers between devices, per_device(): first = lax.all_to_all(pay, 'mp', split_axis=0, concat_axis=0, tiled=True)  7.01 us
    all_to_all x1, starting transfers between devices, per_device(): lax.all_to_all(mixed, 'mp', split_axis=0, concat_axis=0, tiled=True)  5.78 us
    pallas_call x1, Pallas kernels, per_device(): by_channel(partial(table_kernel, M=M), (shape((C, 2 * B, 2 * B), BF16), f...  5.47 us
    pallas_call x1, Pallas kernels, per_device(): by_channel(partial(mixer_kernel, count=H, parts=len(parts)), (shape((mp,...  5.25 us
    pallas_call x1, Pallas kernels, per_device(): by_channel(partial(lift_kernel, count=H), (far((C, 3 * N, 2 * B), BF16),...  4.92 us
  transfers between devices with their start and end apart: 31, of which 5 were waited for; matrix products, arithmetic and copies ran while one was open for 0% of the time, Pallas kernels for 37%

profile of v7, /device:TPU:0, one launch (start us, length us, event | category | flops | bytes accessed | tf_op | source)
XLA Modules:
  0.0 100.7 jit_solution(15168430573195110327)
XLA Ops:
  0.8 2.7 %shard_map.254 = (f32[80,128]{1,0:T(8,128)S(1)}, bf16[16,80,256]{2,1,0:T(8,128)(2,1)}) custom-call(s32[2]{0:T(128)S(1)} %pad_add_fusion.place_ref, bf16[32,4096]{1,0:T(8,128)(2,1)} %x_ref.7, bf16[32,4096]{1,0:T(8,128)(2,1)} %g_ref.1, bf16[32,512]{1,0:T(8,128)(2,1)} %bitcast.26, bf16[32,512]{1,0:T(8,128)(2,1)} %bitcast.27, bf16[1,32]{1,0:T(2,128)(2,1)} %bitcast.28, ...), custom_call_target="tpu_custom_call" | custom-call | flops 3000000000 | bytes 3000000 | tf_op jit(solution)/shard_map/pallas_call | solution.py:762
  3.5 5.1 %collective-permute-start.2 = (f32[80,128]{1,0:T(8,128)S(1)}, f32[80,128]{1,0:T(8,128)S(1)}, u32[]{:S(2)}, u32[]{:S(2)}) collective-permute-start(f32[80,128]{1,0:T(8,128)S(1)} %get-tuple-element.95), channel_id=1, source_target_pairs={{0,12},{1,13},{2,14},{3,15},{4,8},{5,9},{6,10},{7,11},{8,4},{9,5},... | collective-permute-start | bytes 122888 | tf_op jit(solution)/shard_map/ppermute | solution.py:663
  9.2 7.0 %all-to-all-start = ((bf16[16,80,256]{2,1,0:T(8,128)(2,1)}), bf16[16,80,256]{2,1,0:T(8,128)(2,1)S(1)}, u32[]{:S(2)}, u32[]{:S(2)}) async-start(bf16[16,80,256]{2,1,0:T(8,128)(2,1)} %get-tuple-element.109), calls=%async_computation | async-start | bytes 1310720 | tf_op jit(solution)/shard_map/all_to_all | solution.py:776
  17.0 2.0 %collective-permute-start.3 = (f32[80,128]{1,0:T(8,128)S(1)}, f32[80,128]{1,0:T(8,128)S(1)}, u32[]{:S(2)}, u32[]{:S(2)}) collective-permute-start(f32[80,128]{1,0:T(8,128)S(1)} %pad_maximum_fusion.refs_0_), channel_id=1, source_target_pairs={{0,1},{1,0},{2,3},{3,2},{4,5},{5,4},{6,7},{7,6},{8,9},{9,8},{10,11... | collective-permute-start | bytes 122888 | tf_op jit(solution)/shard_map/ppermute | solution.py:663
  19.0 1.5 %collective-permute-start.4 = (f32[80,128]{1,0:T(8,128)S(1)}, f32[80,128]{1,0:T(8,128)S(1)}, u32[]{:S(2)}, u32[]{:S(2)}) collective-permute-start(f32[80,128]{1,0:T(8,128)S(1)} %pad_maximum_fusion.refs_0_), channel_id=1, source_target_pairs={{0,2},{1,3},{2,0},{3,1},{4,6},{5,7},{6,4},{7,5},{8,10},{9,11},{10,... | collective-permute-start | bytes 122888 | tf_op jit(solution)/shard_map/ppermute | solution.py:663
  20.9 5.5 %shard_map.256 = (bf16[32,256,256]{2,1,0:T(8,128)(2,1)S(1)}, bf16[32,256,256]{2,1,0:T(8,128)(2,1)}, bf16[32,384,256]{2,1,0:T(8,128)(2,1)S(1)}) custom-call(f32[2,128,128]{2,1,0:T(8,128)S(1)} %get-tuple-element.122.cols), custom_call_target="tpu_custom_call" | custom-call | flops 6000000000 | bytes 6000000 | tf_op jit(solution)/shard_map/pallas_call | solution.py:788
  26.4 5.3 %shard_map.257 = (bf16[16,32,256]{2,1,0:T(8,128)(2,1)}, f32[32,32,128]{2,1,0:T(8,128)}, f32[32,32,128]{2,1,0:T(8,128)}, f32[32,32,128]{2,1,0:T(8,128)}, f32[2,32,128]{2,1,0:T(8,128)}, /*index=5*/f32[16,128]{1,0:T(8,128)S(1)}) custom-call(s32[1]{0:T(128)S(6)} %copy.33.len_ref, f32[3,32]{1,0:T(4,128)S(1)} %pad_maximum_fusion.1.vec_ref, ...), custom_call_target="tpu_custom_call" | custom-call | flops 6000000000 | bytes 6000000 | tf_op jit(solution)/shard_map/pallas_call | solution.py:799
  36.4 5.8 %all-to-all-start.1 = ((bf16[16,32,256]{2,1,0:T(8,128)(2,1)}), bf16[16,32,256]{2,1,0:T(8,128)(2,1)S(1)}, u32[]{:S(2)}, u32[]{:S(2)}) async-start(bf16[16,32,256]{2,1,0:T(8,128)(2,1)} %get-tuple-element.110), calls=%async_computation.1 | async-start | bytes 524288 | tf_op jit(solution)/shard_map/all_to_all | solution.py:818
  43.3 3.7 %shard_map.258 = (bf16[32,192,512]{2,1,0:T(8,128)(2,1)}, bf16[32,128,256]{2,1,0:T(8,128)(2,1)}) custom-call(f32[2,128,128]{2,1,0:T(8,128)S(1)} %get-tuple-element.122.cols), custom_call_target="tpu_custom_call" | custom-call | flops 4000000000 | bytes 4000000 | tf_op jit(solution)/shard_map/pallas_call | solution.py:825
  47.0 3.7 %all-to-all-done.1.in_ref = bf16[16,32,256]{2,1,0:T(8,128)(2,1)S(1)} async-done(((bf16[16,32,256]{2,1,0:T(8,128)(2,1)}), bf16[16,32,256]{2,1,0:T(8,128)(2,1)S(1)}, u32[]{:S(2)}, u32[]{:S(2)}) %all-to-all-start.1) | async-done | bytes 262176 | tf_op jit(solution)/shard_map/all_to_all | solution.py:818
  50.7 2.4 %shard_map.259 = (bf16[16,64,256]{2,1,0:T(8,128)(2,1)}, bf16[512,256]{1,0:T(8,128)(2,1)S(1)}, bf16[512,256]{1,0:T(8,128)(2,1)S(1)}) custom-call(s32[2]{0:T(128)S(1)} %pad_add_fusion.place_ref, bf16[16,32,256]{2,1,0:T(8,128)(2,1)S(1)} %all-to-all-done.1.in_ref, bf16[16,80,256]{2,1,0:T(8,128)(2,1)S(1)} %all-to-all-done.first_ref, ...), custom_call_target="tpu_custom_call" | custom-call | flops 2000000000 | bytes 2000000 | tf_op jit(solution)/shard_map/pallas_call | solution.py:838
  53.1 3.8 %all-to-all-start.2 = ((bf16[16,64,256]{2,1,0:T(8,128)(2,1)}), bf16[16,64,256]{2,1,0:T(8,128)(2,1)S(1)}, u32[]{:S(2)}, u32[]{:S(2)}) async-start(bf16[16,64,256]{2,1,0:T(8,128)(2,1)} %get-tuple-element.119), calls=%async_computation.2 | async-start | bytes 1048576 | tf_op jit(solution)/shard_map/all_to_all | solution.py:845
  57.5 3.8 %shard_map.261 = (bf16[32,192,512]{2,1,0:T(8,128)(2,1)}, bf16[32,128,256]{2,1,0:T(8,128)(2,1)}) custom-call(f32[2,128,128]{2,1,0:T(8,128)S(1)} %get-tuple-element.122.cols, bf16[32,192,512]{2,1,0:T(8,128)(2,1)} %get-tuple-element.123.refs_0_, bf16[32,128,256]{2,1,0:T(8,128)(2,1)} %get-tuple-element.124.refs_1_), custom_call_target="tpu_custom_call", output_to_operand_aliasing={{0}: (1, {}), {1}: (2, {})} | custom-call | flops 4000000000 | bytes 4000000 | tf_op jit(solution)/shard_map/pallas_call | solution.py:825
  61.2 4.9 %shard_map.260 = (bf16[32,96,256]{2,1,0:T(8,128)(2,1)}, f32[32,32,128]{2,1,0:T(8,128)}) custom-call(s32[1]{0:T(128)S(6)} %copy.33.len_ref, f32[3,32]{1,0:T(4,128)} %copy-done, bf16[32,4096]{1,0:T(8,128)(2,1)} %x_ref.7, f32[2,32,128]{2,1,0:T(8,128)} %get-tuple-element.107.stat_ref, bf16[32,256,256]{2,1,0:T(8,128)(2,1)} %get-tuple-element.120.f_ref), custom_call_target="tpu_custom_call" | custom-call | flops 3000000000 | bytes 3000000 | tf_op jit(solution)/shard_map/pallas_call | solution.py:846
  67.3 1.8 %collective-permute-start.18 = (f32[136,512]{1,0:T(8,128)S(1)}, f32[136,512]{1,0:T(8,128)S(1)}, u32[]{:S(2)}, u32[]{:S(2)}) collective-permute-start(f32[136,512]{1,0:T(8,128)S(1)} %get-tuple-element.139), channel_id=1, source_target_pairs={{0,1},{1,0},{2,3},{3,2},{4,5},{5,4},{6,7},{7,6},{8,9},{9,8},{10,11... | collective-permute-start | bytes 835592 | tf_op jit(solution)/shard_map/ppermute | solution.py:663
  71.8 7.2 %shard_map.262 = (bf16[32,4096]{1,0:T(8,128)(2,1)}, f32[32,4096]{1,0:T(8,128)S(1)}, f32[2,32,128]{2,1,0:T(8,128)S(1)}, f32[32,24,128]{2,1,0:T(8,128)S(1)}, f32[3...) custom-call(s32[1]{0:T(128)S(6)} %copy.33.len_ref, ...), custom_call_target="tpu_custom_call" | custom-call | flops 7000000000 | bytes 7000000 | tf_op jit(solution)/shard_map/pallas_call | solution.py:866
  79.0 2.7 %collective-permute-start.15 = (f32[2,32,128]{2,1,0:T(8,128)S(1)}, f32[2,32,128]{2,1,0:T(8,128)S(1)}, u32[]{:S(2)}, u32[]{:S(2)}) collective-permute-start(f32[2,32,128]{2,1,0:T(8,128)S(1)} %get-tuple-element.133), channel_id=1, source_target_pairs={{0,12},{1,13},{2,14},{3,15},{4,8},{5,9},{6,10},{7,11},{8,4},{9,5},... | collective-permute-start | bytes 98312 | tf_op jit(solution)/shard_map/ppermute | solution.py:663
  81.8 1.6 %collective-permute-start.13 = (f32[2,32,128]{2,1,0:T(8,128)S(1)}, f32[2,32,128]{2,1,0:T(8,128)S(1)}, u32[]{:S(2)}, u32[]{:S(2)}) collective-permute-start(f32[2,32,128]{2,1,0:T(8,128)S(1)} %get-tuple-element.133), channel_id=1, source_target_pairs={{0,4},{1,5},{2,6},{3,7},{4,0},{5,1},{6,2},{7,3},{8,12},{9,13},{10,... | collective-permute-start | bytes 98312 | tf_op jit(solution)/shard_map/ppermute | solution.py:663
  84.4 1.6 %collective-permute-start.21 = (f32[72,512]{1,0:T(8,128)S(1)}, f32[72,512]{1,0:T(8,128)S(1)}, u32[]{:S(2)}, u32[]{:S(2)}) collective-permute-start(f32[72,512]{1,0:T(8,128)S(1)} %get-tuple-element.143), channel_id=1, source_target_pairs={{0,4},{1,5},{2,6},{3,7},{4,0},{5,1},{6,2},{7,3},{8,12},{9,13},{10,... | collective-permute-start | bytes 442376 | tf_op jit(solution)/shard_map/ppermute | solution.py:663
  86.5 1.6 %collective-permute-start.22 = (f32[2,32,128]{2,1,0:T(8,128)S(1)}, f32[2,32,128]{2,1,0:T(8,128)S(1)}, u32[]{:S(2)}, u32[]{:S(2)}) collective-permute-start(f32[2,32,128]{2,1,0:T(8,128)S(1)} %add_add_fusion.1), channel_id=1, source_target_pairs={{0,1},{1,0},{2,3},{3,2},{4,5},{5,4},{6,7},{7,6},{8,9},{9,8},{10,11... | collective-permute-start | bytes 98312 | tf_op jit(solution)/shard_map/ppermute | solution.py:663
  88.1 1.5 %collective-permute-start.23 = (f32[2,32,128]{2,1,0:T(8,128)S(1)}, f32[2,32,128]{2,1,0:T(8,128)S(1)}, u32[]{:S(2)}, u32[]{:S(2)}) collective-permute-start(f32[2,32,128]{2,1,0:T(8,128)S(1)} %add_add_fusion.1), channel_id=1, source_target_pairs={{0,2},{1,3},{2,0},{3,1},{4,6},{5,7},{6,4},{7,5},{8,10},{9,11},{10,... | collective-permute-start | bytes 98312 | tf_op jit(solution)/shard_map/ppermute | solution.py:663
  90.6 2.4 %collective-permute-start.25 = (f32[40,512]{1,0:T(8,128)S(1)}, f32[40,512]{1,0:T(8,128)S(1)}, u32[]{:S(2)}, u32[]{:S(2)}) collective-permute-start(f32[40,512]{1,0:T(8,128)S(1)} %get-tuple-element.155), channel_id=1, source_target_pairs={{0,8},{1,9},{2,10},{3,11},{4,12},{5,13},{6,14},{7,15},{8,0},{9,1},... | collective-permute-start | bytes 245768 | tf_op jit(solution)/shard_map/ppermute | solution.py:663
  93.0 3.8 %shard_map.266.ref = f32[32,40,128]{2,1,0:T(8,128)S(1)} custom-call(bf16[32,96,256]{2,1,0:T(8,128)(2,1)} %get-tuple-element.146.u_ref, f32[32,32,128]{2,1,0:T(8,128)} %get-tuple-element.147.lift_ref, f32[32,32,128]{2,1,0:T(8,128)S(1)} %get-tuple-element.148.g_ref, f32[32,32,128]{2,1,0:T(8,128)S(1)} %get-tuple-element.149.p_ref, ...), custom_call_target="tpu_custom_call" | custom-call | flops 20000000000 | bytes 20000000 | tf_op jit(solution)/shard_map/pallas_call | solution.py:900
  98.8 1.8 %shard_map.270 = (f32[32,512]{1,0:T(8,128)}, f32[32,512]{1,0:T(8,128)}, f32[1,32]{1,0:T(1,128)}, f32[1,32]{1,0:T(1,128)}, f32[1,32]{1,0:T(1,128)}, /*index=5*/f3...) custom-call(s32[2]{0:T(128)S(1)} %pad_add_fusion.place_ref, ...), custom_call_target="tpu_custom_call" | custom-call | flops 1000000000 | bytes 1000000 | tf_op jit(solution)/shard_map/pallas_call | solution.py:924
  (91 shorter events, 16.0 us)
Async XLA Ops:
  3.5 13.5 %collective-permute-start.2 = (f32[80,128]{1,0:T(8,128)S(1)}, f32[80,128]{1,0:T(8,128)S(1)}, u32[]{:S(2)}, u32[]{:S(2)}) collective-permute-start(f32[80,128]{1,0:T(8,128)S(1)} %get-tuple-element.95), channel_id=1, source_target_pairs={{0,12},{1,13},{2,14},{3,15},{4,8},{5,9},{6,10},{7,11},{8,4},{9,5},... | collective-permute-start | bytes 122888 | tf_op jit(solution)/shard_map/ppermute | solution.py:663
  8.6 8.4 %collective-permute-start.1 = (f32[80,128]{1,0:T(8,128)S(1)}, f32[80,128]{1,0:T(8,128)S(1)}, u32[]{:S(2)}, u32[]{:S(2)}) collective-permute-start(f32[80,128]{1,0:T(8,128)S(1)} %get-tuple-element.95), channel_id=1, source_target_pairs={{0,8},{1,9},{2,10},{3,11},{4,12},{5,13},{6,14},{7,15},{8,0},{9,1},... | collective-permute-start | bytes 122888 | tf_op jit(solution)/shard_map/ppermute | solution.py:663
  8.6 8.4 %collective-permute-start = (f32[80,128]{1,0:T(8,128)S(1)}, f32[80,128]{1,0:T(8,128)S(1)}, u32[]{:S(2)}, u32[]{:S(2)}) collective-permute-start(f32[80,128]{1,0:T(8,128)S(1)} %get-tuple-element.95), channel_id=1, source_target_pairs={{0,4},{1,5},{2,6},{3,7},{4,0},{5,1},{6,2},{7,3},{8,12},{9,13},{10,... | collective-permute-start | bytes 122888 | tf_op jit(solution)/shard_map/ppermute | solution.py:663
  9.2 23.6 %all-to-all-start = ((bf16[16,80,256]{2,1,0:T(8,128)(2,1)}), bf16[16,80,256]{2,1,0:T(8,128)(2,1)S(1)}, u32[]{:S(2)}, u32[]{:S(2)}) async-start(bf16[16,80,256]{2,1,0:T(8,128)(2,1)} %get-tuple-element.109), calls=%async_computation | async-start | bytes 1310720 | tf_op jit(solution)/shard_map/all_to_all | solution.py:776
  17.0 9.4 %collective-permute-start.3 = (f32[80,128]{1,0:T(8,128)S(1)}, f32[80,128]{1,0:T(8,128)S(1)}, u32[]{:S(2)}, u32[]{:S(2)}) collective-permute-start(f32[80,128]{1,0:T(8,128)S(1)} %pad_maximum_fusion.refs_0_), channel_id=1, source_target_pairs={{0,1},{1,0},{2,3},{3,2},{4,5},{5,4},{6,7},{7,6},{8,9},{9,8},{10,11... | collective-permute-start | bytes 122888 | tf_op jit(solution)/shard_map/ppermute | solution.py:663
  19.0 7.4 %collective-permute-start.4 = (f32[80,128]{1,0:T(8,128)S(1)}, f32[80,128]{1,0:T(8,128)S(1)}, u32[]{:S(2)}, u32[]{:S(2)}) collective-permute-start(f32[80,128]{1,0:T(8,128)S(1)} %pad_maximum_fusion.refs_0_), channel_id=1, source_target_pairs={{0,2},{1,3},{2,0},{3,1},{4,6},{5,7},{6,4},{7,5},{8,10},{9,11},{10,... | collective-permute-start | bytes 122888 | tf_op jit(solution)/shard_map/ppermute | solution.py:663
  32.8 9.4 %collective-permute-start.6 = (bf16[16,16,256]{2,1,0:T(8,128)(2,1)S(1)}, bf16[16,16,256]{2,1,0:T(8,128)(2,1)S(1)}, u32[]{:S(2)}, u32[]{:S(2)}) collective-permute-start(bf16[16,16,256]{2,1,0:T(8,128)(2,1)S(1)} %slice.59.refs_0_), channel_id=1, source_target_pairs={{0,1},{1,0},{2,3},{3,2},{4,5},{5,4},{6,7},{7,6},{8,9},{9,8},{10,11... | collective-permute-start | bytes 393224 | tf_op jit(solution)/shard_map/ppermute | solution.py:663
  33.7 9.1 %collective-permute-start.7 = (bf16[16,16,256]{2,1,0:T(8,128)(2,1)S(1)}, bf16[16,16,256]{2,1,0:T(8,128)(2,1)S(1)}, u32[]{:S(2)}, u32[]{:S(2)}) collective-permute-start(bf16[16,16,256]{2,1,0:T(8,128)(2,1)S(1)} %slice.59.refs_0_), channel_id=1, source_target_pairs={{0,2},{1,3},{2,0},{3,1},{4,6},{5,7},{6,4},{7,5},{8,10},{9,11},{10,... | collective-permute-start | bytes 393224 | tf_op jit(solution)/shard_map/ppermute | solution.py:663
  35.2 7.7 %collective-permute-start.8 = (bf16[16,16,256]{2,1,0:T(8,128)(2,1)S(1)}, bf16[16,16,256]{2,1,0:T(8,128)(2,1)S(1)}, u32[]{:S(2)}, u32[]{:S(2)}) collective-permute-start(bf16[16,16,256]{2,1,0:T(8,128)(2,1)S(1)} %slice.59.refs_0_), channel_id=1, source_target_pairs={{0,3},{1,2},{2,1},{3,0},{4,7},{5,6},{6,5},{7,4},{8,11},{9,10},{10,... | collective-permute-start | bytes 393224 | tf_op jit(solution)/shard_map/ppermute | solution.py:663
  36.4 14.3 %all-to-all-start.1 = ((bf16[16,32,256]{2,1,0:T(8,128)(2,1)}), bf16[16,32,256]{2,1,0:T(8,128)(2,1)S(1)}, u32[]{:S(2)}, u32[]{:S(2)}) async-start(bf16[16,32,256]{2,1,0:T(8,128)(2,1)} %get-tuple-element.110), calls=%async_computation.1 | async-start | bytes 524288 | tf_op jit(solution)/shard_map/all_to_all | solution.py:818
  42.2 8.5 %collective-permute-start.9 = (bf16[16,16,256]{2,1,0:T(8,128)(2,1)S(1)}, bf16[16,16,256]{2,1,0:T(8,128)(2,1)S(1)}, u32[]{:S(2)}, u32[]{:S(2)}) collective-permute-start(bf16[16,16,256]{2,1,0:T(8,128)(2,1)S(1)} %slice.59.refs_0_), channel_id=1, source_target_pairs={{0,16},{16,0},{1,17},{17,1},{2,18},{18,2},{3,19},{19,3},{4,20},{20... | collective-permute-start | bytes 393224 | tf_op jit(solution)/shard_map/ppermute | solution.py:680
  42.3 8.4 %collective-permute-start.10 = (bf16[16,16,256]{2,1,0:T(8,128)(2,1)S(1)}, bf16[16,16,256]{2,1,0:T(8,128)(2,1)S(1)}, u32[]{:S(2)}, u32[]{:S(2)}) collective-permute-start(bf16[16,16,256]{2,1,0:T(8,128)(2,1)S(1)} %collective-permute-done.6.refs_1_), channel_id=1, source_target_pairs={{0,16},{16,0},{1,17},{17,1},{2,18},{18,2},{3,19},{19,3},{4,20},{20... | collective-permute-start | bytes 393224 | tf_op jit(solution)/shard_map/ppermute | solution.py:680
  42.8 7.9 %collective-permute-start.11 = (bf16[16,16,256]{2,1,0:T(8,128)(2,1)S(1)}, bf16[16,16,256]{2,1,0:T(8,128)(2,1)S(1)}, u32[]{:S(2)}, u32[]{:S(2)}) collective-permute-start(bf16[16,16,256]{2,1,0:T(8,128)(2,1)S(1)} %collective-permute-done.7.refs_2_), channel_id=1, source_target_pairs={{0,16},{16,0},{1,17},{17,1},{2,18},{18,2},{3,19},{19,3},{4,20},{20... | collective-permute-start | bytes 393224 | tf_op jit(solution)/shard_map/ppermute | solution.py:680
  42.8 7.8 %collective-permute-start.12 = (bf16[16,16,256]{2,1,0:T(8,128)(2,1)S(1)}, bf16[16,16,256]{2,1,0:T(8,128)(2,1)S(1)}, u32[]{:S(2)}, u32[]{:S(2)}) collective-permute-start(bf16[16,16,256]{2,1,0:T(8,128)(2,1)S(1)} %collective-permute-done.8.refs_3_), channel_id=1, source_target_pairs={{0,16},{16,0},{1,17},{17,1},{2,18},{18,2},{3,19},{19,3},{4,20},{20... | collective-permute-start | bytes 393224 | tf_op jit(solution)/shard_map/ppermute | solution.py:680
  53.1 18.6 %all-to-all-start.2 = ((bf16[16,64,256]{2,1,0:T(8,128)(2,1)}), bf16[16,64,256]{2,1,0:T(8,128)(2,1)S(1)}, u32[]{:S(2)}, u32[]{:S(2)}) async-start(bf16[16,64,256]{2,1,0:T(8,128)(2,1)} %get-tuple-element.119), calls=%async_computation.2 | async-start | bytes 1048576 | tf_op jit(solution)/shard_map/all_to_all | solution.py:845
  56.9 9.3 %collective-permute-start.16 = (bf16[512,256]{1,0:T(8,128)(2,1)S(1)}, bf16[512,256]{1,0:T(8,128)(2,1)S(1)}, u32[]{:S(2)}, u32[]{:S(2)}) collective-permute-start(bf16[512,256]{1,0:T(8,128)(2,1)S(1)} %get-tuple-element.135), channel_id=1, source_target_pairs={{0,16},{16,0},{1,17},{17,1},{2,18},{18,2},{3,19},{19,3},{4,20},{20... | collective-permute-start | bytes 786440 | tf_op jit(solution)/shard_map/ppermute | solution.py:680
  57.0 9.2 %collective-permute-start.17 = (bf16[512,256]{1,0:T(8,128)(2,1)S(1)}, bf16[512,256]{1,0:T(8,128)(2,1)S(1)}, u32[]{:S(2)}, u32[]{:S(2)}) collective-permute-start(bf16[512,256]{1,0:T(8,128)(2,1)S(1)} %bitcast.19), channel_id=1, source_target_pairs={{0,16},{16,0},{1,17},{17,1},{2,18},{18,2},{3,19},{19,3},{4,20},{20... | collective-permute-start | bytes 786440 | tf_op jit(solution)/shard_map/ppermute | solution.py:680
  67.3 14.4 %collective-permute-start.18 = (f32[136,512]{1,0:T(8,128)S(1)}, f32[136,512]{1,0:T(8,128)S(1)}, u32[]{:S(2)}, u32[]{:S(2)}) collective-permute-start(f32[136,512]{1,0:T(8,128)S(1)} %get-tuple-element.139), channel_id=1, source_target_pairs={{0,1},{1,0},{2,3},{3,2},{4,5},{5,4},{6,7},{7,6},{8,9},{9,8},{10,11... | collective-permute-start | bytes 835592 | tf_op jit(solution)/shard_map/ppermute | solution.py:663
  69.1 14.3 %collective-permute-start.19 = (f32[136,512]{1,0:T(8,128)S(1)}, f32[136,512]{1,0:T(8,128)S(1)}, u32[]{:S(2)}, u32[]{:S(2)}) collective-permute-start(f32[136,512]{1,0:T(8,128)S(1)} %get-tuple-element.140), channel_id=1, source_target_pairs={{0,2},{1,3},{2,0},{3,1},{4,6},{5,7},{6,4},{7,5},{8,10},{9,11},{10,... | collective-permute-start | bytes 835592 | tf_op jit(solution)/shard_map/ppermute | solution.py:663
  70.6 13.2 %collective-permute-start.20 = (f32[136,512]{1,0:T(8,128)S(1)}, f32[136,512]{1,0:T(8,128)S(1)}, u32[]{:S(2)}, u32[]{:S(2)}) collective-permute-start(f32[136,512]{1,0:T(8,128)S(1)} %get-tuple-element.141), channel_id=1, source_target_pairs={{0,3},{1,2},{2,1},{3,0},{4,7},{5,6},{6,5},{7,4},{8,11},{9,10},{10,... | collective-permute-start | bytes 835592 | tf_op jit(solution)/shard_map/ppermute | solution.py:663
  79.0 7.0 %collective-permute-start.15 = (f32[2,32,128]{2,1,0:T(8,128)S(1)}, f32[2,32,128]{2,1,0:T(8,128)S(1)}, u32[]{:S(2)}, u32[]{:S(2)}) collective-permute-start(f32[2,32,128]{2,1,0:T(8,128)S(1)} %get-tuple-element.133), channel_id=1, source_target_pairs={{0,12},{1,13},{2,14},{3,15},{4,8},{5,9},{6,10},{7,11},{8,4},{9,5},... | collective-permute-start | bytes 98312 | tf_op jit(solution)/shard_map/ppermute | solution.py:663
  86.5 10.4 %collective-permute-start.22 = (f32[2,32,128]{2,1,0:T(8,128)S(1)}, f32[2,32,128]{2,1,0:T(8,128)S(1)}, u32[]{:S(2)}, u32[]{:S(2)}) collective-permute-start(f32[2,32,128]{2,1,0:T(8,128)S(1)} %add_add_fusion.1), channel_id=1, source_target_pairs={{0,1},{1,0},{2,3},{3,2},{4,5},{5,4},{6,7},{7,6},{8,9},{9,8},{10,11... | collective-permute-start | bytes 98312 | tf_op jit(solution)/shard_map/ppermute | solution.py:663
  88.1 8.8 %collective-permute-start.23 = (f32[2,32,128]{2,1,0:T(8,128)S(1)}, f32[2,32,128]{2,1,0:T(8,128)S(1)}, u32[]{:S(2)}, u32[]{:S(2)}) collective-permute-start(f32[2,32,128]{2,1,0:T(8,128)S(1)} %add_add_fusion.1), channel_id=1, source_target_pairs={{0,2},{1,3},{2,0},{3,1},{4,6},{5,7},{6,4},{7,5},{8,10},{9,11},{10,... | collective-permute-start | bytes 98312 | tf_op jit(solution)/shard_map/ppermute | solution.py:663
  89.6 7.3 %collective-permute-start.24 = (f32[2,32,128]{2,1,0:T(8,128)S(1)}, f32[2,32,128]{2,1,0:T(8,128)S(1)}, u32[]{:S(2)}, u32[]{:S(2)}) collective-permute-start(f32[2,32,128]{2,1,0:T(8,128)S(1)} %add_add_fusion.1), channel_id=1, source_target_pairs={{0,3},{1,2},{2,1},{3,0},{4,7},{5,6},{6,5},{7,4},{8,11},{9,10},{10,... | collective-permute-start | bytes 98312 | tf_op jit(solution)/shard_map/ppermute | solution.py:663
  (21 other events, 209.9 us)

commit v8 on v7

--- a/solution.py
+++ b/solution.py
@@ -906,7 +906,7 @@
                 [],
                 large,
                 G,
-            )(pin(u_rev), pin(lift), g_pre, p_blk, r_blk, rx_blk, pin(state), pin(state_x), pin(near_tab), jump)
+            )(u_rev, lift, g_pre, p_blk, r_blk, rx_blk, state, state_x, near_tab, jump)
             got, rows, terms = lax.optimization_barrier((got, rows, terms))
         sums = sum(got, sums)
     grad_tokens = call(partial(last_kernel, count=H), shape((C, L), F32), 5)(tokens, grad_out, gn, stat, sums)

time: 101 us -> 100 us (0.990)
  Pallas kernels: 44.8 us -> 43.2 us
    pallas_call x1, Pallas kernels: 3.79 us -> 2.09 us  [per_device(): by_channel(sums_kernel, shape((C, 40, B), F32), [chan(3 * N, 2 * B)] + [c...]
  transfers between devices with their start and end apart: 31 -> 31, of which waited for: 5 -> 6; matrix products, arithmetic and copies ran while one was open for 0% -> 0% of each run, Pallas kernels for 37% -> 36%
where the time goes in v8:
time: 100 us; the launch traced here: 99.9 us
  starting transfers between devices  47.2 us (47%)
  Pallas kernels  43.2 us (43%)
  waiting for transfers between devices  7.43 us (7%)
  between operations  1.84 us (2%)
    ppermute x20, starting transfers between devices, exchange(): return lax.ppermute(v, axis, [(k, k ^ off) for k in range(size)])  28.4 us
    pallas_call x2, Pallas kernels, back_tables(): pl.pallas_call(partial(back_table_kernel, M=M, start=start), grid=(steps,...  7.47 us
    pallas_call x1, Pallas kernels, per_device(): by_channel(partial(back_kernel, count=H), (shape((C, L), BF16), shape((C,...  7.18 us
    all_to_all x1, starting transfers between devices, per_device(): first = lax.all_to_all(pay, 'mp', split_axis=0, concat_axis=0, tiled=True)  7.01 us
    all_to_all x1, starting transfers between devices, per_device(): lax.all_to_all(mixed, 'mp', split_axis=0, concat_axis=0, tiled=True)  5.77 us
    pallas_call x1, Pallas kernels, per_device(): by_channel(partial(table_kernel, M=M), (shape((C, 2 * B, 2 * B), BF16), f...  5.46 us
    pallas_call x1, Pallas kernels, per_device(): by_channel(partial(mixer_kernel, count=H, parts=len(parts)), (shape((mp,...  5.24 us
    pallas_call x1, Pallas kernels, per_device(): by_channel(partial(lift_kernel, count=H), (far((C, 3 * N, 2 * B), BF16),...  4.94 us
  transfers between devices with their start and end apart: 31, of which 6 were waited for; matrix products, arithmetic and copies ran while one was open for 0% of the time, Pallas kernels for 36%

profile of v8, /device:TPU:0, one launch (start us, length us, event | category | flops | bytes accessed | tf_op | source)
XLA Modules:
  0.0 99.9 jit_solution(15177367288024857928)
XLA Ops:
  0.8 2.7 %shard_map.254 = (f32[80,128]{1,0:T(8,128)S(1)}, bf16[16,80,256]{2,1,0:T(8,128)(2,1)}) custom-call(s32[2]{0:T(128)S(1)} %pad_add_fusion.place_ref, bf16[32,4096]{1,0:T(8,128)(2,1)} %x_ref.7, bf16[32,4096]{1,0:T(8,128)(2,1)} %g_ref.1, bf16[32,512]{1,0:T(8,128)(2,1)} %bitcast.26, bf16[32,512]{1,0:T(8,128)(2,1)} %bitcast.27, bf16[1,32]{1,0:T(2,128)(2,1)} %bitcast.28, ...), custom_call_target="tpu_custom_call" | custom-call | flops 3000000000 | bytes 3000000 | tf_op jit(solution)/shard_map/pallas_call | solution.py:762
  3.5 5.1 %collective-permute-start.2 = (f32[80,128]{1,0:T(8,128)S(1)}, f32[80,128]{1,0:T(8,128)S(1)}, u32[]{:S(2)}, u32[]{:S(2)}) collective-permute-start(f32[80,128]{1,0:T(8,128)S(1)} %get-tuple-element.95), channel_id=1, source_target_pairs={{0,12},{1,13},{2,14},{3,15},{4,8},{5,9},{6,10},{7,11},{8,4},{9,5},... | collective-permute-start | bytes 122888 | tf_op jit(solution)/shard_map/ppermute | solution.py:663
  9.2 7.0 %all-to-all-start = ((bf16[16,80,256]{2,1,0:T(8,128)(2,1)}), bf16[16,80,256]{2,1,0:T(8,128)(2,1)S(1)}, u32[]{:S(2)}, u32[]{:S(2)}) async-start(bf16[16,80,256]{2,1,0:T(8,128)(2,1)} %get-tuple-element.109), calls=%async_computation | async-start | bytes 1310720 | tf_op jit(solution)/shard_map/all_to_all | solution.py:776
  17.0 2.0 %collective-permute-start.3 = (f32[80,128]{1,0:T(8,128)S(1)}, f32[80,128]{1,0:T(8,128)S(1)}, u32[]{:S(2)}, u32[]{:S(2)}) collective-permute-start(f32[80,128]{1,0:T(8,128)S(1)} %pad_maximum_fusion.refs_0_), channel_id=1, source_target_pairs={{0,1},{1,0},{2,3},{3,2},{4,5},{5,4},{6,7},{7,6},{8,9},{9,8},{10,11... | collective-permute-start | bytes 122888 | tf_op jit(solution)/shard_map/ppermute | solution.py:663
  20.9 5.5 %shard_map.256 = (bf16[32,256,256]{2,1,0:T(8,128)(2,1)S(1)}, bf16[32,256,256]{2,1,0:T(8,128)(2,1)}, bf16[32,384,256]{2,1,0:T(8,128)(2,1)S(1)}) custom-call(f32[2,128,128]{2,1,0:T(8,128)S(1)} %get-tuple-element.122.cols), custom_call_target="tpu_custom_call" | custom-call | flops 6000000000 | bytes 6000000 | tf_op jit(solution)/shard_map/pallas_call | solution.py:788
  26.4 5.2 %shard_map.257 = (bf16[16,32,256]{2,1,0:T(8,128)(2,1)}, f32[32,32,128]{2,1,0:T(8,128)}, f32[32,32,128]{2,1,0:T(8,128)}, f32[32,32,128]{2,1,0:T(8,128)}, f32[2,32,128]{2,1,0:T(8,128)}, /*index=5*/f32[16,128]{1,0:T(8,128)S(1)}) custom-call(s32[1]{0:T(128)S(6)} %copy.33.len_ref, f32[3,32]{1,0:T(4,128)S(1)} %pad_maximum_fusion.1.vec_ref, ...), custom_call_target="tpu_custom_call" | custom-call | flops 6000000000 | bytes 6000000 | tf_op jit(solution)/shard_map/pallas_call | solution.py:799
  33.7 1.5 %collective-permute-start.7 = (bf16[16,16,256]{2,1,0:T(8,128)(2,1)S(1)}, bf16[16,16,256]{2,1,0:T(8,128)(2,1)S(1)}, u32[]{:S(2)}, u32[]{:S(2)}) collective-permute-start(bf16[16,16,256]{2,1,0:T(8,128)(2,1)S(1)} %slice.59.refs_0_), channel_id=1, source_target_pairs={{0,2},{1,3},{2,0},{3,1},{4,6},{5,7},{6,4},{7,5},{8,10},{9,11},{10,... | collective-permute-start | bytes 393224 | tf_op jit(solution)/shard_map/ppermute | solution.py:663
  36.4 5.8 %all-to-all-start.1 = ((bf16[16,32,256]{2,1,0:T(8,128)(2,1)}), bf16[16,32,256]{2,1,0:T(8,128)(2,1)S(1)}, u32[]{:S(2)}, u32[]{:S(2)}) async-start(bf16[16,32,256]{2,1,0:T(8,128)(2,1)} %get-tuple-element.110), calls=%async_computation.1 | async-start | bytes 524288 | tf_op jit(solution)/shard_map/all_to_all | solution.py:818
  43.3 3.7 %shard_map.258 = (bf16[32,192,512]{2,1,0:T(8,128)(2,1)}, bf16[32,128,256]{2,1,0:T(8,128)(2,1)}) custom-call(f32[2,128,128]{2,1,0:T(8,128)S(1)} %get-tuple-element.122.cols), custom_call_target="tpu_custom_call" | custom-call | flops 4000000000 | bytes 4000000 | tf_op jit(solution)/shard_map/pallas_call | solution.py:825
  47.0 3.7 %all-to-all-done.1.in_ref = bf16[16,32,256]{2,1,0:T(8,128)(2,1)S(1)} async-done(((bf16[16,32,256]{2,1,0:T(8,128)(2,1)}), bf16[16,32,256]{2,1,0:T(8,128)(2,1)S(1)}, u32[]{:S(2)}, u32[]{:S(2)}) %all-to-all-start.1) | async-done | bytes 262176 | tf_op jit(solution)/shard_map/all_to_all | solution.py:818
  50.7 2.4 %shard_map.259 = (bf16[16,64,256]{2,1,0:T(8,128)(2,1)}, bf16[512,256]{1,0:T(8,128)(2,1)S(1)}, bf16[512,256]{1,0:T(8,128)(2,1)S(1)}) custom-call(s32[2]{0:T(128)S(1)} %pad_add_fusion.place_ref, bf16[16,32,256]{2,1,0:T(8,128)(2,1)S(1)} %all-to-all-done.1.in_ref, bf16[16,80,256]{2,1,0:T(8,128)(2,1)S(1)} %all-to-all-done.first_ref, ...), custom_call_target="tpu_custom_call" | custom-call | flops 2000000000 | bytes 2000000 | tf_op jit(solution)/shard_map/pallas_call | solution.py:838
  53.2 3.8 %all-to-all-start.2 = ((bf16[16,64,256]{2,1,0:T(8,128)(2,1)}), bf16[16,64,256]{2,1,0:T(8,128)(2,1)S(1)}, u32[]{:S(2)}, u32[]{:S(2)}) async-start(bf16[16,64,256]{2,1,0:T(8,128)(2,1)} %get-tuple-element.119), calls=%async_computation.2 | async-start | bytes 1048576 | tf_op jit(solution)/shard_map/all_to_all | solution.py:845
  57.5 3.8 %shard_map.261 = (bf16[32,192,512]{2,1,0:T(8,128)(2,1)}, bf16[32,128,256]{2,1,0:T(8,128)(2,1)}) custom-call(f32[2,128,128]{2,1,0:T(8,128)S(1)} %get-tuple-element.122.cols, bf16[32,192,512]{2,1,0:T(8,128)(2,1)} %get-tuple-element.123.refs_0_, bf16[32,128,256]{2,1,0:T(8,128)(2,1)} %get-tuple-element.124.refs_1_), custom_call_target="tpu_custom_call", output_to_operand_aliasing={{0}: (1, {}), {1}: (2, {})} | custom-call | flops 4000000000 | bytes 4000000 | tf_op jit(solution)/shard_map/pallas_call | solution.py:825
  61.2 4.9 %shard_map.260 = (bf16[32,96,256]{2,1,0:T(8,128)(2,1)}, f32[32,32,128]{2,1,0:T(8,128)}) custom-call(s32[1]{0:T(128)S(6)} %copy.33.len_ref, f32[3,32]{1,0:T(4,128)} %copy-done, bf16[32,4096]{1,0:T(8,128)(2,1)} %x_ref.7, f32[2,32,128]{2,1,0:T(8,128)} %get-tuple-element.107.stat_ref, bf16[32,256,256]{2,1,0:T(8,128)(2,1)} %get-tuple-element.120.f_ref), custom_call_target="tpu_custom_call" | custom-call | flops 3000000000 | bytes 3000000 | tf_op jit(solution)/shard_map/pallas_call | solution.py:846
  67.4 1.8 %collective-permute-start.18 = (f32[136,512]{1,0:T(8,128)S(1)}, f32[136,512]{1,0:T(8,128)S(1)}, u32[]{:S(2)}, u32[]{:S(2)}) collective-permute-start(f32[136,512]{1,0:T(8,128)S(1)} %get-tuple-element.139), channel_id=1, source_target_pairs={{0,1},{1,0},{2,3},{3,2},{4,5},{5,4},{6,7},{7,6},{8,9},{9,8},{10,11... | collective-permute-start | bytes 835592 | tf_op jit(solution)/shard_map/ppermute | solution.py:663
  71.8 7.2 %shard_map.262 = (bf16[32,4096]{1,0:T(8,128)(2,1)}, f32[32,4096]{1,0:T(8,128)S(1)}, f32[2,32,128]{2,1,0:T(8,128)S(1)}, f32[32,24,128]{2,1,0:T(8,128)S(1)}, f32[3...) custom-call(s32[1]{0:T(128)S(6)} %copy.33.len_ref, ...), custom_call_target="tpu_custom_call" | custom-call | flops 7000000000 | bytes 7000000 | tf_op jit(solution)/shard_map/pallas_call | solution.py:866
  79.1 2.7 %collective-permute-start.15 = (f32[2,32,128]{2,1,0:T(8,128)S(1)}, f32[2,32,128]{2,1,0:T(8,128)S(1)}, u32[]{:S(2)}, u32[]{:S(2)}) collective-permute-start(f32[2,32,128]{2,1,0:T(8,128)S(1)} %get-tuple-element.133), channel_id=1, source_target_pairs={{0,12},{1,13},{2,14},{3,15},{4,8},{5,9},{6,10},{7,11},{8,4},{9,5},... | collective-permute-start | bytes 98312 | tf_op jit(solution)/shard_map/ppermute | solution.py:663
  81.8 1.7 %collective-permute-start.13 = (f32[2,32,128]{2,1,0:T(8,128)S(1)}, f32[2,32,128]{2,1,0:T(8,128)S(1)}, u32[]{:S(2)}, u32[]{:S(2)}) collective-permute-start(f32[2,32,128]{2,1,0:T(8,128)S(1)} %get-tuple-element.133), channel_id=1, source_target_pairs={{0,4},{1,5},{2,6},{3,7},{4,0},{5,1},{6,2},{7,3},{8,12},{9,13},{10,... | collective-permute-start | bytes 98312 | tf_op jit(solution)/shard_map/ppermute | solution.py:663
  84.4 1.6 %collective-permute-start.21 = (f32[72,512]{1,0:T(8,128)S(1)}, f32[72,512]{1,0:T(8,128)S(1)}, u32[]{:S(2)}, u32[]{:S(2)}) collective-permute-start(f32[72,512]{1,0:T(8,128)S(1)} %get-tuple-element.143), channel_id=1, source_target_pairs={{0,4},{1,5},{2,6},{3,7},{4,0},{5,1},{6,2},{7,3},{8,12},{9,13},{10,... | collective-permute-start | bytes 442376 | tf_op jit(solution)/shard_map/ppermute | solution.py:663
  86.6 1.6 %collective-permute-start.22 = (f32[2,32,128]{2,1,0:T(8,128)S(1)}, f32[2,32,128]{2,1,0:T(8,128)S(1)}, u32[]{:S(2)}, u32[]{:S(2)}) collective-permute-start(f32[2,32,128]{2,1,0:T(8,128)S(1)} %add_add_fusion.1), channel_id=1, source_target_pairs={{0,1},{1,0},{2,3},{3,2},{4,5},{5,4},{6,7},{7,6},{8,9},{9,8},{10,11... | collective-permute-start | bytes 98312 | tf_op jit(solution)/shard_map/ppermute | solution.py:663
  88.2 1.5 %collective-permute-start.23 = (f32[2,32,128]{2,1,0:T(8,128)S(1)}, f32[2,32,128]{2,1,0:T(8,128)S(1)}, u32[]{:S(2)}, u32[]{:S(2)}) collective-permute-start(f32[2,32,128]{2,1,0:T(8,128)S(1)} %add_add_fusion.1), channel_id=1, source_target_pairs={{0,2},{1,3},{2,0},{3,1},{4,6},{5,7},{6,4},{7,5},{8,10},{9,11},{10,... | collective-permute-start | bytes 98312 | tf_op jit(solution)/shard_map/ppermute | solution.py:663
  90.7 2.4 %collective-permute-start.25 = (f32[40,512]{1,0:T(8,128)S(1)}, f32[40,512]{1,0:T(8,128)S(1)}, u32[]{:S(2)}, u32[]{:S(2)}) collective-permute-start(f32[40,512]{1,0:T(8,128)S(1)} %get-tuple-element.155), channel_id=1, source_target_pairs={{0,8},{1,9},{2,10},{3,11},{4,12},{5,13},{6,14},{7,15},{8,0},{9,1},... | collective-permute-start | bytes 245768 | tf_op jit(solution)/shard_map/ppermute | solution.py:663
  93.2 2.1 %shard_map.266.ref = f32[32,40,128]{2,1,0:T(8,128)S(1)} custom-call(bf16[32,96,256]{2,1,0:T(8,128)(2,1)S(1)} %copy-done.11, f32[32,32,128]{2,1,0:T(8,128)S(1)} %copy-done.12, f32[32,32,128]{2,1,0:T(8,128)S(1)} %get-tuple-element.148.g_ref, f32[32,32,128]{2,1,0:T(8,128)S(1)} %get-tuple-element.149.p_ref, f32[32,32,128]{2,1,0:T(8,128)S(1)} %get-tuple-element.150.r_ref, ...), custom_call_target="tpu_custom_call" | custom-call | flops 20000000000 | bytes 20000000 | tf_op jit(solution)/shard_map/pallas_call | solution.py:900
  98.0 1.8 %shard_map.270 = (f32[32,512]{1,0:T(8,128)}, f32[32,512]{1,0:T(8,128)}, f32[1,32]{1,0:T(1,128)}, f32[1,32]{1,0:T(1,128)}, f32[1,32]{1,0:T(1,128)}, /*index=5*/f3...) custom-call(s32[2]{0:T(128)S(1)} %pad_add_fusion.place_ref, ...), custom_call_target="tpu_custom_call" | custom-call | flops 1000000000 | bytes 1000000 | tf_op jit(solution)/shard_map/pallas_call | solution.py:924
  (101 shorter events, 16.7 us)
Async XLA Ops:
  3.5 13.5 %collective-permute-start.2 = (f32[80,128]{1,0:T(8,128)S(1)}, f32[80,128]{1,0:T(8,128)S(1)}, u32[]{:S(2)}, u32[]{:S(2)}) collective-permute-start(f32[80,128]{1,0:T(8,128)S(1)} %get-tuple-element.95), channel_id=1, source_target_pairs={{0,12},{1,13},{2,14},{3,15},{4,8},{5,9},{6,10},{7,11},{8,4},{9,5},... | collective-permute-start | bytes 122888 | tf_op jit(solution)/shard_map/ppermute | solution.py:663
  8.6 8.4 %collective-permute-start.1 = (f32[80,128]{1,0:T(8,128)S(1)}, f32[80,128]{1,0:T(8,128)S(1)}, u32[]{:S(2)}, u32[]{:S(2)}) collective-permute-start(f32[80,128]{1,0:T(8,128)S(1)} %get-tuple-element.95), channel_id=1, source_target_pairs={{0,8},{1,9},{2,10},{3,11},{4,12},{5,13},{6,14},{7,15},{8,0},{9,1},... | collective-permute-start | bytes 122888 | tf_op jit(solution)/shard_map/ppermute | solution.py:663
  8.6 8.4 %collective-permute-start = (f32[80,128]{1,0:T(8,128)S(1)}, f32[80,128]{1,0:T(8,128)S(1)}, u32[]{:S(2)}, u32[]{:S(2)}) collective-permute-start(f32[80,128]{1,0:T(8,128)S(1)} %get-tuple-element.95), channel_id=1, source_target_pairs={{0,4},{1,5},{2,6},{3,7},{4,0},{5,1},{6,2},{7,3},{8,12},{9,13},{10,... | collective-permute-start | bytes 122888 | tf_op jit(solution)/shard_map/ppermute | solution.py:663
  9.2 23.6 %all-to-all-start = ((bf16[16,80,256]{2,1,0:T(8,128)(2,1)}), bf16[16,80,256]{2,1,0:T(8,128)(2,1)S(1)}, u32[]{:S(2)}, u32[]{:S(2)}) async-start(bf16[16,80,256]{2,1,0:T(8,128)(2,1)} %get-tuple-element.109), calls=%async_computation | async-start | bytes 1310720 | tf_op jit(solution)/shard_map/all_to_all | solution.py:776
  17.0 9.4 %collective-permute-start.3 = (f32[80,128]{1,0:T(8,128)S(1)}, f32[80,128]{1,0:T(8,128)S(1)}, u32[]{:S(2)}, u32[]{:S(2)}) collective-permute-start(f32[80,128]{1,0:T(8,128)S(1)} %pad_maximum_fusion.refs_0_), channel_id=1, source_target_pairs={{0,1},{1,0},{2,3},{3,2},{4,5},{5,4},{6,7},{7,6},{8,9},{9,8},{10,11... | collective-permute-start | bytes 122888 | tf_op jit(solution)/shard_map/ppermute | solution.py:663
  19.0 7.4 %collective-permute-start.4 = (f32[80,128]{1,0:T(8,128)S(1)}, f32[80,128]{1,0:T(8,128)S(1)}, u32[]{:S(2)}, u32[]{:S(2)}) collective-permute-start(f32[80,128]{1,0:T(8,128)S(1)} %pad_maximum_fusion.refs_0_), channel_id=1, source_target_pairs={{0,2},{1,3},{2,0},{3,1},{4,6},{5,7},{6,4},{7,5},{8,10},{9,11},{10,... | collective-permute-start | bytes 122888 | tf_op jit(solution)/shard_map/ppermute | solution.py:663
  20.5 5.9 %collective-permute-start.5 = (f32[80,128]{1,0:T(8,128)S(1)}, f32[80,128]{1,0:T(8,128)S(1)}, u32[]{:S(2)}, u32[]{:S(2)}) collective-permute-start(f32[80,128]{1,0:T(8,128)S(1)} %pad_maximum_fusion.refs_0_), channel_id=1, source_target_pairs={{0,3},{1,2},{2,1},{3,0},{4,7},{5,6},{6,5},{7,4},{8,11},{9,10},{10,... | collective-permute-start | bytes 122888 | tf_op jit(solution)/shard_map/ppermute | solution.py:663
  32.9 9.4 %collective-permute-start.6 = (bf16[16,16,256]{2,1,0:T(8,128)(2,1)S(1)}, bf16[16,16,256]{2,1,0:T(8,128)(2,1)S(1)}, u32[]{:S(2)}, u32[]{:S(2)}) collective-permute-start(bf16[16,16,256]{2,1,0:T(8,128)(2,1)S(1)} %slice.59.refs_0_), channel_id=1, source_target_pairs={{0,1},{1,0},{2,3},{3,2},{4,5},{5,4},{6,7},{7,6},{8,9},{9,8},{10,11... | collective-permute-start | bytes 393224 | tf_op jit(solution)/shard_map/ppermute | solution.py:663
  33.7 9.1 %collective-permute-start.7 = (bf16[16,16,256]{2,1,0:T(8,128)(2,1)S(1)}, bf16[16,16,256]{2,1,0:T(8,128)(2,1)S(1)}, u32[]{:S(2)}, u32[]{:S(2)}) collective-permute-start(bf16[16,16,256]{2,1,0:T(8,128)(2,1)S(1)} %slice.59.refs_0_), channel_id=1, source_target_pairs={{0,2},{1,3},{2,0},{3,1},{4,6},{5,7},{6,4},{7,5},{8,10},{9,11},{10,... | collective-permute-start | bytes 393224 | tf_op jit(solution)/shard_map/ppermute | solution.py:663
  35.2 7.7 %collective-permute-start.8 = (bf16[16,16,256]{2,1,0:T(8,128)(2,1)S(1)}, bf16[16,16,256]{2,1,0:T(8,128)(2,1)S(1)}, u32[]{:S(2)}, u32[]{:S(2)}) collective-permute-start(bf16[16,16,256]{2,1,0:T(8,128)(2,1)S(1)} %slice.59.refs_0_), channel_id=1, source_target_pairs={{0,3},{1,2},{2,1},{3,0},{4,7},{5,6},{6,5},{7,4},{8,11},{9,10},{10,... | collective-permute-start | bytes 393224 | tf_op jit(solution)/shard_map/ppermute | solution.py:663
  36.4 14.3 %all-to-all-start.1 = ((bf16[16,32,256]{2,1,0:T(8,128)(2,1)}), bf16[16,32,256]{2,1,0:T(8,128)(2,1)S(1)}, u32[]{:S(2)}, u32[]{:S(2)}) async-start(bf16[16,32,256]{2,1,0:T(8,128)(2,1)} %get-tuple-element.110), calls=%async_computation.1 | async-start | bytes 524288 | tf_op jit(solution)/shard_map/all_to_all | solution.py:818
  42.2 8.5 %collective-permute-start.9 = (bf16[16,16,256]{2,1,0:T(8,128)(2,1)S(1)}, bf16[16,16,256]{2,1,0:T(8,128)(2,1)S(1)}, u32[]{:S(2)}, u32[]{:S(2)}) collective-permute-start(bf16[16,16,256]{2,1,0:T(8,128)(2,1)S(1)} %slice.59.refs_0_), channel_id=1, source_target_pairs={{0,16},{16,0},{1,17},{17,1},{2,18},{18,2},{3,19},{19,3},{4,20},{20... | collective-permute-start | bytes 393224 | tf_op jit(solution)/shard_map/ppermute | solution.py:680
  42.3 8.4 %collective-permute-start.10 = (bf16[16,16,256]{2,1,0:T(8,128)(2,1)S(1)}, bf16[16,16,256]{2,1,0:T(8,128)(2,1)S(1)}, u32[]{:S(2)}, u32[]{:S(2)}) collective-permute-start(bf16[16,16,256]{2,1,0:T(8,128)(2,1)S(1)} %collective-permute-done.6.refs_1_), channel_id=1, source_target_pairs={{0,16},{16,0},{1,17},{17,1},{2,18},{18,2},{3,19},{19,3},{4,20},{20... | collective-permute-start | bytes 393224 | tf_op jit(solution)/shard_map/ppermute | solution.py:680
  42.8 7.9 %collective-permute-start.11 = (bf16[16,16,256]{2,1,0:T(8,128)(2,1)S(1)}, bf16[16,16,256]{2,1,0:T(8,128)(2,1)S(1)}, u32[]{:S(2)}, u32[]{:S(2)}) collective-permute-start(bf16[16,16,256]{2,1,0:T(8,128)(2,1)S(1)} %collective-permute-done.7.refs_2_), channel_id=1, source_target_pairs={{0,16},{16,0},{1,17},{17,1},{2,18},{18,2},{3,19},{19,3},{4,20},{20... | collective-permute-start | bytes 393224 | tf_op jit(solution)/shard_map/ppermute | solution.py:680
  42.9 7.8 %collective-permute-start.12 = (bf16[16,16,256]{2,1,0:T(8,128)(2,1)S(1)}, bf16[16,16,256]{2,1,0:T(8,128)(2,1)S(1)}, u32[]{:S(2)}, u32[]{:S(2)}) collective-permute-start(bf16[16,16,256]{2,1,0:T(8,128)(2,1)S(1)} %collective-permute-done.8.refs_3_), channel_id=1, source_target_pairs={{0,16},{16,0},{1,17},{17,1},{2,18},{18,2},{3,19},{19,3},{4,20},{20... | collective-permute-start | bytes 393224 | tf_op jit(solution)/shard_map/ppermute | solution.py:680
  53.2 18.7 %all-to-all-start.2 = ((bf16[16,64,256]{2,1,0:T(8,128)(2,1)}), bf16[16,64,256]{2,1,0:T(8,128)(2,1)S(1)}, u32[]{:S(2)}, u32[]{:S(2)}) async-start(bf16[16,64,256]{2,1,0:T(8,128)(2,1)} %get-tuple-element.119), calls=%async_computation.2 | async-start | bytes 1048576 | tf_op jit(solution)/shard_map/all_to_all | solution.py:845
  56.9 9.3 %collective-permute-start.16 = (bf16[512,256]{1,0:T(8,128)(2,1)S(1)}, bf16[512,256]{1,0:T(8,128)(2,1)S(1)}, u32[]{:S(2)}, u32[]{:S(2)}) collective-permute-start(bf16[512,256]{1,0:T(8,128)(2,1)S(1)} %get-tuple-element.135), channel_id=1, source_target_pairs={{0,16},{16,0},{1,17},{17,1},{2,18},{18,2},{3,19},{19,3},{4,20},{20... | collective-permute-start | bytes 786440 | tf_op jit(solution)/shard_map/ppermute | solution.py:680
  57.0 9.2 %collective-permute-start.17 = (bf16[512,256]{1,0:T(8,128)(2,1)S(1)}, bf16[512,256]{1,0:T(8,128)(2,1)S(1)}, u32[]{:S(2)}, u32[]{:S(2)}) collective-permute-start(bf16[512,256]{1,0:T(8,128)(2,1)S(1)} %bitcast.19), channel_id=1, source_target_pairs={{0,16},{16,0},{1,17},{17,1},{2,18},{18,2},{3,19},{19,3},{4,20},{20... | collective-permute-start | bytes 786440 | tf_op jit(solution)/shard_map/ppermute | solution.py:680
  67.4 14.4 %collective-permute-start.18 = (f32[136,512]{1,0:T(8,128)S(1)}, f32[136,512]{1,0:T(8,128)S(1)}, u32[]{:S(2)}, u32[]{:S(2)}) collective-permute-start(f32[136,512]{1,0:T(8,128)S(1)} %get-tuple-element.139), channel_id=1, source_target_pairs={{0,1},{1,0},{2,3},{3,2},{4,5},{5,4},{6,7},{7,6},{8,9},{9,8},{10,11... | collective-permute-start | bytes 835592 | tf_op jit(solution)/shard_map/ppermute | solution.py:663
  69.1 14.4 %collective-permute-start.19 = (f32[136,512]{1,0:T(8,128)S(1)}, f32[136,512]{1,0:T(8,128)S(1)}, u32[]{:S(2)}, u32[]{:S(2)}) collective-permute-start(f32[136,512]{1,0:T(8,128)S(1)} %get-tuple-element.140), channel_id=1, source_target_pairs={{0,2},{1,3},{2,0},{3,1},{4,6},{5,7},{6,4},{7,5},{8,10},{9,11},{10,... | collective-permute-start | bytes 835592 | tf_op jit(solution)/shard_map/ppermute | solution.py:663
  70.6 13.2 %collective-permute-start.20 = (f32[136,512]{1,0:T(8,128)S(1)}, f32[136,512]{1,0:T(8,128)S(1)}, u32[]{:S(2)}, u32[]{:S(2)}) collective-permute-start(f32[136,512]{1,0:T(8,128)S(1)} %get-tuple-element.141), channel_id=1, source_target_pairs={{0,3},{1,2},{2,1},{3,0},{4,7},{5,6},{6,5},{7,4},{8,11},{9,10},{10,... | collective-permute-start | bytes 835592 | tf_op jit(solution)/shard_map/ppermute | solution.py:663
  79.1 6.9 %collective-permute-start.15 = (f32[2,32,128]{2,1,0:T(8,128)S(1)}, f32[2,32,128]{2,1,0:T(8,128)S(1)}, u32[]{:S(2)}, u32[]{:S(2)}) collective-permute-start(f32[2,32,128]{2,1,0:T(8,128)S(1)} %get-tuple-element.133), channel_id=1, source_target_pairs={{0,12},{1,13},{2,14},{3,15},{4,8},{5,9},{6,10},{7,11},{8,4},{9,5},... | collective-permute-start | bytes 98312 | tf_op jit(solution)/shard_map/ppermute | solution.py:663
  86.6 8.7 %collective-permute-start.22 = (f32[2,32,128]{2,1,0:T(8,128)S(1)}, f32[2,32,128]{2,1,0:T(8,128)S(1)}, u32[]{:S(2)}, u32[]{:S(2)}) collective-permute-start(f32[2,32,128]{2,1,0:T(8,128)S(1)} %add_add_fusion.1), channel_id=1, source_target_pairs={{0,1},{1,0},{2,3},{3,2},{4,5},{5,4},{6,7},{7,6},{8,9},{9,8},{10,11... | collective-permute-start | bytes 98312 | tf_op jit(solution)/shard_map/ppermute | solution.py:663
  88.2 7.1 %collective-permute-start.23 = (f32[2,32,128]{2,1,0:T(8,128)S(1)}, f32[2,32,128]{2,1,0:T(8,128)S(1)}, u32[]{:S(2)}, u32[]{:S(2)}) collective-permute-start(f32[2,32,128]{2,1,0:T(8,128)S(1)} %add_add_fusion.1), channel_id=1, source_target_pairs={{0,2},{1,3},{2,0},{3,1},{4,6},{5,7},{6,4},{7,5},{8,10},{9,11},{10,... | collective-permute-start | bytes 98312 | tf_op jit(solution)/shard_map/ppermute | solution.py:663
  (26 other events, 280.4 us)

commit v9 on v8

--- a/solution.py
+++ b/solution.py
@@ -909,7 +909,18 @@
             )(u_rev, lift, g_pre, p_blk, r_blk, rx_blk, state, state_x, near_tab, jump)
             got, rows, terms = lax.optimization_barrier((got, rows, terms))
         sums = sum(got, sums)
-    grad_tokens = call(partial(last_kernel, count=H), shape((C, L), F32), 5)(tokens, grad_out, gn, stat, sums)
+    cut = 2
+    wide_block = pl.BlockSpec((C, L // cut), lambda i: (0, i))
+    tall_block = pl.BlockSpec((2, N // cut, B), lambda i: (0, i, 0))
+    grad_tokens = pl.pallas_call(
+        partial(last_kernel, count=H),
+        grid=(cut,),
+        out_shape=shape((C, L), F32),
+        in_specs=[wide_block] * 3 + [tall_block] * 2,
+        out_specs=wide_block,
+        compiler_params=params(small),
+        cost_estimate=cost(1),
+    )(tokens, grad_out, gn, stat, sums)
     rows = call(join_kernel, shape((9, C, B), F32), 2)(plain, rows)
     others = sum_docs(rows, dp, 1) - rows if dp > 2 else partner(rows, dp)
 

time: 100 us -> 101 us (1.010)
  no operation moved by 1% of the time
where the time goes in v9:
time: 101 us; the launch traced here: 100 us
  starting transfers between devices  47.2 us (47%)
  Pallas kernels  43.3 us (43%)
  waiting for transfers between devices  7.43 us (7%)
  between operations  1.84 us (2%)
    ppermute x20, starting transfers between devices, exchange(): return lax.ppermute(v, axis, [(k, k ^ off) for k in range(size)])  28.4 us
    pallas_call x2, Pallas kernels, back_tables(): pl.pallas_call(partial(back_table_kernel, M=M, start=start), grid=(steps,...  7.47 us
    pallas_call x1, Pallas kernels, per_device(): by_channel(partial(back_kernel, count=H), (shape((C, L), BF16), shape((C,...  7.18 us
    all_to_all x1, starting transfers between devices, per_device(): first = lax.all_to_all(pay, 'mp', split_axis=0, concat_axis=0, tiled=True)  7.01 us
    all_to_all x1, starting transfers between devices, per_device(): lax.all_to_all(mixed, 'mp', split_axis=0, concat_axis=0, tiled=True)  5.77 us
    pallas_call x1, Pallas kernels, per_device(): by_channel(partial(table_kernel, M=M), (shape((C, 2 * B, 2 * B), BF16), f...  5.46 us
    pallas_call x1, Pallas kernels, per_device(): by_channel(partial(mixer_kernel, count=H, parts=len(parts)), (shape((mp,...  5.24 us
    pallas_call x1, Pallas kernels, per_device(): by_channel(partial(lift_kernel, count=H), (far((C, 3 * N, 2 * B), BF16),...  4.94 us
  transfers between devices with their start and end apart: 31, of which 6 were waited for; matrix products, arithmetic and copies ran while one was open for 0% of the time, Pallas kernels for 36%

profile of v9, /device:TPU:0, one launch (start us, length us, event | category | flops | bytes accessed | tf_op | source)
XLA Modules:
  0.0 100.0 jit_solution(13479111240586692765)
XLA Ops:
  0.8 2.7 %shard_map.254 = (f32[80,128]{1,0:T(8,128)S(1)}, bf16[16,80,256]{2,1,0:T(8,128)(2,1)}) custom-call(s32[2]{0:T(128)S(1)} %pad_add_fusion.place_ref, bf16[32,4096]{1,0:T(8,128)(2,1)} %x_ref.7, bf16[32,4096]{1,0:T(8,128)(2,1)} %g_ref.1, bf16[32,512]{1,0:T(8,128)(2,1)} %bitcast.26, bf16[32,512]{1,0:T(8,128)(2,1)} %bitcast.27, bf16[1,32]{1,0:T(2,128)(2,1)} %bitcast.28, ...), custom_call_target="tpu_custom_call" | custom-call | flops 3000000000 | bytes 3000000 | tf_op jit(solution)/shard_map/pallas_call | solution.py:762
  3.5 5.1 %collective-permute-start.2 = (f32[80,128]{1,0:T(8,128)S(1)}, f32[80,128]{1,0:T(8,128)S(1)}, u32[]{:S(2)}, u32[]{:S(2)}) collective-permute-start(f32[80,128]{1,0:T(8,128)S(1)} %get-tuple-element.95), channel_id=1, source_target_pairs={{0,12},{1,13},{2,14},{3,15},{4,8},{5,9},{6,10},{7,11},{8,4},{9,5},... | collective-permute-start | bytes 122888 | tf_op jit(solution)/shard_map/ppermute | solution.py:663
  9.2 7.0 %all-to-all-start = ((bf16[16,80,256]{2,1,0:T(8,128)(2,1)}), bf16[16,80,256]{2,1,0:T(8,128)(2,1)S(1)}, u32[]{:S(2)}, u32[]{:S(2)}) async-start(bf16[16,80,256]{2,1,0:T(8,128)(2,1)} %get-tuple-element.109), calls=%async_computation | async-start | bytes 1310720 | tf_op jit(solution)/shard_map/all_to_all | solution.py:776
  17.0 2.0 %collective-permute-start.3 = (f32[80,128]{1,0:T(8,128)S(1)}, f32[80,128]{1,0:T(8,128)S(1)}, u32[]{:S(2)}, u32[]{:S(2)}) collective-permute-start(f32[80,128]{1,0:T(8,128)S(1)} %pad_maximum_fusion.refs_0_), channel_id=1, source_target_pairs={{0,1},{1,0},{2,3},{3,2},{4,5},{5,4},{6,7},{7,6},{8,9},{9,8},{10,11... | collective-permute-start | bytes 122888 | tf_op jit(solution)/shard_map/ppermute | solution.py:663
  20.9 5.5 %shard_map.256 = (bf16[32,256,256]{2,1,0:T(8,128)(2,1)S(1)}, bf16[32,256,256]{2,1,0:T(8,128)(2,1)}, bf16[32,384,256]{2,1,0:T(8,128)(2,1)S(1)}) custom-call(f32[2,128,128]{2,1,0:T(8,128)S(1)} %get-tuple-element.122.cols), custom_call_target="tpu_custom_call" | custom-call | flops 6000000000 | bytes 6000000 | tf_op jit(solution)/shard_map/pallas_call | solution.py:788
  26.4 5.2 %shard_map.257 = (bf16[16,32,256]{2,1,0:T(8,128)(2,1)}, f32[32,32,128]{2,1,0:T(8,128)}, f32[32,32,128]{2,1,0:T(8,128)}, f32[32,32,128]{2,1,0:T(8,128)}, f32[2,32,128]{2,1,0:T(8,128)}, /*index=5*/f32[16,128]{1,0:T(8,128)S(1)}) custom-call(s32[1]{0:T(128)S(6)} %copy.33.len_ref, f32[3,32]{1,0:T(4,128)S(1)} %pad_maximum_fusion.1.vec_ref, ...), custom_call_target="tpu_custom_call" | custom-call | flops 6000000000 | bytes 6000000 | tf_op jit(solution)/shard_map/pallas_call | solution.py:799
  33.7 1.5 %collective-permute-start.7 = (bf16[16,16,256]{2,1,0:T(8,128)(2,1)S(1)}, bf16[16,16,256]{2,1,0:T(8,128)(2,1)S(1)}, u32[]{:S(2)}, u32[]{:S(2)}) collective-permute-start(bf16[16,16,256]{2,1,0:T(8,128)(2,1)S(1)} %slice.59.refs_0_), channel_id=1, source_target_pairs={{0,2},{1,3},{2,0},{3,1},{4,6},{5,7},{6,4},{7,5},{8,10},{9,11},{10,... | collective-permute-start | bytes 393224 | tf_op jit(solution)/shard_map/ppermute | solution.py:663
  36.4 5.8 %all-to-all-start.1 = ((bf16[16,32,256]{2,1,0:T(8,128)(2,1)}), bf16[16,32,256]{2,1,0:T(8,128)(2,1)S(1)}, u32[]{:S(2)}, u32[]{:S(2)}) async-start(bf16[16,32,256]{2,1,0:T(8,128)(2,1)} %get-tuple-element.110), calls=%async_computation.1 | async-start | bytes 524288 | tf_op jit(solution)/shard_map/all_to_all | solution.py:818
  43.3 3.7 %shard_map.258 = (bf16[32,192,512]{2,1,0:T(8,128)(2,1)}, bf16[32,128,256]{2,1,0:T(8,128)(2,1)}) custom-call(f32[2,128,128]{2,1,0:T(8,128)S(1)} %get-tuple-element.122.cols), custom_call_target="tpu_custom_call" | custom-call | flops 4000000000 | bytes 4000000 | tf_op jit(solution)/shard_map/pallas_call | solution.py:825
  47.0 3.7 %all-to-all-done.1.in_ref = bf16[16,32,256]{2,1,0:T(8,128)(2,1)S(1)} async-done(((bf16[16,32,256]{2,1,0:T(8,128)(2,1)}), bf16[16,32,256]{2,1,0:T(8,128)(2,1)S(1)}, u32[]{:S(2)}, u32[]{:S(2)}) %all-to-all-start.1) | async-done | bytes 262176 | tf_op jit(solution)/shard_map/all_to_all | solution.py:818
  50.7 2.4 %shard_map.259 = (bf16[16,64,256]{2,1,0:T(8,128)(2,1)}, bf16[512,256]{1,0:T(8,128)(2,1)S(1)}, bf16[512,256]{1,0:T(8,128)(2,1)S(1)}) custom-call(s32[2]{0:T(128)S(1)} %pad_add_fusion.place_ref, bf16[16,32,256]{2,1,0:T(8,128)(2,1)S(1)} %all-to-all-done.1.in_ref, bf16[16,80,256]{2,1,0:T(8,128)(2,1)S(1)} %all-to-all-done.first_ref, ...), custom_call_target="tpu_custom_call" | custom-call | flops 2000000000 | bytes 2000000 | tf_op jit(solution)/shard_map/pallas_call | solution.py:838
  53.2 3.8 %all-to-all-start.2 = ((bf16[16,64,256]{2,1,0:T(8,128)(2,1)}), bf16[16,64,256]{2,1,0:T(8,128)(2,1)S(1)}, u32[]{:S(2)}, u32[]{:S(2)}) async-start(bf16[16,64,256]{2,1,0:T(8,128)(2,1)} %get-tuple-element.119), calls=%async_computation.2 | async-start | bytes 1048576 | tf_op jit(solution)/shard_map/all_to_all | solution.py:845
  57.5 3.8 %shard_map.261 = (bf16[32,192,512]{2,1,0:T(8,128)(2,1)}, bf16[32,128,256]{2,1,0:T(8,128)(2,1)}) custom-call(f32[2,128,128]{2,1,0:T(8,128)S(1)} %get-tuple-element.122.cols, bf16[32,192,512]{2,1,0:T(8,128)(2,1)} %get-tuple-element.123.refs_0_, bf16[32,128,256]{2,1,0:T(8,128)(2,1)} %get-tuple-element.124.refs_1_), custom_call_target="tpu_custom_call", output_to_operand_aliasing={{0}: (1, {}), {1}: (2, {})} | custom-call | flops 4000000000 | bytes 4000000 | tf_op jit(solution)/shard_map/pallas_call | solution.py:825
  61.2 4.9 %shard_map.260 = (bf16[32,96,256]{2,1,0:T(8,128)(2,1)}, f32[32,32,128]{2,1,0:T(8,128)}) custom-call(s32[1]{0:T(128)S(6)} %copy.33.len_ref, f32[3,32]{1,0:T(4,128)} %copy-done, bf16[32,4096]{1,0:T(8,128)(2,1)} %x_ref.7, f32[2,32,128]{2,1,0:T(8,128)} %get-tuple-element.107.stat_ref, bf16[32,256,256]{2,1,0:T(8,128)(2,1)} %get-tuple-element.120.f_ref), custom_call_target="tpu_custom_call" | custom-call | flops 3000000000 | bytes 3000000 | tf_op jit(solution)/shard_map/pallas_call | solution.py:846
  67.4 1.8 %collective-permute-start.18 = (f32[136,512]{1,0:T(8,128)S(1)}, f32[136,512]{1,0:T(8,128)S(1)}, u32[]{:S(2)}, u32[]{:S(2)}) collective-permute-start(f32[136,512]{1,0:T(8,128)S(1)} %get-tuple-element.139), channel_id=1, source_target_pairs={{0,1},{1,0},{2,3},{3,2},{4,5},{5,4},{6,7},{7,6},{8,9},{9,8},{10,11... | collective-permute-start | bytes 835592 | tf_op jit(solution)/shard_map/ppermute | solution.py:663
  71.8 7.2 %shard_map.262 = (bf16[32,4096]{1,0:T(8,128)(2,1)}, f32[32,4096]{1,0:T(8,128)S(1)}, f32[2,32,128]{2,1,0:T(8,128)S(1)}, f32[32,24,128]{2,1,0:T(8,128)S(1)}, f32[3...) custom-call(s32[1]{0:T(128)S(6)} %copy.33.len_ref, ...), custom_call_target="tpu_custom_call" | custom-call | flops 7000000000 | bytes 7000000 | tf_op jit(solution)/shard_map/pallas_call | solution.py:866
  79.1 2.7 %collective-permute-start.15 = (f32[2,32,128]{2,1,0:T(8,128)S(1)}, f32[2,32,128]{2,1,0:T(8,128)S(1)}, u32[]{:S(2)}, u32[]{:S(2)}) collective-permute-start(f32[2,32,128]{2,1,0:T(8,128)S(1)} %get-tuple-element.133), channel_id=1, source_target_pairs={{0,12},{1,13},{2,14},{3,15},{4,8},{5,9},{6,10},{7,11},{8,4},{9,5},... | collective-permute-start | bytes 98312 | tf_op jit(solution)/shard_map/ppermute | solution.py:663
  81.8 1.7 %collective-permute-start.13 = (f32[2,32,128]{2,1,0:T(8,128)S(1)}, f32[2,32,128]{2,1,0:T(8,128)S(1)}, u32[]{:S(2)}, u32[]{:S(2)}) collective-permute-start(f32[2,32,128]{2,1,0:T(8,128)S(1)} %get-tuple-element.133), channel_id=1, source_target_pairs={{0,4},{1,5},{2,6},{3,7},{4,0},{5,1},{6,2},{7,3},{8,12},{9,13},{10,... | collective-permute-start | bytes 98312 | tf_op jit(solution)/shard_map/ppermute | solution.py:663
  84.4 1.6 %collective-permute-start.21 = (f32[72,512]{1,0:T(8,128)S(1)}, f32[72,512]{1,0:T(8,128)S(1)}, u32[]{:S(2)}, u32[]{:S(2)}) collective-permute-start(f32[72,512]{1,0:T(8,128)S(1)} %get-tuple-element.143), channel_id=1, source_target_pairs={{0,4},{1,5},{2,6},{3,7},{4,0},{5,1},{6,2},{7,3},{8,12},{9,13},{10,... | collective-permute-start | bytes 442376 | tf_op jit(solution)/shard_map/ppermute | solution.py:663
  86.6 1.6 %collective-permute-start.22 = (f32[2,32,128]{2,1,0:T(8,128)S(1)}, f32[2,32,128]{2,1,0:T(8,128)S(1)}, u32[]{:S(2)}, u32[]{:S(2)}) collective-permute-start(f32[2,32,128]{2,1,0:T(8,128)S(1)} %add_add_fusion.1), channel_id=1, source_target_pairs={{0,1},{1,0},{2,3},{3,2},{4,5},{5,4},{6,7},{7,6},{8,9},{9,8},{10,11... | collective-permute-start | bytes 98312 | tf_op jit(solution)/shard_map/ppermute | solution.py:663
  88.2 1.5 %collective-permute-start.23 = (f32[2,32,128]{2,1,0:T(8,128)S(1)}, f32[2,32,128]{2,1,0:T(8,128)S(1)}, u32[]{:S(2)}, u32[]{:S(2)}) collective-permute-start(f32[2,32,128]{2,1,0:T(8,128)S(1)} %add_add_fusion.1), channel_id=1, source_target_pairs={{0,2},{1,3},{2,0},{3,1},{4,6},{5,7},{6,4},{7,5},{8,10},{9,11},{10,... | collective-permute-start | bytes 98312 | tf_op jit(solution)/shard_map/ppermute | solution.py:663
  90.7 2.4 %collective-permute-start.25 = (f32[40,512]{1,0:T(8,128)S(1)}, f32[40,512]{1,0:T(8,128)S(1)}, u32[]{:S(2)}, u32[]{:S(2)}) collective-permute-start(f32[40,512]{1,0:T(8,128)S(1)} %get-tuple-element.155), channel_id=1, source_target_pairs={{0,8},{1,9},{2,10},{3,11},{4,12},{5,13},{6,14},{7,15},{8,0},{9,1},... | collective-permute-start | bytes 245768 | tf_op jit(solution)/shard_map/ppermute | solution.py:663
  93.2 2.1 %shard_map.266.ref = f32[32,40,128]{2,1,0:T(8,128)S(1)} custom-call(bf16[32,96,256]{2,1,0:T(8,128)(2,1)S(1)} %copy-done.11, f32[32,32,128]{2,1,0:T(8,128)S(1)} %copy-done.12, f32[32,32,128]{2,1,0:T(8,128)S(1)} %get-tuple-element.148.g_ref, f32[32,32,128]{2,1,0:T(8,128)S(1)} %get-tuple-element.149.p_ref, f32[32,32,128]{2,1,0:T(8,128)S(1)} %get-tuple-element.150.r_ref, ...), custom_call_target="tpu_custom_call" | custom-call | flops 20000000000 | bytes 20000000 | tf_op jit(solution)/shard_map/pallas_call | solution.py:900
  98.1 1.8 %shard_map.270 = (f32[32,512]{1,0:T(8,128)}, f32[32,512]{1,0:T(8,128)}, f32[1,32]{1,0:T(1,128)}, f32[1,32]{1,0:T(1,128)}, f32[1,32]{1,0:T(1,128)}, /*index=5*/f3...) custom-call(s32[2]{0:T(128)S(1)} %pad_add_fusion.place_ref, ...), custom_call_target="tpu_custom_call" | custom-call | flops 1000000000 | bytes 1000000 | tf_op jit(solution)/shard_map/pallas_call | solution.py:935
  (101 shorter events, 16.8 us)
Async XLA Ops:
  3.5 13.5 %collective-permute-start.2 = (f32[80,128]{1,0:T(8,128)S(1)}, f32[80,128]{1,0:T(8,128)S(1)}, u32[]{:S(2)}, u32[]{:S(2)}) collective-permute-start(f32[80,128]{1,0:T(8,128)S(1)} %get-tuple-element.95), channel_id=1, source_target_pairs={{0,12},{1,13},{2,14},{3,15},{4,8},{5,9},{6,10},{7,11},{8,4},{9,5},... | collective-permute-start | bytes 122888 | tf_op jit(solution)/shard_map/ppermute | solution.py:663
  8.6 8.4 %collective-permute-start.1 = (f32[80,128]{1,0:T(8,128)S(1)}, f32[80,128]{1,0:T(8,128)S(1)}, u32[]{:S(2)}, u32[]{:S(2)}) collective-permute-start(f32[80,128]{1,0:T(8,128)S(1)} %get-tuple-element.95), channel_id=1, source_target_pairs={{0,8},{1,9},{2,10},{3,11},{4,12},{5,13},{6,14},{7,15},{8,0},{9,1},... | collective-permute-start | bytes 122888 | tf_op jit(solution)/shard_map/ppermute | solution.py:663
  8.6 8.4 %collective-permute-start = (f32[80,128]{1,0:T(8,128)S(1)}, f32[80,128]{1,0:T(8,128)S(1)}, u32[]{:S(2)}, u32[]{:S(2)}) collective-permute-start(f32[80,128]{1,0:T(8,128)S(1)} %get-tuple-element.95), channel_id=1, source_target_pairs={{0,4},{1,5},{2,6},{3,7},{4,0},{5,1},{6,2},{7,3},{8,12},{9,13},{10,... | collective-permute-start | bytes 122888 | tf_op jit(solution)/shard_map/ppermute | solution.py:663
  9.2 23.6 %all-to-all-start = ((bf16[16,80,256]{2,1,0:T(8,128)(2,1)}), bf16[16,80,256]{2,1,0:T(8,128)(2,1)S(1)}, u32[]{:S(2)}, u32[]{:S(2)}) async-start(bf16[16,80,256]{2,1,0:T(8,128)(2,1)} %get-tuple-element.109), calls=%async_computation | async-start | bytes 1310720 | tf_op jit(solution)/shard_map/all_to_all | solution.py:776
  17.0 9.4 %collective-permute-start.3 = (f32[80,128]{1,0:T(8,128)S(1)}, f32[80,128]{1,0:T(8,128)S(1)}, u32[]{:S(2)}, u32[]{:S(2)}) collective-permute-start(f32[80,128]{1,0:T(8,128)S(1)} %pad_maximum_fusion.refs_0_), channel_id=1, source_target_pairs={{0,1},{1,0},{2,3},{3,2},{4,5},{5,4},{6,7},{7,6},{8,9},{9,8},{10,11... | collective-permute-start | bytes 122888 | tf_op jit(solution)/shard_map/ppermute | solution.py:663
  19.0 7.4 %collective-permute-start.4 = (f32[80,128]{1,0:T(8,128)S(1)}, f32[80,128]{1,0:T(8,128)S(1)}, u32[]{:S(2)}, u32[]{:S(2)}) collective-permute-start(f32[80,128]{1,0:T(8,128)S(1)} %pad_maximum_fusion.refs_0_), channel_id=1, source_target_pairs={{0,2},{1,3},{2,0},{3,1},{4,6},{5,7},{6,4},{7,5},{8,10},{9,11},{10,... | collective-permute-start | bytes 122888 | tf_op jit(solution)/shard_map/ppermute | solution.py:663
  20.5 5.9 %collective-permute-start.5 = (f32[80,128]{1,0:T(8,128)S(1)}, f32[80,128]{1,0:T(8,128)S(1)}, u32[]{:S(2)}, u32[]{:S(2)}) collective-permute-start(f32[80,128]{1,0:T(8,128)S(1)} %pad_maximum_fusion.refs_0_), channel_id=1, source_target_pairs={{0,3},{1,2},{2,1},{3,0},{4,7},{5,6},{6,5},{7,4},{8,11},{9,10},{10,... | collective-permute-start | bytes 122888 | tf_op jit(solution)/shard_map/ppermute | solution.py:663
  32.9 9.4 %collective-permute-start.6 = (bf16[16,16,256]{2,1,0:T(8,128)(2,1)S(1)}, bf16[16,16,256]{2,1,0:T(8,128)(2,1)S(1)}, u32[]{:S(2)}, u32[]{:S(2)}) collective-permute-start(bf16[16,16,256]{2,1,0:T(8,128)(2,1)S(1)} %slice.59.refs_0_), channel_id=1, source_target_pairs={{0,1},{1,0},{2,3},{3,2},{4,5},{5,4},{6,7},{7,6},{8,9},{9,8},{10,11... | collective-permute-start | bytes 393224 | tf_op jit(solution)/shard_map/ppermute | solution.py:663
  33.7 9.1 %collective-permute-start.7 = (bf16[16,16,256]{2,1,0:T(8,128)(2,1)S(1)}, bf16[16,16,256]{2,1,0:T(8,128)(2,1)S(1)}, u32[]{:S(2)}, u32[]{:S(2)}) collective-permute-start(bf16[16,16,256]{2,1,0:T(8,128)(2,1)S(1)} %slice.59.refs_0_), channel_id=1, source_target_pairs={{0,2},{1,3},{2,0},{3,1},{4,6},{5,7},{6,4},{7,5},{8,10},{9,11},{10,... | collective-permute-start | bytes 393224 | tf_op jit(solution)/shard_map/ppermute | solution.py:663
  35.2 7.7 %collective-permute-start.8 = (bf16[16,16,256]{2,1,0:T(8,128)(2,1)S(1)}, bf16[16,16,256]{2,1,0:T(8,128)(2,1)S(1)}, u32[]{:S(2)}, u32[]{:S(2)}) collective-permute-start(bf16[16,16,256]{2,1,0:T(8,128)(2,1)S(1)} %slice.59.refs_0_), channel_id=1, source_target_pairs={{0,3},{1,2},{2,1},{3,0},{4,7},{5,6},{6,5},{7,4},{8,11},{9,10},{10,... | collective-permute-start | bytes 393224 | tf_op jit(solution)/shard_map/ppermute | solution.py:663
  36.4 14.3 %all-to-all-start.1 = ((bf16[16,32,256]{2,1,0:T(8,128)(2,1)}), bf16[16,32,256]{2,1,0:T(8,128)(2,1)S(1)}, u32[]{:S(2)}, u32[]{:S(2)}) async-start(bf16[16,32,256]{2,1,0:T(8,128)(2,1)} %get-tuple-element.110), calls=%async_computation.1 | async-start | bytes 524288 | tf_op jit(solution)/shard_map/all_to_all | solution.py:818
  42.2 8.5 %collective-permute-start.9 = (bf16[16,16,256]{2,1,0:T(8,128)(2,1)S(1)}, bf16[16,16,256]{2,1,0:T(8,128)(2,1)S(1)}, u32[]{:S(2)}, u32[]{:S(2)}) collective-permute-start(bf16[16,16,256]{2,1,0:T(8,128)(2,1)S(1)} %slice.59.refs_0_), channel_id=1, source_target_pairs={{0,16},{16,0},{1,17},{17,1},{2,18},{18,2},{3,19},{19,3},{4,20},{20... | collective-permute-start | bytes 393224 | tf_op jit(solution)/shard_map/ppermute | solution.py:680
  42.3 8.4 %collective-permute-start.10 = (bf16[16,16,256]{2,1,0:T(8,128)(2,1)S(1)}, bf16[16,16,256]{2,1,0:T(8,128)(2,1)S(1)}, u32[]{:S(2)}, u32[]{:S(2)}) collective-permute-start(bf16[16,16,256]{2,1,0:T(8,128)(2,1)S(1)} %collective-permute-done.6.refs_1_), channel_id=1, source_target_pairs={{0,16},{16,0},{1,17},{17,1},{2,18},{18,2},{3,19},{19,3},{4,20},{20... | collective-permute-start | bytes 393224 | tf_op jit(solution)/shard_map/ppermute | solution.py:680
  42.8 7.9 %collective-permute-start.11 = (bf16[16,16,256]{2,1,0:T(8,128)(2,1)S(1)}, bf16[16,16,256]{2,1,0:T(8,128)(2,1)S(1)}, u32[]{:S(2)}, u32[]{:S(2)}) collective-permute-start(bf16[16,16,256]{2,1,0:T(8,128)(2,1)S(1)} %collective-permute-done.7.refs_2_), channel_id=1, source_target_pairs={{0,16},{16,0},{1,17},{17,1},{2,18},{18,2},{3,19},{19,3},{4,20},{20... | collective-permute-start | bytes 393224 | tf_op jit(solution)/shard_map/ppermute | solution.py:680
  42.9 7.8 %collective-permute-start.12 = (bf16[16,16,256]{2,1,0:T(8,128)(2,1)S(1)}, bf16[16,16,256]{2,1,0:T(8,128)(2,1)S(1)}, u32[]{:S(2)}, u32[]{:S(2)}) collective-permute-start(bf16[16,16,256]{2,1,0:T(8,128)(2,1)S(1)} %collective-permute-done.8.refs_3_), channel_id=1, source_target_pairs={{0,16},{16,0},{1,17},{17,1},{2,18},{18,2},{3,19},{19,3},{4,20},{20... | collective-permute-start | bytes 393224 | tf_op jit(solution)/shard_map/ppermute | solution.py:680
  53.2 18.7 %all-to-all-start.2 = ((bf16[16,64,256]{2,1,0:T(8,128)(2,1)}), bf16[16,64,256]{2,1,0:T(8,128)(2,1)S(1)}, u32[]{:S(2)}, u32[]{:S(2)}) async-start(bf16[16,64,256]{2,1,0:T(8,128)(2,1)} %get-tuple-element.119), calls=%async_computation.2 | async-start | bytes 1048576 | tf_op jit(solution)/shard_map/all_to_all | solution.py:845
  56.9 9.3 %collective-permute-start.16 = (bf16[512,256]{1,0:T(8,128)(2,1)S(1)}, bf16[512,256]{1,0:T(8,128)(2,1)S(1)}, u32[]{:S(2)}, u32[]{:S(2)}) collective-permute-start(bf16[512,256]{1,0:T(8,128)(2,1)S(1)} %get-tuple-element.135), channel_id=1, source_target_pairs={{0,16},{16,0},{1,17},{17,1},{2,18},{18,2},{3,19},{19,3},{4,20},{20... | collective-permute-start | bytes 786440 | tf_op jit(solution)/shard_map/ppermute | solution.py:680
  57.0 9.2 %collective-permute-start.17 = (bf16[512,256]{1,0:T(8,128)(2,1)S(1)}, bf16[512,256]{1,0:T(8,128)(2,1)S(1)}, u32[]{:S(2)}, u32[]{:S(2)}) collective-permute-start(bf16[512,256]{1,0:T(8,128)(2,1)S(1)} %bitcast.19), channel_id=1, source_target_pairs={{0,16},{16,0},{1,17},{17,1},{2,18},{18,2},{3,19},{19,3},{4,20},{20... | collective-permute-start | bytes 786440 | tf_op jit(solution)/shard_map/ppermute | solution.py:680
  67.4 14.4 %collective-permute-start.18 = (f32[136,512]{1,0:T(8,128)S(1)}, f32[136,512]{1,0:T(8,128)S(1)}, u32[]{:S(2)}, u32[]{:S(2)}) collective-permute-start(f32[136,512]{1,0:T(8,128)S(1)} %get-tuple-element.139), channel_id=1, source_target_pairs={{0,1},{1,0},{2,3},{3,2},{4,5},{5,4},{6,7},{7,6},{8,9},{9,8},{10,11... | collective-permute-start | bytes 835592 | tf_op jit(solution)/shard_map/ppermute | solution.py:663
  69.1 14.4 %collective-permute-start.19 = (f32[136,512]{1,0:T(8,128)S(1)}, f32[136,512]{1,0:T(8,128)S(1)}, u32[]{:S(2)}, u32[]{:S(2)}) collective-permute-start(f32[136,512]{1,0:T(8,128)S(1)} %get-tuple-element.140), channel_id=1, source_target_pairs={{0,2},{1,3},{2,0},{3,1},{4,6},{5,7},{6,4},{7,5},{8,10},{9,11},{10,... | collective-permute-start | bytes 835592 | tf_op jit(solution)/shard_map/ppermute | solution.py:663
  70.6 13.2 %collective-permute-start.20 = (f32[136,512]{1,0:T(8,128)S(1)}, f32[136,512]{1,0:T(8,128)S(1)}, u32[]{:S(2)}, u32[]{:S(2)}) collective-permute-start(f32[136,512]{1,0:T(8,128)S(1)} %get-tuple-element.141), channel_id=1, source_target_pairs={{0,3},{1,2},{2,1},{3,0},{4,7},{5,6},{6,5},{7,4},{8,11},{9,10},{10,... | collective-permute-start | bytes 835592 | tf_op jit(solution)/shard_map/ppermute | solution.py:663
  79.1 6.9 %collective-permute-start.15 = (f32[2,32,128]{2,1,0:T(8,128)S(1)}, f32[2,32,128]{2,1,0:T(8,128)S(1)}, u32[]{:S(2)}, u32[]{:S(2)}) collective-permute-start(f32[2,32,128]{2,1,0:T(8,128)S(1)} %get-tuple-element.133), channel_id=1, source_target_pairs={{0,12},{1,13},{2,14},{3,15},{4,8},{5,9},{6,10},{7,11},{8,4},{9,5},... | collective-permute-start | bytes 98312 | tf_op jit(solution)/shard_map/ppermute | solution.py:663
  86.6 8.7 %collective-permute-start.22 = (f32[2,32,128]{2,1,0:T(8,128)S(1)}, f32[2,32,128]{2,1,0:T(8,128)S(1)}, u32[]{:S(2)}, u32[]{:S(2)}) collective-permute-start(f32[2,32,128]{2,1,0:T(8,128)S(1)} %add_add_fusion.1), channel_id=1, source_target_pairs={{0,1},{1,0},{2,3},{3,2},{4,5},{5,4},{6,7},{7,6},{8,9},{9,8},{10,11... | collective-permute-start | bytes 98312 | tf_op jit(solution)/shard_map/ppermute | solution.py:663
  88.2 7.1 %collective-permute-start.23 = (f32[2,32,128]{2,1,0:T(8,128)S(1)}, f32[2,32,128]{2,1,0:T(8,128)S(1)}, u32[]{:S(2)}, u32[]{:S(2)}) collective-permute-start(f32[2,32,128]{2,1,0:T(8,128)S(1)} %add_add_fusion.1), channel_id=1, source_target_pairs={{0,2},{1,3},{2,0},{3,1},{4,6},{5,7},{6,4},{7,5},{8,10},{9,11},{10,... | collective-permute-start | bytes 98312 | tf_op jit(solution)/shard_map/ppermute | solution.py:663
  (26 other events, 280.5 us)
